TPU v7x, 512 devices: a whole 4x8x8 slice. The times are simulated.
512 devices in a mesh: dp: 32 (over y_lo, x, core), tensor: 16 (over y_hi, z).
Axes of the slice: x: 4, y: 8 (y_hi: 2, y_lo: 4; y = y_hi * 4 + y_lo), z: 8, core: 2. Of those that a mesh axis runs over, the one named last changes fastest.
Arguments:
- hidden_in: bfloat16 [4096, 7168], P('dp', 'tensor'), may hold values from -6 to 6
- norm_gain: float32 [7168], replicated, may hold values from 0.1 to 1.9
- norm_bias: float32 [7168], replicated, may hold values from -3 to 3
- w_qkv: bfloat16 [7168, 6144], P('dp', 'tensor'), may hold values from -0.0625 to 0.0625
- b_qkv: float32 [6144], P('tensor'), may hold values from -3 to 3
- w_out: bfloat16 [2048, 7168], P('tensor', 'dp'), may hold values from -0.125 to 0.125
- out_grad: bfloat16 [4096, 7168], P('dp', 'tensor'), may hold values from -2 to 2
Outputs:
- grad_input: bfloat16 [4096, 7168], P('dp', 'tensor')
- grad_out_weight: float32 [2048, 7168], P('tensor', 'dp')
All inputs are finite; a program needn't handle non-finite values.
Results may differ from a plain program's by a relative error of at most 0.03.
Values may be sent and summed in bfloat16 or wider, within the bound.
No kernel may reach another device: no remote copies, remote signals or barrier semaphores. Data moves between devices by JAX's collectives and lax.ppermute only.
A program may use at most 64 MiB of HBM per device.

v0:
```python
import jax
import jax.numpy as jnp
from jax import lax
from jax.sharding import PartitionSpec as P

D = 7168
E = 128
HEADS_DEV = 1
SEQ = 128


norm_eps = 1e-05


def normalize(rows, norm_gain, norm_bias):
    rows_f = rows.astype(jnp.float32)
    center = rows_f - jnp.mean(rows_f, axis=-1, keepdims=True)
    inv_std = lax.rsqrt(jnp.mean(center * center, axis=-1, keepdims=True) + norm_eps)
    scaled = center * inv_std
    normed = (scaled * norm_gain + norm_bias).astype(jnp.bfloat16)
    return (scaled, inv_std, normed)


def body(hidden_in, norm_gain, norm_bias, w_qkv, b_qkv, w_out, out_grad):
    rows_full, grads_full = (
        lax.all_gather(hidden_in, "tensor", axis=1, tiled=True),
        lax.all_gather(out_grad, "tensor", axis=1, tiled=True),
    )
    joined_weight = lax.all_gather(w_qkv, "dp", axis=0, tiled=True)
    out_weight = lax.all_gather(w_out, "dp", axis=1, tiled=True)
    head_count = HEADS_DEV * lax.axis_size("tensor")
    first_head = lax.axis_index("tensor") * HEADS_DEV
    head_ids = first_head + jnp.arange(HEADS_DEV, dtype=jnp.int32)
    slopes = 2.0 ** (-8.0 * (head_ids + 1).astype(jnp.float32) / head_count)
    offsets = (jnp.arange(SEQ)[None, :] - jnp.arange(SEQ)[:, None]).astype(jnp.float32)
    causal = offsets <= 0.0
    scaled, inv_std, normed = normalize(rows_full, norm_gain, norm_bias)
    joined = (jnp.dot(normed, joined_weight, preferred_element_type=jnp.float32) + b_qkv).astype(
        jnp.bfloat16
    )
    joined = joined.reshape(SEQ, HEADS_DEV, 3, E)
    queries = joined[:, :, 0]
    key_rows = joined[:, :, 1]
    values = joined[:, :, 2]
    scores = jnp.einsum(
        "ihe,jhe->hij", queries, key_rows, preferred_element_type=jnp.float32
    ) * E ** (-0.5)
    scores = scores + slopes[:, None, None] * offsets[None]
    scores = jnp.where(causal[None], scores, -1e30)
    soft_weight = jax.nn.softmax(scores, axis=-1)
    soft_round = soft_weight.astype(jnp.bfloat16)
    context = jnp.einsum(
        "hij,jhe->ihe", soft_round, values, preferred_element_type=jnp.float32
    ).astype(jnp.bfloat16)
    out_three = out_weight.reshape(HEADS_DEV, E, D)
    context_grad = jnp.einsum(
        "id,hed->ihe", grads_full, out_three, preferred_element_type=jnp.float32
    ).astype(jnp.bfloat16)
    weight_part = jnp.einsum("ihe,id->hed", context, grads_full, preferred_element_type=jnp.float32)
    weight_part = weight_part.reshape(HEADS_DEV * E, D).astype(jnp.bfloat16)
    weight_total = lax.psum(weight_part, "dp").astype(jnp.float32)
    column_width = D // lax.axis_size("dp")
    grad_out_weight = lax.dynamic_slice_in_dim(
        weight_total, lax.axis_index("dp") * column_width, column_width, 1
    )
    prob_grad = jnp.einsum("ihe,jhe->hij", context_grad, values, preferred_element_type=jnp.float32)
    value_grad = jnp.einsum(
        "hij,ihe->jhe", soft_round, context_grad, preferred_element_type=jnp.float32
    )
    row_dot = jnp.sum(soft_weight * prob_grad, axis=-1, keepdims=True)
    score_grad = (soft_weight * (prob_grad - row_dot) * E ** (-0.5)).astype(jnp.bfloat16)
    query_grad = jnp.einsum(
        "hij,jhe->ihe", score_grad, key_rows, preferred_element_type=jnp.float32
    )
    key_grad = jnp.einsum("hij,ihe->jhe", score_grad, queries, preferred_element_type=jnp.float32)
    joined_grad = jnp.stack([query_grad, key_grad, value_grad], axis=2).astype(jnp.bfloat16)
    joined_grad = joined_grad.reshape(SEQ, HEADS_DEV * 3 * E)
    group_part = lax.dot_general(
        joined_grad, joined_weight, (((1,), (1,)), ((), ())), preferred_element_type=jnp.float32
    )
    group_part = group_part.astype(jnp.bfloat16)
    share_width = D // lax.axis_size("tensor")
    share_start = lax.axis_index("tensor") * share_width
    normed_grad = lax.psum(group_part, "tensor").astype(jnp.float32)
    scaled_grad = normed_grad * norm_gain
    mean_grad = jnp.mean(scaled_grad, axis=-1, keepdims=True)
    mean_cross = jnp.mean(scaled_grad * scaled, axis=-1, keepdims=True)
    whole_grad = inv_std * (scaled_grad - mean_grad - scaled * mean_cross)
    input_grad = lax.dynamic_slice_in_dim(whole_grad, share_start, share_width, 1)
    return (input_grad.astype(jnp.bfloat16), grad_out_weight)


def solution(mesh):
    in_specs = (
        P("dp", "tensor"),
        P(),
        P(),
        P("dp", "tensor"),
        P("tensor"),
        P("tensor", "dp"),
        P("dp", "tensor"),
    )
    out_specs = (P("dp", "tensor"), P("tensor", "dp"))
    return jax.shard_map(body, mesh=mesh, in_specs=in_specs, out_specs=out_specs, check_vma=False)
```

profile of v0, /device:TPU:1, one launch (start us, length us, event | category | flops | bytes accessed | tf_op | source)
XLA Modules:
  0.0 855.2 jit_solution(8694143914107634031)
XLA Ops:
  7.2 0.0 all-gather.5.cloned.1.call-start
  7.2 0.7 all-gather.5.cloned.1.call-update
  7.9 0.0 all-gather.9.cloned.1.call-start
  7.9 0.7 all-gather.9.cloned.1.call-update
  8.6 0.0 all-gather.11.cloned.1.call-start
  8.7 0.7 all-gather.11.cloned.1.call-update
  9.4 0.0 all-gather.7.cloned.1.call-start
  9.4 0.5 all-gather.7.cloned.1.call-update
  10.0 0.0 all-reduce.3.cloned.1.call-start
  10.1 102.6 %all-gather.5.cloned.1.call-done = bf16[128,7168]{0,1:T(8,128)(2,1)} async-done(((bf16[128,448]{0,1:T(8,128)(2,1)}), bf16[128,7168]{0,1:T(8,128)(2,1)}) %all-gather.5.cloned.1.call-update) | async-done | bytes 1835024 | tf_op jit(solution)/shard_map/all_gather | solution.py:26
  112.6 2.8 copy.17
  115.4 0.0 copy-start
  115.4 0.0 copy-start.1
  115.4 0.0 copy-start.2
  115.4 0.3 convert_reduce_fusion
  115.8 0.6 fusion.2
  116.4 95.6 %all-gather.9.cloned.1.call-done = bf16[128,7168]{0,1:T(8,128)(2,1)} async-done(((bf16[128,448]{0,1:T(8,128)(2,1)}), bf16[128,7168]{0,1:T(8,128)(2,1)}) %all-gather.9.cloned.1.call-update) | async-done | bytes 1835024 | tf_op jit(solution)/shard_map/all_gather | solution.py:27
  212.0 65.3 %all-gather.11.cloned.1.call-done = bf16[128,7168]{0,1:T(8,128)(2,1)} async-done(((bf16[128,224]{0,1:T(8,128)(2,1)}), bf16[128,7168]{0,1:T(8,128)(2,1)}) %all-gather.11.cloned.1.call-update) | async-done | bytes 1835024 | tf_op jit(solution)/shard_map/all_gather | solution.py:30
  277.4 2.7 convolution_convert_fusion.6
  280.1 66.4 %all-gather.7.cloned.1.call-done = bf16[7168,384]{1,0:T(8,128)(2,1)} async-done(((bf16[224,384]{1,0:T(8,128)(2,1)}), bf16[7168,384]{1,0:T(8,128)(2,1)}) %all-gather.7.cloned.1.call-update) | async-done | bytes 5505040 | tf_op jit(solution)/shard_map/all_gather | solution.py:29
  346.5 0.0 copy-done
  346.5 0.0 copy-done.1
  346.5 0.0 copy-done.2
  346.5 3.7 fusion.8
  350.2 0.1 copy.18
  350.4 0.2 fusion.28
  350.6 0.2 fusion.13
  350.8 0.2 multiply_reduce_fusion.1
  351.1 0.1 fusion.12
  351.2 0.2 fusion.11
  351.4 5.8 convolution_convert_fusion.1
  357.2 0.0 all-reduce.3.cloned.1.call-update
  357.2 0.0 all-reduce.5.cloned.1.call-start
  357.3 3.5 convolution_convert_fusion
  360.8 0.0 all-reduce.5.cloned.1.call-update
  360.8 191.0 %all-reduce.3.cloned.1.call-done = bf16[128,7168]{1,0:T(8,128)(2,1)} async-done(((bf16[128,7168]{1,0:T(8,128)(2,1)}), bf16[128,7168]{1,0:T(8,128)(2,1)}) %all-reduce.3.cloned.1.call-update) | async-done | bytes 1835024 | tf_op jit(solution)/shard_map/psum | solution.py:84
  551.8 2.6 fusion.6
  554.4 0.3 fusion.17
  554.7 0.8 copy.22
  555.5 291.4 %all-reduce.5.cloned.1.call-done = bf16[128,7168]{0,1:T(8,128)(2,1)} async-done(((bf16[128,7168]{0,1:T(8,128)(2,1)}), bf16[128,7168]{0,1:T(8,128)(2,1)}) %all-reduce.5.cloned.1.call-update) | async-done | bytes 1835024 | tf_op jit(solution)/shard_map/psum | solution.py:61
  846.9 1.5 dynamic-slice_convert_fusion
  (6 shorter events, 0.1 us)
Async XLA Ops:
  7.2 105.4 %all-gather.5.cloned.1.call-start = ((), (), s32[]{:S(2)}) async-start(), calls=%async_computation | async-start | bytes 1949696 | tf_op jit(solution)/shard_map/all_gather | solution.py:26
  7.9 204.1 %all-gather.9.cloned.1.call-start = ((), (), s32[]{:S(2)}) async-start(), calls=%async_computation.2 | async-start | bytes 1949696 | tf_op jit(solution)/shard_map/all_gather | solution.py:27
  8.6 268.7 %all-gather.11.cloned.1.call-start = ((), (), s32[]{:S(2)}) async-start(), calls=%async_computation.3 | async-start | bytes 1892352 | tf_op jit(solution)/shard_map/all_gather | solution.py:30
  9.4 337.1 %all-gather.7.cloned.1.call-start = ((), (), s32[]{:S(2)}) async-start(), calls=%async_computation.1 | async-start | bytes 5677056 | tf_op jit(solution)/shard_map/all_gather | solution.py:29
  10.0 541.8 %all-reduce.3.cloned.1.call-start = ((), (), s32[]{:S(2)}) async-start(), calls=%async_computation.4 | async-start | bytes 3670016 | tf_op jit(solution)/shard_map/psum | solution.py:84
  115.4 231.1 %copy-start = (f32[7168]{0:T(1024)S(1)}, f32[7168]{0:T(1024)}, u32[]{:S(2)}) copy-start(f32[7168]{0:T(1024)} %param.8) | copy-start | bytes 86020
  115.4 231.1 %copy-start.1 = (f32[7168]{0:T(1024)S(1)}, f32[7168]{0:T(1024)}, u32[]{:S(2)}) copy-start(f32[7168]{0:T(1024)} %param.9) | copy-start | bytes 86020
  115.4 231.1 %copy-start.2 = (f32[384]{0:T(512)S(1)}, f32[384]{0:T(512)}, u32[]{:S(2)}) copy-start(f32[384]{0:T(512)} %param.11) | copy-start | bytes 4612
  357.2 489.7 %all-reduce.5.cloned.1.call-start = ((), (), s32[]{:S(2)}) async-start(), calls=%async_computation.5 | async-start | bytes 3670016 | tf_op jit(solution)/shard_map/psum | solution.py:61
Sparse Core Ops, SparseCore 0:
  11.2 101.3 all-gather.4
  115.8 96.1 all-gather.8
  214.2 63.1 all-gather.10
  279.4 67.0 all-gather.6
  357.3 194.3 all-reduce.2
  554.8 292.0 all-reduce.4
where the time goes:
time: 856 us; the launch traced here: 855 us
  waiting for transfers between devices  815 us (95%)
  matrix products  16.7 us (2%)
  between operations  14.2 us (2%)
    psum x1, waiting for transfers between devices, body(): weight_total = lax.psum(weight_part, 'dp').astype(jnp.float32)  291 us
    psum x1, waiting for transfers between devices, body(): normed_grad = lax.psum(group_part, 'tensor').astype(jnp.float32)  191 us
    all_gather x1, waiting for transfers between devices, body(): lax.all_gather(hidden_in, 'tensor', axis=1, tiled=True)  103 us
    all_gather x1, waiting for transfers between devices, body(): lax.all_gather(out_grad, 'tensor', axis=1, tiled=True)  95.6 us
    all_gather x1, waiting for transfers between devices, body(): joined_weight = lax.all_gather(w_qkv, 'dp', axis=0, tiled=True)  66.4 us
    all_gather x1, waiting for transfers between devices, body(): out_weight = lax.all_gather(w_out, 'dp', axis=1, tiled=True)  65.3 us
  transfers between devices with their start and end apart: 6, of which 6 were waited for; matrix products, arithmetic and copies ran while one was open for 2% of the time, Pallas kernels for 0%

commit v1 on v0

v1 whole, which is shorter than its diff:
```python
import jax
import jax.numpy as jnp
from jax import lax
from jax.sharding import PartitionSpec as P

SEQ = 128
E = 128
norm_eps = 1e-05
f32 = jnp.float32
bf16 = jnp.bfloat16


def groups(count, key):
    found = {}
    for i in range(count):
        found.setdefault(key(i), []).append(i)
    return [found[k] for k in sorted(found)]


def swap_cores(x):
    n = lax.axis_size("dp")
    return lax.ppermute(x, "dp", [(i, i ^ 1) for i in range(n)])


def split(x):
    high = lax.reduce_precision(x, 8, 7)
    return high.astype(bf16), (x - high).astype(bf16)


def dot(a, b, dims):
    return lax.dot_general(a, b, (dims, ((), ())), preferred_element_type=f32)


def attention(joined, context_grad, slope):
    queries = joined[:, :E]
    key_rows = joined[:, E : 2 * E]
    values = joined[:, 2 * E :]
    scores = dot(queries, key_rows, ((1,), (1,))) * E ** (-0.5)
    row = lax.broadcasted_iota(jnp.int32, (SEQ, SEQ), 0)
    col = lax.broadcasted_iota(jnp.int32, (SEQ, SEQ), 1)
    offsets = (col - row).astype(f32)
    scores = jnp.where(offsets <= 0.0, scores + slope * offsets, -1e30)
    soft = jax.nn.softmax(scores, axis=-1)
    soft_round = soft.astype(bf16)
    context = dot(soft_round, values, ((1,), (0,))).astype(bf16)
    prob_grad = dot(context_grad, values, ((1,), (1,)))
    value_grad = dot(soft_round, context_grad, ((0,), (0,)))
    row_dot = jnp.sum(soft * prob_grad, axis=-1, keepdims=True)
    score_grad = (soft * (prob_grad - row_dot) * E ** (-0.5)).astype(bf16)
    query_grad = dot(score_grad, key_rows, ((1,), (0,)))
    key_grad = dot(score_grad, queries, ((0,), (0,)))
    joined_grad = jnp.concatenate([query_grad, key_grad, value_grad], axis=1).astype(bf16)
    return context, joined_grad


def body(hidden_in, norm_gain, norm_bias, w_qkv, b_qkv, w_out, out_grad):
    n_dp, n_tensor = lax.axis_size("dp"), lax.axis_size("tensor")
    depth = norm_gain.shape[0]
    width = depth // n_tensor
    part = width // 2
    core = lax.axis_index("dp") % 2
    rank = lax.axis_index("tensor")
    chips = groups(n_dp, lambda i: i % 2)

    weight_block = jnp.concatenate([w_qkv, w_out.T], axis=1)
    weights = lax.all_gather(weight_block, "dp", axis=0, tiled=True, axis_index_groups=chips)

    hidden_t = hidden_in.T
    acts = jnp.concatenate([hidden_t, out_grad.T], axis=1).reshape(2, part, 2 * SEQ)
    mine = jnp.where(core == 0, acts[0], acts[1])
    other = swap_cores(jnp.where(core == 0, acts[1], acts[0]))
    block = jnp.concatenate([mine[:, :SEQ], other[:, :SEQ], mine[:, SEQ:], other[:, SEQ:]], axis=1)
    rows = lax.all_to_all(
        jnp.broadcast_to(block[None], (n_tensor, part, 4 * SEQ)), "tensor", 0, 0, tiled=True
    ).reshape(n_tensor * part, 4 * SEQ)
    hidden = rows[:, : 2 * SEQ].astype(f32)
    grads = rows[:, 2 * SEQ :]

    half = depth // 2
    mean_half = jnp.sum(hidden, axis=0) / half
    square_half = jnp.sum((hidden - mean_half) ** 2, axis=0)
    stats = jnp.stack([mean_half, square_half])
    stats_other = swap_cores(stats)
    stats_other = jnp.concatenate([stats_other[:, SEQ:], stats_other[:, :SEQ]], axis=1)
    mean = 0.5 * (mean_half + stats_other[0])
    square = square_half + stats_other[1] + (mean_half - stats_other[0]) ** 2 * (half / 2)
    inv_std = lax.rsqrt(square / depth + norm_eps)

    def own_half(vector):
        pair = vector.reshape(n_tensor, 2, part)
        return jnp.where(core == 0, pair[:, 0], pair[:, 1]).reshape(half)

    gain, bias = own_half(norm_gain), own_half(norm_bias)
    normed = ((hidden - mean) * inv_std * gain[:, None] + bias[:, None]).astype(bf16)
    joined_weight = weights[:, : 3 * E]
    out_weight = weights[:, 3 * E :]
    joined_part = dot(normed, joined_weight, ((0,), (0,)))
    context_grad_part = dot(grads, out_weight, ((0,), (0,)))
    gain_high, gain_low = split(gain)
    bias_high, bias_low = split(bias)
    vectors = dot(jnp.stack([gain_high, gain_low, bias_high, bias_low]), joined_weight, ((1,), (0,)))
    gain_weight = vectors[0] + vectors[1]
    bias_weight = vectors[2] + vectors[3]

    parts = jnp.concatenate([joined_part, context_grad_part], axis=1)
    whole = parts[:SEQ] + swap_cores(parts[SEQ:])
    joined = (whole[:, : 3 * E] + b_qkv).astype(bf16)
    context_grad = whole[:, 3 * E :].astype(bf16)
    slope = 2.0 ** (-8.0 * (rank + 1).astype(f32) / n_tensor)
    context, joined_grad = attention(joined, context_grad, slope)

    context = jnp.concatenate([context, swap_cores(context)], axis=0)
    weight_part = dot(grads, context, ((1,), (0,))).astype(bf16)
    weight_parts = lax.all_to_all(
        weight_part.reshape(n_tensor, part, E), "dp", 0, 0, tiled=True, axis_index_groups=chips
    )
    grad_out_weight = jnp.sum(weight_parts.astype(f32), axis=0).T

    joined_grad = jnp.concatenate([joined_grad, swap_cores(joined_grad)], axis=0)
    group_part = dot(joined_weight, joined_grad, ((1,), (1,))).astype(bf16)
    joined_grad_f = joined_grad.astype(f32)
    sum_grad = jnp.sum(joined_grad_f * gain_weight, axis=1)
    sum_cross = jnp.sum(joined_grad_f * (joined_part - bias_weight), axis=1)
    extra = jnp.stack([*split(sum_grad), *split(sum_cross)])
    extra = jnp.concatenate([extra, jnp.zeros((12, 2 * SEQ), bf16)])
    extra = jnp.broadcast_to(extra[None], (n_tensor, 16, 2 * SEQ))
    payload = jnp.concatenate([group_part.reshape(n_tensor, part, 2 * SEQ), extra], axis=1)
    group_parts = lax.all_to_all(payload, "tensor", 0, 0, tiled=True)
    total = jnp.sum(group_parts.astype(f32), axis=0)
    total_other = swap_cores(total[:, SEQ:])
    total = total[:, :SEQ]
    normed_grad = jnp.where(
        core == 0,
        jnp.concatenate([total[:part], total_other[:part]]),
        jnp.concatenate([total_other[:part], total[:part]]),
    )
    sums = total[part:] + total_other[part:]
    mean_grad = (sums[0] + sums[1]) / depth
    mean_cross = (sums[2] + sums[3]) / depth

    own_gain = lax.dynamic_slice_in_dim(norm_gain, rank * width, width)
    scaled_grad = normed_grad * own_gain[:, None]
    scaled = (hidden_t.astype(f32) - mean[:SEQ]) * inv_std[:SEQ]
    input_grad = inv_std[:SEQ] * (scaled_grad - mean_grad - scaled * mean_cross)
    return input_grad.astype(bf16).T, grad_out_weight


def solution(mesh):
    in_specs = (
        P("dp", "tensor"),
        P(),
        P(),
        P("dp", "tensor"),
        P("tensor"),
        P("tensor", "dp"),
        P("dp", "tensor"),
    )
    out_specs = (P("dp", "tensor"), P("tensor", "dp"))
    return jax.shard_map(body, mesh=mesh, in_specs=in_specs, out_specs=out_specs, check_vma=False)
```

time: 856 us -> 331 us (0.39)
  the two profiles are of different devices: /device:TPU:1 before, /device:TPU:72 now
where the time goes in v1:
time: 331 us; the launch traced here: 330 us
  waiting for transfers between devices  232 us (70%)
  starting transfers between devices  56.5 us (17%)
  between operations  14.5 us (4%)
  matrix products  13.9 us (4%)
  other arithmetic  9.7 us (3%)
  local copies, waits for them, and re-layouts  3.31 us (1%)
    all_to_all x1, waiting for transfers between devices, body(): lax.all_to_all(jnp.broadcast_to(block[None], (n_tensor, part, 4 * SEQ)),...  134 us
    all_to_all x1, waiting for transfers between devices, body(): group_parts = lax.all_to_all(payload, 'tensor', 0, 0, tiled=True)  40.1 us
    all_gather x1, waiting for transfers between devices, body(): lax.all_gather(weight_block, 'dp', axis=0, tiled=True, axis_index_groups=...  32.6 us
    all_to_all x1, starting transfers between devices, body(): lax.all_to_all(weight_part.reshape(n_tensor, part, E), 'dp', 0, 0, tiled=...  26.5 us
    all_to_all x1, waiting for transfers between devices, body(): lax.all_to_all(weight_part.reshape(n_tensor, part, E), 'dp', 0, 0, tiled=...  20.5 us
    all_to_all x1, starting transfers between devices, body(): lax.all_to_all(jnp.broadcast_to(block[None], (n_tensor, part, 4 * SEQ)),...  14.5 us
    dot_general x11, matrix products, dot(): return lax.dot_general(a, b, (dims, ((), ())), preferred_element_type=f32)  13.9 us
    ppermute x6, starting transfers between devices, swap_cores(): return lax.ppermute(x, 'dp', [(i, i ^ 1) for i in range(n)])  11.9 us
  transfers between devices with their start and end apart: 10, of which 8 were waited for; matrix products, arithmetic and copies ran while one was open for 4% of the time, Pallas kernels for 0%

profile of v1, /device:TPU:72, one launch (start us, length us, event | category | flops | bytes accessed | tf_op | source)
XLA Modules:
  0.0 329.8 jit_solution(2619494523476802553)
XLA Ops:
  7.2 1.0 broadcast_select_fusion.1
  8.2 1.9 collective-permute-start
  10.1 1.3 collective-permute-done
  11.5 2.2 broadcast_in_dim.9
  13.7 14.5 %all-to-all-start = ((bf16[16,224,512]{2,1,0:T(8,128)(2,1)}), bf16[16,224,512]{2,1,0:T(8,128)(2,1)}, u32[]{:S(2)}, u32[]{:S(2)}) async-start(bf16[16,224,512]{2,1,0:T(8,128)(2,1)} %broadcast_in_dim.9), calls=%async_computation | async-start | bytes 7340032 | tf_op jit(solution)/shard_map/all_to_all | solution.py:73
  28.2 0.7 pad_maximum_fusion.3
  29.0 0.1 reshape.192
  29.1 0.1 reshape.193
  29.2 0.1 fusion.54
  29.3 0.1 select_n.97
  29.4 0.1 select_n.101
  29.5 0.1 select_n.99
  29.6 0.1 select_n.102
  29.8 134.3 %all-to-all-done = bf16[16,224,512]{2,1,0:T(8,128)(2,1)} async-done(((bf16[16,224,512]{2,1,0:T(8,128)(2,1)}), bf16[16,224,512]{2,1,0:T(8,128)(2,1)}, u32[]{:S(2)}, u32[]{:S(2)}) %all-to-all-start) | async-done | bytes 3670048 | tf_op jit(solution)/shard_map/all_to_all | solution.py:73
  164.1 2.0 convert_reduce_fusion
  166.1 2.0 fusion.1
  168.2 1.9 collective-permute-start.1
  170.1 32.6 %all-gather.2.cloned.1.call-done = bf16[3584,512]{1,0:T(8,128)(2,1)} async-done(((bf16[224,512]{1,0:T(8,128)(2,1)}), bf16[3584,512]{1,0:T(8,128)(2,1)}) %all-gather.2.cloned.1.call-update) | async-done | bytes 3670032 | tf_op jit(solution)/shard_map/all_gather | solution.py:66
  202.7 2.6 fusion.17
  205.3 0.3 copy-done.6
  205.5 3.8 %fusion.9 = f32[256,384]{1,0:T(8,128)S(1)} fusion(bf16[3584,512]{1,0:T(8,128)(2,1)S(1)} %copy-done.6, f32[3584]{0:T(1024)S(1)} %select_n.99, f32[3584]{0:T(1024)S(1)} %select_n.97, f32[256]{0:T(256)S(1)} %bitcast.40, f32[256]{0:T(256)S(1)} %bitcast.39, bf16[3584,512]{1,0:T(8,128)(2,1)} %bitcast.2), kind=kOutput, calls=%fused_computation.15 | convolution fusion | flops 710148096 | bytes 5015552 | tf_op jit(solution)/shard_map/dot_general | solution.py:31
  209.4 1.9 collective-permute-start.2
  211.3 0.5 fusion.6
  211.8 1.0 collective-permute-done.2
  212.9 0.2 fusion.77
  213.1 0.2 multiply_reduce_fusion
  213.3 0.2 convolution_convert_fusion.5
  213.5 0.1 convolution_convert_fusion.4
  213.6 0.1 convolution_convert_fusion.3
  213.8 2.0 collective-permute-start.3
  215.9 1.1 collective-permute-done.3
  217.0 0.2 fusion.24
  217.2 0.2 concatenate.44
  217.4 2.9 convolution_convert_fusion
  220.3 1.5 pad_maximum_fusion
  221.8 3.6 %all-to-all-start.1 = ((bf16[16,240,256]{2,1,0:T(8,128)(2,1)}), bf16[16,240,256]{2,1,0:T(8,128)(2,1)S(1)}, u32[]{:S(2)}, u32[]{:S(2)}) async-start(bf16[16,240,256]{2,1,0:T(8,128)(2,1)} %pad_maximum_fusion), calls=%async_computation.1 | async-start | bytes 3932160 | tf_op jit(solution)/shard_map/all_to_all | solution.py:128
  225.4 0.2 convolution_convert_fusion.2
  225.6 2.2 collective-permute-start.5
  227.8 1.0 collective-permute-done.5
  228.8 3.1 convolution_convert_fusion.1
  231.9 40.1 %all-to-all-done.1 = bf16[16,240,256]{2,1,0:T(8,128)(2,1)S(1)} async-done(((bf16[16,240,256]{2,1,0:T(8,128)(2,1)}), bf16[16,240,256]{2,1,0:T(8,128)(2,1)S(1)}, u32[]{:S(2)}, u32[]{:S(2)}) %all-to-all-start.1) | async-done | bytes 1966112 | tf_op jit(solution)/shard_map/all_to_all | solution.py:128
  272.1 26.5 %all-to-all-start.2 = ((bf16[16,224,128]{2,1,0:T(8,128)(2,1)}), bf16[16,224,128]{2,1,0:T(8,128)(2,1)S(1)}, u32[]{:S(2)}, u32[]{:S(2)}) async-start(bf16[16,224,128]{2,1,0:T(8,128)(2,1)} %bitcast.25), calls=%async_computation.2 | async-start | bytes 1835008 | tf_op jit(solution)/shard_map/all_to_all | solution.py:114
  298.5 0.1 dynamic_slice.3
  298.6 0.3 convert_reduce_fusion.1
  298.9 1.9 collective-permute-start.4
  300.9 20.5 %all-to-all-done.2 = bf16[16,224,128]{2,1,0:T(8,128)(2,1)S(1)} async-done(((bf16[16,224,128]{2,1,0:T(8,128)(2,1)}), bf16[16,224,128]{2,1,0:T(8,128)(2,1)S(1)}, u32[]{:S(2)}, u32[]{:S(2)}) %all-to-all-start.2) | async-done | bytes 917536 | tf_op jit(solution)/shard_map/all_to_all | solution.py:114
  321.3 0.8 convert_reduce_fusion.2
  322.2 0.8 fusion.34
  (46 shorter events, 0.5 us)
Async XLA Ops:
  8.2 3.2 collective-permute-start
  13.7 14.5 %copy-start.1 = (bf16[224,384]{1,0:T(8,128)(2,1)S(1)}, bf16[224,384]{1,0:T(8,128)(2,1)}, u32[]{:S(2)}) copy-start(bf16[224,384]{1,0:T(8,128)(2,1)} %param.10) | copy-start | bytes 516100
  13.7 14.6 %copy-start.2 = (bf16[128,224]{0,1:T(8,128)(2,1)S(1)}, bf16[128,224]{0,1:T(8,128)(2,1)}, u32[]{:S(2)}) copy-start(bf16[128,224]{0,1:T(8,128)(2,1)} %param.12) | copy-start | bytes 172036
  13.7 15.3 %copy-start.3 = (f32[7168]{0:T(1024)S(1)}, f32[7168]{0:T(1024)}, u32[]{:S(2)}) copy-start(f32[7168]{0:T(1024)} %param.8) | copy-start | bytes 86020
  13.7 15.4 %copy-start.4 = (f32[7168]{0:T(1024)S(1)}, f32[7168]{0:T(1024)}, u32[]{:S(2)}) copy-start(f32[7168]{0:T(1024)} %param.9) | copy-start | bytes 86020
  13.7 150.5 %all-to-all-start = ((bf16[16,224,512]{2,1,0:T(8,128)(2,1)}), bf16[16,224,512]{2,1,0:T(8,128)(2,1)}, u32[]{:S(2)}, u32[]{:S(2)}) async-start(bf16[16,224,512]{2,1,0:T(8,128)(2,1)} %broadcast_in_dim.9), calls=%async_computation | async-start | bytes 7340032 | tf_op jit(solution)/shard_map/all_to_all | solution.py:73
  28.2 174.5 %all-gather.2.cloned.1.call-start = ((), (), s32[]{:S(2)}) async-start(), calls=%async_computation.3 | async-start | bytes 3899392 | tf_op jit(solution)/shard_map/all_gather | solution.py:66
  168.2 37.1 %collective-permute-start.1 = (f32[2,256]{1,0:T(2,128)S(1)}, f32[2,256]{1,0:T(2,128)S(1)}, u32[]{:S(2)}, u32[]{:S(2)}) collective-permute-start(f32[2,256]{1,0:T(2,128)S(1)} %pad_maximum_fusion.7), channel_id=1, source_target_pairs={{0,16},{16,0},{32,48},{48,32},{64,80},{80,64},{96,112},{112,96},{1... | collective-permute-start | bytes 6152 | tf_op jit(solution)/shard_map/ppermute | solution.py:22
  202.6 2.9 copy-start.6
  209.3 3.5 %copy-start.5 = (f32[384]{0:T(512)S(1)}, f32[384]{0:T(512)}, u32[]{:S(2)}) copy-start(f32[384]{0:T(512)} %param.11) | copy-start | bytes 4612
  209.4 3.4 %collective-permute-start.2 = (f32[128,512]{1,0:T(8,128)S(1)}, f32[128,512]{1,0:T(8,128)S(1)}, u32[]{:S(2)}, u32[]{:S(2)}) collective-permute-start(f32[128,512]{1,0:T(8,128)S(1)} %pad_maximum_fusion.1), channel_id=1, source_target_pairs={{0,16},{16,0},{32,48},{48,32},{64,80},{80,64},{96,112},{112,96},{1... | collective-permute-start | bytes 786440 | tf_op jit(solution)/shard_map/ppermute | solution.py:22
  213.8 3.2 collective-permute-start.3
  221.8 50.3 %all-to-all-start.1 = ((bf16[16,240,256]{2,1,0:T(8,128)(2,1)}), bf16[16,240,256]{2,1,0:T(8,128)(2,1)S(1)}, u32[]{:S(2)}, u32[]{:S(2)}) async-start(bf16[16,240,256]{2,1,0:T(8,128)(2,1)} %pad_maximum_fusion), calls=%async_computation.1 | async-start | bytes 3932160 | tf_op jit(solution)/shard_map/all_to_all | solution.py:128
  225.6 96.6 %copy-start = (bf16[128,448]{0,1:T(8,128)(2,1)S(1)}, bf16[128,448]{0,1:T(8,128)(2,1)}, u32[]{:S(2)}) copy-start(bf16[128,448]{0,1:T(8,128)(2,1)} %param.7) | copy-start | bytes 344068
  225.6 3.2 collective-permute-start.5
  272.1 49.3 %all-to-all-start.2 = ((bf16[16,224,128]{2,1,0:T(8,128)(2,1)}), bf16[16,224,128]{2,1,0:T(8,128)(2,1)S(1)}, u32[]{:S(2)}, u32[]{:S(2)}) async-start(bf16[16,224,128]{2,1,0:T(8,128)(2,1)} %bitcast.25), calls=%async_computation.2 | async-start | bytes 1835008 | tf_op jit(solution)/shard_map/all_to_all | solution.py:114
  298.9 23.2 %collective-permute-start.4 = (f32[240,128]{1,0:T(8,128)S(1)}, f32[240,128]{1,0:T(8,128)S(1)}, u32[]{:S(2)}, u32[]{:S(2)}) collective-permute-start(f32[240,128]{1,0:T(8,128)S(1)} %slice.202), channel_id=1, source_target_pairs={{0,16},{16,0},{32,48},{48,32},{64,80},{80,64},{96,112},{112,96},{1... | collective-permute-start | bytes 368648 | tf_op jit(solution)/shard_map/ppermute | solution.py:22
Sparse Core Ops, SparseCore 0:
  31.1 171.5 all-gather.1

commit v2 on v1

--- a/solution.py
+++ b/solution.py
@@ -5,6 +5,7 @@
 
 SEQ = 128
 E = 128
+Z_COUNT = 8
 norm_eps = 1e-05
 f32 = jnp.float32
 bf16 = jnp.bfloat16
@@ -20,6 +21,31 @@
 def swap_cores(x):
     n = lax.axis_size("dp")
     return lax.ppermute(x, "dp", [(i, i ^ 1) for i in range(n)])
+
+
+def ring_gather(own, z_count):
+    n = lax.axis_size("tensor")
+    rank = lax.axis_index("tensor")
+
+    def shift(x, step):
+        return lax.ppermute(
+            x, "tensor", [(i, i - i % z_count + (i + step) % z_count) for i in range(n)]
+        )
+
+    far = lax.ppermute(own, "tensor", [(i, (i + z_count) % n) for i in range(n)])
+    first = rank < z_count
+    pair = jnp.stack([jnp.where(first, own, far), jnp.where(first, far, own)])
+    found = {0: pair}
+    up = down = pair
+    for step in range(1, z_count // 2):
+        up, down = shift(up, 1), shift(down, -1)
+        found[step], found[z_count - step] = up, down
+    found[z_count // 2] = jnp.concatenate([shift(up[:1], 1), shift(down[1:], -1)])
+    blocks = [found[z_count - 1 - j] for j in range(z_count)]
+    line = jnp.stack(blocks + blocks[:-1], axis=1)
+    z = rank % z_count
+    line = lax.dynamic_slice_in_dim(line, z_count - 1 - z, z_count, 1)
+    return line.reshape(n * own.shape[0], own.shape[1])
 
 
 def split(x):
@@ -69,12 +95,8 @@
     acts = jnp.concatenate([hidden_t, out_grad.T], axis=1).reshape(2, part, 2 * SEQ)
     mine = jnp.where(core == 0, acts[0], acts[1])
     other = swap_cores(jnp.where(core == 0, acts[1], acts[0]))
-    block = jnp.concatenate([mine[:, :SEQ], other[:, :SEQ], mine[:, SEQ:], other[:, SEQ:]], axis=1)
-    rows = lax.all_to_all(
-        jnp.broadcast_to(block[None], (n_tensor, part, 4 * SEQ)), "tensor", 0, 0, tiled=True
-    ).reshape(n_tensor * part, 4 * SEQ)
-    hidden = rows[:, : 2 * SEQ].astype(f32)
-    grads = rows[:, 2 * SEQ :]
+    hidden = ring_gather(jnp.concatenate([mine[:, :SEQ], other[:, :SEQ]], axis=1), Z_COUNT).astype(f32)
+    grads = ring_gather(jnp.concatenate([mine[:, SEQ:], other[:, SEQ:]], axis=1), Z_COUNT)
 
     half = depth // 2
     mean_half = jnp.sum(hidden, axis=0) / half
@@ -111,6 +133,7 @@
 
     context = jnp.concatenate([context, swap_cores(context)], axis=0)
     weight_part = dot(grads, context, ((1,), (0,))).astype(bf16)
+    weight_part, joined_grad = lax.optimization_barrier((weight_part, joined_grad))
     weight_parts = lax.all_to_all(
         weight_part.reshape(n_tensor, part, E), "dp", 0, 0, tiled=True, axis_index_groups=chips
     )

time: 331 us -> 224 us (0.68)
  the two profiles are of different devices: /device:TPU:72 before, /device:TPU:112 now
where the time goes in v2:
time: 224 us; the launch traced here: 223 us
  starting transfers between devices  95.8 us (43%)
  blocking collectives  57.1 us (25%)
  waiting for transfers between devices  30.6 us (14%)
  between operations  15.1 us (7%)
  matrix products  10.3 us (5%)
  other arithmetic  9.89 us (4%)
  local copies, waits for them, and re-layouts  3.98 us (2%)
    ppermute x16, starting transfers between devices, shift(): lax.ppermute(x, 'tensor', [(i, i - i % z_count + (i + step) % z_count) fo...  58.8 us
    all_to_all x1, blocking collectives, body(): group_parts = lax.all_to_all(payload, 'tensor', 0, 0, tiled=True)  57.1 us
    all_to_all x1, waiting for transfers between devices, body(): lax.all_to_all(weight_part.reshape(n_tensor, part, E), 'dp', 0, 0, tiled=...  19.2 us
    all_to_all x1, starting transfers between devices, body(): lax.all_to_all(weight_part.reshape(n_tensor, part, E), 'dp', 0, 0, tiled=...  15.5 us
    ppermute x6, starting transfers between devices, swap_cores(): return lax.ppermute(x, 'dp', [(i, i ^ 1) for i in range(n)])  11.8 us
    dot_general x11, matrix products, dot(): return lax.dot_general(a, b, (dims, ((), ())), preferred_element_type=f32)  10.3 us
    ppermute x2, starting transfers between devices, ring_gather(): lax.ppermute(own, 'tensor', [(i, (i + z_count) % n) for i in range(n)])  9.75 us
  transfers between devices with their start and end apart: 26, of which 7 were waited for; matrix products, arithmetic and copies ran while one was open for 5% of the time, Pallas kernels for 0%

profile of v2, /device:TPU:112, one launch (start us, length us, event | category | flops | bytes accessed | tf_op | source)
XLA Modules:
  0.0 222.8 jit_solution(6039615616634864961)
XLA Ops:
  7.2 1.0 broadcast_select_fusion.1
  8.2 1.9 collective-permute-start
  10.2 1.7 pad_maximum_fusion.3
  11.9 0.8 reshape.199
  12.7 0.8 reshape.200
  14.0 3.8 %collective-permute-start.1 = (bf16[224,256]{1,0:T(8,128)(2,1)S(1)}, bf16[224,256]{1,0:T(8,128)(2,1)S(1)}, u32[]{:S(2)}, u32[]{:S(2)}) collective-permute-start(bf16[224,256]{1,0:T(8,128)(2,1)S(1)} %pad_maximum_fusion.6), channel_id=1, source_target_pairs={{0,8},{1,9},{2,10},{3,11},{4,12},{5,13},{6,14},{7,15},{8,0},{9,1},... | collective-permute-start | bytes 344072 | tf_op jit(solution)/shard_map/ppermute | solution.py:35
  17.9 5.9 %collective-permute-start.11 = (bf16[224,256]{1,0:T(8,128)(2,1)S(1)}, bf16[224,256]{1,0:T(8,128)(2,1)S(1)}, u32[]{:S(2)}, u32[]{:S(2)}) collective-permute-start(bf16[224,256]{1,0:T(8,128)(2,1)S(1)} %pad_maximum_fusion.7), channel_id=1, source_target_pairs={{0,8},{1,9},{2,10},{3,11},{4,12},{5,13},{6,14},{7,15},{8,0},{9,1},... | collective-permute-start | bytes 344072 | tf_op jit(solution)/shard_map/ppermute | solution.py:35
  23.8 4.4 %collective-permute-done.1 = bf16[224,256]{1,0:T(8,128)(2,1)S(1)} collective-permute-done((bf16[224,256]{1,0:T(8,128)(2,1)S(1)}, bf16[224,256]{1,0:T(8,128)(2,1)S(1)}, u32[]{:S(2)}, u32[]{:S(2)}) %collective-permute-start.1) | collective-permute-done | bytes 114720 | tf_op jit(solution)/shard_map/ppermute | solution.py:35
  28.2 1.9 collective-permute-start.2
  30.2 4.3 %collective-permute-start.5 = (bf16[2,224,256]{2,1,0:T(8,128)(2,1)S(1)}, bf16[2,224,256]{2,1,0:T(8,128)(2,1)S(1)}, u32[]{:S(2)}, u32[]{:S(2)}) collective-permute-start(bf16[2,224,256]{2,1,0:T(8,128)(2,1)S(1)} %pad_maximum_fusion.2), channel_id=1, source_target_pairs={{0,1},{1,2},{2,3},{3,4},{4,5},{5,6},{6,7},{7,0},{8,9},{9,10},{10,1... | collective-permute-start | bytes 688136 | tf_op jit(solution)/shard_map/ppermute | solution.py:31
  34.6 8.2 %collective-permute-start.12 = (bf16[2,224,256]{2,1,0:T(8,128)(2,1)S(1)}, bf16[2,224,256]{2,1,0:T(8,128)(2,1)S(1)}, u32[]{:S(2)}, u32[]{:S(2)}) collective-permute-start(bf16[2,224,256]{2,1,0:T(8,128)(2,1)S(1)} %pad_maximum_fusion.4), channel_id=1, source_target_pairs={{0,7},{1,0},{2,1},{3,2},{4,3},{5,4},{6,5},{7,6},{8,15},{9,8},{10,9... | collective-permute-start | bytes 688136 | tf_op jit(solution)/shard_map/ppermute | solution.py:31
  43.0 1.9 collective-permute-start.15
  45.0 5.1 %collective-permute-start.3 = (bf16[2,224,256]{2,1,0:T(8,128)(2,1)S(1)}, bf16[2,224,256]{2,1,0:T(8,128)(2,1)S(1)}, u32[]{:S(2)}, u32[]{:S(2)}) collective-permute-start(bf16[2,224,256]{2,1,0:T(8,128)(2,1)S(1)} %collective-permute-done.2), channel_id=1, source_target_pairs={{0,7},{1,0},{2,1},{3,2},{4,3},{5,4},{6,5},{7,6},{8,15},{9,8},{10,9... | collective-permute-start | bytes 688136 | tf_op jit(solution)/shard_map/ppermute | solution.py:31
  50.1 1.9 collective-permute-start.6
  52.1 5.1 %collective-permute-start.13 = (bf16[2,224,256]{2,1,0:T(8,128)(2,1)S(1)}, bf16[2,224,256]{2,1,0:T(8,128)(2,1)S(1)}, u32[]{:S(2)}, u32[]{:S(2)}) collective-permute-start(bf16[2,224,256]{2,1,0:T(8,128)(2,1)S(1)} %collective-permute-done.12), channel_id=1, source_target_pairs={{0,7},{1,0},{2,1},{3,2},{4,3},{5,4},{6,5},{7,6},{8,15},{9,8},{10,9... | collective-permute-start | bytes 688136 | tf_op jit(solution)/shard_map/ppermute | solution.py:31
  57.2 1.9 collective-permute-start.16
  59.2 5.1 %collective-permute-start.4 = (bf16[2,224,256]{2,1,0:T(8,128)(2,1)S(1)}, bf16[2,224,256]{2,1,0:T(8,128)(2,1)S(1)}, u32[]{:S(2)}, u32[]{:S(2)}) collective-permute-start(bf16[2,224,256]{2,1,0:T(8,128)(2,1)S(1)} %collective-permute-done.3), channel_id=1, source_target_pairs={{0,7},{1,0},{2,1},{3,2},{4,3},{5,4},{6,5},{7,6},{8,15},{9,8},{10,9... | collective-permute-start | bytes 688136 | tf_op jit(solution)/shard_map/ppermute | solution.py:31
  64.4 1.9 collective-permute-start.7
  66.3 5.1 %collective-permute-start.14 = (bf16[2,224,256]{2,1,0:T(8,128)(2,1)S(1)}, bf16[2,224,256]{2,1,0:T(8,128)(2,1)S(1)}, u32[]{:S(2)}, u32[]{:S(2)}) collective-permute-start(bf16[2,224,256]{2,1,0:T(8,128)(2,1)S(1)} %collective-permute-done.13), channel_id=1, source_target_pairs={{0,7},{1,0},{2,1},{3,2},{4,3},{5,4},{6,5},{7,6},{8,15},{9,8},{10,9... | collective-permute-start | bytes 688136 | tf_op jit(solution)/shard_map/ppermute | solution.py:31
  71.5 1.9 collective-permute-start.17
  73.5 1.9 collective-permute-start.8
  75.5 5.2 %collective-permute-start.9 = (bf16[1,224,256]{2,1,0:T(8,128)(2,1)S(1)}, bf16[1,224,256]{2,1,0:T(8,128)(2,1)S(1)}, u32[]{:S(2)}, u32[]{:S(2)}) collective-permute-start(bf16[1,224,256]{2,1,0:T(8,128)(2,1)S(1)} %slice.185), channel_id=1, source_target_pairs={{0,7},{1,0},{2,1},{3,2},{4,3},{5,4},{6,5},{7,6},{8,15},{9,8},{10,9... | collective-permute-start | bytes 344072 | tf_op jit(solution)/shard_map/ppermute | solution.py:31
  80.7 1.9 collective-permute-start.18
  82.7 5.1 %collective-permute-start.19 = (bf16[1,224,256]{2,1,0:T(8,128)(2,1)S(1)}, bf16[1,224,256]{2,1,0:T(8,128)(2,1)S(1)}, u32[]{:S(2)}, u32[]{:S(2)}) collective-permute-start(bf16[1,224,256]{2,1,0:T(8,128)(2,1)S(1)} %slice.194), channel_id=1, source_target_pairs={{0,7},{1,0},{2,1},{3,2},{4,3},{5,4},{6,5},{7,6},{8,15},{9,8},{10,9... | collective-permute-start | bytes 344072 | tf_op jit(solution)/shard_map/ppermute | solution.py:31
  88.2 0.5 convert_reduce_fusion.2
  88.7 0.5 multiply_reduce_fusion
  89.3 1.9 collective-permute-start.10
  91.4 0.4 dynamic-slice_convert_fusion
  92.4 2.9 %fusion.3 = bf16[3584,256]{1,0:T(8,128)(2,1)} fusion(f32[2,8,224,256]{3,2,1,0:T(8,128)S(1)} %copy.26, f32[3584]{0:T(1024)S(1)} %select_n.134, f32[3584]{0:T(1024)S(1)} %select_n.132, f32[256]{0:T(256)S(1)} %bitcast.132, f32[256]{0:T(256)S(1)} %bitcast.131), kind=kLoop, calls=%fused_computation.7 | loop fusion | flops 4587520 | bytes 5535744 | tf_op jit(solution)/shard_map/convert_element_type | solution.py:116
  95.3 3.8 %all-gather.2.cloned.1.call-done = bf16[3584,512]{1,0:T(8,128)(2,1)} async-done(((bf16[224,512]{1,0:T(8,128)(2,1)}), bf16[3584,512]{1,0:T(8,128)(2,1)}) %all-gather.2.cloned.1.call-update) | async-done | bytes 3670032 | tf_op jit(solution)/shard_map/all_gather | solution.py:92
  99.2 3.6 %fusion.7 = f32[256,384]{1,0:T(8,128)S(1)} fusion(bf16[3584,256]{1,0:T(8,128)(2,1)} %fusion.3, bf16[3584,512]{1,0:T(8,128)(2,1)} %all-gather.2.cloned.1.call-done), kind=kOutput, calls=%fused_computation.12 | convolution fusion | flops 704643072 | bytes 4980736 | tf_op jit(solution)/shard_map/dot_general | solution.py:57
  102.8 0.7 fusion.11
  103.5 1.9 collective-permute-start.20
  105.5 0.5 fusion.4
  106.0 1.0 collective-permute-done.20
  108.2 2.0 collective-permute-start.21
  110.2 1.0 collective-permute-done.21
  111.3 1.6 convolution_convert_fusion.1
  112.8 2.1 collective-permute-start.22
  114.9 1.1 collective-permute-done.22
  116.4 2.9 %convolution_convert_fusion = bf16[3584,256]{1,0:T(8,128)(2,1)S(1)} fusion(bf16[256,384]{1,0:T(8,128)(2,1)S(1)} %constant_dynamic-update-slice_fusion, bf16[3584,512]{1,0:T(8,128)(2,1)} %all-gather.2.cloned.1.call-done), kind=kOutput, calls=%fused_computation | convolution fusion | flops 705560576 | bytes 4784128 | tf_op jit(solution)/shard_map/dot_general | solution.py:57
  119.5 57.1 %all_to_all.10 = bf16[16,240,256]{2,1,0:T(8,128)(2,1)S(1)} all-to-all(bf16[16,240,256]{2,1,0:T(8,128)(2,1)S(1)} %pad_maximum_fusion), channel_id=1, replica_groups=mesh['dp'=32,'tensor'=16] {'tensor'}, dimensions={0} | all-to-all | bytes 3932160 | tf_op jit(solution)/shard_map/all_to_all | solution.py:151
  176.6 15.5 %all-to-all-start.1 = ((bf16[16,224,128]{2,1,0:T(8,128)(2,1)}), bf16[16,224,128]{2,1,0:T(8,128)(2,1)S(1)}, u32[]{:S(2)}, u32[]{:S(2)}) async-start(bf16[16,224,128]{2,1,0:T(8,128)(2,1)} %bitcast.50), calls=%async_computation.1 | async-start | bytes 1835008 | tf_op jit(solution)/shard_map/all_to_all | solution.py:137
  192.1 0.8 dynamic_slice.11
  193.2 1.9 collective-permute-start.23
  195.1 19.2 %all-to-all-done.1 = bf16[16,224,128]{2,1,0:T(8,128)(2,1)S(1)} async-done(((bf16[16,224,128]{2,1,0:T(8,128)(2,1)}), bf16[16,224,128]{2,1,0:T(8,128)(2,1)S(1)}, u32[]{:S(2)}, u32[]{:S(2)}) %all-to-all-start.1) | async-done | bytes 917536 | tf_op jit(solution)/shard_map/all_to_all | solution.py:137
  214.3 0.8 convert_reduce_fusion.1
  215.2 0.8 fusion.28
  (115 shorter events, 4.0 us)
Async XLA Ops:
  7.2 92.0 %all-gather.2.cloned.1.call-start = ((), (), s32[]{:S(2)}) async-start(), calls=%async_computation.2 | async-start | bytes 3899392 | tf_op jit(solution)/shard_map/all_gather | solution.py:92
  8.2 5.7 %collective-permute-start = (bf16[224,256]{1,0:T(8,128)(2,1)S(1)}, bf16[224,256]{1,0:T(8,128)(2,1)S(1)}, u32[]{:S(2)}, u32[]{:S(2)}) collective-permute-start(bf16[224,256]{1,0:T(8,128)(2,1)S(1)} %get-tuple-element.19), channel_id=1, source_target_pairs={{0,16},{16,0},{32,48},{48,32},{64,80},{80,64},{96,112},{112,96},{1... | collective-permute-start | bytes 344072 | tf_op jit(solution)/shard_map/ppermute | solution.py:23
  14.0 14.2 %collective-permute-start.1 = (bf16[224,256]{1,0:T(8,128)(2,1)S(1)}, bf16[224,256]{1,0:T(8,128)(2,1)S(1)}, u32[]{:S(2)}, u32[]{:S(2)}) collective-permute-start(bf16[224,256]{1,0:T(8,128)(2,1)S(1)} %pad_maximum_fusion.6), channel_id=1, source_target_pairs={{0,8},{1,9},{2,10},{3,11},{4,12},{5,13},{6,14},{7,15},{8,0},{9,1},... | collective-permute-start | bytes 344072 | tf_op jit(solution)/shard_map/ppermute | solution.py:35
  17.9 16.6 %collective-permute-start.11 = (bf16[224,256]{1,0:T(8,128)(2,1)S(1)}, bf16[224,256]{1,0:T(8,128)(2,1)S(1)}, u32[]{:S(2)}, u32[]{:S(2)}) collective-permute-start(bf16[224,256]{1,0:T(8,128)(2,1)S(1)} %pad_maximum_fusion.7), channel_id=1, source_target_pairs={{0,8},{1,9},{2,10},{3,11},{4,12},{5,13},{6,14},{7,15},{8,0},{9,1},... | collective-permute-start | bytes 344072 | tf_op jit(solution)/shard_map/ppermute | solution.py:35
  28.2 16.7 %collective-permute-start.2 = (bf16[2,224,256]{2,1,0:T(8,128)(2,1)S(1)}, bf16[2,224,256]{2,1,0:T(8,128)(2,1)S(1)}, u32[]{:S(2)}, u32[]{:S(2)}) collective-permute-start(bf16[2,224,256]{2,1,0:T(8,128)(2,1)S(1)} %pad_maximum_fusion.2), channel_id=1, source_target_pairs={{0,7},{1,0},{2,1},{3,2},{4,3},{5,4},{6,5},{7,6},{8,15},{9,8},{10,9... | collective-permute-start | bytes 688136 | tf_op jit(solution)/shard_map/ppermute | solution.py:31
  30.2 20.0 %collective-permute-start.5 = (bf16[2,224,256]{2,1,0:T(8,128)(2,1)S(1)}, bf16[2,224,256]{2,1,0:T(8,128)(2,1)S(1)}, u32[]{:S(2)}, u32[]{:S(2)}) collective-permute-start(bf16[2,224,256]{2,1,0:T(8,128)(2,1)S(1)} %pad_maximum_fusion.2), channel_id=1, source_target_pairs={{0,1},{1,2},{2,3},{3,4},{4,5},{5,6},{6,7},{7,0},{8,9},{9,10},{10,1... | collective-permute-start | bytes 688136 | tf_op jit(solution)/shard_map/ppermute | solution.py:31
  34.6 17.5 %collective-permute-start.12 = (bf16[2,224,256]{2,1,0:T(8,128)(2,1)S(1)}, bf16[2,224,256]{2,1,0:T(8,128)(2,1)S(1)}, u32[]{:S(2)}, u32[]{:S(2)}) collective-permute-start(bf16[2,224,256]{2,1,0:T(8,128)(2,1)S(1)} %pad_maximum_fusion.4), channel_id=1, source_target_pairs={{0,7},{1,0},{2,1},{3,2},{4,3},{5,4},{6,5},{7,6},{8,15},{9,8},{10,9... | collective-permute-start | bytes 688136 | tf_op jit(solution)/shard_map/ppermute | solution.py:31
  43.0 14.2 %collective-permute-start.15 = (bf16[2,224,256]{2,1,0:T(8,128)(2,1)S(1)}, bf16[2,224,256]{2,1,0:T(8,128)(2,1)S(1)}, u32[]{:S(2)}, u32[]{:S(2)}) collective-permute-start(bf16[2,224,256]{2,1,0:T(8,128)(2,1)S(1)} %pad_maximum_fusion.4), channel_id=1, source_target_pairs={{0,1},{1,2},{2,3},{3,4},{4,5},{5,6},{6,7},{7,0},{8,9},{9,10},{10,1... | collective-permute-start | bytes 688136 | tf_op jit(solution)/shard_map/ppermute | solution.py:31
  45.0 14.2 %collective-permute-start.3 = (bf16[2,224,256]{2,1,0:T(8,128)(2,1)S(1)}, bf16[2,224,256]{2,1,0:T(8,128)(2,1)S(1)}, u32[]{:S(2)}, u32[]{:S(2)}) collective-permute-start(bf16[2,224,256]{2,1,0:T(8,128)(2,1)S(1)} %collective-permute-done.2), channel_id=1, source_target_pairs={{0,7},{1,0},{2,1},{3,2},{4,3},{5,4},{6,5},{7,6},{8,15},{9,8},{10,9... | collective-permute-start | bytes 688136 | tf_op jit(solution)/shard_map/ppermute | solution.py:31
  50.1 14.2 %collective-permute-start.6 = (bf16[2,224,256]{2,1,0:T(8,128)(2,1)S(1)}, bf16[2,224,256]{2,1,0:T(8,128)(2,1)S(1)}, u32[]{:S(2)}, u32[]{:S(2)}) collective-permute-start(bf16[2,224,256]{2,1,0:T(8,128)(2,1)S(1)} %collective-permute-done.5), channel_id=1, source_target_pairs={{0,1},{1,2},{2,3},{3,4},{4,5},{5,6},{6,7},{7,0},{8,9},{9,10},{10,1... | collective-permute-start | bytes 688136 | tf_op jit(solution)/shard_map/ppermute | solution.py:31
  52.1 14.2 %collective-permute-start.13 = (bf16[2,224,256]{2,1,0:T(8,128)(2,1)S(1)}, bf16[2,224,256]{2,1,0:T(8,128)(2,1)S(1)}, u32[]{:S(2)}, u32[]{:S(2)}) collective-permute-start(bf16[2,224,256]{2,1,0:T(8,128)(2,1)S(1)} %collective-permute-done.12), channel_id=1, source_target_pairs={{0,7},{1,0},{2,1},{3,2},{4,3},{5,4},{6,5},{7,6},{8,15},{9,8},{10,9... | collective-permute-start | bytes 688136 | tf_op jit(solution)/shard_map/ppermute | solution.py:31
  57.2 14.2 %collective-permute-start.16 = (bf16[2,224,256]{2,1,0:T(8,128)(2,1)S(1)}, bf16[2,224,256]{2,1,0:T(8,128)(2,1)S(1)}, u32[]{:S(2)}, u32[]{:S(2)}) collective-permute-start(bf16[2,224,256]{2,1,0:T(8,128)(2,1)S(1)} %collective-permute-done.15), channel_id=1, source_target_pairs={{0,1},{1,2},{2,3},{3,4},{4,5},{5,6},{6,7},{7,0},{8,9},{9,10},{10,1... | collective-permute-start | bytes 688136 | tf_op jit(solution)/shard_map/ppermute | solution.py:31
  59.2 16.2 %collective-permute-start.4 = (bf16[2,224,256]{2,1,0:T(8,128)(2,1)S(1)}, bf16[2,224,256]{2,1,0:T(8,128)(2,1)S(1)}, u32[]{:S(2)}, u32[]{:S(2)}) collective-permute-start(bf16[2,224,256]{2,1,0:T(8,128)(2,1)S(1)} %collective-permute-done.3), channel_id=1, source_target_pairs={{0,7},{1,0},{2,1},{3,2},{4,3},{5,4},{6,5},{7,6},{8,15},{9,8},{10,9... | collective-permute-start | bytes 688136 | tf_op jit(solution)/shard_map/ppermute | solution.py:31
  64.4 9.1 %collective-permute-start.7 = (bf16[2,224,256]{2,1,0:T(8,128)(2,1)S(1)}, bf16[2,224,256]{2,1,0:T(8,128)(2,1)S(1)}, u32[]{:S(2)}, u32[]{:S(2)}) collective-permute-start(bf16[2,224,256]{2,1,0:T(8,128)(2,1)S(1)} %collective-permute-done.6), channel_id=1, source_target_pairs={{0,1},{1,2},{2,3},{3,4},{4,5},{5,6},{6,7},{7,0},{8,9},{9,10},{10,1... | collective-permute-start | bytes 688136 | tf_op jit(solution)/shard_map/ppermute | solution.py:31
  66.3 16.4 %collective-permute-start.14 = (bf16[2,224,256]{2,1,0:T(8,128)(2,1)S(1)}, bf16[2,224,256]{2,1,0:T(8,128)(2,1)S(1)}, u32[]{:S(2)}, u32[]{:S(2)}) collective-permute-start(bf16[2,224,256]{2,1,0:T(8,128)(2,1)S(1)} %collective-permute-done.13), channel_id=1, source_target_pairs={{0,7},{1,0},{2,1},{3,2},{4,3},{5,4},{6,5},{7,6},{8,15},{9,8},{10,9... | collective-permute-start | bytes 688136 | tf_op jit(solution)/shard_map/ppermute | solution.py:31
  71.5 9.2 %collective-permute-start.17 = (bf16[2,224,256]{2,1,0:T(8,128)(2,1)S(1)}, bf16[2,224,256]{2,1,0:T(8,128)(2,1)S(1)}, u32[]{:S(2)}, u32[]{:S(2)}) collective-permute-start(bf16[2,224,256]{2,1,0:T(8,128)(2,1)S(1)} %collective-permute-done.16), channel_id=1, source_target_pairs={{0,1},{1,2},{2,3},{3,4},{4,5},{5,6},{6,7},{7,0},{8,9},{9,10},{10,1... | collective-permute-start | bytes 688136 | tf_op jit(solution)/shard_map/ppermute | solution.py:31
  73.5 14.4 %collective-permute-start.8 = (bf16[1,224,256]{2,1,0:T(8,128)(2,1)S(1)}, bf16[1,224,256]{2,1,0:T(8,128)(2,1)S(1)}, u32[]{:S(2)}, u32[]{:S(2)}) collective-permute-start(bf16[1,224,256]{2,1,0:T(8,128)(2,1)S(1)} %slice.184), channel_id=1, source_target_pairs={{0,1},{1,2},{2,3},{3,4},{4,5},{5,6},{6,7},{7,0},{8,9},{9,10},{10,1... | collective-permute-start | bytes 344072 | tf_op jit(solution)/shard_map/ppermute | solution.py:31
  75.5 12.4 %collective-permute-start.9 = (bf16[1,224,256]{2,1,0:T(8,128)(2,1)S(1)}, bf16[1,224,256]{2,1,0:T(8,128)(2,1)S(1)}, u32[]{:S(2)}, u32[]{:S(2)}) collective-permute-start(bf16[1,224,256]{2,1,0:T(8,128)(2,1)S(1)} %slice.185), channel_id=1, source_target_pairs={{0,7},{1,0},{2,1},{3,2},{4,3},{5,4},{6,5},{7,6},{8,15},{9,8},{10,9... | collective-permute-start | bytes 344072 | tf_op jit(solution)/shard_map/ppermute | solution.py:31
  80.7 10.5 %collective-permute-start.18 = (bf16[1,224,256]{2,1,0:T(8,128)(2,1)S(1)}, bf16[1,224,256]{2,1,0:T(8,128)(2,1)S(1)}, u32[]{:S(2)}, u32[]{:S(2)}) collective-permute-start(bf16[1,224,256]{2,1,0:T(8,128)(2,1)S(1)} %slice.193), channel_id=1, source_target_pairs={{0,1},{1,2},{2,3},{3,4},{4,5},{5,6},{6,7},{7,0},{8,9},{9,10},{10,1... | collective-permute-start | bytes 344072 | tf_op jit(solution)/shard_map/ppermute | solution.py:31
  82.7 8.5 %collective-permute-start.19 = (bf16[1,224,256]{2,1,0:T(8,128)(2,1)S(1)}, bf16[1,224,256]{2,1,0:T(8,128)(2,1)S(1)}, u32[]{:S(2)}, u32[]{:S(2)}) collective-permute-start(bf16[1,224,256]{2,1,0:T(8,128)(2,1)S(1)} %slice.194), channel_id=1, source_target_pairs={{0,7},{1,0},{2,1},{3,2},{4,3},{5,4},{6,5},{7,6},{8,15},{9,8},{10,9... | collective-permute-start | bytes 344072 | tf_op jit(solution)/shard_map/ppermute | solution.py:31
  89.3 3.1 %collective-permute-start.10 = (f32[2,256]{1,0:T(2,128)S(1)}, f32[2,256]{1,0:T(2,128)S(1)}, u32[]{:S(2)}, u32[]{:S(2)}) collective-permute-start(f32[2,256]{1,0:T(2,128)S(1)} %pad_maximum_fusion.9), channel_id=1, source_target_pairs={{0,16},{16,0},{32,48},{48,32},{64,80},{80,64},{96,112},{112,96},{1... | collective-permute-start | bytes 6152 | tf_op jit(solution)/shard_map/ppermute | solution.py:23
  99.2 3.7 %copy-start.2 = (bf16[3584,512]{1,0:T(8,128)(2,1)S(1)}, bf16[3584,512]{1,0:T(8,128)(2,1)}, u32[]{:S(2)}) copy-start(bf16[3584,512]{1,0:T(8,128)(2,1)} %all-gather.2.cloned.1.call-done) | copy-start | bytes 11010052
  102.8 4.2 %copy-start.1 = (f32[384]{0:T(512)S(1)}, f32[384]{0:T(512)}, u32[]{:S(2)}) copy-start(f32[384]{0:T(512)} %param.11) | copy-start | bytes 4612
  103.5 3.4 %collective-permute-start.20 = (f32[128,512]{1,0:T(8,128)S(1)}, f32[128,512]{1,0:T(8,128)S(1)}, u32[]{:S(2)}, u32[]{:S(2)}) collective-permute-start(f32[128,512]{1,0:T(8,128)S(1)} %pad_maximum_fusion.1), channel_id=1, source_target_pairs={{0,16},{16,0},{32,48},{48,32},{64,80},{80,64},{96,112},{112,96},{1... | collective-permute-start | bytes 786440 | tf_op jit(solution)/shard_map/ppermute | solution.py:23
  108.2 3.1 %collective-permute-start.21 = (bf16[128,128]{1,0:T(8,128)(2,1)S(1)}, bf16[128,128]{1,0:T(8,128)(2,1)S(1)}, u32[]{:S(2)}, u32[]{:S(2)}) collective-permute-start(bf16[128,128]{1,0:T(8,128)(2,1)S(1)} %convolution_convert_fusion.5), channel_id=1, source_target_pairs={{0,16},{16,0},{32,48},{48,32},{64,80},{80,64},{96,112},{112,96},{1... | collective-permute-start | bytes 98312 | tf_op jit(solution)/shard_map/ppermute | solution.py:23
  112.8 3.2 %collective-permute-start.22 = (bf16[128,384]{1,0:T(8,128)(2,1)S(1)}, bf16[128,384]{1,0:T(8,128)(2,1)S(1)}, u32[]{:S(2)}, u32[]{:S(2)}) collective-permute-start(bf16[128,384]{1,0:T(8,128)(2,1)S(1)} %pad_maximum_fusion.8), channel_id=1, source_target_pairs={{0,16},{16,0},{32,48},{48,32},{64,80},{80,64},{96,112},{112,96},{1... | collective-permute-start | bytes 294920 | tf_op jit(solution)/shard_map/ppermute | solution.py:23
  176.6 38.5 %copy-start = (bf16[128,448]{0,1:T(8,128)(2,1)S(1)}, bf16[128,448]{0,1:T(8,128)(2,1)}, u32[]{:S(2)}) copy-start(bf16[128,448]{0,1:T(8,128)(2,1)} %param.7) | copy-start | bytes 344068
  176.6 37.7 %all-to-all-start.1 = ((bf16[16,224,128]{2,1,0:T(8,128)(2,1)}), bf16[16,224,128]{2,1,0:T(8,128)(2,1)S(1)}, u32[]{:S(2)}, u32[]{:S(2)}) async-start(bf16[16,224,128]{2,1,0:T(8,128)(2,1)} %bitcast.50), calls=%async_computation.1 | async-start | bytes 1835008 | tf_op jit(solution)/shard_map/all_to_all | solution.py:137
  193.2 21.9 %collective-permute-start.23 = (f32[240,128]{1,0:T(8,128)S(1)}, f32[240,128]{1,0:T(8,128)S(1)}, u32[]{:S(2)}, u32[]{:S(2)}) collective-permute-start(f32[240,128]{1,0:T(8,128)S(1)} %slice.212), channel_id=1, source_target_pairs={{0,16},{16,0},{32,48},{48,32},{64,80},{80,64},{96,112},{112,96},{1... | collective-permute-start | bytes 368648 | tf_op jit(solution)/shard_map/ppermute | solution.py:23
Sparse Core Ops, SparseCore 0:
  12.0 87.1 all-gather.1

commit v3 on v1

--- a/solution.py
+++ b/solution.py
@@ -5,6 +5,8 @@
 
 SEQ = 128
 E = 128
+Z_COUNT = 8
+X_COUNT = 4
 norm_eps = 1e-05
 f32 = jnp.float32
 bf16 = jnp.bfloat16
@@ -20,6 +22,66 @@
 def swap_cores(x):
     n = lax.axis_size("dp")
     return lax.ppermute(x, "dp", [(i, i ^ 1) for i in range(n)])
+
+
+def shift_z(x, step):
+    n = lax.axis_size("tensor")
+    pairs = [(i, i - i % Z_COUNT + (i + step) % Z_COUNT) for i in range(n)]
+    return lax.ppermute(x, "tensor", pairs)
+
+
+def swap_far(x):
+    n = lax.axis_size("tensor")
+    return lax.ppermute(x, "tensor", [(i, (i + Z_COUNT) % n) for i in range(n)])
+
+
+def shift_x(x, step):
+    n = lax.axis_size("dp")
+    row = 2 * X_COUNT
+    return lax.ppermute(x, "dp", [(i, i - i % row + (i + 2 * step) % row) for i in range(n)])
+
+
+def shift_y(x, step):
+    n = lax.axis_size("dp")
+    return lax.ppermute(x, "dp", [(i, (i + 2 * X_COUNT * step) % n) for i in range(n)])
+
+
+def ring_gather(own, shift, count, place):
+    found = {0: own}
+    up = down = own
+    middle = own.shape[0] // 2
+    for step in range(1, count // 2):
+        up, down = shift(up, 1), shift(down, -1)
+        found[step], found[count - step] = up, down
+    found[count // 2] = jnp.concatenate([shift(up[:middle], 1), shift(down[middle:], -1)])
+    blocks = [found[count - 1 - j] for j in range(count)]
+    line = jnp.stack(blocks + blocks[:-1], axis=1)
+    return lax.dynamic_slice_in_dim(line, count - 1 - place, count, 1)
+
+
+def ring_scatter_x(parts, place):
+    def part(step):
+        return lax.dynamic_index_in_dim(parts, (place + step) % X_COUNT, 0, keepdims=False)
+
+    across = part(2)
+    middle = across.shape[0] // 2
+    up = shift_x(across[:middle], 1).astype(f32)
+    down = shift_x(across[middle:], -1).astype(f32)
+    ahead, behind = part(1).astype(f32), part(-1).astype(f32)
+    ahead = jnp.concatenate([ahead[:middle] + up, ahead[middle:]])
+    behind = jnp.concatenate([behind[:middle], behind[middle:] + down])
+    up, down = shift_x(ahead.astype(bf16), 1), shift_x(behind.astype(bf16), -1)
+    return part(0).astype(f32) + up.astype(f32) + down.astype(f32)
+
+
+def scatter_y(parts, place):
+    count = parts.shape[0]
+    sent = parts.astype(bf16)
+    total = lax.dynamic_index_in_dim(parts, place, 0, keepdims=False)
+    for step in range(1, count):
+        one = lax.dynamic_index_in_dim(sent, (place + step) % count, 0, keepdims=False)
+        total = total + shift_y(one, step).astype(f32)
+    return total
 
 
 def split(x):
@@ -60,19 +122,26 @@
     part = width // 2
     core = lax.axis_index("dp") % 2
     rank = lax.axis_index("tensor")
-    chips = groups(n_dp, lambda i: i % 2)
+    lines = groups(n_dp, lambda i: i % (2 * X_COUNT))
+    rings = groups(n_tensor, lambda i: i // Z_COUNT)
+    x = lax.axis_index("dp") // 2 % X_COUNT
+    y = lax.axis_index("dp") // (2 * X_COUNT)
+    z, far = rank % Z_COUNT, rank // Z_COUNT
 
     weight_block = jnp.concatenate([w_qkv, w_out.T], axis=1)
-    weights = lax.all_gather(weight_block, "dp", axis=0, tiled=True, axis_index_groups=chips)
+    column = lax.all_gather(weight_block, "dp", axis=0, axis_index_groups=lines)
+    weights = ring_gather(column, shift_x, X_COUNT, x).reshape(n_tensor * part, 4 * E)
 
     hidden_t = hidden_in.T
     acts = jnp.concatenate([hidden_t, out_grad.T], axis=1).reshape(2, part, 2 * SEQ)
     mine = jnp.where(core == 0, acts[0], acts[1])
     other = swap_cores(jnp.where(core == 0, acts[1], acts[0]))
     block = jnp.concatenate([mine[:, :SEQ], other[:, :SEQ], mine[:, SEQ:], other[:, SEQ:]], axis=1)
-    rows = lax.all_to_all(
-        jnp.broadcast_to(block[None], (n_tensor, part, 4 * SEQ)), "tensor", 0, 0, tiled=True
-    ).reshape(n_tensor * part, 4 * SEQ)
+    block_far = swap_far(block)
+    pair = jnp.stack(
+        [jnp.where(far == 0, block, block_far), jnp.where(far == 0, block_far, block)]
+    )
+    rows = ring_gather(pair, shift_z, Z_COUNT, z).reshape(n_tensor * part, 4 * SEQ)
     hidden = rows[:, : 2 * SEQ].astype(f32)
     grads = rows[:, 2 * SEQ :]
 
@@ -111,10 +180,8 @@
 
     context = jnp.concatenate([context, swap_cores(context)], axis=0)
     weight_part = dot(grads, context, ((1,), (0,))).astype(bf16)
-    weight_parts = lax.all_to_all(
-        weight_part.reshape(n_tensor, part, E), "dp", 0, 0, tiled=True, axis_index_groups=chips
-    )
-    grad_out_weight = jnp.sum(weight_parts.astype(f32), axis=0).T
+    weight_parts = weight_part.reshape(-1, X_COUNT, part, E).swapaxes(0, 1)
+    grad_out_weight = scatter_y(ring_scatter_x(weight_parts, x), y).T
 
     joined_grad = jnp.concatenate([joined_grad, swap_cores(joined_grad)], axis=0)
     group_part = dot(joined_weight, joined_grad, ((1,), (1,))).astype(bf16)
@@ -123,10 +190,22 @@
     sum_cross = jnp.sum(joined_grad_f * (joined_part - bias_weight), axis=1)
     extra = jnp.stack([*split(sum_grad), *split(sum_cross)])
     extra = jnp.concatenate([extra, jnp.zeros((12, 2 * SEQ), bf16)])
-    extra = jnp.broadcast_to(extra[None], (n_tensor, 16, 2 * SEQ))
-    payload = jnp.concatenate([group_part.reshape(n_tensor, part, 2 * SEQ), extra], axis=1)
-    group_parts = lax.all_to_all(payload, "tensor", 0, 0, tiled=True)
-    total = jnp.sum(group_parts.astype(f32), axis=0)
+    extra = jnp.broadcast_to(extra[None], (Z_COUNT, 16, 2 * SEQ))
+    group_part = group_part.reshape(2, Z_COUNT, part, 2 * SEQ)
+    payload = jnp.concatenate([group_part[0], group_part[1], extra], axis=1)
+    group_parts = lax.all_to_all(
+        payload, "tensor", 0, 0, tiled=True, axis_index_groups=rings
+    ).astype(f32)
+    both = jnp.sum(group_parts[:, : 2 * part], axis=0)
+    sums = jnp.sum(group_parts[:, 2 * part :], axis=0)
+    sums = jnp.stack([sums[0] + sums[1], sums[2] + sums[3]])
+    sent = jnp.where(far == 0, both[part:], both[:part]).astype(bf16)
+    sent = jnp.concatenate([sent, *(v[None] for v in split(sums[0]) + split(sums[1]))])
+    sent = jnp.concatenate([sent, jnp.zeros((12, 2 * SEQ), bf16)])
+    sent = swap_far(sent).astype(f32)
+    total = jnp.where(far == 0, both[:part], both[part:]) + sent[:part]
+    sums = sums + jnp.stack([sent[part] + sent[part + 1], sent[part + 2] + sent[part + 3]])
+    total = jnp.concatenate([total, sums, jnp.zeros((6, 2 * SEQ), f32)])
     total_other = swap_cores(total[:, SEQ:])
     total = total[:, :SEQ]
     normed_grad = jnp.where(
@@ -135,8 +214,8 @@
         jnp.concatenate([total_other[:part], total[:part]]),
     )
     sums = total[part:] + total_other[part:]
-    mean_grad = (sums[0] + sums[1]) / depth
-    mean_cross = (sums[2] + sums[3]) / depth
+    mean_grad = sums[0] / depth
+    mean_cross = sums[1] / depth
 
     own_gain = lax.dynamic_slice_in_dim(norm_gain, rank * width, width)
     scaled_grad = normed_grad * own_gain[:, None]

time: 331 us -> 212 us (0.64)
  the two profiles are of different devices: /device:TPU:72 before, /device:TPU:1 now
where the time goes in v3:
time: 212 us; the launch traced here: 211 us
  starting transfers between devices  111 us (52%)
  waiting for transfers between devices  58.5 us (28%)
  blocking collectives  18.3 us (9%)
  other arithmetic  8.58 us (4%)
  matrix products  7.77 us (4%)
  local copies, waits for them, and re-layouts  4.95 us (2%)
    ppermute x8, starting transfers between devices, shift_z(): return lax.ppermute(x, 'tensor', pairs)  31.6 us
    ppermute x6, starting transfers between devices, swap_cores(): return lax.ppermute(x, 'dp', [(i, i ^ 1) for i in range(n)])  29 us
    ppermute x8, starting transfers between devices, shift_x(): lax.ppermute(x, 'dp', [(i, i - i % row + (i + 2 * step) % row) for i in r...  27.5 us
    all_to_all x1, waiting for transfers between devices, body(): lax.all_to_all(payload, 'tensor', 0, 0, tiled=True, axis_index_groups=rings)  21.4 us
    ppermute x8, waiting for transfers between devices, shift_z(): return lax.ppermute(x, 'tensor', pairs)  18.6 us
    all_gather x1, blocking collectives, body(): column = lax.all_gather(weight_block, 'dp', axis=0, axis_index_groups=lines)  18.3 us
    ppermute x2, waiting for transfers between devices, swap_far(): return lax.ppermute(x, 'tensor', [(i, (i + Z_COUNT) % n) for i in range(n)])  13.4 us
    ppermute x2, starting transfers between devices, swap_far(): return lax.ppermute(x, 'tensor', [(i, (i + Z_COUNT) % n) for i in range(n)])  9.36 us
  transfers between devices with their start and end apart: 28, of which 14 were waited for; matrix products, arithmetic and copies ran while one was open for 5% of the time, Pallas kernels for 0%

profile of v3, /device:TPU:1, one launch (start us, length us, event | category | flops | bytes accessed | tf_op | source)
XLA Modules:
  0.0 211.0 jit_solution(13119078632801852303)
XLA Ops:
  0.6 1.0 pad_maximum_fusion.4
  1.6 18.3 %all-gather = bf16[896,512]{1,0:T(8,128)(2,1)S(1)} all-gather(bf16[224,512]{1,0:T(8,128)(2,1)S(1)} %pad_maximum_fusion.4), channel_id=2, replica_groups={{0,128,256,384},{16,144,272,400},{32,160,288,416},{48,176,304,432},{64,..., dimensions={0}, use_global_device_ids=true | all-gather | bytes 1146880 | tf_op jit(solution)/shard_map/all_gather | solution.py:132
  19.9 4.0 %collective-permute-start.12 = (bf16[4,224,512]{2,1,0:T(8,128)(2,1)S(1)}, bf16[4,224,512]{2,1,0:T(8,128)(2,1)S(1)}, u32[]{:S(2)}, u32[]{:S(2)}) collective-permute-start(bf16[4,224,512]{2,1,0:T(8,128)(2,1)S(1)} %bitcast.149), channel_id=1, source_target_pairs={{0,32},{16,48},{32,64},{48,80},{64,96},{80,112},{96,0},{112,16},{1... | collective-permute-start | bytes 2752520 | tf_op jit(solution)/shard_map/ppermute | solution.py:41
  23.9 3.2 %collective-permute-start.11 = (bf16[4,224,512]{2,1,0:T(8,128)(2,1)S(1)}, bf16[4,224,512]{2,1,0:T(8,128)(2,1)S(1)}, u32[]{:S(2)}, u32[]{:S(2)}) collective-permute-start(bf16[4,224,512]{2,1,0:T(8,128)(2,1)S(1)} %bitcast.150), channel_id=1, source_target_pairs={{0,96},{16,112},{32,0},{48,16},{64,32},{80,48},{96,64},{112,80},{1... | collective-permute-start | bytes 2752520 | tf_op jit(solution)/shard_map/ppermute | solution.py:41
  27.1 1.0 broadcast_select_fusion.1
  28.1 8.7 %collective-permute-start = (bf16[224,256]{1,0:T(8,128)(2,1)S(1)}, bf16[224,256]{1,0:T(8,128)(2,1)S(1)}, u32[]{:S(2)}, u32[]{:S(2)}) collective-permute-start(bf16[224,256]{1,0:T(8,128)(2,1)S(1)} %get-tuple-element.32), channel_id=1, source_target_pairs={{0,16},{16,0},{32,48},{48,32},{64,80},{80,64},{96,112},{112,96},{1... | collective-permute-start | bytes 344072 | tf_op jit(solution)/shard_map/ppermute | solution.py:24
  36.8 0.8 reshape.218
  37.7 0.8 reshape.219
  38.8 3.1 %collective-permute-start.1 = (bf16[224,512]{1,0:T(8,128)(2,1)S(1)}, bf16[224,512]{1,0:T(8,128)(2,1)S(1)}, u32[]{:S(2)}, u32[]{:S(2)}) collective-permute-start(bf16[224,512]{1,0:T(8,128)(2,1)S(1)} %pad_maximum_fusion.3), channel_id=1, source_target_pairs={{0,8},{1,9},{2,10},{3,11},{4,12},{5,13},{6,14},{7,15},{8,0},{9,1},... | collective-permute-start | bytes 688136 | tf_op jit(solution)/shard_map/ppermute | solution.py:35
  42.3 13.4 %collective-permute-done.1 = bf16[224,512]{1,0:T(8,128)(2,1)S(1)} collective-permute-done((bf16[224,512]{1,0:T(8,128)(2,1)S(1)}, bf16[224,512]{1,0:T(8,128)(2,1)S(1)}, u32[]{:S(2)}, u32[]{:S(2)}) %collective-permute-start.1) | collective-permute-done | bytes 229408 | tf_op jit(solution)/shard_map/ppermute | solution.py:35
  55.9 9.3 %collective-permute-start.2 = (bf16[2,224,512]{2,1,0:T(8,128)(2,1)S(1)}, bf16[2,224,512]{2,1,0:T(8,128)(2,1)S(1)}, u32[]{:S(2)}, u32[]{:S(2)}) collective-permute-start(bf16[2,224,512]{2,1,0:T(8,128)(2,1)S(1)} %pad_maximum_fusion.1), channel_id=1, source_target_pairs={{0,7},{1,0},{2,1},{3,2},{4,3},{5,4},{6,5},{7,6},{8,15},{9,8},{10,9... | collective-permute-start | bytes 1376264 | tf_op jit(solution)/shard_map/ppermute | solution.py:30
  65.2 1.9 collective-permute-start.5
  67.2 7.0 %collective-permute-done.2 = bf16[2,224,512]{2,1,0:T(8,128)(2,1)S(1)} collective-permute-done((bf16[2,224,512]{2,1,0:T(8,128)(2,1)S(1)}, bf16[2,224,512]{2,1,0:T(8,128)(2,1)S(1)}, u32[]{:S(2)}, u32[]{:S(2)}) %collective-permute-start.2) | collective-permute-done | bytes 458784 | tf_op jit(solution)/shard_map/ppermute | solution.py:30
  74.2 5.3 %collective-permute-start.3 = (bf16[2,224,512]{2,1,0:T(8,128)(2,1)S(1)}, bf16[2,224,512]{2,1,0:T(8,128)(2,1)S(1)}, u32[]{:S(2)}, u32[]{:S(2)}) collective-permute-start(bf16[2,224,512]{2,1,0:T(8,128)(2,1)S(1)} %collective-permute-done.2), channel_id=1, source_target_pairs={{0,7},{1,0},{2,1},{3,2},{4,3},{5,4},{6,5},{7,6},{8,15},{9,8},{10,9... | collective-permute-start | bytes 1376264 | tf_op jit(solution)/shard_map/ppermute | solution.py:30
  79.5 1.9 collective-permute-start.6
  81.6 1.9 collective-permute-start.13
  83.5 4.6 %collective-permute-start.14 = (bf16[2,224,512]{2,1,0:T(8,128)(2,1)S(1)}, bf16[2,224,512]{2,1,0:T(8,128)(2,1)S(1)}, u32[]{:S(2)}, u32[]{:S(2)}) collective-permute-start(bf16[2,224,512]{2,1,0:T(8,128)(2,1)S(1)} %slice.320), channel_id=1, source_target_pairs={{0,96},{16,112},{32,0},{48,16},{64,32},{80,48},{96,64},{112,80},{1... | collective-permute-start | bytes 1376264 | tf_op jit(solution)/shard_map/ppermute | solution.py:41
  88.2 4.7 %collective-permute-start.4 = (bf16[2,224,512]{2,1,0:T(8,128)(2,1)S(1)}, bf16[2,224,512]{2,1,0:T(8,128)(2,1)S(1)}, u32[]{:S(2)}, u32[]{:S(2)}) collective-permute-start(bf16[2,224,512]{2,1,0:T(8,128)(2,1)S(1)} %collective-permute-done.3), channel_id=1, source_target_pairs={{0,7},{1,0},{2,1},{3,2},{4,3},{5,4},{6,5},{7,6},{8,15},{9,8},{10,9... | collective-permute-start | bytes 1376264 | tf_op jit(solution)/shard_map/ppermute | solution.py:30
  92.9 1.9 collective-permute-start.7
  96.4 8.7 %collective-permute-done.7 = bf16[2,224,512]{2,1,0:T(8,128)(2,1)S(1)} collective-permute-done((bf16[2,224,512]{2,1,0:T(8,128)(2,1)S(1)}, bf16[2,224,512]{2,1,0:T(8,128)(2,1)S(1)}, u32[]{:S(2)}, u32[]{:S(2)}) %collective-permute-start.7) | collective-permute-done | bytes 458784 | tf_op jit(solution)/shard_map/ppermute | solution.py:30
  105.0 1.9 collective-permute-start.8
  107.0 4.6 %collective-permute-start.9 = (bf16[1,224,512]{2,1,0:T(8,128)(2,1)S(1)}, bf16[1,224,512]{2,1,0:T(8,128)(2,1)S(1)}, u32[]{:S(2)}, u32[]{:S(2)}) collective-permute-start(bf16[1,224,512]{2,1,0:T(8,128)(2,1)S(1)} %slice.313), channel_id=1, source_target_pairs={{0,7},{1,0},{2,1},{3,2},{4,3},{5,4},{6,5},{7,6},{8,15},{9,8},{10,9... | collective-permute-start | bytes 688136 | tf_op jit(solution)/shard_map/ppermute | solution.py:30
  111.6 1.4 collective-permute-done.8
  113.0 1.5 collective-permute-done.9
  116.4 7.0 %collective-permute-start.10 = (f32[2,256]{1,0:T(2,128)S(1)}, f32[2,256]{1,0:T(2,128)S(1)}, u32[]{:S(2)}, u32[]{:S(2)}) collective-permute-start(f32[2,256]{1,0:T(2,128)S(1)} %pad_maximum_fusion.11), channel_id=1, source_target_pairs={{0,16},{16,0},{32,48},{48,32},{64,80},{80,64},{96,112},{112,96},{1... | collective-permute-start | bytes 6152 | tf_op jit(solution)/shard_map/ppermute | solution.py:24
  124.2 2.3 %fusion.9 = f32[256,384]{1,0:T(8,128)S(1)} fusion(bf16[3584,512]{1,0:T(8,128)(2,1)S(1)} %bitcast.153, f32[3584]{0:T(1024)S(1)} %select_n.212, f32[3584]{0:T(1024)S(1)} %select_n.210, f32[256]{0:T(256)S(1)} %bitcast.175, f32[256]{0:T(256)S(1)} %bitcast.174, bf16[3584,512]{1,0:T(8,128)(2,1)S(1)} %bitcast.147), kind=kOutput, calls=%fused_computation.15 | convolution fusion | flops 710148096 | bytes 5015552 | tf_op jit(solution)/shard_map/dot_general | solution.py:93
  126.5 2.3 %collective-permute-start.15 = (f32[128,512]{1,0:T(8,128)S(1)}, f32[128,512]{1,0:T(8,128)S(1)}, u32[]{:S(2)}, u32[]{:S(2)}) collective-permute-start(f32[128,512]{1,0:T(8,128)S(1)} %pad_maximum_fusion.2), channel_id=1, source_target_pairs={{0,16},{16,0},{32,48},{48,32},{64,80},{80,64},{96,112},{112,96},{1... | collective-permute-start | bytes 786440 | tf_op jit(solution)/shard_map/ppermute | solution.py:24
  131.0 2.3 %collective-permute-start.16 = (bf16[128,384]{1,0:T(8,128)(2,1)S(1)}, bf16[128,384]{1,0:T(8,128)(2,1)S(1)}, u32[]{:S(2)}, u32[]{:S(2)}) collective-permute-start(bf16[128,384]{1,0:T(8,128)(2,1)S(1)} %pad_maximum_fusion.10), channel_id=1, source_target_pairs={{0,16},{16,0},{32,48},{48,32},{64,80},{80,64},{96,112},{112,96},{1... | collective-permute-start | bytes 294920 | tf_op jit(solution)/shard_map/ppermute | solution.py:24
  133.3 0.9 collective-permute-done.16
  134.2 1.2 convolution_convert_fusion
  135.9 1.4 pad_maximum_fusion
  137.3 4.7 %all-to-all-start = ((bf16[8,464,256]{2,1,0:T(8,128)(2,1)}), bf16[8,464,256]{2,1,0:T(8,128)(2,1)S(1)}, u32[]{:S(2)}, u32[]{:S(2)}) async-start(bf16[8,464,256]{2,1,0:T(8,128)(2,1)} %pad_maximum_fusion), calls=%async_computation | async-start | bytes 3801088 | tf_op jit(solution)/shard_map/all_to_all | solution.py:196
  143.0 2.5 %collective-permute-start.19 = (bf16[128,128]{1,0:T(8,128)(2,1)S(1)}, bf16[128,128]{1,0:T(8,128)(2,1)S(1)}, u32[]{:S(2)}, u32[]{:S(2)}) collective-permute-start(bf16[128,128]{1,0:T(8,128)(2,1)S(1)} %convolution_convert_fusion.2), channel_id=1, source_target_pairs={{0,16},{16,0},{32,48},{48,32},{64,80},{80,64},{96,112},{112,96},{1... | collective-permute-start | bytes 98312 | tf_op jit(solution)/shard_map/ppermute | solution.py:24
  145.6 0.8 collective-permute-done.19
  146.4 2.1 %convolution_convert_fusion.1 = bf16[3584,128]{1,0:T(8,128)(2,1)S(1)} fusion(bf16[3584,512]{1,0:T(8,128)(2,1)} %bitcast.148, bf16[128,128]{1,0:T(8,128)(2,1)S(1)} %collective-permute-done.19, bf16[128,128]{1,0:T(8,128)(2,1)S(1)} %convolution_convert_fusion.2), kind=kOutput, calls=%fused_computation.4 | convolution fusion | flops 235470848 | bytes 2818048 | tf_op jit(solution)/shard_map/dot_general | solution.py:93
  148.6 1.9 collective-permute-start.20
  150.5 4.6 %collective-permute-start.22 = (bf16[2,224,128]{2,1,0:T(8,128)(2,1)S(1)}, bf16[2,224,128]{2,1,0:T(8,128)(2,1)S(1)}, u32[]{:S(2)}, u32[]{:S(2)}) collective-permute-start(bf16[2,224,128]{2,1,0:T(8,128)(2,1)S(1)} %get-tuple-element.30), channel_id=1, source_target_pairs={{0,96},{16,112},{32,0},{48,16},{64,32},{80,48},{96,64},{112,80},{1... | collective-permute-start | bytes 344072 | tf_op jit(solution)/shard_map/ppermute | solution.py:41
  155.1 0.9 collective-permute-done.20
  156.1 0.8 collective-permute-done.22
  157.0 2.7 %collective-permute-start.21 = (bf16[4,224,128]{2,1,0:T(8,128)(2,1)S(1)}, bf16[4,224,128]{2,1,0:T(8,128)(2,1)S(1)}, u32[]{:S(2)}, u32[]{:S(2)}) collective-permute-start(bf16[4,224,128]{2,1,0:T(8,128)(2,1)S(1)} %pad_maximum_fusion.5), channel_id=1, source_target_pairs={{0,32},{16,48},{32,64},{48,80},{64,96},{80,112},{96,0},{112,16},{1... | collective-permute-start | bytes 688136 | tf_op jit(solution)/shard_map/ppermute | solution.py:41
  160.4 4.6 %collective-permute-start.23 = (bf16[4,224,128]{2,1,0:T(8,128)(2,1)}, bf16[4,224,128]{2,1,0:T(8,128)(2,1)S(1)}, u32[]{:S(2)}, u32[]{:S(2)}) collective-permute-start(bf16[4,224,128]{2,1,0:T(8,128)(2,1)} %pad_maximum_fusion.6), channel_id=1, source_target_pairs={{0,96},{16,112},{32,0},{48,16},{64,32},{80,48},{96,64},{112,80},{1... | collective-permute-start | bytes 688136 | tf_op jit(solution)/shard_map/ppermute | solution.py:41
  165.0 21.4 %all-to-all-done = bf16[8,464,256]{2,1,0:T(8,128)(2,1)S(1)} async-done(((bf16[8,464,256]{2,1,0:T(8,128)(2,1)}), bf16[8,464,256]{2,1,0:T(8,128)(2,1)S(1)}, u32[]{:S(2)}, u32[]{:S(2)}) %all-to-all-start) | async-done | bytes 1900576 | tf_op jit(solution)/shard_map/all_to_all | solution.py:196
  187.2 6.3 %collective-permute-start.17 = (bf16[240,256]{1,0:T(8,128)(2,1)S(1)}, bf16[240,256]{1,0:T(8,128)(2,1)S(1)}, u32[]{:S(2)}, u32[]{:S(2)}) collective-permute-start(bf16[240,256]{1,0:T(8,128)(2,1)S(1)} %concatenate.71), channel_id=1, source_target_pairs={{0,8},{1,9},{2,10},{3,11},{4,12},{5,13},{6,14},{7,15},{8,0},{9,1},... | collective-permute-start | bytes 368648 | tf_op jit(solution)/shard_map/ppermute | solution.py:35
  193.7 1.9 collective-permute-start.24
  195.6 3.6 %collective-permute-start.25 = (bf16[224,128]{1,0:T(8,128)(2,1)S(1)}, bf16[224,128]{1,0:T(8,128)(2,1)S(1)}, u32[]{:S(2)}, u32[]{:S(2)}) collective-permute-start(bf16[224,128]{1,0:T(8,128)(2,1)S(1)} %get-tuple-element.28), channel_id=1, source_target_pairs={{0,256},{16,272},{32,288},{48,304},{64,320},{80,336},{96,352},{112... | collective-permute-start | bytes 172040 | tf_op jit(solution)/shard_map/ppermute | solution.py:46
  199.2 3.5 %collective-permute-start.26 = (bf16[224,128]{1,0:T(8,128)(2,1)S(1)}, bf16[224,128]{1,0:T(8,128)(2,1)S(1)}, u32[]{:S(2)}, u32[]{:S(2)}) collective-permute-start(bf16[224,128]{1,0:T(8,128)(2,1)S(1)} %get-tuple-element.27), channel_id=1, source_target_pairs={{0,384},{16,400},{32,416},{48,432},{64,448},{80,464},{96,480},{112... | collective-permute-start | bytes 172040 | tf_op jit(solution)/shard_map/ppermute | solution.py:46
  202.9 6.3 %collective-permute-start.18 = (f32[232,128]{1,0:T(8,128)S(1)}, f32[232,128]{1,0:T(8,128)S(1)}, u32[]{:S(2)}, u32[]{:S(2)}) collective-permute-start(f32[232,128]{1,0:T(8,128)S(1)} %fusion.40), channel_id=1, source_target_pairs={{0,16},{16,0},{32,48},{48,32},{64,80},{80,64},{96,112},{112,96},{1... | collective-permute-start | bytes 356360 | tf_op jit(solution)/shard_map/ppermute | solution.py:24
  210.2 0.8 fusion.45
  (126 shorter events, 11.6 us)
Async XLA Ops:
  19.9 61.6 %collective-permute-start.12 = (bf16[4,224,512]{2,1,0:T(8,128)(2,1)S(1)}, bf16[4,224,512]{2,1,0:T(8,128)(2,1)S(1)}, u32[]{:S(2)}, u32[]{:S(2)}) collective-permute-start(bf16[4,224,512]{2,1,0:T(8,128)(2,1)S(1)} %bitcast.149), channel_id=1, source_target_pairs={{0,32},{16,48},{32,64},{48,80},{64,96},{80,112},{96,0},{112,16},{1... | collective-permute-start | bytes 2752520 | tf_op jit(solution)/shard_map/ppermute | solution.py:41
  23.9 59.6 %collective-permute-start.11 = (bf16[4,224,512]{2,1,0:T(8,128)(2,1)S(1)}, bf16[4,224,512]{2,1,0:T(8,128)(2,1)S(1)}, u32[]{:S(2)}, u32[]{:S(2)}) collective-permute-start(bf16[4,224,512]{2,1,0:T(8,128)(2,1)S(1)} %bitcast.150), channel_id=1, source_target_pairs={{0,96},{16,112},{32,0},{48,16},{64,32},{80,48},{96,64},{112,80},{1... | collective-permute-start | bytes 2752520 | tf_op jit(solution)/shard_map/ppermute | solution.py:41
  28.1 10.6 %collective-permute-start = (bf16[224,256]{1,0:T(8,128)(2,1)S(1)}, bf16[224,256]{1,0:T(8,128)(2,1)S(1)}, u32[]{:S(2)}, u32[]{:S(2)}) collective-permute-start(bf16[224,256]{1,0:T(8,128)(2,1)S(1)} %get-tuple-element.32), channel_id=1, source_target_pairs={{0,16},{16,0},{32,48},{48,32},{64,80},{80,64},{96,112},{112,96},{1... | collective-permute-start | bytes 344072 | tf_op jit(solution)/shard_map/ppermute | solution.py:24
  38.8 16.9 %collective-permute-start.1 = (bf16[224,512]{1,0:T(8,128)(2,1)S(1)}, bf16[224,512]{1,0:T(8,128)(2,1)S(1)}, u32[]{:S(2)}, u32[]{:S(2)}) collective-permute-start(bf16[224,512]{1,0:T(8,128)(2,1)S(1)} %pad_maximum_fusion.3), channel_id=1, source_target_pairs={{0,8},{1,9},{2,10},{3,11},{4,12},{5,13},{6,14},{7,15},{8,0},{9,1},... | collective-permute-start | bytes 688136 | tf_op jit(solution)/shard_map/ppermute | solution.py:35
  55.9 18.3 %collective-permute-start.2 = (bf16[2,224,512]{2,1,0:T(8,128)(2,1)S(1)}, bf16[2,224,512]{2,1,0:T(8,128)(2,1)S(1)}, u32[]{:S(2)}, u32[]{:S(2)}) collective-permute-start(bf16[2,224,512]{2,1,0:T(8,128)(2,1)S(1)} %pad_maximum_fusion.1), channel_id=1, source_target_pairs={{0,7},{1,0},{2,1},{3,2},{4,3},{5,4},{6,5},{7,6},{8,15},{9,8},{10,9... | collective-permute-start | bytes 1376264 | tf_op jit(solution)/shard_map/ppermute | solution.py:30
  65.2 14.3 %collective-permute-start.5 = (bf16[2,224,512]{2,1,0:T(8,128)(2,1)S(1)}, bf16[2,224,512]{2,1,0:T(8,128)(2,1)S(1)}, u32[]{:S(2)}, u32[]{:S(2)}) collective-permute-start(bf16[2,224,512]{2,1,0:T(8,128)(2,1)S(1)} %pad_maximum_fusion.1), channel_id=1, source_target_pairs={{0,1},{1,2},{2,3},{3,4},{4,5},{5,6},{6,7},{7,0},{8,9},{9,10},{10,1... | collective-permute-start | bytes 1376264 | tf_op jit(solution)/shard_map/ppermute | solution.py:30
  74.2 14.0 %collective-permute-start.3 = (bf16[2,224,512]{2,1,0:T(8,128)(2,1)S(1)}, bf16[2,224,512]{2,1,0:T(8,128)(2,1)S(1)}, u32[]{:S(2)}, u32[]{:S(2)}) collective-permute-start(bf16[2,224,512]{2,1,0:T(8,128)(2,1)S(1)} %collective-permute-done.2), channel_id=1, source_target_pairs={{0,7},{1,0},{2,1},{3,2},{4,3},{5,4},{6,5},{7,6},{8,15},{9,8},{10,9... | collective-permute-start | bytes 1376264 | tf_op jit(solution)/shard_map/ppermute | solution.py:30
  79.5 13.4 %collective-permute-start.6 = (bf16[2,224,512]{2,1,0:T(8,128)(2,1)S(1)}, bf16[2,224,512]{2,1,0:T(8,128)(2,1)S(1)}, u32[]{:S(2)}, u32[]{:S(2)}) collective-permute-start(bf16[2,224,512]{2,1,0:T(8,128)(2,1)S(1)} %collective-permute-done.5), channel_id=1, source_target_pairs={{0,1},{1,2},{2,3},{3,4},{4,5},{5,6},{6,7},{7,0},{8,9},{9,10},{10,1... | collective-permute-start | bytes 1376264 | tf_op jit(solution)/shard_map/ppermute | solution.py:30
  81.6 13.3 %collective-permute-start.13 = (bf16[2,224,512]{2,1,0:T(8,128)(2,1)S(1)}, bf16[2,224,512]{2,1,0:T(8,128)(2,1)S(1)}, u32[]{:S(2)}, u32[]{:S(2)}) collective-permute-start(bf16[2,224,512]{2,1,0:T(8,128)(2,1)S(1)} %slice.319), channel_id=1, source_target_pairs={{0,32},{16,48},{32,64},{48,80},{64,96},{80,112},{96,0},{112,16},{1... | collective-permute-start | bytes 1376264 | tf_op jit(solution)/shard_map/ppermute | solution.py:41
  83.5 12.1 %collective-permute-start.14 = (bf16[2,224,512]{2,1,0:T(8,128)(2,1)S(1)}, bf16[2,224,512]{2,1,0:T(8,128)(2,1)S(1)}, u32[]{:S(2)}, u32[]{:S(2)}) collective-permute-start(bf16[2,224,512]{2,1,0:T(8,128)(2,1)S(1)} %slice.320), channel_id=1, source_target_pairs={{0,96},{16,112},{32,0},{48,16},{64,32},{80,48},{96,64},{112,80},{1... | collective-permute-start | bytes 1376264 | tf_op jit(solution)/shard_map/ppermute | solution.py:41
  88.2 18.8 %collective-permute-start.4 = (bf16[2,224,512]{2,1,0:T(8,128)(2,1)S(1)}, bf16[2,224,512]{2,1,0:T(8,128)(2,1)S(1)}, u32[]{:S(2)}, u32[]{:S(2)}) collective-permute-start(bf16[2,224,512]{2,1,0:T(8,128)(2,1)S(1)} %collective-permute-done.3), channel_id=1, source_target_pairs={{0,7},{1,0},{2,1},{3,2},{4,3},{5,4},{6,5},{7,6},{8,15},{9,8},{10,9... | collective-permute-start | bytes 1376264 | tf_op jit(solution)/shard_map/ppermute | solution.py:30
  92.9 12.1 %collective-permute-start.7 = (bf16[2,224,512]{2,1,0:T(8,128)(2,1)S(1)}, bf16[2,224,512]{2,1,0:T(8,128)(2,1)S(1)}, u32[]{:S(2)}, u32[]{:S(2)}) collective-permute-start(bf16[2,224,512]{2,1,0:T(8,128)(2,1)S(1)} %collective-permute-done.6), channel_id=1, source_target_pairs={{0,1},{1,2},{2,3},{3,4},{4,5},{5,6},{6,7},{7,0},{8,9},{9,10},{10,1... | collective-permute-start | bytes 1376264 | tf_op jit(solution)/shard_map/ppermute | solution.py:30
  105.0 8.0 %collective-permute-start.8 = (bf16[1,224,512]{2,1,0:T(8,128)(2,1)S(1)}, bf16[1,224,512]{2,1,0:T(8,128)(2,1)S(1)}, u32[]{:S(2)}, u32[]{:S(2)}) collective-permute-start(bf16[1,224,512]{2,1,0:T(8,128)(2,1)S(1)} %slice.312), channel_id=1, source_target_pairs={{0,1},{1,2},{2,3},{3,4},{4,5},{5,6},{6,7},{7,0},{8,9},{9,10},{10,1... | collective-permute-start | bytes 688136 | tf_op jit(solution)/shard_map/ppermute | solution.py:30
  107.0 7.5 %collective-permute-start.9 = (bf16[1,224,512]{2,1,0:T(8,128)(2,1)S(1)}, bf16[1,224,512]{2,1,0:T(8,128)(2,1)S(1)}, u32[]{:S(2)}, u32[]{:S(2)}) collective-permute-start(bf16[1,224,512]{2,1,0:T(8,128)(2,1)S(1)} %slice.313), channel_id=1, source_target_pairs={{0,7},{1,0},{2,1},{3,2},{4,3},{5,4},{6,5},{7,6},{8,15},{9,8},{10,9... | collective-permute-start | bytes 688136 | tf_op jit(solution)/shard_map/ppermute | solution.py:30
  115.3 11.2 %copy-start = (bf16[2,8,224,512]{3,2,1,0:T(8,128)(2,1)}, bf16[2,8,224,512]{3,2,1,0:T(8,128)(2,1)S(1)}, u32[]{:S(2)}) copy-start(bf16[2,8,224,512]{3,2,1,0:T(8,128)(2,1)S(1)} %constant_dynamic-slice_fusion.1) | copy-start | bytes 11010052
  116.4 7.8 %collective-permute-start.10 = (f32[2,256]{1,0:T(2,128)S(1)}, f32[2,256]{1,0:T(2,128)S(1)}, u32[]{:S(2)}, u32[]{:S(2)}) collective-permute-start(f32[2,256]{1,0:T(2,128)S(1)} %pad_maximum_fusion.11), channel_id=1, source_target_pairs={{0,16},{16,0},{32,48},{48,32},{64,80},{80,64},{96,112},{112,96},{1... | collective-permute-start | bytes 6152 | tf_op jit(solution)/shard_map/ppermute | solution.py:24
  126.5 3.5 %copy-start.2 = (f32[384]{0:T(512)S(1)}, f32[384]{0:T(512)}, u32[]{:S(2)}) copy-start(f32[384]{0:T(512)} %param.11) | copy-start | bytes 4612
  126.5 3.4 %collective-permute-start.15 = (f32[128,512]{1,0:T(8,128)S(1)}, f32[128,512]{1,0:T(8,128)S(1)}, u32[]{:S(2)}, u32[]{:S(2)}) collective-permute-start(f32[128,512]{1,0:T(8,128)S(1)} %pad_maximum_fusion.2), channel_id=1, source_target_pairs={{0,16},{16,0},{32,48},{48,32},{64,80},{80,64},{96,112},{112,96},{1... | collective-permute-start | bytes 786440 | tf_op jit(solution)/shard_map/ppermute | solution.py:24
  131.0 3.2 %collective-permute-start.16 = (bf16[128,384]{1,0:T(8,128)(2,1)S(1)}, bf16[128,384]{1,0:T(8,128)(2,1)S(1)}, u32[]{:S(2)}, u32[]{:S(2)}) collective-permute-start(bf16[128,384]{1,0:T(8,128)(2,1)S(1)} %pad_maximum_fusion.10), channel_id=1, source_target_pairs={{0,16},{16,0},{32,48},{48,32},{64,80},{80,64},{96,112},{112,96},{1... | collective-permute-start | bytes 294920 | tf_op jit(solution)/shard_map/ppermute | solution.py:24
  137.3 49.1 %all-to-all-start = ((bf16[8,464,256]{2,1,0:T(8,128)(2,1)}), bf16[8,464,256]{2,1,0:T(8,128)(2,1)S(1)}, u32[]{:S(2)}, u32[]{:S(2)}) async-start(bf16[8,464,256]{2,1,0:T(8,128)(2,1)} %pad_maximum_fusion), calls=%async_computation | async-start | bytes 3801088 | tf_op jit(solution)/shard_map/all_to_all | solution.py:196
  143.0 3.4 %collective-permute-start.19 = (bf16[128,128]{1,0:T(8,128)(2,1)S(1)}, bf16[128,128]{1,0:T(8,128)(2,1)S(1)}, u32[]{:S(2)}, u32[]{:S(2)}) collective-permute-start(bf16[128,128]{1,0:T(8,128)(2,1)S(1)} %convolution_convert_fusion.2), channel_id=1, source_target_pairs={{0,16},{16,0},{32,48},{48,32},{64,80},{80,64},{96,112},{112,96},{1... | collective-permute-start | bytes 98312 | tf_op jit(solution)/shard_map/ppermute | solution.py:24
  148.6 7.5 %collective-permute-start.20 = (bf16[2,224,128]{2,1,0:T(8,128)(2,1)S(1)}, bf16[2,224,128]{2,1,0:T(8,128)(2,1)S(1)}, u32[]{:S(2)}, u32[]{:S(2)}) collective-permute-start(bf16[2,224,128]{2,1,0:T(8,128)(2,1)S(1)} %get-tuple-element.29), channel_id=1, source_target_pairs={{0,32},{16,48},{32,64},{48,80},{64,96},{80,112},{96,0},{112,16},{1... | collective-permute-start | bytes 344072 | tf_op jit(solution)/shard_map/ppermute | solution.py:41
  150.5 6.4 %collective-permute-start.22 = (bf16[2,224,128]{2,1,0:T(8,128)(2,1)S(1)}, bf16[2,224,128]{2,1,0:T(8,128)(2,1)S(1)}, u32[]{:S(2)}, u32[]{:S(2)}) collective-permute-start(bf16[2,224,128]{2,1,0:T(8,128)(2,1)S(1)} %get-tuple-element.30), channel_id=1, source_target_pairs={{0,96},{16,112},{32,0},{48,16},{64,32},{80,48},{96,64},{112,80},{1... | collective-permute-start | bytes 344072 | tf_op jit(solution)/shard_map/ppermute | solution.py:41
  157.0 36.5 %collective-permute-start.21 = (bf16[4,224,128]{2,1,0:T(8,128)(2,1)S(1)}, bf16[4,224,128]{2,1,0:T(8,128)(2,1)S(1)}, u32[]{:S(2)}, u32[]{:S(2)}) collective-permute-start(bf16[4,224,128]{2,1,0:T(8,128)(2,1)S(1)} %pad_maximum_fusion.5), channel_id=1, source_target_pairs={{0,32},{16,48},{32,64},{48,80},{64,96},{80,112},{96,0},{112,16},{1... | collective-permute-start | bytes 688136 | tf_op jit(solution)/shard_map/ppermute | solution.py:41
  160.4 33.1 %collective-permute-start.23 = (bf16[4,224,128]{2,1,0:T(8,128)(2,1)}, bf16[4,224,128]{2,1,0:T(8,128)(2,1)S(1)}, u32[]{:S(2)}, u32[]{:S(2)}) collective-permute-start(bf16[4,224,128]{2,1,0:T(8,128)(2,1)} %pad_maximum_fusion.6), channel_id=1, source_target_pairs={{0,96},{16,112},{32,0},{48,16},{64,32},{80,48},{96,64},{112,80},{1... | collective-permute-start | bytes 688136 | tf_op jit(solution)/shard_map/ppermute | solution.py:41
  186.7 23.5 %copy-start.1 = (bf16[128,448]{0,1:T(8,128)(2,1)S(1)}, bf16[128,448]{0,1:T(8,128)(2,1)}, u32[]{:S(2)}) copy-start(bf16[128,448]{0,1:T(8,128)(2,1)} %param.7) | copy-start | bytes 344068
  187.2 15.5 %collective-permute-start.17 = (bf16[240,256]{1,0:T(8,128)(2,1)S(1)}, bf16[240,256]{1,0:T(8,128)(2,1)S(1)}, u32[]{:S(2)}, u32[]{:S(2)}) collective-permute-start(bf16[240,256]{1,0:T(8,128)(2,1)S(1)} %concatenate.71), channel_id=1, source_target_pairs={{0,8},{1,9},{2,10},{3,11},{4,12},{5,13},{6,14},{7,15},{8,0},{9,1},... | collective-permute-start | bytes 368648 | tf_op jit(solution)/shard_map/ppermute | solution.py:35
  193.7 15.5 %collective-permute-start.24 = (bf16[224,128]{1,0:T(8,128)(2,1)S(1)}, bf16[224,128]{1,0:T(8,128)(2,1)S(1)}, u32[]{:S(2)}, u32[]{:S(2)}) collective-permute-start(bf16[224,128]{1,0:T(8,128)(2,1)S(1)} %get-tuple-element.26), channel_id=1, source_target_pairs={{0,128},{16,144},{32,160},{48,176},{64,192},{80,208},{96,224},{112... | collective-permute-start | bytes 172040 | tf_op jit(solution)/shard_map/ppermute | solution.py:46
  195.6 13.6 %collective-permute-start.25 = (bf16[224,128]{1,0:T(8,128)(2,1)S(1)}, bf16[224,128]{1,0:T(8,128)(2,1)S(1)}, u32[]{:S(2)}, u32[]{:S(2)}) collective-permute-start(bf16[224,128]{1,0:T(8,128)(2,1)S(1)} %get-tuple-element.28), channel_id=1, source_target_pairs={{0,256},{16,272},{32,288},{48,304},{64,320},{80,336},{96,352},{112... | collective-permute-start | bytes 172040 | tf_op jit(solution)/shard_map/ppermute | solution.py:46
  199.2 10.0 %collective-permute-start.26 = (bf16[224,128]{1,0:T(8,128)(2,1)S(1)}, bf16[224,128]{1,0:T(8,128)(2,1)S(1)}, u32[]{:S(2)}, u32[]{:S(2)}) collective-permute-start(bf16[224,128]{1,0:T(8,128)(2,1)S(1)} %get-tuple-element.27), channel_id=1, source_target_pairs={{0,384},{16,400},{32,416},{48,432},{64,448},{80,464},{96,480},{112... | collective-permute-start | bytes 172040 | tf_op jit(solution)/shard_map/ppermute | solution.py:46
  202.9 7.2 %collective-permute-start.18 = (f32[232,128]{1,0:T(8,128)S(1)}, f32[232,128]{1,0:T(8,128)S(1)}, u32[]{:S(2)}, u32[]{:S(2)}) collective-permute-start(f32[232,128]{1,0:T(8,128)S(1)} %fusion.40), channel_id=1, source_target_pairs={{0,16},{16,0},{32,48},{48,32},{64,80},{80,64},{96,112},{112,96},{1... | collective-permute-start | bytes 356360 | tf_op jit(solution)/shard_map/ppermute | solution.py:24

commit v4 on v3

v4 whole, which is shorter than its diff:
```python
import jax
import jax.numpy as jnp
from jax import lax
from jax.sharding import PartitionSpec as P

SEQ = 128
E = 128
Z_COUNT = 8
X_COUNT = 4
norm_eps = 1e-05
f32 = jnp.float32
bf16 = jnp.bfloat16


def groups(count, key):
    found = {}
    for i in range(count):
        found.setdefault(key(i), []).append(i)
    return [found[k] for k in sorted(found)]


def swap_cores(x):
    n = lax.axis_size("dp")
    return lax.ppermute(x, "dp", [(i, i ^ 1) for i in range(n)])


def shift_z(x, step):
    n = lax.axis_size("tensor")
    pairs = [(i, i - i % Z_COUNT + (i + step) % Z_COUNT) for i in range(n)]
    return lax.ppermute(x, "tensor", pairs)


def swap_far(x):
    n = lax.axis_size("tensor")
    return lax.ppermute(x, "tensor", [(i, (i + Z_COUNT) % n) for i in range(n)])


def shift_x(x, step):
    n = lax.axis_size("dp")
    row = 2 * X_COUNT
    return lax.ppermute(x, "dp", [(i, i - i % row + (i + 2 * step) % row) for i in range(n)])


def along_y(x, target):
    n_dp, n_tensor = lax.axis_size("dp"), lax.axis_size("tensor")
    row = 2 * X_COUNT
    pairs = []
    for d in range(n_dp):
        for t in range(n_tensor):
            half, place = target(t // Z_COUNT, d // row)
            to = (place * row + d % row) * n_tensor + half * Z_COUNT + t % Z_COUNT
            pairs.append((d * n_tensor + t, to))
    return lax.ppermute(x, ("dp", "tensor"), pairs)


def move_weights(x):
    return along_y(x, lambda half, place: (place // 2, 2 * half + place % 2))


def ring_gather(own, shift, count, place, axis):
    found = {0: own}
    up = down = own
    middle = own.shape[0] // 2
    for step in range(1, count // 2):
        up, down = shift(up, 1), shift(down, -1)
        found[step], found[count - step] = up, down
    found[count // 2] = jnp.concatenate([shift(up[:middle], 1), shift(down[middle:], -1)])
    blocks = [found[count - 1 - j] for j in range(count)]
    line = jnp.stack(blocks + blocks[:-1], axis=axis)
    return lax.dynamic_slice_in_dim(line, count - 1 - place, count, axis)


def ring_scatter_x(parts, place):
    def part(step):
        return lax.dynamic_index_in_dim(parts, (place + step) % X_COUNT, 0, keepdims=False)

    across = part(2)
    middle = across.shape[0] // 2
    up = shift_x(across[:middle], 1).astype(f32)
    down = shift_x(across[middle:], -1).astype(f32)
    ahead, behind = part(1).astype(f32), part(-1).astype(f32)
    ahead = jnp.concatenate([ahead[:middle] + up, ahead[middle:]])
    behind = jnp.concatenate([behind[:middle], behind[middle:] + down])
    up, down = shift_x(ahead.astype(bf16), 1), shift_x(behind.astype(bf16), -1)
    return part(0).astype(f32) + up.astype(f32) + down.astype(f32)


def scatter_y(parts, place):
    count = parts.shape[0]
    sent = parts.astype(bf16)
    total = None
    for step in range(count):
        one = lax.dynamic_index_in_dim(sent, (place + step) % count, 0, keepdims=False)

        def target(half, place):
            part = (place + step) % count
            return part // 2, 2 * half + part % 2

        one = along_y(one, target).astype(f32)
        total = one if total is None else total + one
    return total


def split(x):
    high = lax.reduce_precision(x, 8, 7)
    return high.astype(bf16), (x - high).astype(bf16)


def dot(a, b, dims):
    return lax.dot_general(a, b, (dims, ((), ())), preferred_element_type=f32)


def attention(joined, context_grad, slope):
    queries = joined[:, :E]
    key_rows = joined[:, E : 2 * E]
    values = joined[:, 2 * E :]
    scores = dot(queries, key_rows, ((1,), (1,))) * E ** (-0.5)
    row = lax.broadcasted_iota(jnp.int32, (SEQ, SEQ), 0)
    col = lax.broadcasted_iota(jnp.int32, (SEQ, SEQ), 1)
    offsets = (col - row).astype(f32)
    scores = jnp.where(offsets <= 0.0, scores + slope * offsets, -1e30)
    soft = jax.nn.softmax(scores, axis=-1)
    soft_round = soft.astype(bf16)
    context = dot(soft_round, values, ((1,), (0,))).astype(bf16)
    prob_grad = dot(context_grad, values, ((1,), (1,)))
    value_grad = dot(soft_round, context_grad, ((0,), (0,)))
    row_dot = jnp.sum(soft * prob_grad, axis=-1, keepdims=True)
    score_grad = (soft * (prob_grad - row_dot) * E ** (-0.5)).astype(bf16)
    query_grad = dot(score_grad, key_rows, ((1,), (0,)))
    key_grad = dot(score_grad, queries, ((0,), (0,)))
    joined_grad = jnp.concatenate([query_grad, key_grad, value_grad], axis=1).astype(bf16)
    return context, joined_grad


def body(hidden_in, norm_gain, norm_bias, w_qkv, b_qkv, w_out, out_grad):
    n_tensor = lax.axis_size("tensor")
    depth = norm_gain.shape[0]
    width = depth // n_tensor
    part = width // 2
    quarter = Z_COUNT * part
    rank = lax.axis_index("tensor")
    z, far = rank % Z_COUNT, rank // Z_COUNT
    dp = lax.axis_index("dp")
    core, x, y = dp % 2, dp // 2 % X_COUNT, dp // (2 * X_COUNT)
    lines = groups(lax.axis_size("dp"), lambda i: i % (2 * X_COUNT))
    rings = groups(n_tensor, lambda i: i // Z_COUNT)

    def by_far(own, other):
        return jnp.stack([jnp.where(far == 0, own, other), jnp.where(far == 0, other, own)])

    hidden_t = hidden_in.T
    acts = jnp.concatenate([hidden_t, out_grad.T], axis=1).reshape(2, part, 2 * SEQ)
    mine = jnp.where(core == 0, acts[0], acts[1])
    other = swap_cores(jnp.where(core == 0, acts[1], acts[0]))
    block = jnp.concatenate([mine[:, :SEQ], other[:, :SEQ], mine[:, SEQ:], other[:, SEQ:]], axis=1)

    weight_block = move_weights(jnp.concatenate([w_qkv, w_out.T], axis=1))
    weight_block, block = lax.optimization_barrier((weight_block, block))
    column = lax.all_gather(weight_block, "dp", axis=0, axis_index_groups=lines)

    rows = ring_gather(block, shift_z, Z_COUNT, z, 0).reshape(quarter, 4 * SEQ)
    hidden = rows[:, : 2 * SEQ].astype(f32)
    grads = rows[:, 2 * SEQ :]
    joined_weight = ring_gather(column[:, :, : 3 * E], shift_x, X_COUNT, x, 1)
    joined_weight = joined_weight.reshape(2, quarter, 3 * E)
    out_weight = ring_gather(column[:, :, 3 * E :], shift_x, X_COUNT, x, 1)
    out_weight = out_weight.reshape(2, quarter, E)

    def merge(stats, stats_other, count):
        gap = stats[0] - stats_other[0]
        return jnp.stack(
            [
                0.5 * (stats[0] + stats_other[0]),
                stats[1] + stats_other[1] + gap * gap * (count / 2),
            ]
        )

    mean_part = jnp.sum(hidden, axis=0) / quarter
    stats = jnp.stack([mean_part, jnp.sum((hidden - mean_part) ** 2, axis=0)])
    stats = merge(stats, swap_far(stats), quarter)
    stats_other = swap_cores(stats)
    stats_other = jnp.concatenate([stats_other[:, SEQ:], stats_other[:, :SEQ]], axis=1)
    stats = merge(stats, stats_other, 2 * quarter)
    mean = stats[0]
    inv_std = lax.rsqrt(stats[1] / depth + norm_eps)

    def own_part(vector):
        vector = vector.reshape(2, Z_COUNT, 2, part)
        vector = jnp.where(far == 0, vector[0], vector[1])
        return jnp.where(core == 0, vector[:, 0], vector[:, 1]).reshape(quarter)

    gain, bias = own_part(norm_gain), own_part(norm_bias)
    normed = ((hidden - mean) * inv_std * gain[:, None] + bias[:, None]).astype(bf16)
    vectors = jnp.stack([*split(gain), *split(bias)])

    def own_head(pair):
        return jnp.where(far == 0, pair[0], pair[1]), jnp.where(far == 0, pair[1], pair[0])

    vector_parts = [dot(vectors, joined_weight[h], ((1,), (0,))) for h in range(2)]
    vector_parts = [
        jnp.stack([v[0] + v[1], v[2] + v[3], jnp.zeros_like(v[0]), jnp.zeros_like(v[0])])
        for v in vector_parts
    ]
    vector_parts = [jnp.concatenate([v, jnp.zeros_like(v)]) for v in vector_parts]
    joined_parts = [dot(normed, joined_weight[h], ((0,), (0,))) for h in range(2)]
    sent = jnp.stack(
        [jnp.concatenate([j[SEQ:], v]) for j, v in zip(joined_parts, vector_parts)]
    )
    kept = jnp.stack(
        [jnp.concatenate([j[:SEQ], v]) for j, v in zip(joined_parts, vector_parts)]
    )
    own, away = own_head(kept + swap_cores(sent))
    away_high, away_low = split(away[SEQ:])
    away = swap_far(jnp.concatenate([away[:SEQ].astype(bf16), away_high, away_low]))
    away = away.astype(f32)
    plain = own[:SEQ] + away[:SEQ]
    vector = own[SEQ:] + away[SEQ : SEQ + 8] + away[SEQ + 8 :]
    gain_weight, bias_weight = vector[0], vector[1]
    joined = (plain + b_qkv).astype(bf16)

    grad_parts = jnp.stack([dot(grads, out_weight[h], ((0,), (0,))) for h in range(2)])
    own, away = own_head(grad_parts[:, :SEQ] + swap_cores(grad_parts[:, SEQ:]))
    context_grad = (own + swap_far(away.astype(bf16)).astype(f32)).astype(bf16)

    slope = 2.0 ** (-8.0 * (rank + 1).astype(f32) / n_tensor)
    context, joined_grad = attention(joined, context_grad, slope)
    joined_grad_f = joined_grad.astype(f32)
    sums = jnp.stack(
        [
            jnp.sum(joined_grad_f * gain_weight, axis=1),
            jnp.sum(joined_grad_f * (plain - bias_weight), axis=1),
        ]
    )

    def pack(sums):
        high, low = split(sums)
        return jnp.concatenate([high, low, jnp.zeros((12, sums.shape[1]), bf16)])

    def unpack(rows):
        rows = rows.astype(f32)
        return rows[0:2] + rows[2:4]

    packed = jnp.pad(pack(sums), ((0, 0), (0, 3 * E)))
    result = jnp.concatenate([jnp.concatenate([context, joined_grad], axis=1), packed])
    result_far = swap_far(result)
    sums = sums + unpack(result_far[SEQ:, :SEQ])
    heads = by_far(result[:SEQ], result_far[:SEQ])
    packed = jnp.pad(pack(sums), ((0, 0), (0, 3 * E)))
    heads_sent = jnp.concatenate([heads, jnp.stack([packed, jnp.zeros_like(packed)])], axis=1)
    heads_other = swap_cores(heads_sent)
    sums = jnp.concatenate([sums, unpack(heads_other[0, SEQ:, :SEQ])], axis=1)
    heads = jnp.concatenate([heads, heads_other[:, :SEQ]], axis=1)

    context_pair = jnp.concatenate([heads[0, :, :E], heads[1, :, :E]], axis=1)
    weight_part = dot(grads, context_pair, ((1,), (0,))).astype(bf16)
    weight_part = weight_part.reshape(2, X_COUNT, part, 2, E)
    weight_parts = weight_part.transpose(1, 3, 0, 2, 4).reshape(X_COUNT, 4, part, E)

    group_part = sum(
        dot(joined_weight[h], heads[h, :, E:], ((1,), (1,))) for h in range(2)
    ).astype(bf16)
    extra = jnp.broadcast_to(pack(sums)[None], (Z_COUNT, 16, 2 * SEQ))
    payload = jnp.concatenate([group_part.reshape(Z_COUNT, part, 2 * SEQ), extra], axis=1)
    group_parts = lax.all_to_all(payload, "tensor", 0, 0, tiled=True, axis_index_groups=rings)
    total = jnp.sum(group_parts.astype(f32), axis=0)
    sums = total[part : part + 2, :SEQ] + total[part + 2 : part + 4, :SEQ]
    total = total[:part]
    total_other = swap_cores(total[:, SEQ:])
    total = total[:, :SEQ]
    normed_grad = jnp.where(
        core == 0,
        jnp.concatenate([total, total_other]),
        jnp.concatenate([total_other, total]),
    )
    mean_grad = sums[0] / depth
    mean_cross = sums[1] / depth

    own_gain = lax.dynamic_slice_in_dim(norm_gain, rank * width, width)
    scaled_grad = normed_grad * own_gain[:, None]
    scaled = (hidden_t.astype(f32) - mean[:SEQ]) * inv_std[:SEQ]
    input_grad = inv_std[:SEQ] * (scaled_grad - mean_grad - scaled * mean_cross)

    grad_out_weight = scatter_y(ring_scatter_x(weight_parts, x), y)
    return input_grad.astype(bf16).T, grad_out_weight.T


def solution(mesh):
    in_specs = (
        P("dp", "tensor"),
        P(),
        P(),
        P("dp", "tensor"),
        P("tensor"),
        P("tensor", "dp"),
        P("dp", "tensor"),
    )
    out_specs = (P("dp", "tensor"), P("tensor", "dp"))
    return jax.shard_map(body, mesh=mesh, in_specs=in_specs, out_specs=out_specs, check_vma=False)
```

time: 212 us -> 239 us (1.13)
  the two profiles are of different devices: /device:TPU:1 before, /device:TPU:17 now
where the time goes in v4:
time: 239 us; the launch traced here: 237 us
  starting transfers between devices  147 us (62%)
  waiting for transfers between devices  38.4 us (16%)
  blocking collectives  16.3 us (7%)
  other arithmetic  14.4 us (6%)
  local copies, waits for them, and re-layouts  10.7 us (4%)
  matrix products  7.9 us (3%)
    ppermute x12, starting transfers between devices, shift_x(): lax.ppermute(x, 'dp', [(i, i - i % row + (i + 2 * step) % row) for i in r...  39.9 us
    ppermute x6, starting transfers between devices, swap_cores(): return lax.ppermute(x, 'dp', [(i, i ^ 1) for i in range(n)])  32.8 us
    ppermute x8, starting transfers between devices, shift_z(): return lax.ppermute(x, 'tensor', pairs)  32.5 us
    ppermute x5, starting transfers between devices, along_y(): return lax.ppermute(x, ('dp', 'tensor'), pairs)  19.2 us
    ppermute x4, starting transfers between devices, swap_far(): return lax.ppermute(x, 'tensor', [(i, (i + Z_COUNT) % n) for i in range(n)])  18.9 us
    all_gather x1, blocking collectives, body(): column = lax.all_gather(weight_block, 'dp', axis=0, axis_index_groups=lines)  16.3 us
    ppermute x4, waiting for transfers between devices, swap_far(): return lax.ppermute(x, 'tensor', [(i, (i + Z_COUNT) % n) for i in range(n)])  15.6 us
    ppermute x12, waiting for transfers between devices, shift_x(): lax.ppermute(x, 'dp', [(i, i - i % row + (i + 2 * step) % row) for i in r...  8.01 us
  transfers between devices with their start and end apart: 36, of which 14 were waited for; matrix products, arithmetic and copies ran while one was open for 11% of the time, Pallas kernels for 0%

profile of v4, /device:TPU:17, one launch (start us, length us, event | category | flops | bytes accessed | tf_op | source)
XLA Modules:
  0.0 236.9 jit_solution(10844720859297621707)
XLA Ops:
  1.6 5.4 %collective-permute-start = (bf16[224,512]{1,0:T(8,128)(2,1)S(1)}, bf16[224,512]{1,0:T(8,128)(2,1)S(1)}, u32[]{:S(2)}, u32[]{:S(2)}) collective-permute-start(bf16[224,512]{1,0:T(8,128)(2,1)S(1)} %pad_maximum_fusion.3), channel_id=1, source_target_pairs={{0,0},{1,1},{2,2},{3,3},{4,4},{5,5},{6,6},{7,7},{8,256},{9,257},{1... | collective-permute-start | bytes 688136 | tf_op jit(solution)/shard_map/ppermute | solution.py:53
  8.1 2.9 %collective-permute-start.1 = (bf16[224,256]{1,0:T(8,128)(2,1)S(1)}, bf16[224,256]{1,0:T(8,128)(2,1)S(1)}, u32[]{:S(2)}, u32[]{:S(2)}) collective-permute-start(bf16[224,256]{1,0:T(8,128)(2,1)S(1)} %get-tuple-element.43), channel_id=1, source_target_pairs={{0,16},{16,0},{32,48},{48,32},{64,80},{80,64},{96,112},{112,96},{1... | collective-permute-start | bytes 344072 | tf_op jit(solution)/shard_map/ppermute | solution.py:24
  14.0 3.1 %collective-permute-done = bf16[224,512]{1,0:T(8,128)(2,1)S(1)} collective-permute-done((bf16[224,512]{1,0:T(8,128)(2,1)S(1)}, bf16[224,512]{1,0:T(8,128)(2,1)S(1)}, u32[]{:S(2)}, u32[]{:S(2)}) %collective-permute-start) | collective-permute-done | bytes 229408 | tf_op jit(solution)/shard_map/ppermute | solution.py:53
  17.0 16.3 %all-gather = bf16[896,512]{1,0:T(8,128)(2,1)S(1)} all-gather(bf16[224,512]{1,0:T(8,128)(2,1)S(1)} %collective-permute-done), channel_id=2, replica_groups={{0,128,256,384},{16,144,272,400},{32,160,288,416},{48,176,304,432},{64,..., dimensions={0}, use_global_device_ids=true | all-gather | bytes 1146880 | tf_op jit(solution)/shard_map/all_gather | solution.py:159
  33.4 4.4 %collective-permute-start.18 = (bf16[4,224,128]{2,1,0:T(8,128)(2,1)S(1)}, bf16[4,224,128]{2,1,0:T(8,128)(2,1)S(1)}, u32[]{:S(2)}, u32[]{:S(2)}) collective-permute-start(bf16[4,224,128]{2,1,0:T(8,128)(2,1)S(1)} %slice.514), channel_id=1, source_target_pairs={{0,96},{16,112},{32,0},{48,16},{64,32},{80,48},{96,64},{112,80},{1... | collective-permute-start | bytes 688136 | tf_op jit(solution)/shard_map/ppermute | solution.py:41
  37.7 1.9 collective-permute-start.19
  39.8 4.6 %collective-permute-start.12 = (bf16[4,224,384]{2,1,0:T(8,128)(2,1)S(1)}, bf16[4,224,384]{2,1,0:T(8,128)(2,1)S(1)}, u32[]{:S(2)}, u32[]{:S(2)}) collective-permute-start(bf16[4,224,384]{2,1,0:T(8,128)(2,1)S(1)} %slice.485), channel_id=1, source_target_pairs={{0,96},{16,112},{32,0},{48,16},{64,32},{80,48},{96,64},{112,80},{1... | collective-permute-start | bytes 2064392 | tf_op jit(solution)/shard_map/ppermute | solution.py:41
  44.4 1.9 collective-permute-start.13
  46.3 10.7 %collective-permute-start.2 = (bf16[224,512]{1,0:T(8,128)(2,1)S(1)}, bf16[224,512]{1,0:T(8,128)(2,1)S(1)}, u32[]{:S(2)}, u32[]{:S(2)}) collective-permute-start(bf16[224,512]{1,0:T(8,128)(2,1)S(1)} %pad_maximum_fusion.4), channel_id=1, source_target_pairs={{0,7},{1,0},{2,1},{3,2},{4,3},{5,4},{6,5},{7,6},{8,15},{9,8},{10,9... | collective-permute-start | bytes 688136 | tf_op jit(solution)/shard_map/ppermute | solution.py:30
  57.0 1.9 collective-permute-start.5
  58.9 4.6 %collective-permute-start.21 = (bf16[2,224,128]{2,1,0:T(8,128)(2,1)S(1)}, bf16[2,224,128]{2,1,0:T(8,128)(2,1)S(1)}, u32[]{:S(2)}, u32[]{:S(2)}) collective-permute-start(bf16[2,224,128]{2,1,0:T(8,128)(2,1)S(1)} %slice.516), channel_id=1, source_target_pairs={{0,96},{16,112},{32,0},{48,16},{64,32},{80,48},{96,64},{112,80},{1... | collective-permute-start | bytes 344072 | tf_op jit(solution)/shard_map/ppermute | solution.py:41
  63.6 1.9 collective-permute-start.20
  65.5 4.6 %collective-permute-start.3 = (bf16[224,512]{1,0:T(8,128)(2,1)S(1)}, bf16[224,512]{1,0:T(8,128)(2,1)S(1)}, u32[]{:S(2)}, u32[]{:S(2)}) collective-permute-start(bf16[224,512]{1,0:T(8,128)(2,1)S(1)} %collective-permute-done.2), channel_id=1, source_target_pairs={{0,7},{1,0},{2,1},{3,2},{4,3},{5,4},{6,5},{7,6},{8,15},{9,8},{10,9... | collective-permute-start | bytes 688136 | tf_op jit(solution)/shard_map/ppermute | solution.py:30
  70.1 1.9 collective-permute-start.6
  73.0 5.0 %collective-permute-start.4 = (bf16[224,512]{1,0:T(8,128)(2,1)S(1)}, bf16[224,512]{1,0:T(8,128)(2,1)S(1)}, u32[]{:S(2)}, u32[]{:S(2)}) collective-permute-start(bf16[224,512]{1,0:T(8,128)(2,1)S(1)} %collective-permute-done.3), channel_id=1, source_target_pairs={{0,7},{1,0},{2,1},{3,2},{4,3},{5,4},{6,5},{7,6},{8,15},{9,8},{10,9... | collective-permute-start | bytes 688136 | tf_op jit(solution)/shard_map/ppermute | solution.py:30
  78.1 1.9 collective-permute-start.7
  80.1 4.6 %collective-permute-start.15 = (bf16[2,224,384]{2,1,0:T(8,128)(2,1)S(1)}, bf16[2,224,384]{2,1,0:T(8,128)(2,1)S(1)}, u32[]{:S(2)}, u32[]{:S(2)}) collective-permute-start(bf16[2,224,384]{2,1,0:T(8,128)(2,1)S(1)} %slice.487), channel_id=1, source_target_pairs={{0,96},{16,112},{32,0},{48,16},{64,32},{80,48},{96,64},{112,80},{1... | collective-permute-start | bytes 1032200 | tf_op jit(solution)/shard_map/ppermute | solution.py:41
  84.7 1.9 collective-permute-start.14
  86.7 4.6 %collective-permute-start.9 = (bf16[112,512]{1,0:T(8,128)(2,1)S(1)}, bf16[112,512]{1,0:T(8,128)(2,1)S(1)}, u32[]{:S(2)}, u32[]{:S(2)}) collective-permute-start(bf16[112,512]{1,0:T(8,128)(2,1)S(1)} %slice.477), channel_id=1, source_target_pairs={{0,7},{1,0},{2,1},{3,2},{4,3},{5,4},{6,5},{7,6},{8,15},{9,8},{10,9... | collective-permute-start | bytes 344072 | tf_op jit(solution)/shard_map/ppermute | solution.py:30
  91.3 1.9 collective-permute-start.8
  93.3 4.7 %collective-permute-done.8 = bf16[112,512]{1,0:T(8,128)(2,1)S(1)} collective-permute-done((bf16[112,512]{1,0:T(8,128)(2,1)S(1)}, bf16[112,512]{1,0:T(8,128)(2,1)S(1)}, u32[]{:S(2)}, u32[]{:S(2)}) %collective-permute-start.8) | collective-permute-done | bytes 114720 | tf_op jit(solution)/shard_map/ppermute | solution.py:30
  99.1 4.8 %collective-permute-start.10 = (f32[2,256]{1,0:T(2,128)S(1)}, f32[2,256]{1,0:T(2,128)S(1)}, u32[]{:S(2)}, u32[]{:S(2)}) collective-permute-start(f32[2,256]{1,0:T(2,128)S(1)} %pad_maximum_fusion.13), channel_id=1, source_target_pairs={{0,8},{1,9},{2,10},{3,11},{4,12},{5,13},{6,14},{7,15},{8,0},{9,1},... | collective-permute-start | bytes 6152 | tf_op jit(solution)/shard_map/ppermute | solution.py:35
  104.8 2.5 %collective-permute-done.10 = f32[2,256]{1,0:T(2,128)S(1)} collective-permute-done((f32[2,256]{1,0:T(2,128)S(1)}, f32[2,256]{1,0:T(2,128)S(1)}, u32[]{:S(2)}, u32[]{:S(2)}) %collective-permute-start.10) | collective-permute-done | bytes 2080 | tf_op jit(solution)/shard_map/ppermute | solution.py:35
  107.9 12.8 %collective-permute-start.11 = (f32[2,256]{1,0:T(2,128)S(1)}, f32[2,256]{1,0:T(2,128)S(1)}, u32[]{:S(2)}, u32[]{:S(2)}) collective-permute-start(f32[2,256]{1,0:T(2,128)S(1)} %pad_maximum_fusion.14), channel_id=1, source_target_pairs={{0,16},{16,0},{32,48},{48,32},{64,80},{80,64},{96,112},{112,96},{1... | collective-permute-start | bytes 6152 | tf_op jit(solution)/shard_map/ppermute | solution.py:24
  121.4 1.9 collective-permute-start.22
  125.1 1.4 fusion.71
  126.5 1.4 fusion.73
  131.1 2.4 %collective-permute-start.16 = (f32[2,136,384]{2,1,0:T(8,128)}, f32[2,136,384]{2,1,0:T(8,128)}, u32[]{:S(2)}, u32[]{:S(2)}) collective-permute-start(f32[2,136,384]{2,1,0:T(8,128)} %pad_maximum_fusion.2), channel_id=1, source_target_pairs={{0,16},{16,0},{32,48},{48,32},{64,80},{80,64},{96,112},{112,96},{1... | collective-permute-start | bytes 1253384 | tf_op jit(solution)/shard_map/ppermute | solution.py:24
  134.5 7.6 %collective-permute-start.23 = (bf16[128,128]{1,0:T(8,128)(2,1)S(1)}, bf16[128,128]{1,0:T(8,128)(2,1)}, u32[]{:S(2)}, u32[]{:S(2)}) collective-permute-start(bf16[128,128]{1,0:T(8,128)(2,1)S(1)} %fusion.45), channel_id=1, source_target_pairs={{0,8},{1,9},{2,10},{3,11},{4,12},{5,13},{6,14},{7,15},{8,0},{9,1},... | collective-permute-start | bytes 98312 | tf_op jit(solution)/shard_map/ppermute | solution.py:35
  142.1 1.7 concatenate.97
  144.9 1.9 collective-permute-start.17
  147.7 7.5 %collective-permute-done.17 = bf16[144,384]{1,0:T(8,128)(2,1)S(1)} collective-permute-done((bf16[144,384]{1,0:T(8,128)(2,1)S(1)}, bf16[144,384]{1,0:T(8,128)(2,1)S(1)}, u32[]{:S(2)}, u32[]{:S(2)}) %collective-permute-start.17) | collective-permute-done | bytes 110624 | tf_op jit(solution)/shard_map/ppermute | solution.py:35
  156.6 4.6 %collective-permute-start.24 = (bf16[144,512]{1,0:T(8,128)(2,1)S(1)}, bf16[144,512]{1,0:T(8,128)(2,1)S(1)}, u32[]{:S(2)}, u32[]{:S(2)}) collective-permute-start(bf16[144,512]{1,0:T(8,128)(2,1)S(1)} %fusion.33), channel_id=1, source_target_pairs={{0,8},{1,9},{2,10},{3,11},{4,12},{5,13},{6,14},{7,15},{8,0},{9,1},... | collective-permute-start | bytes 442376 | tf_op jit(solution)/shard_map/ppermute | solution.py:35
  161.2 5.6 %collective-permute-done.24 = bf16[144,512]{1,0:T(8,128)(2,1)S(1)} collective-permute-done((bf16[144,512]{1,0:T(8,128)(2,1)S(1)}, bf16[144,512]{1,0:T(8,128)(2,1)S(1)}, u32[]{:S(2)}, u32[]{:S(2)}) %collective-permute-start.24) | collective-permute-done | bytes 147488 | tf_op jit(solution)/shard_map/ppermute | solution.py:35
  167.0 7.0 %collective-permute-start.25 = (bf16[2,144,512]{2,1,0:T(8,128)(2,1)S(1)}, bf16[2,144,512]{2,1,0:T(8,128)(2,1)}, u32[]{:S(2)}, u32[]{:S(2)}) collective-permute-start(bf16[2,144,512]{2,1,0:T(8,128)(2,1)S(1)} %fusion.17), channel_id=1, source_target_pairs={{0,16},{16,0},{32,48},{48,32},{64,80},{80,64},{96,112},{112,96},{1... | collective-permute-start | bytes 884744 | tf_op jit(solution)/shard_map/ppermute | solution.py:24
  179.6 3.7 %all-to-all-start = ((bf16[8,240,256]{2,1,0:T(8,128)(2,1)}), bf16[8,240,256]{2,1,0:T(8,128)(2,1)S(1)}, u32[]{:S(2)}, u32[]{:S(2)}) async-start(bf16[8,240,256]{2,1,0:T(8,128)(2,1)} %pad_maximum_fusion), calls=%async_computation | async-start | bytes 1966080 | tf_op jit(solution)/shard_map/all_to_all | solution.py:264
  184.7 2.2 reshape.240
  187.1 1.9 collective-permute-start.27
  189.0 4.8 %collective-permute-start.29 = (bf16[2,224,128]{2,1,0:T(8,128)(2,1)S(1)}, bf16[2,224,128]{2,1,0:T(8,128)(2,1)S(1)}, u32[]{:S(2)}, u32[]{:S(2)}) collective-permute-start(bf16[2,224,128]{2,1,0:T(8,128)(2,1)S(1)} %get-tuple-element.24), channel_id=1, source_target_pairs={{0,96},{16,112},{32,0},{48,16},{64,32},{80,48},{96,64},{112,80},{1... | collective-permute-start | bytes 344072 | tf_op jit(solution)/shard_map/ppermute | solution.py:41
  196.1 5.3 %collective-permute-start.30 = (bf16[4,224,128]{2,1,0:T(8,128)(2,1)S(1)}, bf16[4,224,128]{2,1,0:T(8,128)(2,1)S(1)}, u32[]{:S(2)}, u32[]{:S(2)}) collective-permute-start(bf16[4,224,128]{2,1,0:T(8,128)(2,1)S(1)} %pad_maximum_fusion.6), channel_id=1, source_target_pairs={{0,96},{16,112},{32,0},{48,16},{64,32},{80,48},{96,64},{112,80},{1... | collective-permute-start | bytes 688136 | tf_op jit(solution)/shard_map/ppermute | solution.py:41
  201.4 2.1 collective-permute-start.28
  205.0 5.2 %collective-permute-done.28 = bf16[4,224,128]{2,1,0:T(8,128)(2,1)S(1)} collective-permute-done((bf16[4,224,128]{2,1,0:T(8,128)(2,1)S(1)}, bf16[4,224,128]{2,1,0:T(8,128)(2,1)S(1)}, u32[]{:S(2)}, u32[]{:S(2)}) %collective-permute-start.28) | collective-permute-done | bytes 229408 | tf_op jit(solution)/shard_map/ppermute | solution.py:41
  210.4 1.9 collective-permute-start.34
  212.3 4.2 %collective-permute-start.33 = (bf16[224,128]{1,0:T(8,128)(2,1)S(1)}, bf16[224,128]{1,0:T(8,128)(2,1)S(1)}, u32[]{:S(2)}, u32[]{:S(2)}) collective-permute-start(bf16[224,128]{1,0:T(8,128)(2,1)S(1)} %get-tuple-element.40), channel_id=1, source_target_pairs={{0,8},{1,9},{2,10},{3,11},{4,12},{5,13},{6,14},{7,15},{8,264},{9,2... | collective-permute-start | bytes 172040 | tf_op jit(solution)/shard_map/ppermute | solution.py:53
  216.6 4.1 %collective-permute-start.32 = (bf16[224,128]{1,0:T(8,128)(2,1)S(1)}, bf16[224,128]{1,0:T(8,128)(2,1)S(1)}, u32[]{:S(2)}, u32[]{:S(2)}) collective-permute-start(bf16[224,128]{1,0:T(8,128)(2,1)S(1)} %get-tuple-element.41), channel_id=1, source_target_pairs={{0,128},{1,129},{2,130},{3,131},{4,132},{5,133},{6,134},{7,135},{8... | collective-permute-start | bytes 172040 | tf_op jit(solution)/shard_map/ppermute | solution.py:53
  220.6 3.6 %collective-permute-start.31 = (bf16[224,128]{1,0:T(8,128)(2,1)S(1)}, bf16[224,128]{1,0:T(8,128)(2,1)S(1)}, u32[]{:S(2)}, u32[]{:S(2)}) collective-permute-start(bf16[224,128]{1,0:T(8,128)(2,1)S(1)} %get-tuple-element.38), channel_id=1, source_target_pairs={{0,0},{1,1},{2,2},{3,3},{4,4},{5,5},{6,6},{7,7},{8,256},{9,257},{1... | collective-permute-start | bytes 172040 | tf_op jit(solution)/shard_map/ppermute | solution.py:53
  225.1 3.4 %collective-permute-done.31 = bf16[224,128]{1,0:T(8,128)(2,1)S(1)} collective-permute-done((bf16[224,128]{1,0:T(8,128)(2,1)S(1)}, bf16[224,128]{1,0:T(8,128)(2,1)S(1)}, u32[]{:S(2)}, u32[]{:S(2)}) %collective-permute-start.31) | collective-permute-done | bytes 57376 | tf_op jit(solution)/shard_map/ppermute | solution.py:53
  229.4 5.8 %collective-permute-start.26 = (f32[224,128]{1,0:T(8,128)S(1)}, f32[224,128]{1,0:T(8,128)S(1)}, u32[]{:S(2)}, u32[]{:S(2)}) collective-permute-start(f32[224,128]{1,0:T(8,128)S(1)} %get-tuple-element.36), channel_id=1, source_target_pairs={{0,16},{16,0},{32,48},{48,32},{64,80},{80,64},{96,112},{112,96},{1... | collective-permute-start | bytes 344072 | tf_op jit(solution)/shard_map/ppermute | solution.py:24
  (203 shorter events, 32.7 us)
Async XLA Ops:
  1.6 15.4 %collective-permute-start = (bf16[224,512]{1,0:T(8,128)(2,1)S(1)}, bf16[224,512]{1,0:T(8,128)(2,1)S(1)}, u32[]{:S(2)}, u32[]{:S(2)}) collective-permute-start(bf16[224,512]{1,0:T(8,128)(2,1)S(1)} %pad_maximum_fusion.3), channel_id=1, source_target_pairs={{0,0},{1,1},{2,2},{3,3},{4,4},{5,5},{6,6},{7,7},{8,256},{9,257},{1... | collective-permute-start | bytes 688136 | tf_op jit(solution)/shard_map/ppermute | solution.py:53
  8.1 5.8 %collective-permute-start.1 = (bf16[224,256]{1,0:T(8,128)(2,1)S(1)}, bf16[224,256]{1,0:T(8,128)(2,1)S(1)}, u32[]{:S(2)}, u32[]{:S(2)}) collective-permute-start(bf16[224,256]{1,0:T(8,128)(2,1)S(1)} %get-tuple-element.43), channel_id=1, source_target_pairs={{0,16},{16,0},{32,48},{48,32},{64,80},{80,64},{96,112},{112,96},{1... | collective-permute-start | bytes 344072 | tf_op jit(solution)/shard_map/ppermute | solution.py:24
  33.4 23.6 %collective-permute-start.18 = (bf16[4,224,128]{2,1,0:T(8,128)(2,1)S(1)}, bf16[4,224,128]{2,1,0:T(8,128)(2,1)S(1)}, u32[]{:S(2)}, u32[]{:S(2)}) collective-permute-start(bf16[4,224,128]{2,1,0:T(8,128)(2,1)S(1)} %slice.514), channel_id=1, source_target_pairs={{0,96},{16,112},{32,0},{48,16},{64,32},{80,48},{96,64},{112,80},{1... | collective-permute-start | bytes 688136 | tf_op jit(solution)/shard_map/ppermute | solution.py:41
  37.7 21.2 %collective-permute-start.19 = (bf16[4,224,128]{2,1,0:T(8,128)(2,1)S(1)}, bf16[4,224,128]{2,1,0:T(8,128)(2,1)S(1)}, u32[]{:S(2)}, u32[]{:S(2)}) collective-permute-start(bf16[4,224,128]{2,1,0:T(8,128)(2,1)S(1)} %slice.514), channel_id=1, source_target_pairs={{0,32},{16,48},{32,64},{48,80},{64,96},{80,112},{96,0},{112,16},{1... | collective-permute-start | bytes 688136 | tf_op jit(solution)/shard_map/ppermute | solution.py:41
  39.8 40.3 %collective-permute-start.12 = (bf16[4,224,384]{2,1,0:T(8,128)(2,1)S(1)}, bf16[4,224,384]{2,1,0:T(8,128)(2,1)S(1)}, u32[]{:S(2)}, u32[]{:S(2)}) collective-permute-start(bf16[4,224,384]{2,1,0:T(8,128)(2,1)S(1)} %slice.485), channel_id=1, source_target_pairs={{0,96},{16,112},{32,0},{48,16},{64,32},{80,48},{96,64},{112,80},{1... | collective-permute-start | bytes 2064392 | tf_op jit(solution)/shard_map/ppermute | solution.py:41
  44.4 40.3 %collective-permute-start.13 = (bf16[4,224,384]{2,1,0:T(8,128)(2,1)S(1)}, bf16[4,224,384]{2,1,0:T(8,128)(2,1)S(1)}, u32[]{:S(2)}, u32[]{:S(2)}) collective-permute-start(bf16[4,224,384]{2,1,0:T(8,128)(2,1)S(1)} %slice.485), channel_id=1, source_target_pairs={{0,32},{16,48},{32,64},{48,80},{64,96},{80,112},{96,0},{112,16},{1... | collective-permute-start | bytes 2064392 | tf_op jit(solution)/shard_map/ppermute | solution.py:41
  46.3 17.3 %collective-permute-start.2 = (bf16[224,512]{1,0:T(8,128)(2,1)S(1)}, bf16[224,512]{1,0:T(8,128)(2,1)S(1)}, u32[]{:S(2)}, u32[]{:S(2)}) collective-permute-start(bf16[224,512]{1,0:T(8,128)(2,1)S(1)} %pad_maximum_fusion.4), channel_id=1, source_target_pairs={{0,7},{1,0},{2,1},{3,2},{4,3},{5,4},{6,5},{7,6},{8,15},{9,8},{10,9... | collective-permute-start | bytes 688136 | tf_op jit(solution)/shard_map/ppermute | solution.py:30
  57.0 8.5 %collective-permute-start.5 = (bf16[224,512]{1,0:T(8,128)(2,1)S(1)}, bf16[224,512]{1,0:T(8,128)(2,1)S(1)}, u32[]{:S(2)}, u32[]{:S(2)}) collective-permute-start(bf16[224,512]{1,0:T(8,128)(2,1)S(1)} %pad_maximum_fusion.4), channel_id=1, source_target_pairs={{0,1},{1,2},{2,3},{3,4},{4,5},{5,6},{6,7},{7,0},{8,9},{9,10},{10,1... | collective-permute-start | bytes 688136 | tf_op jit(solution)/shard_map/ppermute | solution.py:30
  58.9 11.2 %collective-permute-start.21 = (bf16[2,224,128]{2,1,0:T(8,128)(2,1)S(1)}, bf16[2,224,128]{2,1,0:T(8,128)(2,1)S(1)}, u32[]{:S(2)}, u32[]{:S(2)}) collective-permute-start(bf16[2,224,128]{2,1,0:T(8,128)(2,1)S(1)} %slice.516), channel_id=1, source_target_pairs={{0,96},{16,112},{32,0},{48,16},{64,32},{80,48},{96,64},{112,80},{1... | collective-permute-start | bytes 344072 | tf_op jit(solution)/shard_map/ppermute | solution.py:41
  63.6 8.5 %collective-permute-start.20 = (bf16[2,224,128]{2,1,0:T(8,128)(2,1)S(1)}, bf16[2,224,128]{2,1,0:T(8,128)(2,1)S(1)}, u32[]{:S(2)}, u32[]{:S(2)}) collective-permute-start(bf16[2,224,128]{2,1,0:T(8,128)(2,1)S(1)} %slice.515), channel_id=1, source_target_pairs={{0,32},{16,48},{32,64},{48,80},{64,96},{80,112},{96,0},{112,16},{1... | collective-permute-start | bytes 344072 | tf_op jit(solution)/shard_map/ppermute | solution.py:41
  65.5 7.5 %collective-permute-start.3 = (bf16[224,512]{1,0:T(8,128)(2,1)S(1)}, bf16[224,512]{1,0:T(8,128)(2,1)S(1)}, u32[]{:S(2)}, u32[]{:S(2)}) collective-permute-start(bf16[224,512]{1,0:T(8,128)(2,1)S(1)} %collective-permute-done.2), channel_id=1, source_target_pairs={{0,7},{1,0},{2,1},{3,2},{4,3},{5,4},{6,5},{7,6},{8,15},{9,8},{10,9... | collective-permute-start | bytes 688136 | tf_op jit(solution)/shard_map/ppermute | solution.py:30
  70.1 8.0 %collective-permute-start.6 = (bf16[224,512]{1,0:T(8,128)(2,1)S(1)}, bf16[224,512]{1,0:T(8,128)(2,1)S(1)}, u32[]{:S(2)}, u32[]{:S(2)}) collective-permute-start(bf16[224,512]{1,0:T(8,128)(2,1)S(1)} %collective-permute-done.5), channel_id=1, source_target_pairs={{0,1},{1,2},{2,3},{3,4},{4,5},{5,6},{6,7},{7,0},{8,9},{9,10},{10,1... | collective-permute-start | bytes 688136 | tf_op jit(solution)/shard_map/ppermute | solution.py:30
  73.0 13.6 %collective-permute-start.4 = (bf16[224,512]{1,0:T(8,128)(2,1)S(1)}, bf16[224,512]{1,0:T(8,128)(2,1)S(1)}, u32[]{:S(2)}, u32[]{:S(2)}) collective-permute-start(bf16[224,512]{1,0:T(8,128)(2,1)S(1)} %collective-permute-done.3), channel_id=1, source_target_pairs={{0,7},{1,0},{2,1},{3,2},{4,3},{5,4},{6,5},{7,6},{8,15},{9,8},{10,9... | collective-permute-start | bytes 688136 | tf_op jit(solution)/shard_map/ppermute | solution.py:30
  78.1 13.2 %collective-permute-start.7 = (bf16[224,512]{1,0:T(8,128)(2,1)S(1)}, bf16[224,512]{1,0:T(8,128)(2,1)S(1)}, u32[]{:S(2)}, u32[]{:S(2)}) collective-permute-start(bf16[224,512]{1,0:T(8,128)(2,1)S(1)} %collective-permute-done.6), channel_id=1, source_target_pairs={{0,1},{1,2},{2,3},{3,4},{4,5},{5,6},{6,7},{7,0},{8,9},{9,10},{10,1... | collective-permute-start | bytes 688136 | tf_op jit(solution)/shard_map/ppermute | solution.py:30
  80.1 43.8 %collective-permute-start.15 = (bf16[2,224,384]{2,1,0:T(8,128)(2,1)S(1)}, bf16[2,224,384]{2,1,0:T(8,128)(2,1)S(1)}, u32[]{:S(2)}, u32[]{:S(2)}) collective-permute-start(bf16[2,224,384]{2,1,0:T(8,128)(2,1)S(1)} %slice.487), channel_id=1, source_target_pairs={{0,96},{16,112},{32,0},{48,16},{64,32},{80,48},{96,64},{112,80},{1... | collective-permute-start | bytes 1032200 | tf_op jit(solution)/shard_map/ppermute | solution.py:41
  84.7 39.2 %collective-permute-start.14 = (bf16[2,224,384]{2,1,0:T(8,128)(2,1)S(1)}, bf16[2,224,384]{2,1,0:T(8,128)(2,1)S(1)}, u32[]{:S(2)}, u32[]{:S(2)}) collective-permute-start(bf16[2,224,384]{2,1,0:T(8,128)(2,1)S(1)} %slice.486), channel_id=1, source_target_pairs={{0,32},{16,48},{32,64},{48,80},{64,96},{80,112},{96,0},{112,16},{1... | collective-permute-start | bytes 1032200 | tf_op jit(solution)/shard_map/ppermute | solution.py:41
  86.7 6.6 %collective-permute-start.9 = (bf16[112,512]{1,0:T(8,128)(2,1)S(1)}, bf16[112,512]{1,0:T(8,128)(2,1)S(1)}, u32[]{:S(2)}, u32[]{:S(2)}) collective-permute-start(bf16[112,512]{1,0:T(8,128)(2,1)S(1)} %slice.477), channel_id=1, source_target_pairs={{0,7},{1,0},{2,1},{3,2},{4,3},{5,4},{6,5},{7,6},{8,15},{9,8},{10,9... | collective-permute-start | bytes 344072 | tf_op jit(solution)/shard_map/ppermute | solution.py:30
  91.3 6.7 %collective-permute-start.8 = (bf16[112,512]{1,0:T(8,128)(2,1)S(1)}, bf16[112,512]{1,0:T(8,128)(2,1)S(1)}, u32[]{:S(2)}, u32[]{:S(2)}) collective-permute-start(bf16[112,512]{1,0:T(8,128)(2,1)S(1)} %slice.476), channel_id=1, source_target_pairs={{0,1},{1,2},{2,3},{3,4},{4,5},{5,6},{6,7},{7,0},{8,9},{9,10},{10,1... | collective-permute-start | bytes 344072 | tf_op jit(solution)/shard_map/ppermute | solution.py:30
  98.5 28.0 %copy-start = (bf16[8,224,512]{2,1,0:T(8,128)(2,1)}, bf16[8,224,512]{2,1,0:T(8,128)(2,1)S(1)}, u32[]{:S(2)}) copy-start(bf16[8,224,512]{2,1,0:T(8,128)(2,1)S(1)} %constant_dynamic-slice_fusion.4) | copy-start | bytes 5505028
  98.7 6.0 %copy-start.8 = (f32[256]{0:T(256)}, f32[256]{0:T(256)S(1)}, u32[]{:S(2)}) copy-start(f32[256]{0:T(256)S(1)} %convert_reduce_fusion) | copy-start | bytes 3076
  99.1 8.2 %collective-permute-start.10 = (f32[2,256]{1,0:T(2,128)S(1)}, f32[2,256]{1,0:T(2,128)S(1)}, u32[]{:S(2)}, u32[]{:S(2)}) collective-permute-start(f32[2,256]{1,0:T(2,128)S(1)} %pad_maximum_fusion.13), channel_id=1, source_target_pairs={{0,8},{1,9},{2,10},{3,11},{4,12},{5,13},{6,14},{7,15},{8,0},{9,1},... | collective-permute-start | bytes 6152 | tf_op jit(solution)/shard_map/ppermute | solution.py:35
  104.8 19.6 %copy-start.2 = (f32[1,256,128]{2,1,0:T(8,128)}, f32[1,256,128]{2,1,0:T(8,128)S(1)}, u32[]{:S(2)}) copy-start(f32[1,256,128]{2,1,0:T(8,128)S(1)} %convolution_bitcast_fusion.1) | copy-start | bytes 393220
  107.9 15.4 %collective-permute-start.11 = (f32[2,256]{1,0:T(2,128)S(1)}, f32[2,256]{1,0:T(2,128)S(1)}, u32[]{:S(2)}, u32[]{:S(2)}) collective-permute-start(f32[2,256]{1,0:T(2,128)S(1)} %pad_maximum_fusion.14), channel_id=1, source_target_pairs={{0,16},{16,0},{32,48},{48,32},{64,80},{80,64},{96,112},{112,96},{1... | collective-permute-start | bytes 6152 | tf_op jit(solution)/shard_map/ppermute | solution.py:24
  121.4 12.2 %collective-permute-start.22 = (f32[2,128,128]{2,1,0:T(8,128)}, f32[2,128,128]{2,1,0:T(8,128)}, u32[]{:S(2)}, u32[]{:S(2)}) collective-permute-start(f32[2,128,128]{2,1,0:T(8,128)} %pad_maximum_fusion.7), channel_id=1, source_target_pairs={{0,16},{16,0},{32,48},{48,32},{64,80},{80,64},{96,112},{112,96},{1... | collective-permute-start | bytes 393224 | tf_op jit(solution)/shard_map/ppermute | solution.py:24
  131.1 12.7 %collective-permute-start.16 = (f32[2,136,384]{2,1,0:T(8,128)}, f32[2,136,384]{2,1,0:T(8,128)}, u32[]{:S(2)}, u32[]{:S(2)}) collective-permute-start(f32[2,136,384]{2,1,0:T(8,128)} %pad_maximum_fusion.2), channel_id=1, source_target_pairs={{0,16},{16,0},{32,48},{48,32},{64,80},{80,64},{96,112},{112,96},{1... | collective-permute-start | bytes 1253384 | tf_op jit(solution)/shard_map/ppermute | solution.py:24
  134.5 12.4 %collective-permute-start.23 = (bf16[128,128]{1,0:T(8,128)(2,1)S(1)}, bf16[128,128]{1,0:T(8,128)(2,1)}, u32[]{:S(2)}, u32[]{:S(2)}) collective-permute-start(bf16[128,128]{1,0:T(8,128)(2,1)S(1)} %fusion.45), channel_id=1, source_target_pairs={{0,8},{1,9},{2,10},{3,11},{4,12},{5,13},{6,14},{7,15},{8,0},{9,1},... | collective-permute-start | bytes 98312 | tf_op jit(solution)/shard_map/ppermute | solution.py:35
  142.1 13.1 %copy-start.14 = (f32[384]{0:T(512)S(1)}, f32[384]{0:T(512)}, u32[]{:S(2)}) copy-start(f32[384]{0:T(512)} %param.11) | copy-start | bytes 4612
  144.9 11.6 %copy-start.10 = (bf16[16]{0:T(256)(128)(2,1)S(1)}, bf16[16]{0:T(256)(128)(2,1)}, u32[]{:S(2)}) copy-start(bf16[16]{0:T(256)(128)(2,1)} %pad.43.clone) | copy-start | bytes 100
  144.9 10.2 %collective-permute-start.17 = (bf16[144,384]{1,0:T(8,128)(2,1)S(1)}, bf16[144,384]{1,0:T(8,128)(2,1)S(1)}, u32[]{:S(2)}, u32[]{:S(2)}) collective-permute-start(bf16[144,384]{1,0:T(8,128)(2,1)S(1)} %pad_maximum_fusion.10), channel_id=1, source_target_pairs={{0,8},{1,9},{2,10},{3,11},{4,12},{5,13},{6,14},{7,15},{8,0},{9,1},... | collective-permute-start | bytes 331784 | tf_op jit(solution)/shard_map/ppermute | solution.py:35
  156.6 10.2 %collective-permute-start.24 = (bf16[144,512]{1,0:T(8,128)(2,1)S(1)}, bf16[144,512]{1,0:T(8,128)(2,1)S(1)}, u32[]{:S(2)}, u32[]{:S(2)}) collective-permute-start(bf16[144,512]{1,0:T(8,128)(2,1)S(1)} %fusion.33), channel_id=1, source_target_pairs={{0,8},{1,9},{2,10},{3,11},{4,12},{5,13},{6,14},{7,15},{8,0},{9,1},... | collective-permute-start | bytes 442376 | tf_op jit(solution)/shard_map/ppermute | solution.py:35
  167.0 8.3 %collective-permute-start.25 = (bf16[2,144,512]{2,1,0:T(8,128)(2,1)S(1)}, bf16[2,144,512]{2,1,0:T(8,128)(2,1)}, u32[]{:S(2)}, u32[]{:S(2)}) collective-permute-start(bf16[2,144,512]{2,1,0:T(8,128)(2,1)S(1)} %fusion.17), channel_id=1, source_target_pairs={{0,16},{16,0},{32,48},{48,32},{64,80},{80,64},{96,112},{112,96},{1... | collective-permute-start | bytes 884744 | tf_op jit(solution)/shard_map/ppermute | solution.py:24
  178.5 4.8 %copy-start.1 = (bf16[8,224,512]{2,1,0:T(8,128)(2,1)S(1)}, bf16[8,224,512]{2,1,0:T(8,128)(2,1)}, u32[]{:S(2)}) copy-start(bf16[8,224,512]{2,1,0:T(8,128)(2,1)} %copy-done) | copy-start | bytes 5505028
  179.6 49.6 %all-to-all-start = ((bf16[8,240,256]{2,1,0:T(8,128)(2,1)}), bf16[8,240,256]{2,1,0:T(8,128)(2,1)S(1)}, u32[]{:S(2)}, u32[]{:S(2)}) async-start(bf16[8,240,256]{2,1,0:T(8,128)(2,1)} %pad_maximum_fusion), calls=%async_computation | async-start | bytes 1966080 | tf_op jit(solution)/shard_map/all_to_all | solution.py:264
  187.0 37.3 %copy-start.7 = (f32[1,256]{1,0:T(1,128)S(1)}, f32[1,256]{1,0:T(1,128)}, u32[]{:S(2)}) copy-start(f32[1,256]{1,0:T(1,128)} %copy-done.6) | copy-start | bytes 3076
  187.0 37.3 %copy-start.9 = (f32[256]{0:T(256)S(1)}, f32[256]{0:T(256)}, u32[]{:S(2)}) copy-start(f32[256]{0:T(256)} %copy-done.8) | copy-start | bytes 3076
  187.0 37.3 %copy-start.11 = (f32[1,256]{1,0:T(1,128)S(1)}, f32[1,256]{1,0:T(1,128)}, u32[]{:S(2)}) copy-start(f32[1,256]{1,0:T(1,128)} %get-tuple-element.15) | copy-start | bytes 3076
  187.0 37.3 %copy-start.12 = (f32[1,256]{1,0:T(1,128)S(1)}, f32[1,256]{1,0:T(1,128)}, u32[]{:S(2)}) copy-start(f32[1,256]{1,0:T(1,128)} %get-tuple-element.62) | copy-start | bytes 3076
  187.0 37.3 %copy-start.13 = (f32[1,256]{1,0:T(1,128)S(1)}, f32[1,256]{1,0:T(1,128)}, u32[]{:S(2)}) copy-start(f32[1,256]{1,0:T(1,128)} %get-tuple-element.63) | copy-start | bytes 3076
  187.1 8.0 %collective-permute-start.27 = (bf16[2,224,128]{2,1,0:T(8,128)(2,1)S(1)}, bf16[2,224,128]{2,1,0:T(8,128)(2,1)S(1)}, u32[]{:S(2)}, u32[]{:S(2)}) collective-permute-start(bf16[2,224,128]{2,1,0:T(8,128)(2,1)S(1)} %get-tuple-element.22), channel_id=1, source_target_pairs={{0,32},{16,48},{32,64},{48,80},{64,96},{80,112},{96,0},{112,16},{1... | collective-permute-start | bytes 344072 | tf_op jit(solution)/shard_map/ppermute | solution.py:41
  189.0 7.0 %collective-permute-start.29 = (bf16[2,224,128]{2,1,0:T(8,128)(2,1)S(1)}, bf16[2,224,128]{2,1,0:T(8,128)(2,1)S(1)}, u32[]{:S(2)}, u32[]{:S(2)}) collective-permute-start(bf16[2,224,128]{2,1,0:T(8,128)(2,1)S(1)} %get-tuple-element.24), channel_id=1, source_target_pairs={{0,96},{16,112},{32,0},{48,16},{64,32},{80,48},{96,64},{112,80},{1... | collective-permute-start | bytes 344072 | tf_op jit(solution)/shard_map/ppermute | solution.py:41
  196.1 9.0 %collective-permute-start.30 = (bf16[4,224,128]{2,1,0:T(8,128)(2,1)S(1)}, bf16[4,224,128]{2,1,0:T(8,128)(2,1)S(1)}, u32[]{:S(2)}, u32[]{:S(2)}) collective-permute-start(bf16[4,224,128]{2,1,0:T(8,128)(2,1)S(1)} %pad_maximum_fusion.6), channel_id=1, source_target_pairs={{0,96},{16,112},{32,0},{48,16},{64,32},{80,48},{96,64},{112,80},{1... | collective-permute-start | bytes 688136 | tf_op jit(solution)/shard_map/ppermute | solution.py:41
  201.4 34.7 %copy-start.3 = (bf16[128,448]{0,1:T(8,128)(2,1)S(1)}, bf16[128,448]{0,1:T(8,128)(2,1)}, u32[]{:S(2)}) copy-start(bf16[128,448]{0,1:T(8,128)(2,1)} %param.7) | copy-start | bytes 344068
  201.4 8.8 %collective-permute-start.28 = (bf16[4,224,128]{2,1,0:T(8,128)(2,1)S(1)}, bf16[4,224,128]{2,1,0:T(8,128)(2,1)S(1)}, u32[]{:S(2)}, u32[]{:S(2)}) collective-permute-start(bf16[4,224,128]{2,1,0:T(8,128)(2,1)S(1)} %pad_maximum_fusion.5), channel_id=1, source_target_pairs={{0,32},{16,48},{32,64},{48,80},{64,96},{80,112},{96,0},{112,16},{1... | collective-permute-start | bytes 688136 | tf_op jit(solution)/shard_map/ppermute | solution.py:41
  210.4 13.9 %collective-permute-start.34 = (bf16[224,128]{1,0:T(8,128)(2,1)S(1)}, bf16[224,128]{1,0:T(8,128)(2,1)S(1)}, u32[]{:S(2)}, u32[]{:S(2)}) collective-permute-start(bf16[224,128]{1,0:T(8,128)(2,1)S(1)} %get-tuple-element.39), channel_id=1, source_target_pairs={{0,136},{1,137},{2,138},{3,139},{4,140},{5,141},{6,142},{7,143},{8... | collective-permute-start | bytes 172040 | tf_op jit(solution)/shard_map/ppermute | solution.py:53
  212.3 12.0 %collective-permute-start.33 = (bf16[224,128]{1,0:T(8,128)(2,1)S(1)}, bf16[224,128]{1,0:T(8,128)(2,1)S(1)}, u32[]{:S(2)}, u32[]{:S(2)}) collective-permute-start(bf16[224,128]{1,0:T(8,128)(2,1)S(1)} %get-tuple-element.40), channel_id=1, source_target_pairs={{0,8},{1,9},{2,10},{3,11},{4,12},{5,13},{6,14},{7,15},{8,264},{9,2... | collective-permute-start | bytes 172040 | tf_op jit(solution)/shard_map/ppermute | solution.py:53
  216.6 8.5 %collective-permute-start.32 = (bf16[224,128]{1,0:T(8,128)(2,1)S(1)}, bf16[224,128]{1,0:T(8,128)(2,1)S(1)}, u32[]{:S(2)}, u32[]{:S(2)}) collective-permute-start(bf16[224,128]{1,0:T(8,128)(2,1)S(1)} %get-tuple-element.41), channel_id=1, source_target_pairs={{0,128},{1,129},{2,130},{3,131},{4,132},{5,133},{6,134},{7,135},{8... | collective-permute-start | bytes 172040 | tf_op jit(solution)/shard_map/ppermute | solution.py:53
  220.6 7.9 %collective-permute-start.31 = (bf16[224,128]{1,0:T(8,128)(2,1)S(1)}, bf16[224,128]{1,0:T(8,128)(2,1)S(1)}, u32[]{:S(2)}, u32[]{:S(2)}) collective-permute-start(bf16[224,128]{1,0:T(8,128)(2,1)S(1)} %get-tuple-element.38), channel_id=1, source_target_pairs={{0,0},{1,1},{2,2},{3,3},{4,4},{5,5},{6,6},{7,7},{8,256},{9,257},{1... | collective-permute-start | bytes 172040 | tf_op jit(solution)/shard_map/ppermute | solution.py:53
  229.4 6.8 %collective-permute-start.26 = (f32[224,128]{1,0:T(8,128)S(1)}, f32[224,128]{1,0:T(8,128)S(1)}, u32[]{:S(2)}, u32[]{:S(2)}) collective-permute-start(f32[224,128]{1,0:T(8,128)S(1)} %get-tuple-element.36), channel_id=1, source_target_pairs={{0,16},{16,0},{32,48},{48,32},{64,80},{80,64},{96,112},{112,96},{1... | collective-permute-start | bytes 344072 | tf_op jit(solution)/shard_map/ppermute | solution.py:24
  (3 other events, 9.5 us)

commit v5 on v4

--- a/solution.py
+++ b/solution.py
@@ -70,11 +70,7 @@
     return lax.dynamic_slice_in_dim(line, count - 1 - place, count, axis)
 
 
-def ring_scatter_x(parts, place):
-    def part(step):
-        return lax.dynamic_index_in_dim(parts, (place + step) % X_COUNT, 0, keepdims=False)
-
-    across = part(2)
+def ring_scatter_x(part, across):
     middle = across.shape[0] // 2
     up = shift_x(across[:middle], 1).astype(f32)
     down = shift_x(across[middle:], -1).astype(f32)
@@ -158,13 +154,11 @@
     weight_block, block = lax.optimization_barrier((weight_block, block))
     column = lax.all_gather(weight_block, "dp", axis=0, axis_index_groups=lines)
 
-    rows = ring_gather(block, shift_z, Z_COUNT, z, 0).reshape(quarter, 4 * SEQ)
+    rows = lax.all_gather(block, "tensor", axis=0, tiled=True, axis_index_groups=rings)
     hidden = rows[:, : 2 * SEQ].astype(f32)
     grads = rows[:, 2 * SEQ :]
-    joined_weight = ring_gather(column[:, :, : 3 * E], shift_x, X_COUNT, x, 1)
-    joined_weight = joined_weight.reshape(2, quarter, 3 * E)
-    out_weight = ring_gather(column[:, :, 3 * E :], shift_x, X_COUNT, x, 1)
-    out_weight = out_weight.reshape(2, quarter, E)
+    weights = ring_gather(column, shift_x, X_COUNT, x, 1).reshape(2, quarter, 4 * E)
+    joined_weight, out_weight = weights[:, :, : 3 * E], weights[:, :, 3 * E :]
 
     def merge(stats, stats_other, count):
         gap = stats[0] - stats_other[0]
@@ -201,26 +195,29 @@
         jnp.stack([v[0] + v[1], v[2] + v[3], jnp.zeros_like(v[0]), jnp.zeros_like(v[0])])
         for v in vector_parts
     ]
-    vector_parts = [jnp.concatenate([v, jnp.zeros_like(v)]) for v in vector_parts]
-    joined_parts = [dot(normed, joined_weight[h], ((0,), (0,))) for h in range(2)]
-    sent = jnp.stack(
-        [jnp.concatenate([j[SEQ:], v]) for j, v in zip(joined_parts, vector_parts)]
-    )
-    kept = jnp.stack(
-        [jnp.concatenate([j[:SEQ], v]) for j, v in zip(joined_parts, vector_parts)]
-    )
+    vector_parts = [jnp.pad(v, ((0, 4), (0, E))) for v in vector_parts]
+    parts = [
+        jnp.concatenate(
+            [
+                dot(normed, joined_weight[h], ((0,), (0,))),
+                dot(grads, out_weight[h], ((0,), (0,))),
+            ],
+            axis=1,
+        )
+        for h in range(2)
+    ]
+    sent = jnp.stack([jnp.concatenate([p[SEQ:], v]) for p, v in zip(parts, vector_parts)])
+    kept = jnp.stack([jnp.concatenate([p[:SEQ], v]) for p, v in zip(parts, vector_parts)])
     own, away = own_head(kept + swap_cores(sent))
     away_high, away_low = split(away[SEQ:])
     away = swap_far(jnp.concatenate([away[:SEQ].astype(bf16), away_high, away_low]))
     away = away.astype(f32)
-    plain = own[:SEQ] + away[:SEQ]
     vector = own[SEQ:] + away[SEQ : SEQ + 8] + away[SEQ + 8 :]
-    gain_weight, bias_weight = vector[0], vector[1]
+    gain_weight, bias_weight = vector[0, : 3 * E], vector[1, : 3 * E]
+    whole = own[:SEQ] + away[:SEQ]
+    plain = whole[:, : 3 * E]
     joined = (plain + b_qkv).astype(bf16)
-
-    grad_parts = jnp.stack([dot(grads, out_weight[h], ((0,), (0,))) for h in range(2)])
-    own, away = own_head(grad_parts[:, :SEQ] + swap_cores(grad_parts[:, SEQ:]))
-    context_grad = (own + swap_far(away.astype(bf16)).astype(f32)).astype(bf16)
+    context_grad = whole[:, 3 * E :].astype(bf16)
 
     slope = 2.0 ** (-8.0 * (rank + 1).astype(f32) / n_tensor)
     context, joined_grad = attention(joined, context_grad, slope)
@@ -251,10 +248,18 @@
     sums = jnp.concatenate([sums, unpack(heads_other[0, SEQ:, :SEQ])], axis=1)
     heads = jnp.concatenate([heads, heads_other[:, :SEQ]], axis=1)
 
-    context_pair = jnp.concatenate([heads[0, :, :E], heads[1, :, :E]], axis=1)
-    weight_part = dot(grads, context_pair, ((1,), (0,))).astype(bf16)
-    weight_part = weight_part.reshape(2, X_COUNT, part, 2, E)
-    weight_parts = weight_part.transpose(1, 3, 0, 2, 4).reshape(X_COUNT, 4, part, E)
+    weight_parts = [
+        dot(grads, heads[h, :, :E], ((1,), (0,))).astype(bf16).reshape(2, X_COUNT, part, E)
+        for h in range(2)
+    ]
+
+    def weight_to(step):
+        place = (x + step) % X_COUNT
+        return jnp.concatenate(
+            [lax.dynamic_index_in_dim(w, place, 1, keepdims=False) for w in weight_parts]
+        )
+
+    across, heads = lax.optimization_barrier((weight_to(2), heads))
 
     group_part = sum(
         dot(joined_weight[h], heads[h, :, E:], ((1,), (1,))) for h in range(2)
@@ -280,7 +285,7 @@
     scaled = (hidden_t.astype(f32) - mean[:SEQ]) * inv_std[:SEQ]
     input_grad = inv_std[:SEQ] * (scaled_grad - mean_grad - scaled * mean_cross)
 
-    grad_out_weight = scatter_y(ring_scatter_x(weight_parts, x), y)
+    grad_out_weight = scatter_y(ring_scatter_x(weight_to, across), y)
     return input_grad.astype(bf16).T, grad_out_weight.T
 
 

time: 239 us -> 220 us (0.921)
  the two profiles are of different devices: /device:TPU:17 before, /device:TPU:1 now
where the time goes in v5:
time: 220 us; the launch traced here: 217 us
  starting transfers between devices  99.3 us (45%)
  waiting for transfers between devices  53.4 us (24%)
  blocking collectives  21.6 us (10%)
  between operations  15.1 us (7%)
  other arithmetic  12.2 us (6%)
  matrix products  9.83 us (4%)
  local copies, waits for them, and re-layouts  5.79 us (3%)
    ppermute x5, starting transfers between devices, swap_cores(): return lax.ppermute(x, 'dp', [(i, i ^ 1) for i in range(n)])  30.6 us
    ppermute x8, waiting for transfers between devices, shift_x(): lax.ppermute(x, 'dp', [(i, i - i % row + (i + 2 * step) % row) for i in r...  28.6 us
    ppermute x3, starting transfers between devices, swap_far(): return lax.ppermute(x, 'tensor', [(i, (i + Z_COUNT) % n) for i in range(n)])  24.6 us
    ppermute x8, starting transfers between devices, shift_x(): lax.ppermute(x, 'dp', [(i, i - i % row + (i + 2 * step) % row) for i in r...  24 us
    all_gather x1, blocking collectives, body(): column = lax.all_gather(weight_block, 'dp', axis=0, axis_index_groups=lines)  21.6 us
    ppermute x5, starting transfers between devices, along_y(): return lax.ppermute(x, ('dp', 'tensor'), pairs)  14.3 us
    all_gather x1, waiting for transfers between devices, body(): lax.all_gather(block, 'tensor', axis=0, tiled=True, axis_index_groups=rings)  10.4 us
    dot_general x16, matrix products, dot(): return lax.dot_general(a, b, (dims, ((), ())), preferred_element_type=f32)  9.83 us
  transfers between devices with their start and end apart: 23, of which 14 were waited for; matrix products, arithmetic and copies ran while one was open for 6% of the time, Pallas kernels for 0%

profile of v5, /device:TPU:1, one launch (start us, length us, event | category | flops | bytes accessed | tf_op | source)
XLA Modules:
  0.0 217.2 jit_solution(11237657822992789764)
XLA Ops:
  7.2 1.0 pad_maximum_fusion.5
  8.9 1.0 broadcast_select_fusion.1
  9.9 8.8 %collective-permute-start.1 = (bf16[224,256]{1,0:T(8,128)(2,1)S(1)}, bf16[224,256]{1,0:T(8,128)(2,1)S(1)}, u32[]{:S(2)}, u32[]{:S(2)}) collective-permute-start(bf16[224,256]{1,0:T(8,128)(2,1)S(1)} %get-tuple-element.41), channel_id=1, source_target_pairs={{0,16},{16,0},{32,48},{48,32},{64,80},{80,64},{96,112},{112,96},{1... | collective-permute-start | bytes 344072 | tf_op jit(solution)/shard_map/ppermute | solution.py:24
  18.8 0.9 collective-permute-done.1
  20.4 21.6 %all-gather = bf16[896,512]{1,0:T(8,128)(2,1)S(1)} all-gather(bf16[224,512]{1,0:T(8,128)(2,1)S(1)} %collective-permute-done), channel_id=2, replica_groups={{0,128,256,384},{16,144,272,400},{32,160,288,416},{48,176,304,432},{64,..., dimensions={0}, use_global_device_ids=true | all-gather | bytes 1146880 | tf_op jit(solution)/shard_map/all_gather | solution.py:155
  42.1 4.4 %collective-permute-start.4 = (bf16[4,224,512]{2,1,0:T(8,128)(2,1)S(1)}, bf16[4,224,512]{2,1,0:T(8,128)(2,1)S(1)}, u32[]{:S(2)}, u32[]{:S(2)}) collective-permute-start(bf16[4,224,512]{2,1,0:T(8,128)(2,1)S(1)} %bitcast.145), channel_id=1, source_target_pairs={{0,96},{16,112},{32,0},{48,16},{64,32},{80,48},{96,64},{112,80},{1... | collective-permute-start | bytes 2752520 | tf_op jit(solution)/shard_map/ppermute | solution.py:41
  46.4 1.9 collective-permute-start.5
  48.9 13.5 %collective-permute-done.4 = bf16[4,224,512]{2,1,0:T(8,128)(2,1)S(1)} collective-permute-done((bf16[4,224,512]{2,1,0:T(8,128)(2,1)S(1)}, bf16[4,224,512]{2,1,0:T(8,128)(2,1)S(1)}, u32[]{:S(2)}, u32[]{:S(2)}) %collective-permute-start.4) | collective-permute-done | bytes 917536 | tf_op jit(solution)/shard_map/ppermute | solution.py:41
  63.2 5.3 %collective-permute-start.7 = (bf16[2,224,512]{2,1,0:T(8,128)(2,1)}, bf16[2,224,512]{2,1,0:T(8,128)(2,1)S(1)}, u32[]{:S(2)}, u32[]{:S(2)}) collective-permute-start(bf16[2,224,512]{2,1,0:T(8,128)(2,1)} %slice.417), channel_id=1, source_target_pairs={{0,96},{16,112},{32,0},{48,16},{64,32},{80,48},{96,64},{112,80},{1... | collective-permute-start | bytes 1376264 | tf_op jit(solution)/shard_map/ppermute | solution.py:41
  68.5 0.8 slice.416
  69.3 1.9 collective-permute-start.6
  71.6 2.6 %collective-permute-done.7 = bf16[2,224,512]{2,1,0:T(8,128)(2,1)S(1)} collective-permute-done((bf16[2,224,512]{2,1,0:T(8,128)(2,1)}, bf16[2,224,512]{2,1,0:T(8,128)(2,1)S(1)}, u32[]{:S(2)}, u32[]{:S(2)}) %collective-permute-start.7) | collective-permute-done | bytes 458784 | tf_op jit(solution)/shard_map/ppermute | solution.py:41
  74.2 6.1 %collective-permute-done.6 = bf16[2,224,512]{2,1,0:T(8,128)(2,1)} collective-permute-done((bf16[2,224,512]{2,1,0:T(8,128)(2,1)}, bf16[2,224,512]{2,1,0:T(8,128)(2,1)}, u32[]{:S(2)}, u32[]{:S(2)}) %collective-permute-start.6) | collective-permute-done | bytes 458784 | tf_op jit(solution)/shard_map/ppermute | solution.py:41
  80.4 1.1 fusion.14
  81.7 1.1 fusion.15
  83.5 1.4 copy-done
  85.3 10.4 %all-gather.3.cloned.1.call-done = bf16[1792,512]{1,0:T(8,128)(2,1)} async-done(((bf16[224,512]{1,0:T(8,128)(2,1)}), bf16[1792,512]{1,0:T(8,128)(2,1)}) %all-gather.3.cloned.1.call-update) | async-done | bytes 1835024 | tf_op jit(solution)/shard_map/all_gather | solution.py:157
  95.7 1.6 convert_reduce_fusion
  97.3 1.5 fusion.2
  98.8 7.5 %collective-permute-start.2 = (f32[2,256]{1,0:T(2,128)S(1)}, f32[2,256]{1,0:T(2,128)S(1)}, u32[]{:S(2)}, u32[]{:S(2)}) collective-permute-start(f32[2,256]{1,0:T(2,128)S(1)} %pad_maximum_fusion.15), channel_id=1, source_target_pairs={{0,8},{1,9},{2,10},{3,11},{4,12},{5,13},{6,14},{7,15},{8,0},{9,1},... | collective-permute-start | bytes 6152 | tf_op jit(solution)/shard_map/ppermute | solution.py:35
  106.3 1.7 fusion.18
  108.1 6.8 %collective-permute-start.3 = (f32[2,256]{1,0:T(2,128)S(1)}, f32[2,256]{1,0:T(2,128)S(1)}, u32[]{:S(2)}, u32[]{:S(2)}) collective-permute-start(f32[2,256]{1,0:T(2,128)S(1)} %pad_maximum_fusion.16), channel_id=1, source_target_pairs={{0,16},{16,0},{32,48},{48,32},{64,80},{80,64},{96,112},{112,96},{1... | collective-permute-start | bytes 6152 | tf_op jit(solution)/shard_map/ppermute | solution.py:24
  114.9 1.6 fusion.20
  116.6 1.4 fusion.13
  118.1 1.4 fusion.11
  119.6 1.9 collective-permute-start.8
  121.5 1.9 collective-permute-done.8
  123.7 7.2 %collective-permute-start.9 = (bf16[144,512]{1,0:T(8,128)(2,1)S(1)}, bf16[144,512]{1,0:T(8,128)(2,1)S(1)}, u32[]{:S(2)}, u32[]{:S(2)}) collective-permute-start(bf16[144,512]{1,0:T(8,128)(2,1)S(1)} %pad_maximum_fusion.10), channel_id=1, source_target_pairs={{0,8},{1,9},{2,10},{3,11},{4,12},{5,13},{6,14},{7,15},{8,0},{9,1},... | collective-permute-start | bytes 442376 | tf_op jit(solution)/shard_map/ppermute | solution.py:35
  131.0 3.8 %collective-permute-done.9 = bf16[144,512]{1,0:T(8,128)(2,1)S(1)} collective-permute-done((bf16[144,512]{1,0:T(8,128)(2,1)S(1)}, bf16[144,512]{1,0:T(8,128)(2,1)S(1)}, u32[]{:S(2)}, u32[]{:S(2)}) %collective-permute-start.9) | collective-permute-done | bytes 147488 | tf_op jit(solution)/shard_map/ppermute | solution.py:35
  136.3 9.9 %collective-permute-start.10 = (bf16[144,512]{1,0:T(8,128)(2,1)S(1)}, bf16[144,512]{1,0:T(8,128)(2,1)S(1)}, u32[]{:S(2)}, u32[]{:S(2)}) collective-permute-start(bf16[144,512]{1,0:T(8,128)(2,1)S(1)} %fusion.49), channel_id=1, source_target_pairs={{0,8},{1,9},{2,10},{3,11},{4,12},{5,13},{6,14},{7,15},{8,0},{9,1},... | collective-permute-start | bytes 442376 | tf_op jit(solution)/shard_map/ppermute | solution.py:35
  146.2 2.6 %collective-permute-done.10 = bf16[144,512]{1,0:T(8,128)(2,1)S(1)} collective-permute-done((bf16[144,512]{1,0:T(8,128)(2,1)S(1)}, bf16[144,512]{1,0:T(8,128)(2,1)S(1)}, u32[]{:S(2)}, u32[]{:S(2)}) %collective-permute-start.10) | collective-permute-done | bytes 147488 | tf_op jit(solution)/shard_map/ppermute | solution.py:35
  149.0 6.9 %collective-permute-start.11 = (bf16[2,144,512]{2,1,0:T(8,128)(2,1)S(1)}, bf16[2,144,512]{2,1,0:T(8,128)(2,1)S(1)}, u32[]{:S(2)}, u32[]{:S(2)}) collective-permute-start(bf16[2,144,512]{2,1,0:T(8,128)(2,1)S(1)} %fusion.23), channel_id=1, source_target_pairs={{0,16},{16,0},{32,48},{48,32},{64,80},{80,64},{96,112},{112,96},{1... | collective-permute-start | bytes 884744 | tf_op jit(solution)/shard_map/ppermute | solution.py:24
  155.9 1.1 collective-permute-done.11
  158.1 1.1 copy-done.2
  160.5 1.9 collective-permute-start.15
  162.5 1.1 pad_maximum_fusion
  163.6 5.8 %all-to-all-start = ((bf16[8,240,256]{2,1,0:T(8,128)(2,1)}), bf16[8,240,256]{2,1,0:T(8,128)(2,1)S(1)}, u32[]{:S(2)}, u32[]{:S(2)}) async-start(bf16[8,240,256]{2,1,0:T(8,128)(2,1)} %pad_maximum_fusion), calls=%async_computation | async-start | bytes 1966080 | tf_op jit(solution)/shard_map/all_to_all | solution.py:269
  169.4 1.9 collective-permute-start.13
  171.4 4.6 %collective-permute-start.16 = (bf16[4,224,128]{2,1,0:T(8,128)(2,1)S(1)}, bf16[4,224,128]{2,1,0:T(8,128)(2,1)S(1)}, u32[]{:S(2)}, u32[]{:S(2)}) collective-permute-start(bf16[4,224,128]{2,1,0:T(8,128)(2,1)S(1)} %pad_maximum_fusion.9), channel_id=1, source_target_pairs={{0,96},{16,112},{32,0},{48,16},{64,32},{80,48},{96,64},{112,80},{1... | collective-permute-start | bytes 688136 | tf_op jit(solution)/shard_map/ppermute | solution.py:41
  176.2 2.1 collective-permute-start.14
  178.4 1.2 collective-permute-done.16
  179.6 5.0 %collective-permute-done.14 = bf16[4,224,128]{2,1,0:T(8,128)(2,1)S(1)} collective-permute-done((bf16[4,224,128]{2,1,0:T(8,128)(2,1)S(1)}, bf16[4,224,128]{2,1,0:T(8,128)(2,1)S(1)}, u32[]{:S(2)}, u32[]{:S(2)}) %collective-permute-start.14) | collective-permute-done | bytes 229408 | tf_op jit(solution)/shard_map/ppermute | solution.py:41
  184.7 6.7 %collective-permute-start.20 = (bf16[224,128]{1,0:T(8,128)(2,1)S(1)}, bf16[224,128]{1,0:T(8,128)(2,1)S(1)}, u32[]{:S(2)}, u32[]{:S(2)}) collective-permute-start(bf16[224,128]{1,0:T(8,128)(2,1)S(1)} %get-tuple-element.35), channel_id=1, source_target_pairs={{0,136},{1,137},{2,138},{3,139},{4,140},{5,141},{6,142},{7,143},{8... | collective-permute-start | bytes 172040 | tf_op jit(solution)/shard_map/ppermute | solution.py:53
  191.4 3.2 %collective-permute-start.19 = (bf16[224,128]{1,0:T(8,128)(2,1)S(1)}, bf16[224,128]{1,0:T(8,128)(2,1)S(1)}, u32[]{:S(2)}, u32[]{:S(2)}) collective-permute-start(bf16[224,128]{1,0:T(8,128)(2,1)S(1)} %get-tuple-element.36), channel_id=1, source_target_pairs={{0,8},{1,9},{2,10},{3,11},{4,12},{5,13},{6,14},{7,15},{8,264},{9,2... | collective-permute-start | bytes 172040 | tf_op jit(solution)/shard_map/ppermute | solution.py:53
  194.7 3.0 %collective-permute-start.18 = (bf16[224,128]{1,0:T(8,128)(2,1)S(1)}, bf16[224,128]{1,0:T(8,128)(2,1)S(1)}, u32[]{:S(2)}, u32[]{:S(2)}) collective-permute-start(bf16[224,128]{1,0:T(8,128)(2,1)S(1)} %get-tuple-element.37), channel_id=1, source_target_pairs={{0,128},{1,129},{2,130},{3,131},{4,132},{5,133},{6,134},{7,135},{8... | collective-permute-start | bytes 172040 | tf_op jit(solution)/shard_map/ppermute | solution.py:53
  198.4 3.2 %collective-permute-done.18 = bf16[224,128]{1,0:T(8,128)(2,1)S(1)} collective-permute-done((bf16[224,128]{1,0:T(8,128)(2,1)S(1)}, bf16[224,128]{1,0:T(8,128)(2,1)S(1)}, u32[]{:S(2)}, u32[]{:S(2)}) %collective-permute-start.18) | collective-permute-done | bytes 57376 | tf_op jit(solution)/shard_map/ppermute | solution.py:53
  202.5 6.2 %collective-permute-start.12 = (f32[224,128]{1,0:T(8,128)S(1)}, f32[224,128]{1,0:T(8,128)S(1)}, u32[]{:S(2)}, u32[]{:S(2)}) collective-permute-start(f32[224,128]{1,0:T(8,128)S(1)} %get-tuple-element.32), channel_id=1, source_target_pairs={{0,16},{16,0},{32,48},{48,32},{64,80},{80,64},{96,112},{112,96},{1... | collective-permute-start | bytes 344072 | tf_op jit(solution)/shard_map/ppermute | solution.py:24
  208.7 0.9 collective-permute-done.12
  (130 shorter events, 11.6 us)
Async XLA Ops:
  7.2 41.2 %copy-start.5 = (f32[7168]{0:T(1024)S(1)}, f32[7168]{0:T(1024)}, u32[]{:S(2)}) copy-start(f32[7168]{0:T(1024)} %param.8) | copy-start | bytes 86020
  7.2 41.3 %copy-start.6 = (f32[7168]{0:T(1024)S(1)}, f32[7168]{0:T(1024)}, u32[]{:S(2)}) copy-start(f32[7168]{0:T(1024)} %param.9) | copy-start | bytes 86020
  7.2 88.5 %all-gather.3.cloned.1.call-start = ((), (), s32[]{:S(2)}) async-start(), calls=%async_computation.1 | async-start | bytes 2064384 | tf_op jit(solution)/shard_map/all_gather | solution.py:157
  8.2 12.2 %collective-permute-start = (bf16[224,512]{1,0:T(8,128)(2,1)S(1)}, bf16[224,512]{1,0:T(8,128)(2,1)S(1)}, u32[]{:S(2)}, u32[]{:S(2)}) collective-permute-start(bf16[224,512]{1,0:T(8,128)(2,1)S(1)} %pad_maximum_fusion.5), channel_id=1, source_target_pairs={{0,0},{1,1},{2,2},{3,3},{4,4},{5,5},{6,6},{7,7},{8,256},{9,257},{1... | collective-permute-start | bytes 688136 | tf_op jit(solution)/shard_map/ppermute | solution.py:53
  9.9 9.7 %collective-permute-start.1 = (bf16[224,256]{1,0:T(8,128)(2,1)S(1)}, bf16[224,256]{1,0:T(8,128)(2,1)S(1)}, u32[]{:S(2)}, u32[]{:S(2)}) collective-permute-start(bf16[224,256]{1,0:T(8,128)(2,1)S(1)} %get-tuple-element.41), channel_id=1, source_target_pairs={{0,16},{16,0},{32,48},{48,32},{64,80},{80,64},{96,112},{112,96},{1... | collective-permute-start | bytes 344072 | tf_op jit(solution)/shard_map/ppermute | solution.py:24
  42.1 20.3 %collective-permute-start.4 = (bf16[4,224,512]{2,1,0:T(8,128)(2,1)S(1)}, bf16[4,224,512]{2,1,0:T(8,128)(2,1)S(1)}, u32[]{:S(2)}, u32[]{:S(2)}) collective-permute-start(bf16[4,224,512]{2,1,0:T(8,128)(2,1)S(1)} %bitcast.145), channel_id=1, source_target_pairs={{0,96},{16,112},{32,0},{48,16},{64,32},{80,48},{96,64},{112,80},{1... | collective-permute-start | bytes 2752520 | tf_op jit(solution)/shard_map/ppermute | solution.py:41
  46.4 22.1 %collective-permute-start.5 = (bf16[4,224,512]{2,1,0:T(8,128)(2,1)S(1)}, bf16[4,224,512]{2,1,0:T(8,128)(2,1)S(1)}, u32[]{:S(2)}, u32[]{:S(2)}) collective-permute-start(bf16[4,224,512]{2,1,0:T(8,128)(2,1)S(1)} %bitcast.146), channel_id=1, source_target_pairs={{0,32},{16,48},{32,64},{48,80},{64,96},{80,112},{96,0},{112,16},{1... | collective-permute-start | bytes 2752520 | tf_op jit(solution)/shard_map/ppermute | solution.py:41
  63.2 11.0 %collective-permute-start.7 = (bf16[2,224,512]{2,1,0:T(8,128)(2,1)}, bf16[2,224,512]{2,1,0:T(8,128)(2,1)S(1)}, u32[]{:S(2)}, u32[]{:S(2)}) collective-permute-start(bf16[2,224,512]{2,1,0:T(8,128)(2,1)} %slice.417), channel_id=1, source_target_pairs={{0,96},{16,112},{32,0},{48,16},{64,32},{80,48},{96,64},{112,80},{1... | collective-permute-start | bytes 1376264 | tf_op jit(solution)/shard_map/ppermute | solution.py:41
  69.3 11.0 %collective-permute-start.6 = (bf16[2,224,512]{2,1,0:T(8,128)(2,1)}, bf16[2,224,512]{2,1,0:T(8,128)(2,1)}, u32[]{:S(2)}, u32[]{:S(2)}) collective-permute-start(bf16[2,224,512]{2,1,0:T(8,128)(2,1)} %slice.416), channel_id=1, source_target_pairs={{0,32},{16,48},{32,64},{48,80},{64,96},{80,112},{96,0},{112,16},{1... | collective-permute-start | bytes 1376264 | tf_op jit(solution)/shard_map/ppermute | solution.py:41
  83.2 1.8 copy-start
  95.7 19.2 %copy-start.1 = (bf16[4,4,224,512]{3,2,1,0:T(8,128)(2,1)S(1)}, bf16[4,4,224,512]{3,2,1,0:T(8,128)(2,1)}, u32[]{:S(2)}) copy-start(bf16[4,4,224,512]{3,2,1,0:T(8,128)(2,1)} %copy-done) | copy-start | bytes 11010052
  98.8 17.8 %copy-start.3 = (bf16[1792,512]{1,0:T(8,128)(2,1)S(1)}, bf16[1792,512]{1,0:T(8,128)(2,1)}, u32[]{:S(2)}) copy-start(bf16[1792,512]{1,0:T(8,128)(2,1)} %all-gather.3.cloned.1.call-done) | copy-start | bytes 5505028
  98.8 9.3 %collective-permute-start.2 = (f32[2,256]{1,0:T(2,128)S(1)}, f32[2,256]{1,0:T(2,128)S(1)}, u32[]{:S(2)}, u32[]{:S(2)}) collective-permute-start(f32[2,256]{1,0:T(2,128)S(1)} %pad_maximum_fusion.15), channel_id=1, source_target_pairs={{0,8},{1,9},{2,10},{3,11},{4,12},{5,13},{6,14},{7,15},{8,0},{9,1},... | collective-permute-start | bytes 6152 | tf_op jit(solution)/shard_map/ppermute | solution.py:35
  108.1 8.4 %collective-permute-start.3 = (f32[2,256]{1,0:T(2,128)S(1)}, f32[2,256]{1,0:T(2,128)S(1)}, u32[]{:S(2)}, u32[]{:S(2)}) collective-permute-start(f32[2,256]{1,0:T(2,128)S(1)} %pad_maximum_fusion.16), channel_id=1, source_target_pairs={{0,16},{16,0},{32,48},{48,32},{64,80},{80,64},{96,112},{112,96},{1... | collective-permute-start | bytes 6152 | tf_op jit(solution)/shard_map/ppermute | solution.py:24
  119.6 3.9 %collective-permute-start.8 = (f32[2,136,512]{2,1,0:T(8,128)S(1)}, f32[2,136,512]{2,1,0:T(8,128)S(1)}, u32[]{:S(2)}, u32[]{:S(2)}) collective-permute-start(f32[2,136,512]{2,1,0:T(8,128)S(1)} %pad_maximum_fusion.1), channel_id=1, source_target_pairs={{0,16},{16,0},{32,48},{48,32},{64,80},{80,64},{96,112},{112,96},{1... | collective-permute-start | bytes 1671176 | tf_op jit(solution)/shard_map/ppermute | solution.py:24
  123.6 11.3 %copy-start.7 = (f32[384]{0:T(512)S(1)}, f32[384]{0:T(512)}, u32[]{:S(2)}) copy-start(f32[384]{0:T(512)} %param.11) | copy-start | bytes 4612
  123.7 11.1 %collective-permute-start.9 = (bf16[144,512]{1,0:T(8,128)(2,1)S(1)}, bf16[144,512]{1,0:T(8,128)(2,1)S(1)}, u32[]{:S(2)}, u32[]{:S(2)}) collective-permute-start(bf16[144,512]{1,0:T(8,128)(2,1)S(1)} %pad_maximum_fusion.10), channel_id=1, source_target_pairs={{0,8},{1,9},{2,10},{3,11},{4,12},{5,13},{6,14},{7,15},{8,0},{9,1},... | collective-permute-start | bytes 442376 | tf_op jit(solution)/shard_map/ppermute | solution.py:35
  136.3 12.5 %collective-permute-start.10 = (bf16[144,512]{1,0:T(8,128)(2,1)S(1)}, bf16[144,512]{1,0:T(8,128)(2,1)S(1)}, u32[]{:S(2)}, u32[]{:S(2)}) collective-permute-start(bf16[144,512]{1,0:T(8,128)(2,1)S(1)} %fusion.49), channel_id=1, source_target_pairs={{0,8},{1,9},{2,10},{3,11},{4,12},{5,13},{6,14},{7,15},{8,0},{9,1},... | collective-permute-start | bytes 442376 | tf_op jit(solution)/shard_map/ppermute | solution.py:35
  149.0 8.1 %collective-permute-start.11 = (bf16[2,144,512]{2,1,0:T(8,128)(2,1)S(1)}, bf16[2,144,512]{2,1,0:T(8,128)(2,1)S(1)}, u32[]{:S(2)}, u32[]{:S(2)}) collective-permute-start(bf16[2,144,512]{2,1,0:T(8,128)(2,1)S(1)} %fusion.23), channel_id=1, source_target_pairs={{0,16},{16,0},{32,48},{48,32},{64,80},{80,64},{96,112},{112,96},{1... | collective-permute-start | bytes 884744 | tf_op jit(solution)/shard_map/ppermute | solution.py:24
  157.1 2.0 copy-start.2
  160.5 10.8 %collective-permute-start.15 = (bf16[2,224,128]{2,1,0:T(8,128)(2,1)S(1)}, bf16[2,224,128]{2,1,0:T(8,128)(2,1)S(1)}, u32[]{:S(2)}, u32[]{:S(2)}) collective-permute-start(bf16[2,224,128]{2,1,0:T(8,128)(2,1)S(1)} %get-tuple-element.39), channel_id=1, source_target_pairs={{0,96},{16,112},{32,0},{48,16},{64,32},{80,48},{96,64},{112,80},{1... | collective-permute-start | bytes 344072 | tf_op jit(solution)/shard_map/ppermute | solution.py:41
  163.6 38.7 %all-to-all-start = ((bf16[8,240,256]{2,1,0:T(8,128)(2,1)}), bf16[8,240,256]{2,1,0:T(8,128)(2,1)S(1)}, u32[]{:S(2)}, u32[]{:S(2)}) async-start(bf16[8,240,256]{2,1,0:T(8,128)(2,1)} %pad_maximum_fusion), calls=%async_computation | async-start | bytes 1966080 | tf_op jit(solution)/shard_map/all_to_all | solution.py:269
  169.4 6.7 %collective-permute-start.13 = (bf16[2,224,128]{2,1,0:T(8,128)(2,1)S(1)}, bf16[2,224,128]{2,1,0:T(8,128)(2,1)S(1)}, u32[]{:S(2)}, u32[]{:S(2)}) collective-permute-start(bf16[2,224,128]{2,1,0:T(8,128)(2,1)S(1)} %get-tuple-element.38), channel_id=1, source_target_pairs={{0,32},{16,48},{32,64},{48,80},{64,96},{80,112},{96,0},{112,16},{1... | collective-permute-start | bytes 344072 | tf_op jit(solution)/shard_map/ppermute | solution.py:41
  171.4 8.2 %collective-permute-start.16 = (bf16[4,224,128]{2,1,0:T(8,128)(2,1)S(1)}, bf16[4,224,128]{2,1,0:T(8,128)(2,1)S(1)}, u32[]{:S(2)}, u32[]{:S(2)}) collective-permute-start(bf16[4,224,128]{2,1,0:T(8,128)(2,1)S(1)} %pad_maximum_fusion.9), channel_id=1, source_target_pairs={{0,96},{16,112},{32,0},{48,16},{64,32},{80,48},{96,64},{112,80},{1... | collective-permute-start | bytes 688136 | tf_op jit(solution)/shard_map/ppermute | solution.py:41
  176.2 33.5 %copy-start.4 = (bf16[128,448]{0,1:T(8,128)(2,1)S(1)}, bf16[128,448]{0,1:T(8,128)(2,1)}, u32[]{:S(2)}) copy-start(bf16[128,448]{0,1:T(8,128)(2,1)} %param.7) | copy-start | bytes 344068
  176.2 8.4 %collective-permute-start.14 = (bf16[4,224,128]{2,1,0:T(8,128)(2,1)S(1)}, bf16[4,224,128]{2,1,0:T(8,128)(2,1)S(1)}, u32[]{:S(2)}, u32[]{:S(2)}) collective-permute-start(bf16[4,224,128]{2,1,0:T(8,128)(2,1)S(1)} %pad_maximum_fusion.8), channel_id=1, source_target_pairs={{0,32},{16,48},{32,64},{48,80},{64,96},{80,112},{96,0},{112,16},{1... | collective-permute-start | bytes 688136 | tf_op jit(solution)/shard_map/ppermute | solution.py:41
  184.7 13.7 %collective-permute-start.20 = (bf16[224,128]{1,0:T(8,128)(2,1)S(1)}, bf16[224,128]{1,0:T(8,128)(2,1)S(1)}, u32[]{:S(2)}, u32[]{:S(2)}) collective-permute-start(bf16[224,128]{1,0:T(8,128)(2,1)S(1)} %get-tuple-element.35), channel_id=1, source_target_pairs={{0,136},{1,137},{2,138},{3,139},{4,140},{5,141},{6,142},{7,143},{8... | collective-permute-start | bytes 172040 | tf_op jit(solution)/shard_map/ppermute | solution.py:53
  191.4 7.0 %collective-permute-start.19 = (bf16[224,128]{1,0:T(8,128)(2,1)S(1)}, bf16[224,128]{1,0:T(8,128)(2,1)S(1)}, u32[]{:S(2)}, u32[]{:S(2)}) collective-permute-start(bf16[224,128]{1,0:T(8,128)(2,1)S(1)} %get-tuple-element.36), channel_id=1, source_target_pairs={{0,8},{1,9},{2,10},{3,11},{4,12},{5,13},{6,14},{7,15},{8,264},{9,2... | collective-permute-start | bytes 172040 | tf_op jit(solution)/shard_map/ppermute | solution.py:53
  194.7 6.9 %collective-permute-start.18 = (bf16[224,128]{1,0:T(8,128)(2,1)S(1)}, bf16[224,128]{1,0:T(8,128)(2,1)S(1)}, u32[]{:S(2)}, u32[]{:S(2)}) collective-permute-start(bf16[224,128]{1,0:T(8,128)(2,1)S(1)} %get-tuple-element.37), channel_id=1, source_target_pairs={{0,128},{1,129},{2,130},{3,131},{4,132},{5,133},{6,134},{7,135},{8... | collective-permute-start | bytes 172040 | tf_op jit(solution)/shard_map/ppermute | solution.py:53
  197.7 3.9 %collective-permute-start.17 = (bf16[224,128]{1,0:T(8,128)(2,1)S(1)}, bf16[224,128]{1,0:T(8,128)(2,1)S(1)}, u32[]{:S(2)}, u32[]{:S(2)}) collective-permute-start(bf16[224,128]{1,0:T(8,128)(2,1)S(1)} %get-tuple-element.34), channel_id=1, source_target_pairs={{0,0},{1,1},{2,2},{3,3},{4,4},{5,5},{6,6},{7,7},{8,256},{9,257},{1... | collective-permute-start | bytes 172040 | tf_op jit(solution)/shard_map/ppermute | solution.py:53
  202.5 7.2 %collective-permute-start.12 = (f32[224,128]{1,0:T(8,128)S(1)}, f32[224,128]{1,0:T(8,128)S(1)}, u32[]{:S(2)}, u32[]{:S(2)}) collective-permute-start(f32[224,128]{1,0:T(8,128)S(1)} %get-tuple-element.32), channel_id=1, source_target_pairs={{0,16},{16,0},{32,48},{48,32},{64,80},{80,64},{96,112},{112,96},{1... | collective-permute-start | bytes 344072 | tf_op jit(solution)/shard_map/ppermute | solution.py:24
Sparse Core Ops, SparseCore 0:
  49.0 46.6 all-gather.2

commit v6 on v5

--- a/solution.py
+++ b/solution.py
@@ -57,35 +57,28 @@
     return along_y(x, lambda half, place: (place // 2, 2 * half + place % 2))
 
 
-def ring_gather(own, shift, count, place, axis):
-    found = {0: own}
-    up = down = own
+def x_gather(own, place, early):
     middle = own.shape[0] // 2
-    for step in range(1, count // 2):
-        up, down = shift(up, 1), shift(down, -1)
-        found[step], found[count - step] = up, down
-    found[count // 2] = jnp.concatenate([shift(up[:middle], 1), shift(down[middle:], -1)])
-    blocks = [found[count - 1 - j] for j in range(count)]
-    line = jnp.stack(blocks + blocks[:-1], axis=axis)
-    return lax.dynamic_slice_in_dim(line, count - 1 - place, count, axis)
+    up, down = shift_x(own, 1), shift_x(own, -1)
+    up, down, early = lax.optimization_barrier((up, down, early))
+    across = jnp.concatenate([shift_x(up[:middle], 1), shift_x(down[middle:], -1)])
+    line = jnp.stack([down, across, up, own, down, across, up], axis=1)
+    return lax.dynamic_slice_in_dim(line, X_COUNT - 1 - place, X_COUNT, 1), early
 
 
 def ring_scatter_x(part, across):
-    middle = across.shape[0] // 2
-    up = shift_x(across[:middle], 1).astype(f32)
-    down = shift_x(across[middle:], -1).astype(f32)
-    ahead, behind = part(1).astype(f32), part(-1).astype(f32)
-    ahead = jnp.concatenate([ahead[:middle] + up, ahead[middle:]])
-    behind = jnp.concatenate([behind[:middle], behind[middle:] + down])
-    up, down = shift_x(ahead.astype(bf16), 1), shift_x(behind.astype(bf16), -1)
+    ahead = part(1).astype(f32) + shift_x(across, 1).astype(f32)
+    up, down = shift_x(ahead.astype(bf16), 1), shift_x(part(-1), -1)
     return part(0).astype(f32) + up.astype(f32) + down.astype(f32)
 
 
-def scatter_y(parts, place):
+def scatter_y(parts, place, early):
     count = parts.shape[0]
     sent = parts.astype(bf16)
     total = None
     for step in range(count):
+        if step == count // 2:
+            sent, early = lax.optimization_barrier((sent, early))
         one = lax.dynamic_index_in_dim(sent, (place + step) % count, 0, keepdims=False)
 
         def target(half, place):
@@ -94,7 +87,7 @@
 
         one = along_y(one, target).astype(f32)
         total = one if total is None else total + one
-    return total
+    return total, early
 
 
 def split(x):
@@ -157,7 +150,10 @@
     rows = lax.all_gather(block, "tensor", axis=0, tiled=True, axis_index_groups=rings)
     hidden = rows[:, : 2 * SEQ].astype(f32)
     grads = rows[:, 2 * SEQ :]
-    weights = ring_gather(column, shift_x, X_COUNT, x, 1).reshape(2, quarter, 4 * E)
+    mean_part = jnp.sum(hidden, axis=0) / quarter
+    stats = jnp.stack([mean_part, jnp.sum((hidden - mean_part) ** 2, axis=0)])
+    weights, stats = x_gather(column, x, stats)
+    weights = weights.reshape(2, quarter, 4 * E)
     joined_weight, out_weight = weights[:, :, : 3 * E], weights[:, :, 3 * E :]
 
     def merge(stats, stats_other, count):
@@ -169,8 +165,6 @@
             ]
         )
 
-    mean_part = jnp.sum(hidden, axis=0) / quarter
-    stats = jnp.stack([mean_part, jnp.sum((hidden - mean_part) ** 2, axis=0)])
     stats = merge(stats, swap_far(stats), quarter)
     stats_other = swap_cores(stats)
     stats_other = jnp.concatenate([stats_other[:, SEQ:], stats_other[:, :SEQ]], axis=1)
@@ -268,6 +262,8 @@
     payload = jnp.concatenate([group_part.reshape(Z_COUNT, part, 2 * SEQ), extra], axis=1)
     group_parts = lax.all_to_all(payload, "tensor", 0, 0, tiled=True, axis_index_groups=rings)
     total = jnp.sum(group_parts.astype(f32), axis=0)
+    weight_parts = ring_scatter_x(weight_to, across)
+    grad_out_weight, total = scatter_y(weight_parts, y, total)
     sums = total[part : part + 2, :SEQ] + total[part + 2 : part + 4, :SEQ]
     total = total[:part]
     total_other = swap_cores(total[:, SEQ:])
@@ -285,7 +281,6 @@
     scaled = (hidden_t.astype(f32) - mean[:SEQ]) * inv_std[:SEQ]
     input_grad = inv_std[:SEQ] * (scaled_grad - mean_grad - scaled * mean_cross)
 
-    grad_out_weight = scatter_y(ring_scatter_x(weight_to, across), y)
     return input_grad.astype(bf16).T, grad_out_weight.T
 
 

time: 220 us -> 204 us (0.927)
  starting transfers between devices: 99.3 us -> 82.3 us
  blocking collectives: 21.6 us -> 27.5 us
  matrix products: 9.83 us -> 7.38 us
  other arithmetic: 12.2 us -> 9.88 us
    ppermute x8 -> x7, waiting for transfers between devices: 28.6 us -> 9.71 us  [shift_x(): lax.ppermute(x, 'dp', [(i, i - i % row + (i + 2 * step) % row) for i in r...]
    ppermute x3, starting transfers between devices: 24.6 us -> 11.1 us  [swap_far(): return lax.ppermute(x, 'tensor', [(i, (i + Z_COUNT) % n) for i in range(n)])]
    ppermute x3, waiting for transfers between devices: 6.34 us -> 16.7 us  [swap_far(): return lax.ppermute(x, 'tensor', [(i, (i + Z_COUNT) % n) for i in range(n)])]
    all_gather x1, waiting for transfers between devices: 10.4 us -> 18.8 us  [body(): lax.all_gather(block, 'tensor', axis=0, tiled=True, axis_index_groups=rings)]
    all_gather x1, blocking collectives: 21.6 us -> 27.5 us  [body(): column = lax.all_gather(weight_block, 'dp', axis=0, axis_index_groups=lines)]
    all_to_all x1, waiting for transfers between devices: 0.01 us -> 5.29 us  [body(): lax.all_to_all(payload, 'tensor', 0, 0, tiled=True, axis_index_groups=rings)]
    ppermute x5, starting transfers between devices: 14.3 us -> 10.4 us  [along_y(): return lax.ppermute(x, ('dp', 'tensor'), pairs)]
    all_to_all x1, starting transfers between devices: 5.77 us -> 9.5 us  [body(): lax.all_to_all(payload, 'tensor', 0, 0, tiled=True, axis_index_groups=rings)]
  transfers between devices with their start and end apart: 23 -> 22, of which waited for: 14 -> 10; matrix products, arithmetic and copies ran while one was open for 6% -> 3% of each run, Pallas kernels for 0% -> 0%
where the time goes in v6:
time: 204 us; the launch traced here: 202 us
  starting transfers between devices  82.3 us (40%)
  waiting for transfers between devices  54.1 us (27%)
  blocking collectives  27.5 us (13%)
  between operations  15.1 us (7%)
  other arithmetic  9.88 us (5%)
  matrix products  7.38 us (4%)
  local copies, waits for them, and re-layouts  5.36 us (3%)
    ppermute x5, starting transfers between devices, swap_cores(): return lax.ppermute(x, 'dp', [(i, i ^ 1) for i in range(n)])  29.8 us
    all_gather x1, blocking collectives, body(): column = lax.all_gather(weight_block, 'dp', axis=0, axis_index_groups=lines)  27.5 us
    ppermute x7, starting transfers between devices, shift_x(): lax.ppermute(x, 'dp', [(i, i - i % row + (i + 2 * step) % row) for i in r...  21.5 us
    all_gather x1, waiting for transfers between devices, body(): lax.all_gather(block, 'tensor', axis=0, tiled=True, axis_index_groups=rings)  18.8 us
    ppermute x3, waiting for transfers between devices, swap_far(): return lax.ppermute(x, 'tensor', [(i, (i + Z_COUNT) % n) for i in range(n)])  16.7 us
    ppermute x3, starting transfers between devices, swap_far(): return lax.ppermute(x, 'tensor', [(i, (i + Z_COUNT) % n) for i in range(n)])  11.1 us
    ppermute x5, starting transfers between devices, along_y(): return lax.ppermute(x, ('dp', 'tensor'), pairs)  10.4 us
    ppermute x7, waiting for transfers between devices, shift_x(): lax.ppermute(x, 'dp', [(i, i - i % row + (i + 2 * step) % row) for i in r...  9.71 us
  transfers between devices with their start and end apart: 22, of which 10 were waited for; matrix products, arithmetic and copies ran while one was open for 3% of the time, Pallas kernels for 0%

profile of v6, /device:TPU:1, one launch (start us, length us, event | category | flops | bytes accessed | tf_op | source)
XLA Modules:
  0.0 201.7 jit_solution(3864189839624809481)
XLA Ops:
  7.2 1.0 broadcast_select_fusion.1
  8.3 8.8 %collective-permute-start.1 = (bf16[224,256]{1,0:T(8,128)(2,1)S(1)}, bf16[224,256]{1,0:T(8,128)(2,1)S(1)}, u32[]{:S(2)}, u32[]{:S(2)}) collective-permute-start(bf16[224,256]{1,0:T(8,128)(2,1)S(1)} %get-tuple-element.47), channel_id=1, source_target_pairs={{0,16},{16,0},{32,48},{48,32},{64,80},{80,64},{96,112},{112,96},{1... | collective-permute-start | bytes 344072 | tf_op jit(solution)/shard_map/ppermute | solution.py:24
  17.1 1.0 pad_maximum_fusion.5
  18.0 0.7 collective-permute-start
  18.8 0.7 pad_maximum_fusion.6
  19.9 27.5 %all-gather = bf16[896,512]{1,0:T(8,128)(2,1)S(1)} all-gather(bf16[224,512]{1,0:T(8,128)(2,1)S(1)} %collective-permute-done), channel_id=2, replica_groups={{0,128,256,384},{16,144,272,400},{32,160,288,416},{48,176,304,432},{64,..., dimensions={0}, use_global_device_ids=true | all-gather | bytes 1146880 | tf_op jit(solution)/shard_map/all_gather | solution.py:148
  47.4 3.1 %collective-permute-start.2 = (bf16[4,224,512]{2,1,0:T(8,128)(2,1)S(1)}, bf16[4,224,512]{2,1,0:T(8,128)(2,1)S(1)}, u32[]{:S(2)}, u32[]{:S(2)}) collective-permute-start(bf16[4,224,512]{2,1,0:T(8,128)(2,1)S(1)} %bitcast.141), channel_id=1, source_target_pairs={{0,32},{16,48},{32,64},{48,80},{64,96},{80,112},{96,0},{112,16},{1... | collective-permute-start | bytes 2752520 | tf_op jit(solution)/shard_map/ppermute | solution.py:41
  50.6 3.4 %collective-permute-start.3 = (bf16[4,224,512]{2,1,0:T(8,128)(2,1)S(1)}, bf16[4,224,512]{2,1,0:T(8,128)(2,1)S(1)}, u32[]{:S(2)}, u32[]{:S(2)}) collective-permute-start(bf16[4,224,512]{2,1,0:T(8,128)(2,1)S(1)} %bitcast.142), channel_id=1, source_target_pairs={{0,96},{16,112},{32,0},{48,16},{64,32},{80,48},{96,64},{112,80},{1... | collective-permute-start | bytes 2752520 | tf_op jit(solution)/shard_map/ppermute | solution.py:41
  54.1 18.8 %all-gather.3.cloned.1.call-done = bf16[1792,512]{1,0:T(8,128)(2,1)} async-done(((bf16[224,512]{1,0:T(8,128)(2,1)}), bf16[1792,512]{1,0:T(8,128)(2,1)}) %all-gather.3.cloned.1.call-update) | async-done | bytes 1835024 | tf_op jit(solution)/shard_map/all_gather | solution.py:150
  72.8 1.4 convert_reduce_fusion
  74.3 1.5 fusion.2
  75.8 7.1 %collective-permute-start.4 = (f32[2,256]{1,0:T(2,128)S(1)}, f32[2,256]{1,0:T(2,128)S(1)}, u32[]{:S(2)}, u32[]{:S(2)}) collective-permute-start(f32[2,256]{1,0:T(2,128)S(1)} %pad_maximum_fusion.14), channel_id=1, source_target_pairs={{0,8},{1,9},{2,10},{3,11},{4,12},{5,13},{6,14},{7,15},{8,0},{9,1},... | collective-permute-start | bytes 6152 | tf_op jit(solution)/shard_map/ppermute | solution.py:35
  83.2 3.1 %collective-permute-start.6 = (bf16[2,224,512]{2,1,0:T(8,128)(2,1)S(1)}, bf16[2,224,512]{2,1,0:T(8,128)(2,1)S(1)}, u32[]{:S(2)}, u32[]{:S(2)}) collective-permute-start(bf16[2,224,512]{2,1,0:T(8,128)(2,1)S(1)} %slice.335), channel_id=1, source_target_pairs={{0,32},{16,48},{32,64},{48,80},{64,96},{80,112},{96,0},{112,16},{1... | collective-permute-start | bytes 1376264 | tf_op jit(solution)/shard_map/ppermute | solution.py:41
  86.3 3.4 %collective-permute-start.7 = (bf16[2,224,512]{2,1,0:T(8,128)(2,1)S(1)}, bf16[2,224,512]{2,1,0:T(8,128)(2,1)S(1)}, u32[]{:S(2)}, u32[]{:S(2)}) collective-permute-start(bf16[2,224,512]{2,1,0:T(8,128)(2,1)S(1)} %slice.336), channel_id=1, source_target_pairs={{0,96},{16,112},{32,0},{48,16},{64,32},{80,48},{96,64},{112,80},{1... | collective-permute-start | bytes 1376264 | tf_op jit(solution)/shard_map/ppermute | solution.py:41
  89.8 7.4 %collective-permute-start.5 = (f32[2,256]{1,0:T(2,128)S(1)}, f32[2,256]{1,0:T(2,128)S(1)}, u32[]{:S(2)}, u32[]{:S(2)}) collective-permute-start(f32[2,256]{1,0:T(2,128)S(1)} %pad_maximum_fusion.15), channel_id=1, source_target_pairs={{0,16},{16,0},{32,48},{48,32},{64,80},{80,64},{96,112},{112,96},{1... | collective-permute-start | bytes 6152 | tf_op jit(solution)/shard_map/ppermute | solution.py:24
  97.3 0.7 collective-permute-done.5
  99.4 2.2 %copy-done.2 = bf16[1792,512]{1,0:T(8,128)(2,1)S(1)} copy-done((bf16[1792,512]{1,0:T(8,128)(2,1)S(1)}, bf16[1792,512]{1,0:T(8,128)(2,1)}, u32[]{:S(2)}) %copy-start.2) | copy-done | bytes 1835032
  101.6 0.4 fusion.20
  102.1 1.4 fusion.11
  103.6 0.4 fusion.18
  104.1 1.4 fusion.13
  105.6 5.8 %collective-permute-start.8 = (f32[2,136,512]{2,1,0:T(8,128)S(1)}, f32[2,136,512]{2,1,0:T(8,128)S(1)}, u32[]{:S(2)}, u32[]{:S(2)}) collective-permute-start(f32[2,136,512]{2,1,0:T(8,128)S(1)} %pad_maximum_fusion.1), channel_id=1, source_target_pairs={{0,16},{16,0},{32,48},{48,32},{64,80},{80,64},{96,112},{112,96},{1... | collective-permute-start | bytes 1671176 | tf_op jit(solution)/shard_map/ppermute | solution.py:24
  111.4 1.6 collective-permute-done.8
  113.2 2.1 %collective-permute-start.9 = (bf16[144,512]{1,0:T(8,128)(2,1)S(1)}, bf16[144,512]{1,0:T(8,128)(2,1)S(1)}, u32[]{:S(2)}, u32[]{:S(2)}) collective-permute-start(bf16[144,512]{1,0:T(8,128)(2,1)S(1)} %pad_maximum_fusion.9), channel_id=1, source_target_pairs={{0,8},{1,9},{2,10},{3,11},{4,12},{5,13},{6,14},{7,15},{8,0},{9,1},... | collective-permute-start | bytes 442376 | tf_op jit(solution)/shard_map/ppermute | solution.py:35
  115.4 8.8 %collective-permute-done.9 = bf16[144,512]{1,0:T(8,128)(2,1)S(1)} collective-permute-done((bf16[144,512]{1,0:T(8,128)(2,1)S(1)}, bf16[144,512]{1,0:T(8,128)(2,1)S(1)}, u32[]{:S(2)}, u32[]{:S(2)}) %collective-permute-start.9) | collective-permute-done | bytes 147488 | tf_op jit(solution)/shard_map/ppermute | solution.py:35
  125.7 1.9 collective-permute-start.10
  127.6 7.9 %collective-permute-done.10 = bf16[144,512]{1,0:T(8,128)(2,1)S(1)} collective-permute-done((bf16[144,512]{1,0:T(8,128)(2,1)S(1)}, bf16[144,512]{1,0:T(8,128)(2,1)S(1)}, u32[]{:S(2)}, u32[]{:S(2)}) %collective-permute-start.10) | collective-permute-done | bytes 147488 | tf_op jit(solution)/shard_map/ppermute | solution.py:35
  135.7 4.2 %collective-permute-start.11 = (bf16[2,144,512]{2,1,0:T(8,128)(2,1)S(1)}, bf16[2,144,512]{2,1,0:T(8,128)(2,1)S(1)}, u32[]{:S(2)}, u32[]{:S(2)}) collective-permute-start(bf16[2,144,512]{2,1,0:T(8,128)(2,1)S(1)} %fusion.23), channel_id=1, source_target_pairs={{0,16},{16,0},{32,48},{48,32},{64,80},{80,64},{96,112},{112,96},{1... | collective-permute-start | bytes 884744 | tf_op jit(solution)/shard_map/ppermute | solution.py:24
  140.1 1.1 collective-permute-done.11
  141.2 0.4 convolution_convert_fusion.1
  142.2 1.5 copy-done.1
  143.7 0.7 fusion.9
  144.4 0.7 fusion
  145.2 1.0 pad_maximum_fusion
  146.2 9.5 %all-to-all-start = ((bf16[8,240,256]{2,1,0:T(8,128)(2,1)}), bf16[8,240,256]{2,1,0:T(8,128)(2,1)S(1)}, u32[]{:S(2)}, u32[]{:S(2)}) async-start(bf16[8,240,256]{2,1,0:T(8,128)(2,1)} %pad_maximum_fusion), calls=%async_computation | async-start | bytes 1966080 | tf_op jit(solution)/shard_map/all_to_all | solution.py:263
  155.7 3.1 %collective-permute-start.12 = (bf16[4,224,128]{2,1,0:T(8,128)(2,1)S(1)}, bf16[4,224,128]{2,1,0:T(8,128)(2,1)S(1)}, u32[]{:S(2)}, u32[]{:S(2)}) collective-permute-start(bf16[4,224,128]{2,1,0:T(8,128)(2,1)S(1)} %pad_maximum_fusion.7), channel_id=1, source_target_pairs={{0,32},{16,48},{32,64},{48,80},{64,96},{80,112},{96,0},{112,16},{1... | collective-permute-start | bytes 688136 | tf_op jit(solution)/shard_map/ppermute | solution.py:41
  158.8 3.4 %collective-permute-start.14 = (bf16[4,224,128]{2,1,0:T(8,128)(2,1)S(1)}, bf16[4,224,128]{2,1,0:T(8,128)(2,1)S(1)}, u32[]{:S(2)}, u32[]{:S(2)}) collective-permute-start(bf16[4,224,128]{2,1,0:T(8,128)(2,1)S(1)} %pad_maximum_fusion.8), channel_id=1, source_target_pairs={{0,96},{16,112},{32,0},{48,16},{64,32},{80,48},{96,64},{112,80},{1... | collective-permute-start | bytes 688136 | tf_op jit(solution)/shard_map/ppermute | solution.py:41
  162.2 3.1 %collective-permute-done.12 = bf16[4,224,128]{2,1,0:T(8,128)(2,1)S(1)} collective-permute-done((bf16[4,224,128]{2,1,0:T(8,128)(2,1)S(1)}, bf16[4,224,128]{2,1,0:T(8,128)(2,1)S(1)}, u32[]{:S(2)}, u32[]{:S(2)}) %collective-permute-start.12) | collective-permute-done | bytes 229408 | tf_op jit(solution)/shard_map/ppermute | solution.py:41
  165.4 2.1 %collective-permute-start.13 = (bf16[4,224,128]{2,1,0:T(8,128)(2,1)S(1)}, bf16[4,224,128]{2,1,0:T(8,128)(2,1)S(1)}, u32[]{:S(2)}, u32[]{:S(2)}) collective-permute-start(bf16[4,224,128]{2,1,0:T(8,128)(2,1)S(1)} %add_convert_fusion.1), channel_id=1, source_target_pairs={{0,32},{16,48},{32,64},{48,80},{64,96},{80,112},{96,0},{112,16},{1... | collective-permute-start | bytes 688136 | tf_op jit(solution)/shard_map/ppermute | solution.py:41
  167.6 6.6 %collective-permute-done.13 = bf16[4,224,128]{2,1,0:T(8,128)(2,1)S(1)} collective-permute-done((bf16[4,224,128]{2,1,0:T(8,128)(2,1)S(1)}, bf16[4,224,128]{2,1,0:T(8,128)(2,1)S(1)}, u32[]{:S(2)}, u32[]{:S(2)}) %collective-permute-start.13) | collective-permute-done | bytes 229408 | tf_op jit(solution)/shard_map/ppermute | solution.py:41
  174.4 0.7 collective-permute-start.16
  175.0 3.1 %collective-permute-start.17 = (bf16[224,128]{1,0:T(8,128)(2,1)S(1)}, bf16[224,128]{1,0:T(8,128)(2,1)S(1)}, u32[]{:S(2)}, u32[]{:S(2)}) collective-permute-start(bf16[224,128]{1,0:T(8,128)(2,1)S(1)} %get-tuple-element.43), channel_id=1, source_target_pairs={{0,128},{1,129},{2,130},{3,131},{4,132},{5,133},{6,134},{7,135},{8... | collective-permute-start | bytes 172040 | tf_op jit(solution)/shard_map/ppermute | solution.py:53
  178.2 5.3 %all-to-all-done = bf16[8,240,256]{2,1,0:T(8,128)(2,1)S(1)} async-done(((bf16[8,240,256]{2,1,0:T(8,128)(2,1)}), bf16[8,240,256]{2,1,0:T(8,128)(2,1)S(1)}, u32[]{:S(2)}, u32[]{:S(2)}) %all-to-all-start) | async-done | bytes 983072 | tf_op jit(solution)/shard_map/all_to_all | solution.py:263
  183.7 2.6 %collective-permute-start.18 = (bf16[224,128]{1,0:T(8,128)(2,1)S(1)}, bf16[224,128]{1,0:T(8,128)(2,1)S(1)}, u32[]{:S(2)}, u32[]{:S(2)}) collective-permute-start(bf16[224,128]{1,0:T(8,128)(2,1)S(1)} %get-tuple-element.44), channel_id=1, source_target_pairs={{0,8},{1,9},{2,10},{3,11},{4,12},{5,13},{6,14},{7,15},{8,264},{9,2... | collective-permute-start | bytes 172040 | tf_op jit(solution)/shard_map/ppermute | solution.py:53
  186.3 3.3 %collective-permute-start.19 = (bf16[224,128]{1,0:T(8,128)(2,1)S(1)}, bf16[224,128]{1,0:T(8,128)(2,1)S(1)}, u32[]{:S(2)}, u32[]{:S(2)}) collective-permute-start(bf16[224,128]{1,0:T(8,128)(2,1)S(1)} %get-tuple-element.45), channel_id=1, source_target_pairs={{0,136},{1,137},{2,138},{3,139},{4,140},{5,141},{6,142},{7,143},{8... | collective-permute-start | bytes 172040 | tf_op jit(solution)/shard_map/ppermute | solution.py:53
  189.6 3.6 %collective-permute-start.15 = (f32[224,128]{1,0:T(8,128)S(1)}, f32[224,128]{1,0:T(8,128)S(1)}, u32[]{:S(2)}, u32[]{:S(2)}) collective-permute-start(f32[224,128]{1,0:T(8,128)S(1)} %get-tuple-element.40), channel_id=1, source_target_pairs={{0,16},{16,0},{32,48},{48,32},{64,80},{80,64},{96,112},{112,96},{1... | collective-permute-start | bytes 344072 | tf_op jit(solution)/shard_map/ppermute | solution.py:24
  193.2 0.7 add_bitcast_fusion
  194.1 0.8 fusion.50
  (121 shorter events, 5.7 us)
Async XLA Ops:
  7.2 12.4 %copy-start.4 = (f32[7168]{0:T(1024)S(1)}, f32[7168]{0:T(1024)}, u32[]{:S(2)}) copy-start(f32[7168]{0:T(1024)} %param.8) | copy-start | bytes 86020
  7.2 12.5 %copy-start.5 = (f32[7168]{0:T(1024)S(1)}, f32[7168]{0:T(1024)}, u32[]{:S(2)}) copy-start(f32[7168]{0:T(1024)} %param.9) | copy-start | bytes 86020
  7.2 65.6 %all-gather.3.cloned.1.call-start = ((), (), s32[]{:S(2)}) async-start(), calls=%async_computation.1 | async-start | bytes 2064384 | tf_op jit(solution)/shard_map/all_gather | solution.py:150
  8.3 10.5 %collective-permute-start.1 = (bf16[224,256]{1,0:T(8,128)(2,1)S(1)}, bf16[224,256]{1,0:T(8,128)(2,1)S(1)}, u32[]{:S(2)}, u32[]{:S(2)}) collective-permute-start(bf16[224,256]{1,0:T(8,128)(2,1)S(1)} %get-tuple-element.47), channel_id=1, source_target_pairs={{0,16},{16,0},{32,48},{48,32},{64,80},{80,64},{96,112},{112,96},{1... | collective-permute-start | bytes 344072 | tf_op jit(solution)/shard_map/ppermute | solution.py:24
  18.0 1.5 collective-permute-start
  47.4 28.3 %collective-permute-start.2 = (bf16[4,224,512]{2,1,0:T(8,128)(2,1)S(1)}, bf16[4,224,512]{2,1,0:T(8,128)(2,1)S(1)}, u32[]{:S(2)}, u32[]{:S(2)}) collective-permute-start(bf16[4,224,512]{2,1,0:T(8,128)(2,1)S(1)} %bitcast.141), channel_id=1, source_target_pairs={{0,32},{16,48},{32,64},{48,80},{64,96},{80,112},{96,0},{112,16},{1... | collective-permute-start | bytes 2752520 | tf_op jit(solution)/shard_map/ppermute | solution.py:41
  50.6 25.2 %collective-permute-start.3 = (bf16[4,224,512]{2,1,0:T(8,128)(2,1)S(1)}, bf16[4,224,512]{2,1,0:T(8,128)(2,1)S(1)}, u32[]{:S(2)}, u32[]{:S(2)}) collective-permute-start(bf16[4,224,512]{2,1,0:T(8,128)(2,1)S(1)} %bitcast.142), channel_id=1, source_target_pairs={{0,96},{16,112},{32,0},{48,16},{64,32},{80,48},{96,64},{112,80},{1... | collective-permute-start | bytes 2752520 | tf_op jit(solution)/shard_map/ppermute | solution.py:41
  75.8 14.0 %collective-permute-start.4 = (f32[2,256]{1,0:T(2,128)S(1)}, f32[2,256]{1,0:T(2,128)S(1)}, u32[]{:S(2)}, u32[]{:S(2)}) collective-permute-start(f32[2,256]{1,0:T(2,128)S(1)} %pad_maximum_fusion.14), channel_id=1, source_target_pairs={{0,8},{1,9},{2,10},{3,11},{4,12},{5,13},{6,14},{7,15},{8,0},{9,1},... | collective-permute-start | bytes 6152 | tf_op jit(solution)/shard_map/ppermute | solution.py:35
  83.2 14.8 %collective-permute-start.6 = (bf16[2,224,512]{2,1,0:T(8,128)(2,1)S(1)}, bf16[2,224,512]{2,1,0:T(8,128)(2,1)S(1)}, u32[]{:S(2)}, u32[]{:S(2)}) collective-permute-start(bf16[2,224,512]{2,1,0:T(8,128)(2,1)S(1)} %slice.335), channel_id=1, source_target_pairs={{0,32},{16,48},{32,64},{48,80},{64,96},{80,112},{96,0},{112,16},{1... | collective-permute-start | bytes 1376264 | tf_op jit(solution)/shard_map/ppermute | solution.py:41
  86.3 11.7 %collective-permute-start.7 = (bf16[2,224,512]{2,1,0:T(8,128)(2,1)S(1)}, bf16[2,224,512]{2,1,0:T(8,128)(2,1)S(1)}, u32[]{:S(2)}, u32[]{:S(2)}) collective-permute-start(bf16[2,224,512]{2,1,0:T(8,128)(2,1)S(1)} %slice.336), channel_id=1, source_target_pairs={{0,96},{16,112},{32,0},{48,16},{64,32},{80,48},{96,64},{112,80},{1... | collective-permute-start | bytes 1376264 | tf_op jit(solution)/shard_map/ppermute | solution.py:41
  89.8 8.2 %collective-permute-start.5 = (f32[2,256]{1,0:T(2,128)S(1)}, f32[2,256]{1,0:T(2,128)S(1)}, u32[]{:S(2)}, u32[]{:S(2)}) collective-permute-start(f32[2,256]{1,0:T(2,128)S(1)} %pad_maximum_fusion.15), channel_id=1, source_target_pairs={{0,16},{16,0},{32,48},{48,32},{64,80},{80,64},{96,112},{112,96},{1... | collective-permute-start | bytes 6152 | tf_op jit(solution)/shard_map/ppermute | solution.py:24
  98.8 5.3 %copy-start = (bf16[4,4,224,512]{3,2,1,0:T(8,128)(2,1)}, bf16[4,4,224,512]{3,2,1,0:T(8,128)(2,1)S(1)}, u32[]{:S(2)}) copy-start(bf16[4,4,224,512]{3,2,1,0:T(8,128)(2,1)S(1)} %constant_dynamic-slice_fusion) | copy-start | bytes 11010052
  98.8 2.8 %copy-start.2 = (bf16[1792,512]{1,0:T(8,128)(2,1)S(1)}, bf16[1792,512]{1,0:T(8,128)(2,1)}, u32[]{:S(2)}) copy-start(bf16[1792,512]{1,0:T(8,128)(2,1)} %all-gather.3.cloned.1.call-done) | copy-start | bytes 5505028
  105.6 7.4 %collective-permute-start.8 = (f32[2,136,512]{2,1,0:T(8,128)S(1)}, f32[2,136,512]{2,1,0:T(8,128)S(1)}, u32[]{:S(2)}, u32[]{:S(2)}) collective-permute-start(f32[2,136,512]{2,1,0:T(8,128)S(1)} %pad_maximum_fusion.1), channel_id=1, source_target_pairs={{0,16},{16,0},{32,48},{48,32},{64,80},{80,64},{96,112},{112,96},{1... | collective-permute-start | bytes 1671176 | tf_op jit(solution)/shard_map/ppermute | solution.py:24
  113.1 11.3 %copy-start.6 = (f32[384]{0:T(512)S(1)}, f32[384]{0:T(512)}, u32[]{:S(2)}) copy-start(f32[384]{0:T(512)} %param.11) | copy-start | bytes 4612
  113.2 11.0 %collective-permute-start.9 = (bf16[144,512]{1,0:T(8,128)(2,1)S(1)}, bf16[144,512]{1,0:T(8,128)(2,1)S(1)}, u32[]{:S(2)}, u32[]{:S(2)}) collective-permute-start(bf16[144,512]{1,0:T(8,128)(2,1)S(1)} %pad_maximum_fusion.9), channel_id=1, source_target_pairs={{0,8},{1,9},{2,10},{3,11},{4,12},{5,13},{6,14},{7,15},{8,0},{9,1},... | collective-permute-start | bytes 442376 | tf_op jit(solution)/shard_map/ppermute | solution.py:35
  125.7 9.8 %collective-permute-start.10 = (bf16[144,512]{1,0:T(8,128)(2,1)S(1)}, bf16[144,512]{1,0:T(8,128)(2,1)S(1)}, u32[]{:S(2)}, u32[]{:S(2)}) collective-permute-start(bf16[144,512]{1,0:T(8,128)(2,1)S(1)} %fusion.47), channel_id=1, source_target_pairs={{0,8},{1,9},{2,10},{3,11},{4,12},{5,13},{6,14},{7,15},{8,0},{9,1},... | collective-permute-start | bytes 442376 | tf_op jit(solution)/shard_map/ppermute | solution.py:35
  135.7 5.4 %collective-permute-start.11 = (bf16[2,144,512]{2,1,0:T(8,128)(2,1)S(1)}, bf16[2,144,512]{2,1,0:T(8,128)(2,1)S(1)}, u32[]{:S(2)}, u32[]{:S(2)}) collective-permute-start(bf16[2,144,512]{2,1,0:T(8,128)(2,1)S(1)} %fusion.23), channel_id=1, source_target_pairs={{0,16},{16,0},{32,48},{48,32},{64,80},{80,64},{96,112},{112,96},{1... | collective-permute-start | bytes 884744 | tf_op jit(solution)/shard_map/ppermute | solution.py:24
  141.6 2.0 %copy-start.1 = (bf16[4,4,224,512]{3,2,1,0:T(8,128)(2,1)S(1)}, bf16[4,4,224,512]{3,2,1,0:T(8,128)(2,1)}, u32[]{:S(2)}) copy-start(bf16[4,4,224,512]{3,2,1,0:T(8,128)(2,1)} %copy-done) | copy-start | bytes 11010052
  146.2 37.3 %all-to-all-start = ((bf16[8,240,256]{2,1,0:T(8,128)(2,1)}), bf16[8,240,256]{2,1,0:T(8,128)(2,1)S(1)}, u32[]{:S(2)}, u32[]{:S(2)}) async-start(bf16[8,240,256]{2,1,0:T(8,128)(2,1)} %pad_maximum_fusion), calls=%async_computation | async-start | bytes 1966080 | tf_op jit(solution)/shard_map/all_to_all | solution.py:263
  155.7 9.6 %collective-permute-start.12 = (bf16[4,224,128]{2,1,0:T(8,128)(2,1)S(1)}, bf16[4,224,128]{2,1,0:T(8,128)(2,1)S(1)}, u32[]{:S(2)}, u32[]{:S(2)}) collective-permute-start(bf16[4,224,128]{2,1,0:T(8,128)(2,1)S(1)} %pad_maximum_fusion.7), channel_id=1, source_target_pairs={{0,32},{16,48},{32,64},{48,80},{64,96},{80,112},{96,0},{112,16},{1... | collective-permute-start | bytes 688136 | tf_op jit(solution)/shard_map/ppermute | solution.py:41
  158.8 8.8 %collective-permute-start.14 = (bf16[4,224,128]{2,1,0:T(8,128)(2,1)S(1)}, bf16[4,224,128]{2,1,0:T(8,128)(2,1)S(1)}, u32[]{:S(2)}, u32[]{:S(2)}) collective-permute-start(bf16[4,224,128]{2,1,0:T(8,128)(2,1)S(1)} %pad_maximum_fusion.8), channel_id=1, source_target_pairs={{0,96},{16,112},{32,0},{48,16},{64,32},{80,48},{96,64},{112,80},{1... | collective-permute-start | bytes 688136 | tf_op jit(solution)/shard_map/ppermute | solution.py:41
  165.4 28.7 %copy-start.3 = (bf16[128,448]{0,1:T(8,128)(2,1)S(1)}, bf16[128,448]{0,1:T(8,128)(2,1)}, u32[]{:S(2)}) copy-start(bf16[128,448]{0,1:T(8,128)(2,1)} %param.7) | copy-start | bytes 344068
  165.4 8.8 %collective-permute-start.13 = (bf16[4,224,128]{2,1,0:T(8,128)(2,1)S(1)}, bf16[4,224,128]{2,1,0:T(8,128)(2,1)S(1)}, u32[]{:S(2)}, u32[]{:S(2)}) collective-permute-start(bf16[4,224,128]{2,1,0:T(8,128)(2,1)S(1)} %add_convert_fusion.1), channel_id=1, source_target_pairs={{0,32},{16,48},{32,64},{48,80},{64,96},{80,112},{96,0},{112,16},{1... | collective-permute-start | bytes 688136 | tf_op jit(solution)/shard_map/ppermute | solution.py:41
  174.4 18.8 %collective-permute-start.16 = (bf16[224,128]{1,0:T(8,128)(2,1)S(1)}, bf16[224,128]{1,0:T(8,128)(2,1)S(1)}, u32[]{:S(2)}, u32[]{:S(2)}) collective-permute-start(bf16[224,128]{1,0:T(8,128)(2,1)S(1)} %get-tuple-element.42), channel_id=1, source_target_pairs={{0,0},{1,1},{2,2},{3,3},{4,4},{5,5},{6,6},{7,7},{8,256},{9,257},{1... | collective-permute-start | bytes 172040 | tf_op jit(solution)/shard_map/ppermute | solution.py:53
  175.0 18.1 %collective-permute-start.17 = (bf16[224,128]{1,0:T(8,128)(2,1)S(1)}, bf16[224,128]{1,0:T(8,128)(2,1)S(1)}, u32[]{:S(2)}, u32[]{:S(2)}) collective-permute-start(bf16[224,128]{1,0:T(8,128)(2,1)S(1)} %get-tuple-element.43), channel_id=1, source_target_pairs={{0,128},{1,129},{2,130},{3,131},{4,132},{5,133},{6,134},{7,135},{8... | collective-permute-start | bytes 172040 | tf_op jit(solution)/shard_map/ppermute | solution.py:53
  183.7 9.5 %collective-permute-start.18 = (bf16[224,128]{1,0:T(8,128)(2,1)S(1)}, bf16[224,128]{1,0:T(8,128)(2,1)S(1)}, u32[]{:S(2)}, u32[]{:S(2)}) collective-permute-start(bf16[224,128]{1,0:T(8,128)(2,1)S(1)} %get-tuple-element.44), channel_id=1, source_target_pairs={{0,8},{1,9},{2,10},{3,11},{4,12},{5,13},{6,14},{7,15},{8,264},{9,2... | collective-permute-start | bytes 172040 | tf_op jit(solution)/shard_map/ppermute | solution.py:53
  186.3 6.9 %collective-permute-start.19 = (bf16[224,128]{1,0:T(8,128)(2,1)S(1)}, bf16[224,128]{1,0:T(8,128)(2,1)S(1)}, u32[]{:S(2)}, u32[]{:S(2)}) collective-permute-start(bf16[224,128]{1,0:T(8,128)(2,1)S(1)} %get-tuple-element.45), channel_id=1, source_target_pairs={{0,136},{1,137},{2,138},{3,139},{4,140},{5,141},{6,142},{7,143},{8... | collective-permute-start | bytes 172040 | tf_op jit(solution)/shard_map/ppermute | solution.py:53
  189.6 4.5 %collective-permute-start.15 = (f32[224,128]{1,0:T(8,128)S(1)}, f32[224,128]{1,0:T(8,128)S(1)}, u32[]{:S(2)}, u32[]{:S(2)}) collective-permute-start(f32[224,128]{1,0:T(8,128)S(1)} %get-tuple-element.40), channel_id=1, source_target_pairs={{0,16},{16,0},{32,48},{48,32},{64,80},{80,64},{96,112},{112,96},{1... | collective-permute-start | bytes 344072 | tf_op jit(solution)/shard_map/ppermute | solution.py:24
Sparse Core Ops, SparseCore 0:
  19.6 53.1 all-gather.2

commit v7 on v6

--- a/solution.py
+++ b/solution.py
@@ -62,12 +62,16 @@
     up, down = shift_x(own, 1), shift_x(own, -1)
     up, down, early = lax.optimization_barrier((up, down, early))
     across = jnp.concatenate([shift_x(up[:middle], 1), shift_x(down[middle:], -1)])
-    line = jnp.stack([down, across, up, own, down, across, up], axis=1)
-    return lax.dynamic_slice_in_dim(line, X_COUNT - 1 - place, X_COUNT, 1), early
+    return [own, down, across, up], early
+
+
+def in_order(blocks, place):
+    line = jnp.stack(blocks[1:] + blocks, axis=1)
+    return lax.dynamic_slice_in_dim(line, X_COUNT - 1 - place, X_COUNT, 1)
 
 
 def ring_scatter_x(part, across):
-    ahead = part(1).astype(f32) + shift_x(across, 1).astype(f32)
+    ahead = part(1).astype(f32) + across.astype(f32)
     up, down = shift_x(ahead.astype(bf16), 1), shift_x(part(-1), -1)
     return part(0).astype(f32) + up.astype(f32) + down.astype(f32)
 
@@ -144,17 +148,19 @@
     block = jnp.concatenate([mine[:, :SEQ], other[:, :SEQ], mine[:, SEQ:], other[:, SEQ:]], axis=1)
 
     weight_block = move_weights(jnp.concatenate([w_qkv, w_out.T], axis=1))
-    weight_block, block = lax.optimization_barrier((weight_block, block))
+    hidden = lax.all_gather(
+        block[:, : 2 * SEQ], "tensor", axis=0, tiled=True, axis_index_groups=rings
+    )
+    weight_block, hidden = lax.optimization_barrier((weight_block, hidden))
     column = lax.all_gather(weight_block, "dp", axis=0, axis_index_groups=lines)
-
-    rows = lax.all_gather(block, "tensor", axis=0, tiled=True, axis_index_groups=rings)
-    hidden = rows[:, : 2 * SEQ].astype(f32)
-    grads = rows[:, 2 * SEQ :]
+    column, block = lax.optimization_barrier((column, block))
+    grads = lax.all_gather(
+        block[:, 2 * SEQ :], "tensor", axis=0, tiled=True, axis_index_groups=rings
+    )
+    blocks, grads = x_gather(column, x, grads)
+    hidden = hidden.astype(f32)
     mean_part = jnp.sum(hidden, axis=0) / quarter
     stats = jnp.stack([mean_part, jnp.sum((hidden - mean_part) ** 2, axis=0)])
-    weights, stats = x_gather(column, x, stats)
-    weights = weights.reshape(2, quarter, 4 * E)
-    joined_weight, out_weight = weights[:, :, : 3 * E], weights[:, :, 3 * E :]
 
     def merge(stats, stats_other, count):
         gap = stats[0] - stats_other[0]
@@ -179,29 +185,31 @@
 
     gain, bias = own_part(norm_gain), own_part(norm_bias)
     normed = ((hidden - mean) * inv_std * gain[:, None] + bias[:, None]).astype(bf16)
-    vectors = jnp.stack([*split(gain), *split(bias)])
+    vectors = jnp.stack([*split(gain), *split(bias)] + [jnp.zeros_like(gain, bf16)] * 4)
+    left = jnp.concatenate([normed, vectors.T], axis=1).reshape(2, X_COUNT, part, 2 * SEQ + 8)
+    right = grads.reshape(2, X_COUNT, part, 2 * SEQ)
 
     def own_head(pair):
         return jnp.where(far == 0, pair[0], pair[1]), jnp.where(far == 0, pair[1], pair[0])
 
-    vector_parts = [dot(vectors, joined_weight[h], ((1,), (0,))) for h in range(2)]
-    vector_parts = [
-        jnp.stack([v[0] + v[1], v[2] + v[3], jnp.zeros_like(v[0]), jnp.zeros_like(v[0])])
-        for v in vector_parts
-    ]
-    vector_parts = [jnp.pad(v, ((0, 4), (0, E))) for v in vector_parts]
-    parts = [
-        jnp.concatenate(
-            [
-                dot(normed, joined_weight[h], ((0,), (0,))),
-                dot(grads, out_weight[h], ((0,), (0,))),
-            ],
-            axis=1,
-        )
-        for h in range(2)
-    ]
-    sent = jnp.stack([jnp.concatenate([p[SEQ:], v]) for p, v in zip(parts, vector_parts)])
-    kept = jnp.stack([jnp.concatenate([p[:SEQ], v]) for p, v in zip(parts, vector_parts)])
+    joined_parts, grad_parts = [0.0, 0.0], [0.0, 0.0]
+    for step in (0, 3, 1, 2):
+        place = (x + step) % X_COUNT
+        left_part = lax.dynamic_index_in_dim(left, place, 1, keepdims=False)
+        right_part = lax.dynamic_index_in_dim(right, place, 1, keepdims=False)
+        left_part = left_part.reshape(2 * part, 2 * SEQ + 8)
+        right_part = right_part.reshape(2 * part, 2 * SEQ)
+        for h in range(2):
+            weight = blocks[step][2 * h : 2 * h + 2].reshape(2 * part, 4 * E)
+            joined_parts[h] += dot(left_part, weight[:, : 3 * E], ((0,), (0,)))
+            grad_parts[h] += dot(right_part, weight[:, 3 * E :], ((0,), (0,)))
+    parts = []
+    for j, g in zip(joined_parts, grad_parts):
+        v = j[2 * SEQ :]
+        v = jnp.stack([v[0] + v[1], v[2] + v[3]])
+        parts.append((jnp.concatenate([j[: 2 * SEQ], g], axis=1), jnp.pad(v, ((0, 6), (0, E)))))
+    sent = jnp.stack([jnp.concatenate([p[SEQ:], v]) for p, v in parts])
+    kept = jnp.stack([jnp.concatenate([p[:SEQ], v]) for p, v in parts])
     own, away = own_head(kept + swap_cores(sent))
     away_high, away_low = split(away[SEQ:])
     away = swap_far(jnp.concatenate([away[:SEQ].astype(bf16), away_high, away_low]))
@@ -242,6 +250,7 @@
     sums = jnp.concatenate([sums, unpack(heads_other[0, SEQ:, :SEQ])], axis=1)
     heads = jnp.concatenate([heads, heads_other[:, :SEQ]], axis=1)
 
+    joined_weight = in_order([b[:, :, : 3 * E] for b in blocks], x).reshape(2, quarter, 3 * E)
     weight_parts = [
         dot(grads, heads[h, :, :E], ((1,), (0,))).astype(bf16).reshape(2, X_COUNT, part, E)
         for h in range(2)
@@ -253,7 +262,8 @@
             [lax.dynamic_index_in_dim(w, place, 1, keepdims=False) for w in weight_parts]
         )
 
-    across, heads = lax.optimization_barrier((weight_to(2), heads))
+    across = shift_x(weight_to(2), 1)
+    across, heads = lax.optimization_barrier((across, heads))
 
     group_part = sum(
         dot(joined_weight[h], heads[h, :, E:], ((1,), (1,))) for h in range(2)

time: 204 us -> 226 us (1.11)
  blocking collectives: 27.5 us -> 64.9 us
  between operations: 15.1 us -> 1.83 us
    all_gather x0 -> x2, blocking collectives: none -> 44.1 us  [the longest x1 22.3 us: body(): lax.all_gather(block[:, 2 * SEQ:], 'tensor', axis=0, tiled=True, axis_ind...]
    all_gather x1 -> x0, waiting for transfers between devices: 18.8 us -> none  [body(): lax.all_gather(block, 'tensor', axis=0, tiled=True, axis_index_groups=rings)]
    ppermute x7, waiting for transfers between devices: 9.71 us -> 22.1 us  [shift_x(): lax.ppermute(x, 'dp', [(i, i - i % row + (i + 2 * step) % row) for i in r...]
    all_to_all x1, waiting for transfers between devices: 5.29 us -> 13.9 us  [body(): lax.all_to_all(payload, 'tensor', 0, 0, tiled=True, axis_index_groups=rings)]
    all_gather x1, blocking collectives: 27.5 us -> 20.8 us  [body(): column = lax.all_gather(weight_block, 'dp', axis=0, axis_index_groups=lines)]
    all_to_all x1, starting transfers between devices: 9.5 us -> 3.55 us  [body(): lax.all_to_all(payload, 'tensor', 0, 0, tiled=True, axis_index_groups=rings)]
    ppermute x3, starting transfers between devices: 11.1 us -> 15.1 us  [swap_far(): return lax.ppermute(x, 'tensor', [(i, (i + Z_COUNT) % n) for i in range(n)])]
    unnamed x18 -> x8, local copies, waits for them, and re-layouts: 3.95 us -> 0.46 us
  transfers between devices with their start and end apart: 22 -> 21, of which waited for: 10 -> 12; matrix products, arithmetic and copies ran while one was open for 3% -> 5% of each run, Pallas kernels for 0% -> 0%
where the time goes in v7:
time: 226 us; the launch traced here: 225 us
  starting transfers between devices  83.3 us (37%)
  blocking collectives  64.9 us (29%)
  waiting for transfers between devices  54.3 us (24%)
  other arithmetic  9.17 us (4%)
  matrix products  7.82 us (3%)
  local copies, waits for them, and re-layouts  3.34 us (1%)
    ppermute x5, starting transfers between devices, swap_cores(): return lax.ppermute(x, 'dp', [(i, i ^ 1) for i in range(n)])  32.9 us
    all_gather x1, blocking collectives, body(): lax.all_gather(block[:, 2 * SEQ:], 'tensor', axis=0, tiled=True, axis_ind...  22.3 us
    ppermute x7, waiting for transfers between devices, shift_x(): lax.ppermute(x, 'dp', [(i, i - i % row + (i + 2 * step) % row) for i in r...  22.1 us
    all_gather x1, blocking collectives, body(): lax.all_gather(block[:, :2 * SEQ], 'tensor', axis=0, tiled=True, axis_ind...  21.8 us
    all_gather x1, blocking collectives, body(): column = lax.all_gather(weight_block, 'dp', axis=0, axis_index_groups=lines)  20.8 us
    ppermute x7, starting transfers between devices, shift_x(): lax.ppermute(x, 'dp', [(i, i - i % row + (i + 2 * step) % row) for i in r...  19.3 us
    ppermute x3, waiting for transfers between devices, swap_far(): return lax.ppermute(x, 'tensor', [(i, (i + Z_COUNT) % n) for i in range(n)])  15.3 us
    ppermute x3, starting transfers between devices, swap_far(): return lax.ppermute(x, 'tensor', [(i, (i + Z_COUNT) % n) for i in range(n)])  15.1 us
  transfers between devices with their start and end apart: 21, of which 12 were waited for; matrix products, arithmetic and copies ran while one was open for 5% of the time, Pallas kernels for 0%

profile of v7, /device:TPU:1, one launch (start us, length us, event | category | flops | bytes accessed | tf_op | source)
XLA Modules:
  0.0 224.7 jit_solution(5923371041783468531)
XLA Ops:
  0.6 1.0 pad_maximum_fusion.11
  1.6 0.7 collective-permute-start
  2.3 1.0 broadcast_select_fusion.1
  3.3 8.8 %collective-permute-start.1 = (bf16[224,256]{1,0:T(8,128)(2,1)S(1)}, bf16[224,256]{1,0:T(8,128)(2,1)S(1)}, u32[]{:S(2)}, u32[]{:S(2)}) collective-permute-start(bf16[224,256]{1,0:T(8,128)(2,1)S(1)} %get-tuple-element.75), channel_id=1, source_target_pairs={{0,16},{16,0},{32,48},{48,32},{64,80},{80,64},{96,112},{112,96},{1... | collective-permute-start | bytes 344072 | tf_op jit(solution)/shard_map/ppermute | solution.py:24
  12.1 0.8 slice_select_fusion.3
  13.0 0.8 slice_select_fusion.2
  15.0 21.8 %all_gather.12 = bf16[1792,256]{1,0:T(8,128)(2,1)S(1)} all-gather(bf16[224,256]{1,0:T(8,128)(2,1)S(1)} %pad_maximum_fusion.18), channel_id=1, replica_groups={{0,1,2,3,4,5,6,7},{8,9,10,11,12,13,14,15},{16,17,18,19,20,21,22,23},{24..., dimensions={0}, use_global_device_ids=true | all-gather | bytes 1032192 | tf_op jit(solution)/shard_map/all_gather | solution.py:151
  36.8 20.8 %all-gather = bf16[896,512]{1,0:T(8,128)(2,1)S(1)} all-gather(bf16[224,512]{1,0:T(8,128)(2,1)S(1)} %collective-permute-done), channel_id=2, replica_groups={{0,128,256,384},{16,144,272,400},{32,160,288,416},{48,176,304,432},{64,..., dimensions={0}, use_global_device_ids=true | all-gather | bytes 1146880 | tf_op jit(solution)/shard_map/all_gather | solution.py:155
  57.6 3.1 %collective-permute-start.4 = (bf16[4,224,512]{2,1,0:T(8,128)(2,1)S(1)}, bf16[4,224,512]{2,1,0:T(8,128)(2,1)S(1)}, u32[]{:S(2)}, u32[]{:S(2)}) collective-permute-start(bf16[4,224,512]{2,1,0:T(8,128)(2,1)S(1)} %bitcast.160), channel_id=1, source_target_pairs={{0,32},{16,48},{32,64},{48,80},{64,96},{80,112},{96,0},{112,16},{1... | collective-permute-start | bytes 2752520 | tf_op jit(solution)/shard_map/ppermute | solution.py:41
  60.8 3.4 %collective-permute-start.5 = (bf16[4,224,512]{2,1,0:T(8,128)(2,1)S(1)}, bf16[4,224,512]{2,1,0:T(8,128)(2,1)S(1)}, u32[]{:S(2)}, u32[]{:S(2)}) collective-permute-start(bf16[4,224,512]{2,1,0:T(8,128)(2,1)S(1)} %bitcast.161), channel_id=1, source_target_pairs={{0,96},{16,112},{32,0},{48,16},{64,32},{80,48},{96,64},{112,80},{1... | collective-permute-start | bytes 2752520 | tf_op jit(solution)/shard_map/ppermute | solution.py:41
  64.7 3.7 %collective-permute-start.2 = (f32[2,256]{1,0:T(2,128)S(1)}, f32[2,256]{1,0:T(2,128)S(1)}, u32[]{:S(2)}, u32[]{:S(2)}) collective-permute-start(f32[2,256]{1,0:T(2,128)S(1)} %pad_maximum_fusion.20), channel_id=1, source_target_pairs={{0,8},{1,9},{2,10},{3,11},{4,12},{5,13},{6,14},{7,15},{8,0},{9,1},... | collective-permute-start | bytes 6152 | tf_op jit(solution)/shard_map/ppermute | solution.py:35
  68.4 22.3 %all_gather.15 = bf16[1792,256]{1,0:T(8,128)(2,1)S(1)} all-gather(bf16[224,256]{1,0:T(8,128)(2,1)S(1)} %slice.388), channel_id=1, replica_groups={{0,1,2,3,4,5,6,7},{8,9,10,11,12,13,14,15},{16,17,18,19,20,21,22,23},{24..., dimensions={0}, use_global_device_ids=true | all-gather | bytes 1032192 | tf_op jit(solution)/shard_map/all_gather | solution.py:157
  90.8 15.3 %collective-permute-start.3 = (f32[2,256]{1,0:T(2,128)S(1)}, f32[2,256]{1,0:T(2,128)S(1)}, u32[]{:S(2)}, u32[]{:S(2)}) collective-permute-start(f32[2,256]{1,0:T(2,128)S(1)} %pad_maximum_fusion.21), channel_id=1, source_target_pairs={{0,16},{16,0},{32,48},{48,32},{64,80},{80,64},{96,112},{112,96},{1... | collective-permute-start | bytes 6152 | tf_op jit(solution)/shard_map/ppermute | solution.py:24
  106.2 0.7 collective-permute-done.3
  106.9 0.5 fusion.6
  109.3 3.3 %collective-permute-start.7 = (bf16[2,224,512]{2,1,0:T(8,128)(2,1)S(1)}, bf16[2,224,512]{2,1,0:T(8,128)(2,1)S(1)}, u32[]{:S(2)}, u32[]{:S(2)}) collective-permute-start(bf16[2,224,512]{2,1,0:T(8,128)(2,1)S(1)} %get-tuple-element.41), channel_id=1, source_target_pairs={{0,96},{16,112},{32,0},{48,16},{64,32},{80,48},{96,64},{112,80},{1... | collective-permute-start | bytes 1376264 | tf_op jit(solution)/shard_map/ppermute | solution.py:41
  112.6 1.9 collective-permute-start.6
  117.0 5.9 %collective-permute-done.7 = bf16[2,224,512]{2,1,0:T(8,128)(2,1)S(1)} collective-permute-done((bf16[2,224,512]{2,1,0:T(8,128)(2,1)S(1)}, bf16[2,224,512]{2,1,0:T(8,128)(2,1)S(1)}, u32[]{:S(2)}, u32[]{:S(2)}) %collective-permute-start.7) | collective-permute-done | bytes 458784 | tf_op jit(solution)/shard_map/ppermute | solution.py:41
  123.3 3.9 %collective-permute-done.6 = bf16[2,224,512]{2,1,0:T(8,128)(2,1)S(1)} collective-permute-done((bf16[2,224,512]{2,1,0:T(8,128)(2,1)S(1)}, bf16[2,224,512]{2,1,0:T(8,128)(2,1)S(1)}, u32[]{:S(2)}, u32[]{:S(2)}) %collective-permute-start.6) | collective-permute-done | bytes 458784 | tf_op jit(solution)/shard_map/ppermute | solution.py:41
  128.3 3.4 %collective-permute-start.8 = (f32[2,136,512]{2,1,0:T(8,128)S(1)}, f32[2,136,512]{2,1,0:T(8,128)S(1)}, u32[]{:S(2)}, u32[]{:S(2)}) collective-permute-start(f32[2,136,512]{2,1,0:T(8,128)S(1)} %pad_maximum_fusion.3), channel_id=1, source_target_pairs={{0,16},{16,0},{32,48},{48,32},{64,80},{80,64},{96,112},{112,96},{1... | collective-permute-start | bytes 1671176 | tf_op jit(solution)/shard_map/ppermute | solution.py:24
  132.1 1.2 collective-permute-done.8
  133.5 5.4 %collective-permute-start.9 = (bf16[144,512]{1,0:T(8,128)(2,1)S(1)}, bf16[144,512]{1,0:T(8,128)(2,1)S(1)}, u32[]{:S(2)}, u32[]{:S(2)}) collective-permute-start(bf16[144,512]{1,0:T(8,128)(2,1)S(1)} %pad_maximum_fusion.15), channel_id=1, source_target_pairs={{0,8},{1,9},{2,10},{3,11},{4,12},{5,13},{6,14},{7,15},{8,0},{9,1},... | collective-permute-start | bytes 442376 | tf_op jit(solution)/shard_map/ppermute | solution.py:35
  139.0 8.5 %collective-permute-done.9 = bf16[144,512]{1,0:T(8,128)(2,1)S(1)} collective-permute-done((bf16[144,512]{1,0:T(8,128)(2,1)S(1)}, bf16[144,512]{1,0:T(8,128)(2,1)S(1)}, u32[]{:S(2)}, u32[]{:S(2)}) %collective-permute-start.9) | collective-permute-done | bytes 147488 | tf_op jit(solution)/shard_map/ppermute | solution.py:35
  149.0 6.1 %collective-permute-start.10 = (bf16[144,512]{1,0:T(8,128)(2,1)S(1)}, bf16[144,512]{1,0:T(8,128)(2,1)S(1)}, u32[]{:S(2)}, u32[]{:S(2)}) collective-permute-start(bf16[144,512]{1,0:T(8,128)(2,1)S(1)} %fusion.43), channel_id=1, source_target_pairs={{0,8},{1,9},{2,10},{3,11},{4,12},{5,13},{6,14},{7,15},{8,0},{9,1},... | collective-permute-start | bytes 442376 | tf_op jit(solution)/shard_map/ppermute | solution.py:35
  155.4 6.8 %collective-permute-done.10 = bf16[144,512]{1,0:T(8,128)(2,1)S(1)} collective-permute-done((bf16[144,512]{1,0:T(8,128)(2,1)S(1)}, bf16[144,512]{1,0:T(8,128)(2,1)S(1)}, u32[]{:S(2)}, u32[]{:S(2)}) %collective-permute-start.10) | collective-permute-done | bytes 147488 | tf_op jit(solution)/shard_map/ppermute | solution.py:35
  162.4 2.5 %collective-permute-start.11 = (bf16[2,144,512]{2,1,0:T(8,128)(2,1)S(1)}, bf16[2,144,512]{2,1,0:T(8,128)(2,1)S(1)}, u32[]{:S(2)}, u32[]{:S(2)}) collective-permute-start(bf16[2,144,512]{2,1,0:T(8,128)(2,1)S(1)} %fusion.23), channel_id=1, source_target_pairs={{0,16},{16,0},{32,48},{48,32},{64,80},{80,64},{96,112},{112,96},{1... | collective-permute-start | bytes 884744 | tf_op jit(solution)/shard_map/ppermute | solution.py:24
  165.3 0.7 collective-permute-done.11
  166.1 0.4 convolution_convert_fusion
  166.5 0.4 convolution_convert_fusion.1
  167.1 2.1 collective-permute-start.12
  169.3 7.7 %collective-permute-done.12 = bf16[4,224,128]{2,1,0:T(8,128)(2,1)S(1)} collective-permute-done((bf16[4,224,128]{2,1,0:T(8,128)(2,1)S(1)}, bf16[4,224,128]{2,1,0:T(8,128)(2,1)S(1)}, u32[]{:S(2)}, u32[]{:S(2)}) %collective-permute-start.12) | collective-permute-done | bytes 229408 | tf_op jit(solution)/shard_map/ppermute | solution.py:41
  177.0 0.7 fusion.39
  177.6 0.7 fusion
  178.3 1.0 pad_maximum_fusion.1
  179.4 3.6 %all-to-all-start = ((bf16[8,240,256]{2,1,0:T(8,128)(2,1)}), bf16[8,240,256]{2,1,0:T(8,128)(2,1)S(1)}, u32[]{:S(2)}, u32[]{:S(2)}) async-start(bf16[8,240,256]{2,1,0:T(8,128)(2,1)} %pad_maximum_fusion.1), calls=%async_computation | async-start | bytes 1966080 | tf_op jit(solution)/shard_map/all_to_all | solution.py:273
  183.0 1.9 collective-permute-start.14
  185.0 3.5 %collective-permute-start.13 = (bf16[4,224,128]{2,1,0:T(8,128)(2,1)S(1)}, bf16[4,224,128]{2,1,0:T(8,128)(2,1)S(1)}, u32[]{:S(2)}, u32[]{:S(2)}) collective-permute-start(bf16[4,224,128]{2,1,0:T(8,128)(2,1)S(1)} %add_convert_fusion.1), channel_id=1, source_target_pairs={{0,32},{16,48},{32,64},{48,80},{64,96},{80,112},{96,0},{112,16},{1... | collective-permute-start | bytes 688136 | tf_op jit(solution)/shard_map/ppermute | solution.py:41
  188.6 0.8 dynamic_slice.87
  189.4 1.2 collective-permute-done.14
  190.6 3.4 %collective-permute-done.13 = bf16[4,224,128]{2,1,0:T(8,128)(2,1)S(1)} collective-permute-done((bf16[4,224,128]{2,1,0:T(8,128)(2,1)S(1)}, bf16[4,224,128]{2,1,0:T(8,128)(2,1)S(1)}, u32[]{:S(2)}, u32[]{:S(2)}) %collective-permute-start.13) | collective-permute-done | bytes 229408 | tf_op jit(solution)/shard_map/ppermute | solution.py:41
  194.1 1.9 collective-permute-start.17
  196.0 0.7 collective-permute-start.16
  196.7 13.9 %all-to-all-done = bf16[8,240,256]{2,1,0:T(8,128)(2,1)S(1)} async-done(((bf16[8,240,256]{2,1,0:T(8,128)(2,1)}), bf16[8,240,256]{2,1,0:T(8,128)(2,1)S(1)}, u32[]{:S(2)}, u32[]{:S(2)}) %all-to-all-start) | async-done | bytes 983072 | tf_op jit(solution)/shard_map/all_to_all | solution.py:273
  210.8 2.5 %collective-permute-start.19 = (bf16[224,128]{1,0:T(8,128)(2,1)S(1)}, bf16[224,128]{1,0:T(8,128)(2,1)S(1)}, u32[]{:S(2)}, u32[]{:S(2)}) collective-permute-start(bf16[224,128]{1,0:T(8,128)(2,1)S(1)} %get-tuple-element.73), channel_id=1, source_target_pairs={{0,136},{1,137},{2,138},{3,139},{4,140},{5,141},{6,142},{7,143},{8... | collective-permute-start | bytes 172040 | tf_op jit(solution)/shard_map/ppermute | solution.py:53
  213.3 6.7 %collective-permute-start.18 = (bf16[224,128]{1,0:T(8,128)(2,1)S(1)}, bf16[224,128]{1,0:T(8,128)(2,1)S(1)}, u32[]{:S(2)}, u32[]{:S(2)}) collective-permute-start(bf16[224,128]{1,0:T(8,128)(2,1)S(1)} %get-tuple-element.72), channel_id=1, source_target_pairs={{0,8},{1,9},{2,10},{3,11},{4,12},{5,13},{6,14},{7,15},{8,264},{9,2... | collective-permute-start | bytes 172040 | tf_op jit(solution)/shard_map/ppermute | solution.py:53
  220.0 3.0 %collective-permute-start.15 = (f32[224,128]{1,0:T(8,128)S(1)}, f32[224,128]{1,0:T(8,128)S(1)}, u32[]{:S(2)}, u32[]{:S(2)}) collective-permute-start(f32[224,128]{1,0:T(8,128)S(1)} %get-tuple-element.68), channel_id=1, source_target_pairs={{0,16},{16,0},{32,48},{48,32},{64,80},{80,64},{96,112},{112,96},{1... | collective-permute-start | bytes 344072 | tf_op jit(solution)/shard_map/ppermute | solution.py:24
  223.0 0.7 add_bitcast_fusion
  223.9 0.8 fusion.56
  (134 shorter events, 11.1 us)
Async XLA Ops:
  1.6 35.2 %collective-permute-start = (bf16[224,512]{1,0:T(8,128)(2,1)S(1)}, bf16[224,512]{1,0:T(8,128)(2,1)S(1)}, u32[]{:S(2)}, u32[]{:S(2)}) collective-permute-start(bf16[224,512]{1,0:T(8,128)(2,1)S(1)} %pad_maximum_fusion.11), channel_id=1, source_target_pairs={{0,0},{1,1},{2,2},{3,3},{4,4},{5,5},{6,6},{7,7},{8,256},{9,257},{1... | collective-permute-start | bytes 688136 | tf_op jit(solution)/shard_map/ppermute | solution.py:53
  3.3 11.6 %collective-permute-start.1 = (bf16[224,256]{1,0:T(8,128)(2,1)S(1)}, bf16[224,256]{1,0:T(8,128)(2,1)S(1)}, u32[]{:S(2)}, u32[]{:S(2)}) collective-permute-start(bf16[224,256]{1,0:T(8,128)(2,1)S(1)} %get-tuple-element.75), channel_id=1, source_target_pairs={{0,16},{16,0},{32,48},{48,32},{64,80},{80,64},{96,112},{112,96},{1... | collective-permute-start | bytes 344072 | tf_op jit(solution)/shard_map/ppermute | solution.py:24
  57.6 50.9 %collective-permute-start.4 = (bf16[4,224,512]{2,1,0:T(8,128)(2,1)S(1)}, bf16[4,224,512]{2,1,0:T(8,128)(2,1)S(1)}, u32[]{:S(2)}, u32[]{:S(2)}) collective-permute-start(bf16[4,224,512]{2,1,0:T(8,128)(2,1)S(1)} %bitcast.160), channel_id=1, source_target_pairs={{0,32},{16,48},{32,64},{48,80},{64,96},{80,112},{96,0},{112,16},{1... | collective-permute-start | bytes 2752520 | tf_op jit(solution)/shard_map/ppermute | solution.py:41
  60.8 47.8 %collective-permute-start.5 = (bf16[4,224,512]{2,1,0:T(8,128)(2,1)S(1)}, bf16[4,224,512]{2,1,0:T(8,128)(2,1)S(1)}, u32[]{:S(2)}, u32[]{:S(2)}) collective-permute-start(bf16[4,224,512]{2,1,0:T(8,128)(2,1)S(1)} %bitcast.161), channel_id=1, source_target_pairs={{0,96},{16,112},{32,0},{48,16},{64,32},{80,48},{96,64},{112,80},{1... | collective-permute-start | bytes 2752520 | tf_op jit(solution)/shard_map/ppermute | solution.py:41
  64.7 26.0 %collective-permute-start.2 = (f32[2,256]{1,0:T(2,128)S(1)}, f32[2,256]{1,0:T(2,128)S(1)}, u32[]{:S(2)}, u32[]{:S(2)}) collective-permute-start(f32[2,256]{1,0:T(2,128)S(1)} %pad_maximum_fusion.20), channel_id=1, source_target_pairs={{0,8},{1,9},{2,10},{3,11},{4,12},{5,13},{6,14},{7,15},{8,0},{9,1},... | collective-permute-start | bytes 6152 | tf_op jit(solution)/shard_map/ppermute | solution.py:35
  90.8 16.1 %collective-permute-start.3 = (f32[2,256]{1,0:T(2,128)S(1)}, f32[2,256]{1,0:T(2,128)S(1)}, u32[]{:S(2)}, u32[]{:S(2)}) collective-permute-start(f32[2,256]{1,0:T(2,128)S(1)} %pad_maximum_fusion.21), channel_id=1, source_target_pairs={{0,16},{16,0},{32,48},{48,32},{64,80},{80,64},{96,112},{112,96},{1... | collective-permute-start | bytes 6152 | tf_op jit(solution)/shard_map/ppermute | solution.py:24
  109.3 13.7 %collective-permute-start.7 = (bf16[2,224,512]{2,1,0:T(8,128)(2,1)S(1)}, bf16[2,224,512]{2,1,0:T(8,128)(2,1)S(1)}, u32[]{:S(2)}, u32[]{:S(2)}) collective-permute-start(bf16[2,224,512]{2,1,0:T(8,128)(2,1)S(1)} %get-tuple-element.41), channel_id=1, source_target_pairs={{0,96},{16,112},{32,0},{48,16},{64,32},{80,48},{96,64},{112,80},{1... | collective-permute-start | bytes 1376264 | tf_op jit(solution)/shard_map/ppermute | solution.py:41
  112.6 14.6 %collective-permute-start.6 = (bf16[2,224,512]{2,1,0:T(8,128)(2,1)S(1)}, bf16[2,224,512]{2,1,0:T(8,128)(2,1)S(1)}, u32[]{:S(2)}, u32[]{:S(2)}) collective-permute-start(bf16[2,224,512]{2,1,0:T(8,128)(2,1)S(1)} %get-tuple-element.42), channel_id=1, source_target_pairs={{0,32},{16,48},{32,64},{48,80},{64,96},{80,112},{96,0},{112,16},{1... | collective-permute-start | bytes 1376264 | tf_op jit(solution)/shard_map/ppermute | solution.py:41
  128.3 5.0 %collective-permute-start.8 = (f32[2,136,512]{2,1,0:T(8,128)S(1)}, f32[2,136,512]{2,1,0:T(8,128)S(1)}, u32[]{:S(2)}, u32[]{:S(2)}) collective-permute-start(f32[2,136,512]{2,1,0:T(8,128)S(1)} %pad_maximum_fusion.3), channel_id=1, source_target_pairs={{0,16},{16,0},{32,48},{48,32},{64,80},{80,64},{96,112},{112,96},{1... | collective-permute-start | bytes 1671176 | tf_op jit(solution)/shard_map/ppermute | solution.py:24
  133.4 14.2 %copy-start.1 = (f32[384]{0:T(512)S(1)}, f32[384]{0:T(512)}, u32[]{:S(2)}) copy-start(f32[384]{0:T(512)} %param.11) | copy-start | bytes 4612
  133.5 14.0 %collective-permute-start.9 = (bf16[144,512]{1,0:T(8,128)(2,1)S(1)}, bf16[144,512]{1,0:T(8,128)(2,1)S(1)}, u32[]{:S(2)}, u32[]{:S(2)}) collective-permute-start(bf16[144,512]{1,0:T(8,128)(2,1)S(1)} %pad_maximum_fusion.15), channel_id=1, source_target_pairs={{0,8},{1,9},{2,10},{3,11},{4,12},{5,13},{6,14},{7,15},{8,0},{9,1},... | collective-permute-start | bytes 442376 | tf_op jit(solution)/shard_map/ppermute | solution.py:35
  149.0 13.2 %collective-permute-start.10 = (bf16[144,512]{1,0:T(8,128)(2,1)S(1)}, bf16[144,512]{1,0:T(8,128)(2,1)S(1)}, u32[]{:S(2)}, u32[]{:S(2)}) collective-permute-start(bf16[144,512]{1,0:T(8,128)(2,1)S(1)} %fusion.43), channel_id=1, source_target_pairs={{0,8},{1,9},{2,10},{3,11},{4,12},{5,13},{6,14},{7,15},{8,0},{9,1},... | collective-permute-start | bytes 442376 | tf_op jit(solution)/shard_map/ppermute | solution.py:35
  162.4 3.7 %collective-permute-start.11 = (bf16[2,144,512]{2,1,0:T(8,128)(2,1)S(1)}, bf16[2,144,512]{2,1,0:T(8,128)(2,1)S(1)}, u32[]{:S(2)}, u32[]{:S(2)}) collective-permute-start(bf16[2,144,512]{2,1,0:T(8,128)(2,1)S(1)} %fusion.23), channel_id=1, source_target_pairs={{0,16},{16,0},{32,48},{48,32},{64,80},{80,64},{96,112},{112,96},{1... | collective-permute-start | bytes 884744 | tf_op jit(solution)/shard_map/ppermute | solution.py:24
  167.1 9.9 %collective-permute-start.12 = (bf16[4,224,128]{2,1,0:T(8,128)(2,1)S(1)}, bf16[4,224,128]{2,1,0:T(8,128)(2,1)S(1)}, u32[]{:S(2)}, u32[]{:S(2)}) collective-permute-start(bf16[4,224,128]{2,1,0:T(8,128)(2,1)S(1)} %pad_maximum_fusion.13), channel_id=1, source_target_pairs={{0,32},{16,48},{32,64},{48,80},{64,96},{80,112},{96,0},{112,16},{1... | collective-permute-start | bytes 688136 | tf_op jit(solution)/shard_map/ppermute | solution.py:41
  179.4 31.3 %all-to-all-start = ((bf16[8,240,256]{2,1,0:T(8,128)(2,1)}), bf16[8,240,256]{2,1,0:T(8,128)(2,1)S(1)}, u32[]{:S(2)}, u32[]{:S(2)}) async-start(bf16[8,240,256]{2,1,0:T(8,128)(2,1)} %pad_maximum_fusion.1), calls=%async_computation | async-start | bytes 1966080 | tf_op jit(solution)/shard_map/all_to_all | solution.py:273
  183.0 7.7 %collective-permute-start.14 = (bf16[4,224,128]{2,1,0:T(8,128)(2,1)S(1)}, bf16[4,224,128]{2,1,0:T(8,128)(2,1)S(1)}, u32[]{:S(2)}, u32[]{:S(2)}) collective-permute-start(bf16[4,224,128]{2,1,0:T(8,128)(2,1)S(1)} %pad_maximum_fusion.14), channel_id=1, source_target_pairs={{0,96},{16,112},{32,0},{48,16},{64,32},{80,48},{96,64},{112,80},{1... | collective-permute-start | bytes 688136 | tf_op jit(solution)/shard_map/ppermute | solution.py:41
  185.0 39.0 %copy-start = (bf16[128,448]{0,1:T(8,128)(2,1)S(1)}, bf16[128,448]{0,1:T(8,128)(2,1)}, u32[]{:S(2)}) copy-start(bf16[128,448]{0,1:T(8,128)(2,1)} %param.7) | copy-start | bytes 344068
  185.0 9.0 %collective-permute-start.13 = (bf16[4,224,128]{2,1,0:T(8,128)(2,1)S(1)}, bf16[4,224,128]{2,1,0:T(8,128)(2,1)S(1)}, u32[]{:S(2)}, u32[]{:S(2)}) collective-permute-start(bf16[4,224,128]{2,1,0:T(8,128)(2,1)S(1)} %add_convert_fusion.1), channel_id=1, source_target_pairs={{0,32},{16,48},{32,64},{48,80},{64,96},{80,112},{96,0},{112,16},{1... | collective-permute-start | bytes 688136 | tf_op jit(solution)/shard_map/ppermute | solution.py:41
  194.1 28.9 %collective-permute-start.17 = (bf16[224,128]{1,0:T(8,128)(2,1)S(1)}, bf16[224,128]{1,0:T(8,128)(2,1)S(1)}, u32[]{:S(2)}, u32[]{:S(2)}) collective-permute-start(bf16[224,128]{1,0:T(8,128)(2,1)S(1)} %get-tuple-element.71), channel_id=1, source_target_pairs={{0,128},{1,129},{2,130},{3,131},{4,132},{5,133},{6,134},{7,135},{8... | collective-permute-start | bytes 172040 | tf_op jit(solution)/shard_map/ppermute | solution.py:53
  196.0 27.0 %collective-permute-start.16 = (bf16[224,128]{1,0:T(8,128)(2,1)S(1)}, bf16[224,128]{1,0:T(8,128)(2,1)S(1)}, u32[]{:S(2)}, u32[]{:S(2)}) collective-permute-start(bf16[224,128]{1,0:T(8,128)(2,1)S(1)} %get-tuple-element.70), channel_id=1, source_target_pairs={{0,0},{1,1},{2,2},{3,3},{4,4},{5,5},{6,6},{7,7},{8,256},{9,257},{1... | collective-permute-start | bytes 172040 | tf_op jit(solution)/shard_map/ppermute | solution.py:53
  210.8 12.2 %collective-permute-start.19 = (bf16[224,128]{1,0:T(8,128)(2,1)S(1)}, bf16[224,128]{1,0:T(8,128)(2,1)S(1)}, u32[]{:S(2)}, u32[]{:S(2)}) collective-permute-start(bf16[224,128]{1,0:T(8,128)(2,1)S(1)} %get-tuple-element.73), channel_id=1, source_target_pairs={{0,136},{1,137},{2,138},{3,139},{4,140},{5,141},{6,142},{7,143},{8... | collective-permute-start | bytes 172040 | tf_op jit(solution)/shard_map/ppermute | solution.py:53
  213.3 9.7 %collective-permute-start.18 = (bf16[224,128]{1,0:T(8,128)(2,1)S(1)}, bf16[224,128]{1,0:T(8,128)(2,1)S(1)}, u32[]{:S(2)}, u32[]{:S(2)}) collective-permute-start(bf16[224,128]{1,0:T(8,128)(2,1)S(1)} %get-tuple-element.72), channel_id=1, source_target_pairs={{0,8},{1,9},{2,10},{3,11},{4,12},{5,13},{6,14},{7,15},{8,264},{9,2... | collective-permute-start | bytes 172040 | tf_op jit(solution)/shard_map/ppermute | solution.py:53
  220.0 3.9 %collective-permute-start.15 = (f32[224,128]{1,0:T(8,128)S(1)}, f32[224,128]{1,0:T(8,128)S(1)}, u32[]{:S(2)}, u32[]{:S(2)}) collective-permute-start(f32[224,128]{1,0:T(8,128)S(1)} %get-tuple-element.68), channel_id=1, source_target_pairs={{0,16},{16,0},{32,48},{48,32},{64,80},{80,64},{96,112},{112,96},{1... | collective-permute-start | bytes 344072 | tf_op jit(solution)/shard_map/ppermute | solution.py:24

commit v8 on v7

--- a/solution.py
+++ b/solution.py
@@ -41,37 +41,40 @@
     return lax.ppermute(x, "dp", [(i, i - i % row + (i + 2 * step) % row) for i in range(n)])
 
 
-def along_y(x, target):
+def swap_heads(x):
+    n = lax.axis_size("tensor")
+    return lax.ppermute(x, "tensor", [(i, i ^ 1) for i in range(n)])
+
+
+def to_pair(x, step):
     n_dp, n_tensor = lax.axis_size("dp"), lax.axis_size("tensor")
     row = 2 * X_COUNT
     pairs = []
     for d in range(n_dp):
         for t in range(n_tensor):
-            half, place = target(t // Z_COUNT, d // row)
-            to = (place * row + d % row) * n_tensor + half * Z_COUNT + t % Z_COUNT
-            pairs.append((d * n_tensor + t, to))
+            same = d // 2 % 2 == t % 2
+            to, head = (d, t) if same else (d ^ 2, t ^ 1)
+            pairs.append((d * n_tensor + t, (to + row * step) % n_dp * n_tensor + head))
     return lax.ppermute(x, ("dp", "tensor"), pairs)
 
 
-def move_weights(x):
-    return along_y(x, lambda half, place: (place // 2, 2 * half + place % 2))
-
-
-def x_gather(own, place, early):
+def z_gather(pair, place):
+    count = Z_COUNT // 2
+    up, down = shift_z(pair, 2), shift_z(pair, -2)
+    across = jnp.concatenate([shift_z(up[:1], 2), shift_z(down[1:], -2)])
+    line = jnp.stack([down, across, up, pair, down, across, up], axis=1)
+    return lax.dynamic_slice_in_dim(line, count - 1 - place, count, 1)
+
+
+def x_gather(own):
     middle = own.shape[0] // 2
     up, down = shift_x(own, 1), shift_x(own, -1)
-    up, down, early = lax.optimization_barrier((up, down, early))
     across = jnp.concatenate([shift_x(up[:middle], 1), shift_x(down[middle:], -1)])
-    return [own, down, across, up], early
-
-
-def in_order(blocks, place):
-    line = jnp.stack(blocks[1:] + blocks, axis=1)
-    return lax.dynamic_slice_in_dim(line, X_COUNT - 1 - place, X_COUNT, 1)
+    return [own, down, across, up]
 
 
 def ring_scatter_x(part, across):
-    ahead = part(1).astype(f32) + across.astype(f32)
+    ahead = part(1).astype(f32) + shift_x(across, 1).astype(f32)
     up, down = shift_x(ahead.astype(bf16), 1), shift_x(part(-1), -1)
     return part(0).astype(f32) + up.astype(f32) + down.astype(f32)
 
@@ -84,12 +87,7 @@
         if step == count // 2:
             sent, early = lax.optimization_barrier((sent, early))
         one = lax.dynamic_index_in_dim(sent, (place + step) % count, 0, keepdims=False)
-
-        def target(half, place):
-            part = (place + step) % count
-            return part // 2, 2 * half + part % 2
-
-        one = along_y(one, target).astype(f32)
+        one = to_pair(one, step).astype(f32)
         total = one if total is None else total + one
     return total, early
 
@@ -133,13 +131,14 @@
     quarter = Z_COUNT * part
     rank = lax.axis_index("tensor")
     z, far = rank % Z_COUNT, rank // Z_COUNT
+    parity = z % 2
     dp = lax.axis_index("dp")
     core, x, y = dp % 2, dp // 2 % X_COUNT, dp // (2 * X_COUNT)
     lines = groups(lax.axis_size("dp"), lambda i: i % (2 * X_COUNT))
-    rings = groups(n_tensor, lambda i: i // Z_COUNT)
-
-    def by_far(own, other):
-        return jnp.stack([jnp.where(far == 0, own, other), jnp.where(far == 0, other, own)])
+    rings = groups(n_tensor, lambda i: i % 2)
+
+    def pick(condition, pair):
+        return tuple(jnp.where(condition, p, q) for p, q in (pair, pair[::-1]))
 
     hidden_t = hidden_in.T
     acts = jnp.concatenate([hidden_t, out_grad.T], axis=1).reshape(2, part, 2 * SEQ)
@@ -147,18 +146,14 @@
     other = swap_cores(jnp.where(core == 0, acts[1], acts[0]))
     block = jnp.concatenate([mine[:, :SEQ], other[:, :SEQ], mine[:, SEQ:], other[:, SEQ:]], axis=1)
 
-    weight_block = move_weights(jnp.concatenate([w_qkv, w_out.T], axis=1))
-    hidden = lax.all_gather(
-        block[:, : 2 * SEQ], "tensor", axis=0, tiled=True, axis_index_groups=rings
-    )
-    weight_block, hidden = lax.optimization_barrier((weight_block, hidden))
+    weight_block = to_pair(jnp.concatenate([w_qkv, w_out.T], axis=1), 0)
+    pair = jnp.stack(pick(far == 0, (block, swap_far(block))))
+    weight_block, pair = lax.optimization_barrier((weight_block, pair))
     column = lax.all_gather(weight_block, "dp", axis=0, axis_index_groups=lines)
-    column, block = lax.optimization_barrier((column, block))
-    grads = lax.all_gather(
-        block[:, 2 * SEQ :], "tensor", axis=0, tiled=True, axis_index_groups=rings
-    )
-    blocks, grads = x_gather(column, x, grads)
-    hidden = hidden.astype(f32)
+    rows = z_gather(pair, z // 2).reshape(quarter, 4 * SEQ)
+    hidden = rows[:, : 2 * SEQ].astype(f32)
+    grads = rows[:, 2 * SEQ :]
+    blocks = x_gather(column)
     mean_part = jnp.sum(hidden, axis=0) / quarter
     stats = jnp.stack([mean_part, jnp.sum((hidden - mean_part) ** 2, axis=0)])
 
@@ -171,7 +166,7 @@
             ]
         )
 
-    stats = merge(stats, swap_far(stats), quarter)
+    stats = merge(stats, swap_heads(stats), quarter)
     stats_other = swap_cores(stats)
     stats_other = jnp.concatenate([stats_other[:, SEQ:], stats_other[:, :SEQ]], axis=1)
     stats = merge(stats, stats_other, 2 * quarter)
@@ -179,30 +174,25 @@
     inv_std = lax.rsqrt(stats[1] / depth + norm_eps)
 
     def own_part(vector):
-        vector = vector.reshape(2, Z_COUNT, 2, part)
-        vector = jnp.where(far == 0, vector[0], vector[1])
+        vector = vector.reshape(Z_COUNT, 2, 2, part)
+        vector = jnp.where(parity == 0, vector[:, 0], vector[:, 1])
         return jnp.where(core == 0, vector[:, 0], vector[:, 1]).reshape(quarter)
 
     gain, bias = own_part(norm_gain), own_part(norm_bias)
     normed = ((hidden - mean) * inv_std * gain[:, None] + bias[:, None]).astype(bf16)
     vectors = jnp.stack([*split(gain), *split(bias)] + [jnp.zeros_like(gain, bf16)] * 4)
-    left = jnp.concatenate([normed, vectors.T], axis=1).reshape(2, X_COUNT, part, 2 * SEQ + 8)
-    right = grads.reshape(2, X_COUNT, part, 2 * SEQ)
-
-    def own_head(pair):
-        return jnp.where(far == 0, pair[0], pair[1]), jnp.where(far == 0, pair[1], pair[0])
+    left = jnp.concatenate([normed, vectors.T], axis=1)
+    left = left.reshape(4, 2, part, 2 * SEQ + 8)
+    right = grads.reshape(4, 2, part, 2 * SEQ)
 
     joined_parts, grad_parts = [0.0, 0.0], [0.0, 0.0]
     for step in (0, 3, 1, 2):
-        place = (x + step) % X_COUNT
-        left_part = lax.dynamic_index_in_dim(left, place, 1, keepdims=False)
-        right_part = lax.dynamic_index_in_dim(right, place, 1, keepdims=False)
-        left_part = left_part.reshape(2 * part, 2 * SEQ + 8)
-        right_part = right_part.reshape(2 * part, 2 * SEQ)
-        for h in range(2):
-            weight = blocks[step][2 * h : 2 * h + 2].reshape(2 * part, 4 * E)
-            joined_parts[h] += dot(left_part, weight[:, : 3 * E], ((0,), (0,)))
-            grad_parts[h] += dot(right_part, weight[:, 3 * E :], ((0,), (0,)))
+        half = (x + step) % X_COUNT // 2
+        left_part = jnp.where(half == 0, left[:, 0], left[:, 1]).reshape(quarter // 2, -1)
+        right_part = jnp.where(half == 0, right[:, 0], right[:, 1]).reshape(quarter // 2, -1)
+        weight = blocks[step].reshape(quarter // 2, 4 * E)
+        joined_parts[step % 2] += dot(left_part, weight[:, : 3 * E], ((0,), (0,)))
+        grad_parts[step % 2] += dot(right_part, weight[:, 3 * E :], ((0,), (0,)))
     parts = []
     for j, g in zip(joined_parts, grad_parts):
         v = j[2 * SEQ :]
@@ -210,9 +200,10 @@
         parts.append((jnp.concatenate([j[: 2 * SEQ], g], axis=1), jnp.pad(v, ((0, 6), (0, E)))))
     sent = jnp.stack([jnp.concatenate([p[SEQ:], v]) for p, v in parts])
     kept = jnp.stack([jnp.concatenate([p[:SEQ], v]) for p, v in parts])
-    own, away = own_head(kept + swap_cores(sent))
+    own_first = x % 2 == parity
+    own, away = pick(own_first, tuple(kept + swap_cores(sent)))
     away_high, away_low = split(away[SEQ:])
-    away = swap_far(jnp.concatenate([away[:SEQ].astype(bf16), away_high, away_low]))
+    away = swap_heads(jnp.concatenate([away[:SEQ].astype(bf16), away_high, away_low]))
     away = away.astype(f32)
     vector = own[SEQ:] + away[SEQ : SEQ + 8] + away[SEQ + 8 :]
     gain_weight, bias_weight = vector[0, : 3 * E], vector[1, : 3 * E]
@@ -241,33 +232,38 @@
 
     packed = jnp.pad(pack(sums), ((0, 0), (0, 3 * E)))
     result = jnp.concatenate([jnp.concatenate([context, joined_grad], axis=1), packed])
-    result_far = swap_far(result)
-    sums = sums + unpack(result_far[SEQ:, :SEQ])
-    heads = by_far(result[:SEQ], result_far[:SEQ])
+    result_pair = swap_heads(result)
+    sums = sums + unpack(result_pair[SEQ:, :SEQ])
+    heads = jnp.stack(pick(own_first, (result[:SEQ], result_pair[:SEQ])))
     packed = jnp.pad(pack(sums), ((0, 0), (0, 3 * E)))
     heads_sent = jnp.concatenate([heads, jnp.stack([packed, jnp.zeros_like(packed)])], axis=1)
     heads_other = swap_cores(heads_sent)
     sums = jnp.concatenate([sums, unpack(heads_other[0, SEQ:, :SEQ])], axis=1)
     heads = jnp.concatenate([heads, heads_other[:, :SEQ]], axis=1)
 
-    joined_weight = in_order([b[:, :, : 3 * E] for b in blocks], x).reshape(2, quarter, 3 * E)
     weight_parts = [
-        dot(grads, heads[h, :, :E], ((1,), (0,))).astype(bf16).reshape(2, X_COUNT, part, E)
+        dot(grads, heads[h, :, :E], ((1,), (0,))).astype(bf16).reshape(4, 2, part, E)
         for h in range(2)
     ]
 
     def weight_to(step):
-        place = (x + step) % X_COUNT
-        return jnp.concatenate(
-            [lax.dynamic_index_in_dim(w, place, 1, keepdims=False) for w in weight_parts]
-        )
-
-    across = shift_x(weight_to(2), 1)
-    across, heads = lax.optimization_barrier((across, heads))
-
-    group_part = sum(
-        dot(joined_weight[h], heads[h, :, E:], ((1,), (1,))) for h in range(2)
-    ).astype(bf16)
+        pair = weight_parts[step % 2]
+        return jnp.where((x + step) % X_COUNT // 2 == 0, pair[:, 0], pair[:, 1])
+
+    across, heads = lax.optimization_barrier((weight_to(2), heads))
+
+    near, away = pick(x % 2 == 0, (blocks[1][:, :, : 3 * E], blocks[3][:, :, : 3 * E]))
+
+    def group_product(first, second):
+        return sum(
+            dot(w.reshape(quarter // 2, 3 * E), heads[h, :, E:], ((1,), (1,)))
+            for h, w in enumerate((first[:, :, : 3 * E], second))
+        ).astype(bf16).reshape(4, part, 2 * SEQ)
+
+    group_part = pick(
+        x // 2 == 0, (group_product(blocks[0], near), group_product(blocks[2], away))
+    )
+    group_part = jnp.stack(group_part, axis=1)
     extra = jnp.broadcast_to(pack(sums)[None], (Z_COUNT, 16, 2 * SEQ))
     payload = jnp.concatenate([group_part.reshape(Z_COUNT, part, 2 * SEQ), extra], axis=1)
     group_parts = lax.all_to_all(payload, "tensor", 0, 0, tiled=True, axis_index_groups=rings)

time: 226 us -> 208 us (0.920)
  the two profiles are of different devices: /device:TPU:1 before, /device:TPU:63 now
where the time goes in v8:
time: 208 us; the launch traced here: 207 us
  starting transfers between devices  111 us (53%)
  waiting for transfers between devices  48.5 us (23%)
  blocking collectives  18 us (9%)
  other arithmetic  14.1 us (7%)
  matrix products  6.68 us (3%)
  local copies, waits for them, and re-layouts  6.34 us (3%)
  between operations  2.18 us (1%)
    ppermute x5, starting transfers between devices, to_pair(): return lax.ppermute(x, ('dp', 'tensor'), pairs)  27.9 us
    ppermute x5, starting transfers between devices, swap_cores(): return lax.ppermute(x, 'dp', [(i, i ^ 1) for i in range(n)])  23.7 us
    ppermute x7, starting transfers between devices, shift_x(): lax.ppermute(x, 'dp', [(i, i - i % row + (i + 2 * step) % row) for i in r...  20.6 us
    ppermute x4, starting transfers between devices, shift_z(): return lax.ppermute(x, 'tensor', pairs)  18.5 us
    all_gather x1, blocking collectives, body(): column = lax.all_gather(weight_block, 'dp', axis=0, axis_index_groups=lines)  18 us
    ppermute x7, waiting for transfers between devices, shift_x(): lax.ppermute(x, 'dp', [(i, i - i % row + (i + 2 * step) % row) for i in r...  17 us
    ppermute x1, waiting for transfers between devices, swap_far(): return lax.ppermute(x, 'tensor', [(i, (i + Z_COUNT) % n) for i in range(n)])  13.2 us
    ppermute x3, waiting for transfers between devices, swap_heads(): return lax.ppermute(x, 'tensor', [(i, i ^ 1) for i in range(n)])  8.73 us
  transfers between devices with their start and end apart: 26, of which 13 were waited for; matrix products, arithmetic and copies ran while one was open for 7% of the time, Pallas kernels for 0%

profile of v8, /device:TPU:63, one launch (start us, length us, event | category | flops | bytes accessed | tf_op | source)
XLA Modules:
  0.0 206.7 jit_solution(16421103129644725555)
XLA Ops:
  0.6 1.0 pad_maximum_fusion.12
  1.6 4.3 %collective-permute-start = (bf16[224,512]{1,0:T(8,128)(2,1)S(1)}, bf16[224,512]{1,0:T(8,128)(2,1)S(1)}, u32[]{:S(2)}, u32[]{:S(2)}) collective-permute-start(bf16[224,512]{1,0:T(8,128)(2,1)S(1)} %pad_maximum_fusion.12), channel_id=1, source_target_pairs={{0,0},{1,32},{2,2},{3,34},{4,4},{5,36},{6,6},{7,38},{8,8},{9,40},{... | collective-permute-start | bytes 688136 | tf_op jit(solution)/shard_map/ppermute | solution.py:58
  5.9 1.0 broadcast_select_fusion.13
  6.9 2.9 %collective-permute-start.1 = (bf16[224,256]{1,0:T(8,128)(2,1)S(1)}, bf16[224,256]{1,0:T(8,128)(2,1)S(1)}, u32[]{:S(2)}, u32[]{:S(2)}) collective-permute-start(bf16[224,256]{1,0:T(8,128)(2,1)S(1)} %get-tuple-element.55), channel_id=1, source_target_pairs={{0,16},{16,0},{32,48},{48,32},{64,80},{80,64},{96,112},{112,96},{1... | collective-permute-start | bytes 344072 | tf_op jit(solution)/shard_map/ppermute | solution.py:24
  11.9 4.4 %collective-permute-start.2 = (bf16[224,512]{1,0:T(8,128)(2,1)S(1)}, bf16[224,512]{1,0:T(8,128)(2,1)S(1)}, u32[]{:S(2)}, u32[]{:S(2)}) collective-permute-start(bf16[224,512]{1,0:T(8,128)(2,1)S(1)} %pad_maximum_fusion.13), channel_id=1, source_target_pairs={{0,8},{1,9},{2,10},{3,11},{4,12},{5,13},{6,14},{7,15},{8,0},{9,1},... | collective-permute-start | bytes 688136 | tf_op jit(solution)/shard_map/ppermute | solution.py:35
  16.4 13.2 %collective-permute-done.2 = bf16[224,512]{1,0:T(8,128)(2,1)S(1)} collective-permute-done((bf16[224,512]{1,0:T(8,128)(2,1)S(1)}, bf16[224,512]{1,0:T(8,128)(2,1)S(1)}, u32[]{:S(2)}, u32[]{:S(2)}) %collective-permute-start.2) | collective-permute-done | bytes 229408 | tf_op jit(solution)/shard_map/ppermute | solution.py:35
  29.7 9.8 %collective-permute-start.3 = (bf16[2,224,512]{2,1,0:T(8,128)(2,1)S(1)}, bf16[2,224,512]{2,1,0:T(8,128)(2,1)S(1)}, u32[]{:S(2)}, u32[]{:S(2)}) collective-permute-start(bf16[2,224,512]{2,1,0:T(8,128)(2,1)S(1)} %pad_maximum_fusion.5), channel_id=1, source_target_pairs={{0,6},{1,7},{2,0},{3,1},{4,2},{5,3},{6,4},{7,5},{8,14},{9,15},{10,... | collective-permute-start | bytes 1376264 | tf_op jit(solution)/shard_map/ppermute | solution.py:30
  39.5 1.9 collective-permute-start.4
  42.2 18.0 %all-gather = bf16[896,512]{1,0:T(8,128)(2,1)S(1)} all-gather(bf16[224,512]{1,0:T(8,128)(2,1)S(1)} %collective-permute-done), channel_id=2, replica_groups={{0,128,256,384},{16,144,272,400},{32,160,288,416},{48,176,304,432},{64,..., dimensions={0}, use_global_device_ids=true | all-gather | bytes 1146880 | tf_op jit(solution)/shard_map/all_gather | solution.py:152
  60.1 1.9 collective-permute-start.11
  62.0 4.6 %collective-permute-start.9 = (bf16[4,224,512]{2,1,0:T(8,128)(2,1)S(1)}, bf16[4,224,512]{2,1,0:T(8,128)(2,1)S(1)}, u32[]{:S(2)}, u32[]{:S(2)}) collective-permute-start(bf16[4,224,512]{2,1,0:T(8,128)(2,1)S(1)} %bitcast.215), channel_id=1, source_target_pairs={{0,32},{16,48},{32,64},{48,80},{64,96},{80,112},{96,0},{112,16},{1... | collective-permute-start | bytes 2752520 | tf_op jit(solution)/shard_map/ppermute | solution.py:41
  66.7 4.9 %collective-permute-start.6 = (bf16[1,224,512]{2,1,0:T(8,128)(2,1)S(1)}, bf16[1,224,512]{2,1,0:T(8,128)(2,1)S(1)}, u32[]{:S(2)}, u32[]{:S(2)}) collective-permute-start(bf16[1,224,512]{2,1,0:T(8,128)(2,1)S(1)} %slice.438), channel_id=1, source_target_pairs={{0,6},{1,7},{2,0},{3,1},{4,2},{5,3},{6,4},{7,5},{8,14},{9,15},{10,... | collective-permute-start | bytes 688136 | tf_op jit(solution)/shard_map/ppermute | solution.py:30
  71.6 1.9 collective-permute-start.5
  73.6 1.9 collective-permute-done.6
  75.5 5.1 %collective-permute-done.5 = bf16[1,224,512]{2,1,0:T(8,128)(2,1)S(1)} collective-permute-done((bf16[1,224,512]{2,1,0:T(8,128)(2,1)S(1)}, bf16[1,224,512]{2,1,0:T(8,128)(2,1)S(1)}, u32[]{:S(2)}, u32[]{:S(2)}) %collective-permute-start.5) | collective-permute-done | bytes 229408 | tf_op jit(solution)/shard_map/ppermute | solution.py:30
  81.7 1.9 collective-permute-start.7
  83.7 2.6 %collective-permute-done.7 = f32[2,256]{1,0:T(2,128)S(1)} collective-permute-done((f32[2,256]{1,0:T(2,128)S(1)}, f32[2,256]{1,0:T(2,128)S(1)}, u32[]{:S(2)}, u32[]{:S(2)}) %collective-permute-start.7) | collective-permute-done | bytes 2080 | tf_op jit(solution)/shard_map/ppermute | solution.py:46
  86.3 9.1 %collective-permute-start.8 = (f32[2,256]{1,0:T(2,128)S(1)}, f32[2,256]{1,0:T(2,128)S(1)}, u32[]{:S(2)}, u32[]{:S(2)}) collective-permute-start(f32[2,256]{1,0:T(2,128)S(1)} %pad_maximum_fusion.19), channel_id=1, source_target_pairs={{0,16},{16,0},{32,48},{48,32},{64,80},{80,64},{96,112},{112,96},{1... | collective-permute-start | bytes 6152 | tf_op jit(solution)/shard_map/ppermute | solution.py:24
  96.2 1.1 fusion.5
  99.1 2.5 %collective-permute-start.10 = (bf16[2,224,512]{2,1,0:T(8,128)(2,1)S(1)}, bf16[2,224,512]{2,1,0:T(8,128)(2,1)S(1)}, u32[]{:S(2)}, u32[]{:S(2)}) collective-permute-start(bf16[2,224,512]{2,1,0:T(8,128)(2,1)S(1)} %slice.458), channel_id=1, source_target_pairs={{0,32},{16,48},{32,64},{48,80},{64,96},{80,112},{96,0},{112,16},{1... | collective-permute-start | bytes 1376264 | tf_op jit(solution)/shard_map/ppermute | solution.py:41
  101.7 2.8 %collective-permute-start.12 = (bf16[2,224,512]{2,1,0:T(8,128)(2,1)S(1)}, bf16[2,224,512]{2,1,0:T(8,128)(2,1)S(1)}, u32[]{:S(2)}, u32[]{:S(2)}) collective-permute-start(bf16[2,224,512]{2,1,0:T(8,128)(2,1)S(1)} %slice.459), channel_id=1, source_target_pairs={{0,96},{16,112},{32,0},{48,16},{64,32},{80,48},{96,64},{112,80},{1... | collective-permute-start | bytes 1376264 | tf_op jit(solution)/shard_map/ppermute | solution.py:41
  105.4 7.3 %collective-permute-done.10 = bf16[2,224,512]{2,1,0:T(8,128)(2,1)S(1)} collective-permute-done((bf16[2,224,512]{2,1,0:T(8,128)(2,1)S(1)}, bf16[2,224,512]{2,1,0:T(8,128)(2,1)S(1)}, u32[]{:S(2)}, u32[]{:S(2)}) %collective-permute-start.10) | collective-permute-done | bytes 458784 | tf_op jit(solution)/shard_map/ppermute | solution.py:41
  112.8 3.4 %collective-permute-done.12 = bf16[2,224,512]{2,1,0:T(8,128)(2,1)S(1)} collective-permute-done((bf16[2,224,512]{2,1,0:T(8,128)(2,1)S(1)}, bf16[2,224,512]{2,1,0:T(8,128)(2,1)S(1)}, u32[]{:S(2)}, u32[]{:S(2)}) %collective-permute-start.12) | collective-permute-done | bytes 458784 | tf_op jit(solution)/shard_map/ppermute | solution.py:41
  117.3 0.9 pad_maximum_fusion.3
  118.2 3.4 %collective-permute-start.13 = (f32[2,136,512]{2,1,0:T(8,128)}, f32[2,136,512]{2,1,0:T(8,128)}, u32[]{:S(2)}, u32[]{:S(2)}) collective-permute-start(f32[2,136,512]{2,1,0:T(8,128)} %pad_maximum_fusion.3), channel_id=1, source_target_pairs={{0,16},{16,0},{32,48},{48,32},{64,80},{80,64},{96,112},{112,96},{1... | collective-permute-start | bytes 1671176 | tf_op jit(solution)/shard_map/ppermute | solution.py:24
  121.6 1.9 collective-permute-done.13
  123.5 1.2 maximum_add_fusion
  124.7 3.5 %collective-permute-start.14 = (bf16[144,512]{1,0:T(8,128)(2,1)S(1)}, bf16[144,512]{1,0:T(8,128)(2,1)S(1)}, u32[]{:S(2)}, u32[]{:S(2)}) collective-permute-start(bf16[144,512]{1,0:T(8,128)(2,1)S(1)} %pad_maximum_fusion.14), channel_id=1, source_target_pairs={{0,1},{1,0},{2,3},{3,2},{4,5},{5,4},{6,7},{7,6},{8,9},{9,8},{10,11... | collective-permute-start | bytes 442376 | tf_op jit(solution)/shard_map/ppermute | solution.py:46
  128.3 3.6 %collective-permute-done.14 = bf16[144,512]{1,0:T(8,128)(2,1)S(1)} collective-permute-done((bf16[144,512]{1,0:T(8,128)(2,1)S(1)}, bf16[144,512]{1,0:T(8,128)(2,1)S(1)}, u32[]{:S(2)}, u32[]{:S(2)}) %collective-permute-start.14) | collective-permute-done | bytes 147488 | tf_op jit(solution)/shard_map/ppermute | solution.py:46
  133.4 3.3 %collective-permute-start.15 = (bf16[144,512]{1,0:T(8,128)(2,1)S(1)}, bf16[144,512]{1,0:T(8,128)(2,1)S(1)}, u32[]{:S(2)}, u32[]{:S(2)}) collective-permute-start(bf16[144,512]{1,0:T(8,128)(2,1)S(1)} %fusion.54), channel_id=1, source_target_pairs={{0,1},{1,0},{2,3},{3,2},{4,5},{5,4},{6,7},{7,6},{8,9},{9,8},{10,11... | collective-permute-start | bytes 442376 | tf_op jit(solution)/shard_map/ppermute | solution.py:46
  136.7 2.6 %collective-permute-done.15 = bf16[144,512]{1,0:T(8,128)(2,1)S(1)} collective-permute-done((bf16[144,512]{1,0:T(8,128)(2,1)S(1)}, bf16[144,512]{1,0:T(8,128)(2,1)S(1)}, u32[]{:S(2)}, u32[]{:S(2)}) %collective-permute-start.15) | collective-permute-done | bytes 147488 | tf_op jit(solution)/shard_map/ppermute | solution.py:46
  139.5 4.2 %collective-permute-start.16 = (bf16[2,144,512]{2,1,0:T(8,128)(2,1)S(1)}, bf16[2,144,512]{2,1,0:T(8,128)(2,1)}, u32[]{:S(2)}, u32[]{:S(2)}) collective-permute-start(bf16[2,144,512]{2,1,0:T(8,128)(2,1)S(1)} %fusion.22), channel_id=1, source_target_pairs={{0,16},{16,0},{32,48},{48,32},{64,80},{80,64},{96,112},{112,96},{1... | collective-permute-start | bytes 884744 | tf_op jit(solution)/shard_map/ppermute | solution.py:24
  143.7 1.2 slice.508
  145.0 1.2 broadcast_select_fusion.1
  146.3 1.0 slice.501
  147.3 0.9 pad_maximum_fusion.4
  152.0 1.0 pad_maximum_fusion.1
  153.1 7.1 %all-to-all-start = ((bf16[8,240,256]{2,1,0:T(8,128)(2,1)}), bf16[8,240,256]{2,1,0:T(8,128)(2,1)S(1)}, u32[]{:S(2)}, u32[]{:S(2)}) async-start(bf16[8,240,256]{2,1,0:T(8,128)(2,1)} %pad_maximum_fusion.1), calls=%async_computation | async-start | bytes 1966080 | tf_op jit(solution)/shard_map/all_to_all | solution.py:269
  160.2 2.1 %collective-permute-start.17 = (bf16[4,224,128]{2,1,0:T(8,128)(2,1)}, bf16[4,224,128]{2,1,0:T(8,128)(2,1)S(1)}, u32[]{:S(2)}, u32[]{:S(2)}) collective-permute-start(bf16[4,224,128]{2,1,0:T(8,128)(2,1)} %select_bitcast_fusion.1), channel_id=1, source_target_pairs={{0,32},{16,48},{32,64},{48,80},{64,96},{80,112},{96,0},{112,16},{1... | collective-permute-start | bytes 688136 | tf_op jit(solution)/shard_map/ppermute | solution.py:41
  162.7 3.3 %collective-permute-start.19 = (bf16[4,224,128]{2,1,0:T(8,128)(2,1)S(1)}, bf16[4,224,128]{2,1,0:T(8,128)(2,1)S(1)}, u32[]{:S(2)}, u32[]{:S(2)}) collective-permute-start(bf16[4,224,128]{2,1,0:T(8,128)(2,1)S(1)} %select_bitcast_fusion), channel_id=1, source_target_pairs={{0,96},{16,112},{32,0},{48,16},{64,32},{80,48},{96,64},{112,80},{1... | collective-permute-start | bytes 688136 | tf_op jit(solution)/shard_map/ppermute | solution.py:41
  166.0 2.8 %collective-permute-done.17 = bf16[4,224,128]{2,1,0:T(8,128)(2,1)S(1)} collective-permute-done((bf16[4,224,128]{2,1,0:T(8,128)(2,1)}, bf16[4,224,128]{2,1,0:T(8,128)(2,1)S(1)}, u32[]{:S(2)}, u32[]{:S(2)}) %collective-permute-start.17) | collective-permute-done | bytes 229408 | tf_op jit(solution)/shard_map/ppermute | solution.py:41
  169.0 3.4 %collective-permute-start.18 = (bf16[4,224,128]{2,1,0:T(8,128)(2,1)S(1)}, bf16[4,224,128]{2,1,0:T(8,128)(2,1)S(1)}, u32[]{:S(2)}, u32[]{:S(2)}) collective-permute-start(bf16[4,224,128]{2,1,0:T(8,128)(2,1)S(1)} %fusion.17), channel_id=1, source_target_pairs={{0,32},{16,48},{32,64},{48,80},{64,96},{80,112},{96,0},{112,16},{1... | collective-permute-start | bytes 688136 | tf_op jit(solution)/shard_map/ppermute | solution.py:41
  173.3 3.3 %collective-permute-done.18 = bf16[4,224,128]{2,1,0:T(8,128)(2,1)S(1)} collective-permute-done((bf16[4,224,128]{2,1,0:T(8,128)(2,1)S(1)}, bf16[4,224,128]{2,1,0:T(8,128)(2,1)S(1)}, u32[]{:S(2)}, u32[]{:S(2)}) %collective-permute-start.18) | collective-permute-done | bytes 229408 | tf_op jit(solution)/shard_map/ppermute | solution.py:41
  176.8 3.6 %collective-permute-start.22 = (bf16[224,128]{1,0:T(8,128)(2,1)S(1)}, bf16[224,128]{1,0:T(8,128)(2,1)S(1)}, u32[]{:S(2)}, u32[]{:S(2)}) collective-permute-start(bf16[224,128]{1,0:T(8,128)(2,1)S(1)} %get-tuple-element.51), channel_id=1, source_target_pairs={{0,128},{1,160},{2,130},{3,162},{4,132},{5,164},{6,134},{7,166},{8... | collective-permute-start | bytes 172040 | tf_op jit(solution)/shard_map/ppermute | solution.py:58
  180.4 4.7 %collective-permute-start.21 = (bf16[224,128]{1,0:T(8,128)(2,1)S(1)}, bf16[224,128]{1,0:T(8,128)(2,1)S(1)}, u32[]{:S(2)}, u32[]{:S(2)}) collective-permute-start(bf16[224,128]{1,0:T(8,128)(2,1)S(1)} %get-tuple-element.50), channel_id=1, source_target_pairs={{0,0},{1,32},{2,2},{3,34},{4,4},{5,36},{6,6},{7,38},{8,8},{9,40},{... | collective-permute-start | bytes 172040 | tf_op jit(solution)/shard_map/ppermute | solution.py:58
  185.4 3.9 %collective-permute-start.24 = (bf16[224,128]{1,0:T(8,128)(2,1)S(1)}, bf16[224,128]{1,0:T(8,128)(2,1)S(1)}, u32[]{:S(2)}, u32[]{:S(2)}) collective-permute-start(bf16[224,128]{1,0:T(8,128)(2,1)S(1)} %get-tuple-element.53), channel_id=1, source_target_pairs={{0,384},{1,416},{2,386},{3,418},{4,388},{5,420},{6,390},{7,422},{8... | collective-permute-start | bytes 172040 | tf_op jit(solution)/shard_map/ppermute | solution.py:58
  189.3 11.4 %collective-permute-start.23 = (bf16[224,128]{1,0:T(8,128)(2,1)S(1)}, bf16[224,128]{1,0:T(8,128)(2,1)S(1)}, u32[]{:S(2)}, u32[]{:S(2)}) collective-permute-start(bf16[224,128]{1,0:T(8,128)(2,1)S(1)} %get-tuple-element.52), channel_id=1, source_target_pairs={{0,256},{1,288},{2,258},{3,290},{4,260},{5,292},{6,262},{7,294},{8... | collective-permute-start | bytes 172040 | tf_op jit(solution)/shard_map/ppermute | solution.py:58
  200.8 4.2 %collective-permute-start.20 = (f32[224,128]{1,0:T(8,128)S(1)}, f32[224,128]{1,0:T(8,128)S(1)}, u32[]{:S(2)}, u32[]{:S(2)}) collective-permute-start(f32[224,128]{1,0:T(8,128)S(1)} %get-tuple-element.48), channel_id=1, source_target_pairs={{0,16},{16,0},{32,48},{48,32},{64,80},{80,64},{96,112},{112,96},{1... | collective-permute-start | bytes 344072 | tf_op jit(solution)/shard_map/ppermute | solution.py:24
  (156 shorter events, 17.3 us)
Async XLA Ops:
  1.6 28.1 %collective-permute-start = (bf16[224,512]{1,0:T(8,128)(2,1)S(1)}, bf16[224,512]{1,0:T(8,128)(2,1)S(1)}, u32[]{:S(2)}, u32[]{:S(2)}) collective-permute-start(bf16[224,512]{1,0:T(8,128)(2,1)S(1)} %pad_maximum_fusion.12), channel_id=1, source_target_pairs={{0,0},{1,32},{2,2},{3,34},{4,4},{5,36},{6,6},{7,38},{8,8},{9,40},{... | collective-permute-start | bytes 688136 | tf_op jit(solution)/shard_map/ppermute | solution.py:58
  6.9 4.9 %collective-permute-start.1 = (bf16[224,256]{1,0:T(8,128)(2,1)S(1)}, bf16[224,256]{1,0:T(8,128)(2,1)S(1)}, u32[]{:S(2)}, u32[]{:S(2)}) collective-permute-start(bf16[224,256]{1,0:T(8,128)(2,1)S(1)} %get-tuple-element.55), channel_id=1, source_target_pairs={{0,16},{16,0},{32,48},{48,32},{64,80},{80,64},{96,112},{112,96},{1... | collective-permute-start | bytes 344072 | tf_op jit(solution)/shard_map/ppermute | solution.py:24
  11.9 17.6 %collective-permute-start.2 = (bf16[224,512]{1,0:T(8,128)(2,1)S(1)}, bf16[224,512]{1,0:T(8,128)(2,1)S(1)}, u32[]{:S(2)}, u32[]{:S(2)}) collective-permute-start(bf16[224,512]{1,0:T(8,128)(2,1)S(1)} %pad_maximum_fusion.13), channel_id=1, source_target_pairs={{0,8},{1,9},{2,10},{3,11},{4,12},{5,13},{6,14},{7,15},{8,0},{9,1},... | collective-permute-start | bytes 688136 | tf_op jit(solution)/shard_map/ppermute | solution.py:35
  29.7 36.9 %collective-permute-start.3 = (bf16[2,224,512]{2,1,0:T(8,128)(2,1)S(1)}, bf16[2,224,512]{2,1,0:T(8,128)(2,1)S(1)}, u32[]{:S(2)}, u32[]{:S(2)}) collective-permute-start(bf16[2,224,512]{2,1,0:T(8,128)(2,1)S(1)} %pad_maximum_fusion.5), channel_id=1, source_target_pairs={{0,6},{1,7},{2,0},{3,1},{4,2},{5,3},{6,4},{7,5},{8,14},{9,15},{10,... | collective-permute-start | bytes 1376264 | tf_op jit(solution)/shard_map/ppermute | solution.py:30
  39.5 32.1 %collective-permute-start.4 = (bf16[2,224,512]{2,1,0:T(8,128)(2,1)S(1)}, bf16[2,224,512]{2,1,0:T(8,128)(2,1)S(1)}, u32[]{:S(2)}, u32[]{:S(2)}) collective-permute-start(bf16[2,224,512]{2,1,0:T(8,128)(2,1)S(1)} %pad_maximum_fusion.5), channel_id=1, source_target_pairs={{0,2},{1,3},{2,4},{3,5},{4,6},{5,7},{6,0},{7,1},{8,10},{9,11},{10,... | collective-permute-start | bytes 1376264 | tf_op jit(solution)/shard_map/ppermute | solution.py:30
  60.1 37.6 %copy-start.2 = (bf16[896,512]{1,0:T(8,128)(2,1)}, bf16[896,512]{1,0:T(8,128)(2,1)S(1)}, u32[]{:S(2)}) copy-start(bf16[896,512]{1,0:T(8,128)(2,1)S(1)} %all-gather) | copy-start | bytes 2752516
  60.1 38.1 %collective-permute-start.11 = (bf16[4,224,512]{2,1,0:T(8,128)(2,1)S(1)}, bf16[4,224,512]{2,1,0:T(8,128)(2,1)S(1)}, u32[]{:S(2)}, u32[]{:S(2)}) collective-permute-start(bf16[4,224,512]{2,1,0:T(8,128)(2,1)S(1)} %bitcast.214), channel_id=1, source_target_pairs={{0,96},{16,112},{32,0},{48,16},{64,32},{80,48},{96,64},{112,80},{1... | collective-permute-start | bytes 2752520 | tf_op jit(solution)/shard_map/ppermute | solution.py:41
  62.0 37.0 %collective-permute-start.9 = (bf16[4,224,512]{2,1,0:T(8,128)(2,1)S(1)}, bf16[4,224,512]{2,1,0:T(8,128)(2,1)S(1)}, u32[]{:S(2)}, u32[]{:S(2)}) collective-permute-start(bf16[4,224,512]{2,1,0:T(8,128)(2,1)S(1)} %bitcast.215), channel_id=1, source_target_pairs={{0,32},{16,48},{32,64},{48,80},{64,96},{80,112},{96,0},{112,16},{1... | collective-permute-start | bytes 2752520 | tf_op jit(solution)/shard_map/ppermute | solution.py:41
  66.7 8.8 %collective-permute-start.6 = (bf16[1,224,512]{2,1,0:T(8,128)(2,1)S(1)}, bf16[1,224,512]{2,1,0:T(8,128)(2,1)S(1)}, u32[]{:S(2)}, u32[]{:S(2)}) collective-permute-start(bf16[1,224,512]{2,1,0:T(8,128)(2,1)S(1)} %slice.438), channel_id=1, source_target_pairs={{0,6},{1,7},{2,0},{3,1},{4,2},{5,3},{6,4},{7,5},{8,14},{9,15},{10,... | collective-permute-start | bytes 688136 | tf_op jit(solution)/shard_map/ppermute | solution.py:30
  71.6 9.0 %collective-permute-start.5 = (bf16[1,224,512]{2,1,0:T(8,128)(2,1)S(1)}, bf16[1,224,512]{2,1,0:T(8,128)(2,1)S(1)}, u32[]{:S(2)}, u32[]{:S(2)}) collective-permute-start(bf16[1,224,512]{2,1,0:T(8,128)(2,1)S(1)} %slice.437), channel_id=1, source_target_pairs={{0,2},{1,3},{2,4},{3,5},{4,6},{5,7},{6,0},{7,1},{8,10},{9,11},{10,... | collective-permute-start | bytes 688136 | tf_op jit(solution)/shard_map/ppermute | solution.py:30
  81.7 4.6 %collective-permute-start.7 = (f32[2,256]{1,0:T(2,128)S(1)}, f32[2,256]{1,0:T(2,128)S(1)}, u32[]{:S(2)}, u32[]{:S(2)}) collective-permute-start(f32[2,256]{1,0:T(2,128)S(1)} %pad_maximum_fusion.18), channel_id=1, source_target_pairs={{0,1},{1,0},{2,3},{3,2},{4,5},{5,4},{6,7},{7,6},{8,9},{9,8},{10,11... | collective-permute-start | bytes 6152 | tf_op jit(solution)/shard_map/ppermute | solution.py:46
  86.3 9.9 %collective-permute-start.8 = (f32[2,256]{1,0:T(2,128)S(1)}, f32[2,256]{1,0:T(2,128)S(1)}, u32[]{:S(2)}, u32[]{:S(2)}) collective-permute-start(f32[2,256]{1,0:T(2,128)S(1)} %pad_maximum_fusion.19), channel_id=1, source_target_pairs={{0,16},{16,0},{32,48},{48,32},{64,80},{80,64},{96,112},{112,96},{1... | collective-permute-start | bytes 6152 | tf_op jit(solution)/shard_map/ppermute | solution.py:24
  98.2 3.5 %copy-start.3 = (bf16[4,224,512]{2,1,0:T(8,128)(2,1)}, bf16[4,224,512]{2,1,0:T(8,128)(2,1)S(1)}, u32[]{:S(2)}) copy-start(bf16[4,224,512]{2,1,0:T(8,128)(2,1)S(1)} %collective-permute-done.11) | copy-start | bytes 2752516
  99.1 13.7 %collective-permute-start.10 = (bf16[2,224,512]{2,1,0:T(8,128)(2,1)S(1)}, bf16[2,224,512]{2,1,0:T(8,128)(2,1)S(1)}, u32[]{:S(2)}, u32[]{:S(2)}) collective-permute-start(bf16[2,224,512]{2,1,0:T(8,128)(2,1)S(1)} %slice.458), channel_id=1, source_target_pairs={{0,32},{16,48},{32,64},{48,80},{64,96},{80,112},{96,0},{112,16},{1... | collective-permute-start | bytes 1376264 | tf_op jit(solution)/shard_map/ppermute | solution.py:41
  101.7 14.5 %collective-permute-start.12 = (bf16[2,224,512]{2,1,0:T(8,128)(2,1)S(1)}, bf16[2,224,512]{2,1,0:T(8,128)(2,1)S(1)}, u32[]{:S(2)}, u32[]{:S(2)}) collective-permute-start(bf16[2,224,512]{2,1,0:T(8,128)(2,1)S(1)} %slice.459), channel_id=1, source_target_pairs={{0,96},{16,112},{32,0},{48,16},{64,32},{80,48},{96,64},{112,80},{1... | collective-permute-start | bytes 1376264 | tf_op jit(solution)/shard_map/ppermute | solution.py:41
  116.3 0.9 copy-start
  118.2 5.3 %collective-permute-start.13 = (f32[2,136,512]{2,1,0:T(8,128)}, f32[2,136,512]{2,1,0:T(8,128)}, u32[]{:S(2)}, u32[]{:S(2)}) collective-permute-start(f32[2,136,512]{2,1,0:T(8,128)} %pad_maximum_fusion.3), channel_id=1, source_target_pairs={{0,16},{16,0},{32,48},{48,32},{64,80},{80,64},{96,112},{112,96},{1... | collective-permute-start | bytes 1671176 | tf_op jit(solution)/shard_map/ppermute | solution.py:24
  123.5 8.5 %copy-start.8 = (f32[384]{0:T(512)S(1)}, f32[384]{0:T(512)}, u32[]{:S(2)}) copy-start(f32[384]{0:T(512)} %param.11) | copy-start | bytes 4612
  124.7 7.1 %collective-permute-start.14 = (bf16[144,512]{1,0:T(8,128)(2,1)S(1)}, bf16[144,512]{1,0:T(8,128)(2,1)S(1)}, u32[]{:S(2)}, u32[]{:S(2)}) collective-permute-start(bf16[144,512]{1,0:T(8,128)(2,1)S(1)} %pad_maximum_fusion.14), channel_id=1, source_target_pairs={{0,1},{1,0},{2,3},{3,2},{4,5},{5,4},{6,7},{7,6},{8,9},{9,8},{10,11... | collective-permute-start | bytes 442376 | tf_op jit(solution)/shard_map/ppermute | solution.py:46
  133.4 5.9 %collective-permute-start.15 = (bf16[144,512]{1,0:T(8,128)(2,1)S(1)}, bf16[144,512]{1,0:T(8,128)(2,1)S(1)}, u32[]{:S(2)}, u32[]{:S(2)}) collective-permute-start(bf16[144,512]{1,0:T(8,128)(2,1)S(1)} %fusion.54), channel_id=1, source_target_pairs={{0,1},{1,0},{2,3},{3,2},{4,5},{5,4},{6,7},{7,6},{8,9},{9,8},{10,11... | collective-permute-start | bytes 442376 | tf_op jit(solution)/shard_map/ppermute | solution.py:46
  139.5 6.8 %copy-start.6 = (bf16[1,128,512]{2,1,0:T(8,128)(2,1)}, bf16[1,128,512]{2,1,0:T(8,128)(2,1)S(1)}, u32[]{:S(2)}) copy-start(bf16[1,128,512]{2,1,0:T(8,128)(2,1)S(1)} %get-tuple-element.45) | copy-start | bytes 393220
  139.5 6.8 %collective-permute-start.16 = (bf16[2,144,512]{2,1,0:T(8,128)(2,1)S(1)}, bf16[2,144,512]{2,1,0:T(8,128)(2,1)}, u32[]{:S(2)}, u32[]{:S(2)}) collective-permute-start(bf16[2,144,512]{2,1,0:T(8,128)(2,1)S(1)} %fusion.22), channel_id=1, source_target_pairs={{0,16},{16,0},{32,48},{48,32},{64,80},{80,64},{96,112},{112,96},{1... | collective-permute-start | bytes 884744 | tf_op jit(solution)/shard_map/ppermute | solution.py:24
  143.7 2.5 %copy-start.1 = (bf16[4,224,512]{2,1,0:T(8,128)(2,1)S(1)}, bf16[4,224,512]{2,1,0:T(8,128)(2,1)}, u32[]{:S(2)}) copy-start(bf16[4,224,512]{2,1,0:T(8,128)(2,1)} %copy-done) | copy-start | bytes 2752516
  148.6 1.9 copy-start.4
  153.1 32.1 %all-to-all-start = ((bf16[8,240,256]{2,1,0:T(8,128)(2,1)}), bf16[8,240,256]{2,1,0:T(8,128)(2,1)S(1)}, u32[]{:S(2)}, u32[]{:S(2)}) async-start(bf16[8,240,256]{2,1,0:T(8,128)(2,1)} %pad_maximum_fusion.1), calls=%async_computation | async-start | bytes 1966080 | tf_op jit(solution)/shard_map/all_to_all | solution.py:269
  160.2 8.7 %collective-permute-start.17 = (bf16[4,224,128]{2,1,0:T(8,128)(2,1)}, bf16[4,224,128]{2,1,0:T(8,128)(2,1)S(1)}, u32[]{:S(2)}, u32[]{:S(2)}) collective-permute-start(bf16[4,224,128]{2,1,0:T(8,128)(2,1)} %select_bitcast_fusion.1), channel_id=1, source_target_pairs={{0,32},{16,48},{32,64},{48,80},{64,96},{80,112},{96,0},{112,16},{1... | collective-permute-start | bytes 688136 | tf_op jit(solution)/shard_map/ppermute | solution.py:41
  162.7 14.0 %copy-start.5 = (bf16[1792,128]{1,0:T(8,128)(2,1)S(1)}, bf16[1792,128]{1,0:T(8,128)(2,1)}, u32[]{:S(2)}) copy-start(bf16[1792,128]{1,0:T(8,128)(2,1)} %copy-done.4) | copy-start | bytes 1376260
  162.7 10.6 %collective-permute-start.19 = (bf16[4,224,128]{2,1,0:T(8,128)(2,1)S(1)}, bf16[4,224,128]{2,1,0:T(8,128)(2,1)S(1)}, u32[]{:S(2)}, u32[]{:S(2)}) collective-permute-start(bf16[4,224,128]{2,1,0:T(8,128)(2,1)S(1)} %select_bitcast_fusion), channel_id=1, source_target_pairs={{0,96},{16,112},{32,0},{48,16},{64,32},{80,48},{96,64},{112,80},{1... | collective-permute-start | bytes 688136 | tf_op jit(solution)/shard_map/ppermute | solution.py:41
  169.0 36.9 %copy-start.7 = (bf16[128,448]{0,1:T(8,128)(2,1)S(1)}, bf16[128,448]{0,1:T(8,128)(2,1)}, u32[]{:S(2)}) copy-start(bf16[128,448]{0,1:T(8,128)(2,1)} %param.7) | copy-start | bytes 344068
  169.0 7.7 %collective-permute-start.18 = (bf16[4,224,128]{2,1,0:T(8,128)(2,1)S(1)}, bf16[4,224,128]{2,1,0:T(8,128)(2,1)S(1)}, u32[]{:S(2)}, u32[]{:S(2)}) collective-permute-start(bf16[4,224,128]{2,1,0:T(8,128)(2,1)S(1)} %fusion.17), channel_id=1, source_target_pairs={{0,32},{16,48},{32,64},{48,80},{64,96},{80,112},{96,0},{112,16},{1... | collective-permute-start | bytes 688136 | tf_op jit(solution)/shard_map/ppermute | solution.py:41
  176.8 28.1 %collective-permute-start.22 = (bf16[224,128]{1,0:T(8,128)(2,1)S(1)}, bf16[224,128]{1,0:T(8,128)(2,1)S(1)}, u32[]{:S(2)}, u32[]{:S(2)}) collective-permute-start(bf16[224,128]{1,0:T(8,128)(2,1)S(1)} %get-tuple-element.51), channel_id=1, source_target_pairs={{0,128},{1,160},{2,130},{3,162},{4,132},{5,164},{6,134},{7,166},{8... | collective-permute-start | bytes 172040 | tf_op jit(solution)/shard_map/ppermute | solution.py:58
  180.4 24.5 %collective-permute-start.21 = (bf16[224,128]{1,0:T(8,128)(2,1)S(1)}, bf16[224,128]{1,0:T(8,128)(2,1)S(1)}, u32[]{:S(2)}, u32[]{:S(2)}) collective-permute-start(bf16[224,128]{1,0:T(8,128)(2,1)S(1)} %get-tuple-element.50), channel_id=1, source_target_pairs={{0,0},{1,32},{2,2},{3,34},{4,4},{5,36},{6,6},{7,38},{8,8},{9,40},{... | collective-permute-start | bytes 172040 | tf_op jit(solution)/shard_map/ppermute | solution.py:58
  185.4 19.6 %collective-permute-start.24 = (bf16[224,128]{1,0:T(8,128)(2,1)S(1)}, bf16[224,128]{1,0:T(8,128)(2,1)S(1)}, u32[]{:S(2)}, u32[]{:S(2)}) collective-permute-start(bf16[224,128]{1,0:T(8,128)(2,1)S(1)} %get-tuple-element.53), channel_id=1, source_target_pairs={{0,384},{1,416},{2,386},{3,418},{4,388},{5,420},{6,390},{7,422},{8... | collective-permute-start | bytes 172040 | tf_op jit(solution)/shard_map/ppermute | solution.py:58
  189.3 15.7 %collective-permute-start.23 = (bf16[224,128]{1,0:T(8,128)(2,1)S(1)}, bf16[224,128]{1,0:T(8,128)(2,1)S(1)}, u32[]{:S(2)}, u32[]{:S(2)}) collective-permute-start(bf16[224,128]{1,0:T(8,128)(2,1)S(1)} %get-tuple-element.52), channel_id=1, source_target_pairs={{0,256},{1,288},{2,258},{3,290},{4,260},{5,292},{6,262},{7,294},{8... | collective-permute-start | bytes 172040 | tf_op jit(solution)/shard_map/ppermute | solution.py:58
  200.8 5.1 %collective-permute-start.20 = (f32[224,128]{1,0:T(8,128)S(1)}, f32[224,128]{1,0:T(8,128)S(1)}, u32[]{:S(2)}, u32[]{:S(2)}) collective-permute-start(f32[224,128]{1,0:T(8,128)S(1)} %get-tuple-element.48), channel_id=1, source_target_pairs={{0,16},{16,0},{32,48},{48,32},{64,80},{80,64},{96,112},{112,96},{1... | collective-permute-start | bytes 344072 | tf_op jit(solution)/shard_map/ppermute | solution.py:24

commit v9 on v8

--- a/solution.py
+++ b/solution.py
@@ -58,19 +58,17 @@
     return lax.ppermute(x, ("dp", "tensor"), pairs)
 
 
-def z_gather(pair, place):
+def gather_both(pair, place, column):
+    middle = column.shape[0] // 2
+    x_up, x_down = shift_x(column, 1), shift_x(column, -1)
+    z_up, z_down = shift_z(pair, 2), shift_z(pair, -2)
+    x_up, x_down, z_up, z_down = lax.optimization_barrier((x_up, x_down, z_up, z_down))
+    x_across = jnp.concatenate([shift_x(x_up[:middle], 1), shift_x(x_down[middle:], -1)])
+    z_across = jnp.concatenate([shift_z(z_up[:1], 2), shift_z(z_down[1:], -2)])
     count = Z_COUNT // 2
-    up, down = shift_z(pair, 2), shift_z(pair, -2)
-    across = jnp.concatenate([shift_z(up[:1], 2), shift_z(down[1:], -2)])
-    line = jnp.stack([down, across, up, pair, down, across, up], axis=1)
-    return lax.dynamic_slice_in_dim(line, count - 1 - place, count, 1)
-
-
-def x_gather(own):
-    middle = own.shape[0] // 2
-    up, down = shift_x(own, 1), shift_x(own, -1)
-    across = jnp.concatenate([shift_x(up[:middle], 1), shift_x(down[middle:], -1)])
-    return [own, down, across, up]
+    line = jnp.stack([z_down, z_across, z_up, pair, z_down, z_across, z_up], axis=1)
+    rows = lax.dynamic_slice_in_dim(line, count - 1 - place, count, 1)
+    return rows, [column, x_down, x_across, x_up]
 
 
 def ring_scatter_x(part, across):
@@ -79,17 +77,15 @@
     return part(0).astype(f32) + up.astype(f32) + down.astype(f32)
 
 
-def scatter_y(parts, place, early):
+def scatter_y(parts, place):
     count = parts.shape[0]
     sent = parts.astype(bf16)
     total = None
     for step in range(count):
-        if step == count // 2:
-            sent, early = lax.optimization_barrier((sent, early))
         one = lax.dynamic_index_in_dim(sent, (place + step) % count, 0, keepdims=False)
         one = to_pair(one, step).astype(f32)
         total = one if total is None else total + one
-    return total, early
+    return total
 
 
 def split(x):
@@ -147,31 +143,26 @@
     block = jnp.concatenate([mine[:, :SEQ], other[:, :SEQ], mine[:, SEQ:], other[:, SEQ:]], axis=1)
 
     weight_block = to_pair(jnp.concatenate([w_qkv, w_out.T], axis=1), 0)
+
+    slice_f = hidden_t.astype(f32)
+    mean_part = jnp.mean(slice_f, axis=0)
+    stats = jnp.stack([mean_part, jnp.sum((slice_f - mean_part) ** 2, axis=0)])
+    stats = lax.all_to_all(
+        jnp.broadcast_to(stats[None], (n_tensor, 2, SEQ)), "tensor", 0, 0, tiled=True
+    )
+    weight_block, stats = lax.optimization_barrier((weight_block, stats))
+    column = lax.all_gather(weight_block, "dp", axis=0, axis_index_groups=lines)
+    mean = jnp.mean(stats[:, 0], axis=0)
+    square = jnp.sum(stats[:, 1], axis=0) + width * jnp.sum((stats[:, 0] - mean) ** 2, axis=0)
+    stats = jnp.stack([mean, lax.rsqrt(square / depth + norm_eps)])
+    mean, inv_std = jnp.concatenate([stats, swap_cores(stats)], axis=1)
+
     pair = jnp.stack(pick(far == 0, (block, swap_far(block))))
-    weight_block, pair = lax.optimization_barrier((weight_block, pair))
-    column = lax.all_gather(weight_block, "dp", axis=0, axis_index_groups=lines)
-    rows = z_gather(pair, z // 2).reshape(quarter, 4 * SEQ)
+    column, pair = lax.optimization_barrier((column, pair))
+    rows, blocks = gather_both(pair, z // 2, column)
+    rows = rows.reshape(quarter, 4 * SEQ)
     hidden = rows[:, : 2 * SEQ].astype(f32)
     grads = rows[:, 2 * SEQ :]
-    blocks = x_gather(column)
-    mean_part = jnp.sum(hidden, axis=0) / quarter
-    stats = jnp.stack([mean_part, jnp.sum((hidden - mean_part) ** 2, axis=0)])
-
-    def merge(stats, stats_other, count):
-        gap = stats[0] - stats_other[0]
-        return jnp.stack(
-            [
-                0.5 * (stats[0] + stats_other[0]),
-                stats[1] + stats_other[1] + gap * gap * (count / 2),
-            ]
-        )
-
-    stats = merge(stats, swap_heads(stats), quarter)
-    stats_other = swap_cores(stats)
-    stats_other = jnp.concatenate([stats_other[:, SEQ:], stats_other[:, :SEQ]], axis=1)
-    stats = merge(stats, stats_other, 2 * quarter)
-    mean = stats[0]
-    inv_std = lax.rsqrt(stats[1] / depth + norm_eps)
 
     def own_part(vector):
         vector = vector.reshape(Z_COUNT, 2, 2, part)
@@ -252,24 +243,19 @@
 
     across, heads = lax.optimization_barrier((weight_to(2), heads))
 
-    near, away = pick(x % 2 == 0, (blocks[1][:, :, : 3 * E], blocks[3][:, :, : 3 * E]))
-
-    def group_product(first, second):
-        return sum(
-            dot(w.reshape(quarter // 2, 3 * E), heads[h, :, E:], ((1,), (1,)))
-            for h, w in enumerate((first[:, :, : 3 * E], second))
-        ).astype(bf16).reshape(4, part, 2 * SEQ)
-
-    group_part = pick(
-        x // 2 == 0, (group_product(blocks[0], near), group_product(blocks[2], away))
-    )
-    group_part = jnp.stack(group_part, axis=1)
+    products = [
+        dot(w[:, :, : 3 * E].reshape(quarter // 2, 3 * E), heads[i % 2, :, E:], ((1,), (1,)))
+        for i, w in enumerate(blocks)
+    ]
+    near, away = pick(x % 2 == 0, (products[1], products[3]))
+    group_part = pick(x // 2 == 0, (products[0] + near, products[2] + away))
+    group_part = jnp.stack([g.astype(bf16).reshape(4, part, 2 * SEQ) for g in group_part], axis=1)
     extra = jnp.broadcast_to(pack(sums)[None], (Z_COUNT, 16, 2 * SEQ))
     payload = jnp.concatenate([group_part.reshape(Z_COUNT, part, 2 * SEQ), extra], axis=1)
     group_parts = lax.all_to_all(payload, "tensor", 0, 0, tiled=True, axis_index_groups=rings)
     total = jnp.sum(group_parts.astype(f32), axis=0)
     weight_parts = ring_scatter_x(weight_to, across)
-    grad_out_weight, total = scatter_y(weight_parts, y, total)
+    grad_out_weight = scatter_y(weight_parts, y)
     sums = total[part : part + 2, :SEQ] + total[part + 2 : part + 4, :SEQ]
     total = total[:part]
     total_other = swap_cores(total[:, SEQ:])

time: 208 us -> 215 us (1.034)
  the two profiles are of different devices: /device:TPU:63 before, /device:TPU:59 now
where the time goes in v9:
time: 215 us; the launch traced here: 214 us
  starting transfers between devices  108 us (50%)
  waiting for transfers between devices  43.8 us (20%)
  blocking collectives  25.5 us (12%)
  other arithmetic  15.3 us (7%)
  local copies, waits for them, and re-layouts  10 us (5%)
  matrix products  8.75 us (4%)
  between operations  2.2 us (1%)
    all_gather x1, blocking collectives, body(): column = lax.all_gather(weight_block, 'dp', axis=0, axis_index_groups=lines)  25.5 us
    ppermute x5, starting transfers between devices, swap_cores(): return lax.ppermute(x, 'dp', [(i, i ^ 1) for i in range(n)])  21.9 us
    ppermute x7, starting transfers between devices, shift_x(): lax.ppermute(x, 'dp', [(i, i - i % row + (i + 2 * step) % row) for i in r...  19.6 us
    ppermute x5, starting transfers between devices, to_pair(): return lax.ppermute(x, ('dp', 'tensor'), pairs)  17.9 us
    ppermute x4, waiting for transfers between devices, shift_z(): return lax.ppermute(x, 'tensor', pairs)  15.5 us
    all_to_all x1, starting transfers between devices, body(): lax.all_to_all(jnp.broadcast_to(stats[None], (n_tensor, 2, SEQ)), 'tensor...  15.1 us
    ppermute x4, starting transfers between devices, shift_z(): return lax.ppermute(x, 'tensor', pairs)  14.8 us
    ppermute x7, waiting for transfers between devices, shift_x(): lax.ppermute(x, 'dp', [(i, i - i % row + (i + 2 * step) % row) for i in r...  12.1 us
  transfers between devices with their start and end apart: 26, of which 13 were waited for; matrix products, arithmetic and copies ran while one was open for 10% of the time, Pallas kernels for 0%

profile of v9, /device:TPU:59, one launch (start us, length us, event | category | flops | bytes accessed | tf_op | source)
XLA Modules:
  0.0 213.5 jit_solution(10133085532715453842)
XLA Ops:
  0.6 1.0 broadcast_select_fusion.9
  1.7 2.6 %collective-permute-start.1 = (bf16[224,256]{1,0:T(8,128)(2,1)S(1)}, bf16[224,256]{1,0:T(8,128)(2,1)S(1)}, u32[]{:S(2)}, u32[]{:S(2)}) collective-permute-start(bf16[224,256]{1,0:T(8,128)(2,1)S(1)} %get-tuple-element.57), channel_id=1, source_target_pairs={{0,16},{16,0},{32,48},{48,32},{64,80},{80,64},{96,112},{112,96},{1... | collective-permute-start | bytes 344072 | tf_op jit(solution)/shard_map/ppermute | solution.py:24
  6.8 15.1 %all-to-all-start = ((f32[16,2,128]{2,1,0:T(2,128)}), f32[16,2,128]{2,1,0:T(2,128)S(1)}, u32[]{:S(2)}, u32[]{:S(2)}) async-start(f32[16,2,128]{2,1,0:T(2,128)} %broadcast_in_dim.10), calls=%async_computation | async-start | bytes 32768 | tf_op jit(solution)/shard_map/all_to_all | solution.py:150
  23.0 3.1 %collective-permute-start = (bf16[224,512]{1,0:T(8,128)(2,1)S(1)}, bf16[224,512]{1,0:T(8,128)(2,1)S(1)}, u32[]{:S(2)}, u32[]{:S(2)}) collective-permute-start(bf16[224,512]{1,0:T(8,128)(2,1)S(1)} %pad_maximum_fusion.12), channel_id=1, source_target_pairs={{0,0},{1,32},{2,2},{3,34},{4,4},{5,36},{6,6},{7,38},{8,8},{9,40},{... | collective-permute-start | bytes 688136 | tf_op jit(solution)/shard_map/ppermute | solution.py:58
  28.6 2.2 %collective-permute-start.2 = (bf16[224,512]{1,0:T(8,128)(2,1)S(1)}, bf16[224,512]{1,0:T(8,128)(2,1)S(1)}, u32[]{:S(2)}, u32[]{:S(2)}) collective-permute-start(bf16[224,512]{1,0:T(8,128)(2,1)S(1)} %pad_maximum_fusion.13), channel_id=1, source_target_pairs={{0,8},{1,9},{2,10},{3,11},{4,12},{5,13},{6,14},{7,15},{8,0},{9,1},... | collective-permute-start | bytes 688136 | tf_op jit(solution)/shard_map/ppermute | solution.py:35
  30.8 1.6 collective-permute-done
  32.4 25.5 %all-gather = bf16[896,512]{1,0:T(8,128)(2,1)S(1)} all-gather(bf16[224,512]{1,0:T(8,128)(2,1)S(1)} %collective-permute-done), channel_id=2, replica_groups={{0,128,256,384},{16,144,272,400},{32,160,288,416},{48,176,304,432},{64,..., dimensions={0}, use_global_device_ids=true | all-gather | bytes 1146880 | tf_op jit(solution)/shard_map/all_gather | solution.py:154
  58.0 1.9 collective-permute-start.3
  60.0 3.4 %collective-permute-start.4 = (bf16[4,224,512]{2,1,0:T(8,128)(2,1)S(1)}, bf16[4,224,512]{2,1,0:T(8,128)(2,1)S(1)}, u32[]{:S(2)}, u32[]{:S(2)}) collective-permute-start(bf16[4,224,512]{2,1,0:T(8,128)(2,1)S(1)} %bitcast.215), channel_id=1, source_target_pairs={{0,96},{16,112},{32,0},{48,16},{64,32},{80,48},{96,64},{112,80},{1... | collective-permute-start | bytes 2752520 | tf_op jit(solution)/shard_map/ppermute | solution.py:41
  63.4 4.0 %collective-permute-start.5 = (bf16[2,224,512]{2,1,0:T(8,128)(2,1)S(1)}, bf16[2,224,512]{2,1,0:T(8,128)(2,1)S(1)}, u32[]{:S(2)}, u32[]{:S(2)}) collective-permute-start(bf16[2,224,512]{2,1,0:T(8,128)(2,1)S(1)} %pad_maximum_fusion.5), channel_id=1, source_target_pairs={{0,2},{1,3},{2,4},{3,5},{4,6},{5,7},{6,0},{7,1},{8,10},{9,11},{10,... | collective-permute-start | bytes 1376264 | tf_op jit(solution)/shard_map/ppermute | solution.py:30
  67.4 3.4 %collective-permute-start.6 = (bf16[2,224,512]{2,1,0:T(8,128)(2,1)S(1)}, bf16[2,224,512]{2,1,0:T(8,128)(2,1)S(1)}, u32[]{:S(2)}, u32[]{:S(2)}) collective-permute-start(bf16[2,224,512]{2,1,0:T(8,128)(2,1)S(1)} %pad_maximum_fusion.5), channel_id=1, source_target_pairs={{0,6},{1,7},{2,0},{3,1},{4,2},{5,3},{6,4},{7,5},{8,14},{9,15},{10,... | collective-permute-start | bytes 1376264 | tf_op jit(solution)/shard_map/ppermute | solution.py:30
  70.8 4.8 %collective-permute-start.9 = (f32[2,128]{1,0:T(2,128)S(1)}, f32[2,128]{1,0:T(2,128)S(1)}, u32[]{:S(2)}, u32[]{:S(2)}) collective-permute-start(f32[2,128]{1,0:T(2,128)S(1)} %pad_maximum_fusion.21), channel_id=1, source_target_pairs={{0,16},{16,0},{32,48},{48,32},{64,80},{80,64},{96,112},{112,96},{1... | collective-permute-start | bytes 3080 | tf_op jit(solution)/shard_map/ppermute | solution.py:24
  75.7 1.0 copy.107
  76.7 1.7 collective-permute-done.5
  78.5 13.8 %collective-permute-done.6 = bf16[2,224,512]{2,1,0:T(8,128)(2,1)S(1)} collective-permute-done((bf16[2,224,512]{2,1,0:T(8,128)(2,1)S(1)}, bf16[2,224,512]{2,1,0:T(8,128)(2,1)S(1)}, u32[]{:S(2)}, u32[]{:S(2)}) %collective-permute-start.6) | collective-permute-done | bytes 458784 | tf_op jit(solution)/shard_map/ppermute | solution.py:30
  92.3 4.1 %collective-permute-start.7 = (bf16[1,224,512]{2,1,0:T(8,128)(2,1)S(1)}, bf16[1,224,512]{2,1,0:T(8,128)(2,1)S(1)}, u32[]{:S(2)}, u32[]{:S(2)}) collective-permute-start(bf16[1,224,512]{2,1,0:T(8,128)(2,1)S(1)} %slice.332), channel_id=1, source_target_pairs={{0,2},{1,3},{2,4},{3,5},{4,6},{5,7},{6,0},{7,1},{8,10},{9,11},{10,... | collective-permute-start | bytes 688136 | tf_op jit(solution)/shard_map/ppermute | solution.py:30
  96.4 3.3 %collective-permute-start.8 = (bf16[1,224,512]{2,1,0:T(8,128)(2,1)S(1)}, bf16[1,224,512]{2,1,0:T(8,128)(2,1)S(1)}, u32[]{:S(2)}, u32[]{:S(2)}) collective-permute-start(bf16[1,224,512]{2,1,0:T(8,128)(2,1)S(1)} %slice.333), channel_id=1, source_target_pairs={{0,6},{1,7},{2,0},{3,1},{4,2},{5,3},{6,4},{7,5},{8,14},{9,15},{10,... | collective-permute-start | bytes 688136 | tf_op jit(solution)/shard_map/ppermute | solution.py:30
  99.7 1.0 slice.347
  100.8 1.9 collective-permute-start.10
  102.7 3.4 %collective-permute-start.11 = (bf16[2,224,512]{2,1,0:T(8,128)(2,1)S(1)}, bf16[2,224,512]{2,1,0:T(8,128)(2,1)S(1)}, u32[]{:S(2)}, u32[]{:S(2)}) collective-permute-start(bf16[2,224,512]{2,1,0:T(8,128)(2,1)S(1)} %slice.348), channel_id=1, source_target_pairs={{0,96},{16,112},{32,0},{48,16},{64,32},{80,48},{96,64},{112,80},{1... | collective-permute-start | bytes 1376264 | tf_op jit(solution)/shard_map/ppermute | solution.py:41
  106.7 1.1 add_convert_fusion
  108.2 1.6 fusion.3
  110.5 1.3 fusion.30
  113.1 2.8 %collective-permute-done.11 = bf16[2,224,512]{2,1,0:T(8,128)(2,1)S(1)} collective-permute-done((bf16[2,224,512]{2,1,0:T(8,128)(2,1)S(1)}, bf16[2,224,512]{2,1,0:T(8,128)(2,1)S(1)}, u32[]{:S(2)}, u32[]{:S(2)}) %collective-permute-start.11) | collective-permute-done | bytes 458784 | tf_op jit(solution)/shard_map/ppermute | solution.py:41
  117.7 4.3 %collective-permute-start.12 = (f32[2,136,512]{2,1,0:T(8,128)}, f32[2,136,512]{2,1,0:T(8,128)}, u32[]{:S(2)}, u32[]{:S(2)}) collective-permute-start(f32[2,136,512]{2,1,0:T(8,128)} %pad_maximum_fusion.3), channel_id=1, source_target_pairs={{0,16},{16,0},{32,48},{48,32},{64,80},{80,64},{96,112},{112,96},{1... | collective-permute-start | bytes 1671176 | tf_op jit(solution)/shard_map/ppermute | solution.py:24
  122.1 1.9 collective-permute-done.12
  124.0 1.1 maximum_add_fusion
  125.2 3.4 %collective-permute-start.13 = (bf16[144,512]{1,0:T(8,128)(2,1)S(1)}, bf16[144,512]{1,0:T(8,128)(2,1)S(1)}, u32[]{:S(2)}, u32[]{:S(2)}) collective-permute-start(bf16[144,512]{1,0:T(8,128)(2,1)S(1)} %pad_maximum_fusion.14), channel_id=1, source_target_pairs={{0,1},{1,0},{2,3},{3,2},{4,5},{5,4},{6,7},{7,6},{8,9},{9,8},{10,11... | collective-permute-start | bytes 442376 | tf_op jit(solution)/shard_map/ppermute | solution.py:46
  128.8 3.5 %collective-permute-done.13 = bf16[144,512]{1,0:T(8,128)(2,1)S(1)} collective-permute-done((bf16[144,512]{1,0:T(8,128)(2,1)S(1)}, bf16[144,512]{1,0:T(8,128)(2,1)S(1)}, u32[]{:S(2)}, u32[]{:S(2)}) %collective-permute-start.13) | collective-permute-done | bytes 147488 | tf_op jit(solution)/shard_map/ppermute | solution.py:46
  133.7 3.3 %collective-permute-start.14 = (bf16[144,512]{1,0:T(8,128)(2,1)S(1)}, bf16[144,512]{1,0:T(8,128)(2,1)S(1)}, u32[]{:S(2)}, u32[]{:S(2)}) collective-permute-start(bf16[144,512]{1,0:T(8,128)(2,1)S(1)} %fusion.50), channel_id=1, source_target_pairs={{0,1},{1,0},{2,3},{3,2},{4,5},{5,4},{6,7},{7,6},{8,9},{9,8},{10,11... | collective-permute-start | bytes 442376 | tf_op jit(solution)/shard_map/ppermute | solution.py:46
  137.1 2.5 %collective-permute-done.14 = bf16[144,512]{1,0:T(8,128)(2,1)S(1)} collective-permute-done((bf16[144,512]{1,0:T(8,128)(2,1)S(1)}, bf16[144,512]{1,0:T(8,128)(2,1)S(1)}, u32[]{:S(2)}, u32[]{:S(2)}) %collective-permute-start.14) | collective-permute-done | bytes 147488 | tf_op jit(solution)/shard_map/ppermute | solution.py:46
  139.8 4.2 %collective-permute-start.15 = (bf16[2,144,512]{2,1,0:T(8,128)(2,1)S(1)}, bf16[2,144,512]{2,1,0:T(8,128)(2,1)}, u32[]{:S(2)}, u32[]{:S(2)}) collective-permute-start(bf16[2,144,512]{2,1,0:T(8,128)(2,1)S(1)} %fusion.14), channel_id=1, source_target_pairs={{0,16},{16,0},{32,48},{48,32},{64,80},{80,64},{96,112},{112,96},{1... | collective-permute-start | bytes 884744 | tf_op jit(solution)/shard_map/ppermute | solution.py:24
  144.1 1.2 slice.331
  145.4 1.2 slice.400
  152.6 1.0 pad_maximum_fusion.1
  153.6 9.7 %all-to-all-start.1 = ((bf16[8,240,256]{2,1,0:T(8,128)(2,1)}), bf16[8,240,256]{2,1,0:T(8,128)(2,1)S(1)}, u32[]{:S(2)}, u32[]{:S(2)}) async-start(bf16[8,240,256]{2,1,0:T(8,128)(2,1)} %pad_maximum_fusion.1), calls=%async_computation.1 | async-start | bytes 1966080 | tf_op jit(solution)/shard_map/all_to_all | solution.py:255
  163.3 3.2 %collective-permute-start.17 = (bf16[4,224,128]{2,1,0:T(8,128)(2,1)}, bf16[4,224,128]{2,1,0:T(8,128)(2,1)S(1)}, u32[]{:S(2)}, u32[]{:S(2)}) collective-permute-start(bf16[4,224,128]{2,1,0:T(8,128)(2,1)} %fusion.37), channel_id=1, source_target_pairs={{0,32},{16,48},{32,64},{48,80},{64,96},{80,112},{96,0},{112,16},{1... | collective-permute-start | bytes 688136 | tf_op jit(solution)/shard_map/ppermute | solution.py:41
  167.0 2.0 collective-permute-start.19
  169.1 3.0 %collective-permute-done.17 = bf16[4,224,128]{2,1,0:T(8,128)(2,1)S(1)} collective-permute-done((bf16[4,224,128]{2,1,0:T(8,128)(2,1)}, bf16[4,224,128]{2,1,0:T(8,128)(2,1)S(1)}, u32[]{:S(2)}, u32[]{:S(2)}) %collective-permute-start.17) | collective-permute-done | bytes 229408 | tf_op jit(solution)/shard_map/ppermute | solution.py:41
  172.1 3.8 %collective-permute-start.18 = (bf16[4,224,128]{2,1,0:T(8,128)(2,1)S(1)}, bf16[4,224,128]{2,1,0:T(8,128)(2,1)S(1)}, u32[]{:S(2)}, u32[]{:S(2)}) collective-permute-start(bf16[4,224,128]{2,1,0:T(8,128)(2,1)S(1)} %fusion.9), channel_id=1, source_target_pairs={{0,32},{16,48},{32,64},{48,80},{64,96},{80,112},{96,0},{112,16},{1... | collective-permute-start | bytes 688136 | tf_op jit(solution)/shard_map/ppermute | solution.py:41
  176.7 5.6 %collective-permute-done.18 = bf16[4,224,128]{2,1,0:T(8,128)(2,1)S(1)} collective-permute-done((bf16[4,224,128]{2,1,0:T(8,128)(2,1)S(1)}, bf16[4,224,128]{2,1,0:T(8,128)(2,1)S(1)}, u32[]{:S(2)}, u32[]{:S(2)}) %collective-permute-start.18) | collective-permute-done | bytes 229408 | tf_op jit(solution)/shard_map/ppermute | solution.py:41
  182.3 1.2 fusion.11
  183.5 5.2 %collective-permute-start.20 = (bf16[224,128]{1,0:T(8,128)(2,1)S(1)}, bf16[224,128]{1,0:T(8,128)(2,1)S(1)}, u32[]{:S(2)}, u32[]{:S(2)}) collective-permute-start(bf16[224,128]{1,0:T(8,128)(2,1)S(1)} %get-tuple-element.52), channel_id=1, source_target_pairs={{0,0},{1,32},{2,2},{3,34},{4,4},{5,36},{6,6},{7,38},{8,8},{9,40},{... | collective-permute-start | bytes 172040 | tf_op jit(solution)/shard_map/ppermute | solution.py:58
  188.7 2.4 %collective-permute-start.21 = (bf16[224,128]{1,0:T(8,128)(2,1)S(1)}, bf16[224,128]{1,0:T(8,128)(2,1)S(1)}, u32[]{:S(2)}, u32[]{:S(2)}) collective-permute-start(bf16[224,128]{1,0:T(8,128)(2,1)S(1)} %get-tuple-element.55), channel_id=1, source_target_pairs={{0,128},{1,160},{2,130},{3,162},{4,132},{5,164},{6,134},{7,166},{8... | collective-permute-start | bytes 172040 | tf_op jit(solution)/shard_map/ppermute | solution.py:58
  191.1 5.4 %collective-permute-start.22 = (bf16[224,128]{1,0:T(8,128)(2,1)S(1)}, bf16[224,128]{1,0:T(8,128)(2,1)S(1)}, u32[]{:S(2)}, u32[]{:S(2)}) collective-permute-start(bf16[224,128]{1,0:T(8,128)(2,1)S(1)} %get-tuple-element.54), channel_id=1, source_target_pairs={{0,256},{1,288},{2,258},{3,290},{4,260},{5,292},{6,262},{7,294},{8... | collective-permute-start | bytes 172040 | tf_op jit(solution)/shard_map/ppermute | solution.py:58
  196.5 1.9 collective-permute-start.23
  199.7 5.3 %collective-permute-done.23 = bf16[224,128]{1,0:T(8,128)(2,1)S(1)} collective-permute-done((bf16[224,128]{1,0:T(8,128)(2,1)S(1)}, bf16[224,128]{1,0:T(8,128)(2,1)S(1)}, u32[]{:S(2)}, u32[]{:S(2)}) %collective-permute-start.23) | collective-permute-done | bytes 57376 | tf_op jit(solution)/shard_map/ppermute | solution.py:58
  205.9 5.9 %collective-permute-start.16 = (f32[224,128]{1,0:T(8,128)S(1)}, f32[224,128]{1,0:T(8,128)S(1)}, u32[]{:S(2)}, u32[]{:S(2)}) collective-permute-start(f32[224,128]{1,0:T(8,128)S(1)} %get-tuple-element.50), channel_id=1, source_target_pairs={{0,16},{16,0},{32,48},{48,32},{64,80},{80,64},{96,112},{112,96},{1... | collective-permute-start | bytes 344072 | tf_op jit(solution)/shard_map/ppermute | solution.py:24
  (158 shorter events, 23.5 us)
Async XLA Ops:
  1.7 26.8 %collective-permute-start.1 = (bf16[224,256]{1,0:T(8,128)(2,1)S(1)}, bf16[224,256]{1,0:T(8,128)(2,1)S(1)}, u32[]{:S(2)}, u32[]{:S(2)}) collective-permute-start(bf16[224,256]{1,0:T(8,128)(2,1)S(1)} %get-tuple-element.57), channel_id=1, source_target_pairs={{0,16},{16,0},{32,48},{48,32},{64,80},{80,64},{96,112},{112,96},{1... | collective-permute-start | bytes 344072 | tf_op jit(solution)/shard_map/ppermute | solution.py:24
  6.8 23.9 %all-to-all-start = ((f32[16,2,128]{2,1,0:T(2,128)}), f32[16,2,128]{2,1,0:T(2,128)S(1)}, u32[]{:S(2)}, u32[]{:S(2)}) async-start(f32[16,2,128]{2,1,0:T(2,128)} %broadcast_in_dim.10), calls=%async_computation | async-start | bytes 32768 | tf_op jit(solution)/shard_map/all_to_all | solution.py:150
  23.0 9.4 %collective-permute-start = (bf16[224,512]{1,0:T(8,128)(2,1)S(1)}, bf16[224,512]{1,0:T(8,128)(2,1)S(1)}, u32[]{:S(2)}, u32[]{:S(2)}) collective-permute-start(bf16[224,512]{1,0:T(8,128)(2,1)S(1)} %pad_maximum_fusion.12), channel_id=1, source_target_pairs={{0,0},{1,32},{2,2},{3,34},{4,4},{5,36},{6,6},{7,38},{8,8},{9,40},{... | collective-permute-start | bytes 688136 | tf_op jit(solution)/shard_map/ppermute | solution.py:58
  28.6 29.3 %collective-permute-start.2 = (bf16[224,512]{1,0:T(8,128)(2,1)S(1)}, bf16[224,512]{1,0:T(8,128)(2,1)S(1)}, u32[]{:S(2)}, u32[]{:S(2)}) collective-permute-start(bf16[224,512]{1,0:T(8,128)(2,1)S(1)} %pad_maximum_fusion.13), channel_id=1, source_target_pairs={{0,8},{1,9},{2,10},{3,11},{4,12},{5,13},{6,14},{7,15},{8,0},{9,1},... | collective-permute-start | bytes 688136 | tf_op jit(solution)/shard_map/ppermute | solution.py:35
  57.9 48.3 %copy-start.2 = (bf16[896,512]{1,0:T(8,128)(2,1)}, bf16[896,512]{1,0:T(8,128)(2,1)S(1)}, u32[]{:S(2)}) copy-start(bf16[896,512]{1,0:T(8,128)(2,1)S(1)} %all-gather) | copy-start | bytes 2752516
  58.0 34.2 %collective-permute-start.3 = (bf16[4,224,512]{2,1,0:T(8,128)(2,1)S(1)}, bf16[4,224,512]{2,1,0:T(8,128)(2,1)}, u32[]{:S(2)}, u32[]{:S(2)}) collective-permute-start(bf16[4,224,512]{2,1,0:T(8,128)(2,1)S(1)} %bitcast.214), channel_id=1, source_target_pairs={{0,32},{16,48},{32,64},{48,80},{64,96},{80,112},{96,0},{112,16},{1... | collective-permute-start | bytes 2752520 | tf_op jit(solution)/shard_map/ppermute | solution.py:41
  60.0 32.3 %collective-permute-start.4 = (bf16[4,224,512]{2,1,0:T(8,128)(2,1)S(1)}, bf16[4,224,512]{2,1,0:T(8,128)(2,1)S(1)}, u32[]{:S(2)}, u32[]{:S(2)}) collective-permute-start(bf16[4,224,512]{2,1,0:T(8,128)(2,1)S(1)} %bitcast.215), channel_id=1, source_target_pairs={{0,96},{16,112},{32,0},{48,16},{64,32},{80,48},{96,64},{112,80},{1... | collective-permute-start | bytes 2752520 | tf_op jit(solution)/shard_map/ppermute | solution.py:41
  63.4 15.1 %collective-permute-start.5 = (bf16[2,224,512]{2,1,0:T(8,128)(2,1)S(1)}, bf16[2,224,512]{2,1,0:T(8,128)(2,1)S(1)}, u32[]{:S(2)}, u32[]{:S(2)}) collective-permute-start(bf16[2,224,512]{2,1,0:T(8,128)(2,1)S(1)} %pad_maximum_fusion.5), channel_id=1, source_target_pairs={{0,2},{1,3},{2,4},{3,5},{4,6},{5,7},{6,0},{7,1},{8,10},{9,11},{10,... | collective-permute-start | bytes 1376264 | tf_op jit(solution)/shard_map/ppermute | solution.py:30
  67.4 24.9 %collective-permute-start.6 = (bf16[2,224,512]{2,1,0:T(8,128)(2,1)S(1)}, bf16[2,224,512]{2,1,0:T(8,128)(2,1)S(1)}, u32[]{:S(2)}, u32[]{:S(2)}) collective-permute-start(bf16[2,224,512]{2,1,0:T(8,128)(2,1)S(1)} %pad_maximum_fusion.5), channel_id=1, source_target_pairs={{0,6},{1,7},{2,0},{3,1},{4,2},{5,3},{6,4},{7,5},{8,14},{9,15},{10,... | collective-permute-start | bytes 1376264 | tf_op jit(solution)/shard_map/ppermute | solution.py:30
  70.8 5.9 %collective-permute-start.9 = (f32[2,128]{1,0:T(2,128)S(1)}, f32[2,128]{1,0:T(2,128)S(1)}, u32[]{:S(2)}, u32[]{:S(2)}) collective-permute-start(f32[2,128]{1,0:T(2,128)S(1)} %pad_maximum_fusion.21), channel_id=1, source_target_pairs={{0,16},{16,0},{32,48},{48,32},{64,80},{80,64},{96,112},{112,96},{1... | collective-permute-start | bytes 3080 | tf_op jit(solution)/shard_map/ppermute | solution.py:24
  92.3 13.9 %collective-permute-start.7 = (bf16[1,224,512]{2,1,0:T(8,128)(2,1)S(1)}, bf16[1,224,512]{2,1,0:T(8,128)(2,1)S(1)}, u32[]{:S(2)}, u32[]{:S(2)}) collective-permute-start(bf16[1,224,512]{2,1,0:T(8,128)(2,1)S(1)} %slice.332), channel_id=1, source_target_pairs={{0,2},{1,3},{2,4},{3,5},{4,6},{5,7},{6,0},{7,1},{8,10},{9,11},{10,... | collective-permute-start | bytes 688136 | tf_op jit(solution)/shard_map/ppermute | solution.py:30
  96.4 9.7 %collective-permute-start.8 = (bf16[1,224,512]{2,1,0:T(8,128)(2,1)S(1)}, bf16[1,224,512]{2,1,0:T(8,128)(2,1)S(1)}, u32[]{:S(2)}, u32[]{:S(2)}) collective-permute-start(bf16[1,224,512]{2,1,0:T(8,128)(2,1)S(1)} %slice.333), channel_id=1, source_target_pairs={{0,6},{1,7},{2,0},{3,1},{4,2},{5,3},{6,4},{7,5},{8,14},{9,15},{10,... | collective-permute-start | bytes 688136 | tf_op jit(solution)/shard_map/ppermute | solution.py:30
  100.8 12.3 %collective-permute-start.10 = (bf16[2,224,512]{2,1,0:T(8,128)(2,1)S(1)}, bf16[2,224,512]{2,1,0:T(8,128)(2,1)S(1)}, u32[]{:S(2)}, u32[]{:S(2)}) collective-permute-start(bf16[2,224,512]{2,1,0:T(8,128)(2,1)S(1)} %slice.347), channel_id=1, source_target_pairs={{0,32},{16,48},{32,64},{48,80},{64,96},{80,112},{96,0},{112,16},{1... | collective-permute-start | bytes 1376264 | tf_op jit(solution)/shard_map/ppermute | solution.py:41
  102.7 13.2 %collective-permute-start.11 = (bf16[2,224,512]{2,1,0:T(8,128)(2,1)S(1)}, bf16[2,224,512]{2,1,0:T(8,128)(2,1)S(1)}, u32[]{:S(2)}, u32[]{:S(2)}) collective-permute-start(bf16[2,224,512]{2,1,0:T(8,128)(2,1)S(1)} %slice.348), channel_id=1, source_target_pairs={{0,96},{16,112},{32,0},{48,16},{64,32},{80,48},{96,64},{112,80},{1... | collective-permute-start | bytes 1376264 | tf_op jit(solution)/shard_map/ppermute | solution.py:41
  106.6 1.2 copy-start.6
  109.8 2.0 copy-start.3
  115.9 1.0 copy-start
  116.9 15.4 %copy-start.8 = (f32[384]{0:T(512)S(1)}, f32[384]{0:T(512)}, u32[]{:S(2)}) copy-start(f32[384]{0:T(512)} %param.11) | copy-start | bytes 4612
  117.7 6.3 %collective-permute-start.12 = (f32[2,136,512]{2,1,0:T(8,128)}, f32[2,136,512]{2,1,0:T(8,128)}, u32[]{:S(2)}, u32[]{:S(2)}) collective-permute-start(f32[2,136,512]{2,1,0:T(8,128)} %pad_maximum_fusion.3), channel_id=1, source_target_pairs={{0,16},{16,0},{32,48},{48,32},{64,80},{80,64},{96,112},{112,96},{1... | collective-permute-start | bytes 1671176 | tf_op jit(solution)/shard_map/ppermute | solution.py:24
  125.2 7.0 %collective-permute-start.13 = (bf16[144,512]{1,0:T(8,128)(2,1)S(1)}, bf16[144,512]{1,0:T(8,128)(2,1)S(1)}, u32[]{:S(2)}, u32[]{:S(2)}) collective-permute-start(bf16[144,512]{1,0:T(8,128)(2,1)S(1)} %pad_maximum_fusion.14), channel_id=1, source_target_pairs={{0,1},{1,0},{2,3},{3,2},{4,5},{5,4},{6,7},{7,6},{8,9},{9,8},{10,11... | collective-permute-start | bytes 442376 | tf_op jit(solution)/shard_map/ppermute | solution.py:46
  133.7 5.9 %collective-permute-start.14 = (bf16[144,512]{1,0:T(8,128)(2,1)S(1)}, bf16[144,512]{1,0:T(8,128)(2,1)S(1)}, u32[]{:S(2)}, u32[]{:S(2)}) collective-permute-start(bf16[144,512]{1,0:T(8,128)(2,1)S(1)} %fusion.50), channel_id=1, source_target_pairs={{0,1},{1,0},{2,3},{3,2},{4,5},{5,4},{6,7},{7,6},{8,9},{9,8},{10,11... | collective-permute-start | bytes 442376 | tf_op jit(solution)/shard_map/ppermute | solution.py:46
  139.8 6.9 %copy-start.7 = (bf16[1,128,512]{2,1,0:T(8,128)(2,1)}, bf16[1,128,512]{2,1,0:T(8,128)(2,1)S(1)}, u32[]{:S(2)}) copy-start(bf16[1,128,512]{2,1,0:T(8,128)(2,1)S(1)} %get-tuple-element.47) | copy-start | bytes 393220
  139.8 6.9 %collective-permute-start.15 = (bf16[2,144,512]{2,1,0:T(8,128)(2,1)S(1)}, bf16[2,144,512]{2,1,0:T(8,128)(2,1)}, u32[]{:S(2)}, u32[]{:S(2)}) collective-permute-start(bf16[2,144,512]{2,1,0:T(8,128)(2,1)S(1)} %fusion.14), channel_id=1, source_target_pairs={{0,16},{16,0},{32,48},{48,32},{64,80},{80,64},{96,112},{112,96},{1... | collective-permute-start | bytes 884744 | tf_op jit(solution)/shard_map/ppermute | solution.py:24
  144.1 2.5 %copy-start.1 = (bf16[4,224,512]{2,1,0:T(8,128)(2,1)S(1)}, bf16[4,224,512]{2,1,0:T(8,128)(2,1)}, u32[]{:S(2)}) copy-start(bf16[4,224,512]{2,1,0:T(8,128)(2,1)} %copy-done) | copy-start | bytes 2752516
  149.1 0.9 copy-start.5
  153.6 52.1 %all-to-all-start.1 = ((bf16[8,240,256]{2,1,0:T(8,128)(2,1)}), bf16[8,240,256]{2,1,0:T(8,128)(2,1)S(1)}, u32[]{:S(2)}, u32[]{:S(2)}) async-start(bf16[8,240,256]{2,1,0:T(8,128)(2,1)} %pad_maximum_fusion.1), calls=%async_computation.1 | async-start | bytes 1966080 | tf_op jit(solution)/shard_map/all_to_all | solution.py:255
  163.3 8.7 %collective-permute-start.17 = (bf16[4,224,128]{2,1,0:T(8,128)(2,1)}, bf16[4,224,128]{2,1,0:T(8,128)(2,1)S(1)}, u32[]{:S(2)}, u32[]{:S(2)}) collective-permute-start(bf16[4,224,128]{2,1,0:T(8,128)(2,1)} %fusion.37), channel_id=1, source_target_pairs={{0,32},{16,48},{32,64},{48,80},{64,96},{80,112},{96,0},{112,16},{1... | collective-permute-start | bytes 688136 | tf_op jit(solution)/shard_map/ppermute | solution.py:41
  167.0 45.8 %copy-start.4 = (bf16[128,448]{0,1:T(8,128)(2,1)S(1)}, bf16[128,448]{0,1:T(8,128)(2,1)}, u32[]{:S(2)}) copy-start(bf16[128,448]{0,1:T(8,128)(2,1)} %param.7) | copy-start | bytes 344068
  167.0 9.7 %collective-permute-start.19 = (bf16[4,224,128]{2,1,0:T(8,128)(2,1)S(1)}, bf16[4,224,128]{2,1,0:T(8,128)(2,1)S(1)}, u32[]{:S(2)}, u32[]{:S(2)}) collective-permute-start(bf16[4,224,128]{2,1,0:T(8,128)(2,1)S(1)} %select_bitcast_fusion), channel_id=1, source_target_pairs={{0,96},{16,112},{32,0},{48,16},{64,32},{80,48},{96,64},{112,80},{1... | collective-permute-start | bytes 688136 | tf_op jit(solution)/shard_map/ppermute | solution.py:41
  172.1 10.2 %collective-permute-start.18 = (bf16[4,224,128]{2,1,0:T(8,128)(2,1)S(1)}, bf16[4,224,128]{2,1,0:T(8,128)(2,1)S(1)}, u32[]{:S(2)}, u32[]{:S(2)}) collective-permute-start(bf16[4,224,128]{2,1,0:T(8,128)(2,1)S(1)} %fusion.9), channel_id=1, source_target_pairs={{0,32},{16,48},{32,64},{48,80},{64,96},{80,112},{96,0},{112,16},{1... | collective-permute-start | bytes 688136 | tf_op jit(solution)/shard_map/ppermute | solution.py:41
  183.5 15.7 %collective-permute-start.20 = (bf16[224,128]{1,0:T(8,128)(2,1)S(1)}, bf16[224,128]{1,0:T(8,128)(2,1)S(1)}, u32[]{:S(2)}, u32[]{:S(2)}) collective-permute-start(bf16[224,128]{1,0:T(8,128)(2,1)S(1)} %get-tuple-element.52), channel_id=1, source_target_pairs={{0,0},{1,32},{2,2},{3,34},{4,4},{5,36},{6,6},{7,38},{8,8},{9,40},{... | collective-permute-start | bytes 172040 | tf_op jit(solution)/shard_map/ppermute | solution.py:58
  188.7 10.5 %collective-permute-start.21 = (bf16[224,128]{1,0:T(8,128)(2,1)S(1)}, bf16[224,128]{1,0:T(8,128)(2,1)S(1)}, u32[]{:S(2)}, u32[]{:S(2)}) collective-permute-start(bf16[224,128]{1,0:T(8,128)(2,1)S(1)} %get-tuple-element.55), channel_id=1, source_target_pairs={{0,128},{1,160},{2,130},{3,162},{4,132},{5,164},{6,134},{7,166},{8... | collective-permute-start | bytes 172040 | tf_op jit(solution)/shard_map/ppermute | solution.py:58
  191.1 8.7 %collective-permute-start.22 = (bf16[224,128]{1,0:T(8,128)(2,1)S(1)}, bf16[224,128]{1,0:T(8,128)(2,1)S(1)}, u32[]{:S(2)}, u32[]{:S(2)}) collective-permute-start(bf16[224,128]{1,0:T(8,128)(2,1)S(1)} %get-tuple-element.54), channel_id=1, source_target_pairs={{0,256},{1,288},{2,258},{3,290},{4,260},{5,292},{6,262},{7,294},{8... | collective-permute-start | bytes 172040 | tf_op jit(solution)/shard_map/ppermute | solution.py:58
  196.5 8.5 %collective-permute-start.23 = (bf16[224,128]{1,0:T(8,128)(2,1)S(1)}, bf16[224,128]{1,0:T(8,128)(2,1)S(1)}, u32[]{:S(2)}, u32[]{:S(2)}) collective-permute-start(bf16[224,128]{1,0:T(8,128)(2,1)S(1)} %get-tuple-element.53), channel_id=1, source_target_pairs={{0,384},{1,416},{2,386},{3,418},{4,388},{5,420},{6,390},{7,422},{8... | collective-permute-start | bytes 172040 | tf_op jit(solution)/shard_map/ppermute | solution.py:58
  205.9 6.9 %collective-permute-start.16 = (f32[224,128]{1,0:T(8,128)S(1)}, f32[224,128]{1,0:T(8,128)S(1)}, u32[]{:S(2)}, u32[]{:S(2)}) collective-permute-start(f32[224,128]{1,0:T(8,128)S(1)} %get-tuple-element.50), channel_id=1, source_target_pairs={{0,16},{16,0},{32,48},{48,32},{64,80},{80,64},{96,112},{112,96},{1... | collective-permute-start | bytes 344072 | tf_op jit(solution)/shard_map/ppermute | solution.py:24

commit v10 on v7

--- a/solution.py
+++ b/solution.py
@@ -71,18 +71,16 @@
 
 
 def ring_scatter_x(part, across):
-    ahead = part(1).astype(f32) + across.astype(f32)
+    ahead = part(1).astype(f32) + shift_x(across, 1).astype(f32)
     up, down = shift_x(ahead.astype(bf16), 1), shift_x(part(-1), -1)
     return part(0).astype(f32) + up.astype(f32) + down.astype(f32)
 
 
-def scatter_y(parts, place, early):
+def scatter_y(parts, place):
     count = parts.shape[0]
     sent = parts.astype(bf16)
     total = None
     for step in range(count):
-        if step == count // 2:
-            sent, early = lax.optimization_barrier((sent, early))
         one = lax.dynamic_index_in_dim(sent, (place + step) % count, 0, keepdims=False)
 
         def target(half, place):
@@ -91,7 +89,7 @@
 
         one = along_y(one, target).astype(f32)
         total = one if total is None else total + one
-    return total, early
+    return total
 
 
 def split(x):
@@ -148,35 +146,25 @@
     block = jnp.concatenate([mine[:, :SEQ], other[:, :SEQ], mine[:, SEQ:], other[:, SEQ:]], axis=1)
 
     weight_block = move_weights(jnp.concatenate([w_qkv, w_out.T], axis=1))
-    hidden = lax.all_gather(
-        block[:, : 2 * SEQ], "tensor", axis=0, tiled=True, axis_index_groups=rings
-    )
-    weight_block, hidden = lax.optimization_barrier((weight_block, hidden))
+
+    slice_f = hidden_t.astype(f32)
+    mean_part = jnp.mean(slice_f, axis=0)
+    stats = jnp.stack([mean_part, jnp.sum((slice_f - mean_part) ** 2, axis=0)])
+    block, stats = lax.optimization_barrier((block, stats))
+    stats = lax.all_to_all(
+        jnp.broadcast_to(stats[None], (n_tensor, 2, SEQ)), "tensor", 0, 0, tiled=True
+    )
+    weight_block, stats = lax.optimization_barrier((weight_block, stats))
     column = lax.all_gather(weight_block, "dp", axis=0, axis_index_groups=lines)
-    column, block = lax.optimization_barrier((column, block))
-    grads = lax.all_gather(
-        block[:, 2 * SEQ :], "tensor", axis=0, tiled=True, axis_index_groups=rings
-    )
-    blocks, grads = x_gather(column, x, grads)
-    hidden = hidden.astype(f32)
-    mean_part = jnp.sum(hidden, axis=0) / quarter
-    stats = jnp.stack([mean_part, jnp.sum((hidden - mean_part) ** 2, axis=0)])
-
-    def merge(stats, stats_other, count):
-        gap = stats[0] - stats_other[0]
-        return jnp.stack(
-            [
-                0.5 * (stats[0] + stats_other[0]),
-                stats[1] + stats_other[1] + gap * gap * (count / 2),
-            ]
-        )
-
-    stats = merge(stats, swap_far(stats), quarter)
-    stats_other = swap_cores(stats)
-    stats_other = jnp.concatenate([stats_other[:, SEQ:], stats_other[:, :SEQ]], axis=1)
-    stats = merge(stats, stats_other, 2 * quarter)
-    mean = stats[0]
-    inv_std = lax.rsqrt(stats[1] / depth + norm_eps)
+    mean = jnp.mean(stats[:, 0], axis=0)
+    square = jnp.sum(stats[:, 1], axis=0) + width * jnp.sum((stats[:, 0] - mean) ** 2, axis=0)
+    stats = jnp.stack([mean, lax.rsqrt(square / depth + norm_eps)])
+    mean, inv_std = jnp.concatenate([stats, swap_cores(stats)], axis=1)
+
+    rows = lax.all_gather(block, "tensor", axis=0, tiled=True, axis_index_groups=rings)
+    blocks, rows = x_gather(column, x, rows)
+    hidden = rows[:, : 2 * SEQ].astype(f32)
+    grads = rows[:, 2 * SEQ :]
 
     def own_part(vector):
         vector = vector.reshape(2, Z_COUNT, 2, part)
@@ -262,8 +250,7 @@
             [lax.dynamic_index_in_dim(w, place, 1, keepdims=False) for w in weight_parts]
         )
 
-    across = shift_x(weight_to(2), 1)
-    across, heads = lax.optimization_barrier((across, heads))
+    across, heads = lax.optimization_barrier((weight_to(2), heads))
 
     group_part = sum(
         dot(joined_weight[h], heads[h, :, E:], ((1,), (1,))) for h in range(2)
@@ -273,7 +260,7 @@
     group_parts = lax.all_to_all(payload, "tensor", 0, 0, tiled=True, axis_index_groups=rings)
     total = jnp.sum(group_parts.astype(f32), axis=0)
     weight_parts = ring_scatter_x(weight_to, across)
-    grad_out_weight, total = scatter_y(weight_parts, y, total)
+    grad_out_weight = scatter_y(weight_parts, y)
     sums = total[part : part + 2, :SEQ] + total[part + 2 : part + 4, :SEQ]
     total = total[:part]
     total_other = swap_cores(total[:, SEQ:])

time: 226 us -> 208 us (0.920)
  blocking collectives: 64.9 us -> 17.2 us
  between operations: 1.83 us -> 15.3 us
  waiting for transfers between devices: 54.3 us -> 63.9 us
  starting transfers between devices: 83.3 us -> 88.4 us
    all_gather x2 -> x0, blocking collectives: 44.1 us -> none  [the longest x1 22.3 us: body(): lax.all_gather(block[:, 2 * SEQ:], 'tensor', axis=0, tiled=True, axis_ind...]
    all_to_all x1, waiting for transfers between devices: 13.9 us -> 0.01 us  [body(): lax.all_to_all(payload, 'tensor', 0, 0, tiled=True, axis_index_groups=rings)]
    all_to_all x0 -> x1, starting transfers between devices: none -> 11.3 us  [body(): lax.all_to_all(jnp.broadcast_to(stats[None], (n_tensor, 2, SEQ)), 'tensor...]
    all_to_all x0 -> x1, waiting for transfers between devices: none -> 11 us  [body(): lax.all_to_all(jnp.broadcast_to(stats[None], (n_tensor, 2, SEQ)), 'tensor...]
    ppermute x3 -> x2, starting transfers between devices: 15.1 us -> 4.92 us  [swap_far(): return lax.ppermute(x, 'tensor', [(i, (i + Z_COUNT) % n) for i in range(n)])]
    ppermute x7, waiting for transfers between devices: 22.1 us -> 28.3 us  [shift_x(): lax.ppermute(x, 'dp', [(i, i - i % row + (i + 2 * step) % row) for i in r...]
    all_gather x1, blocking collectives: 20.8 us -> 17.2 us  [body(): column = lax.all_gather(weight_block, 'dp', axis=0, axis_index_groups=lines)]
    ppermute x5, waiting for transfers between devices: 0.01 us -> 3.54 us  [along_y(): return lax.ppermute(x, ('dp', 'tensor'), pairs)]
  transfers between devices with their start and end apart: 21 -> 22, of which waited for: 12 -> 14; matrix products, arithmetic and copies ran while one was open for 5% -> 4% of each run, Pallas kernels for 0% -> 0%
where the time goes in v10:
time: 208 us; the launch traced here: 207 us
  starting transfers between devices  88.4 us (42%)
  waiting for transfers between devices  63.9 us (31%)
  blocking collectives  17.2 us (8%)
  between operations  15.3 us (7%)
  other arithmetic  10.3 us (5%)
  matrix products  7.82 us (4%)
  local copies, waits for them, and re-layouts  4.08 us (2%)
    ppermute x5, starting transfers between devices, swap_cores(): return lax.ppermute(x, 'dp', [(i, i ^ 1) for i in range(n)])  33.7 us
    ppermute x7, waiting for transfers between devices, shift_x(): lax.ppermute(x, 'dp', [(i, i - i % row + (i + 2 * step) % row) for i in r...  28.3 us
    ppermute x7, starting transfers between devices, shift_x(): lax.ppermute(x, 'dp', [(i, i - i % row + (i + 2 * step) % row) for i in r...  20.1 us
    ppermute x2, waiting for transfers between devices, swap_far(): return lax.ppermute(x, 'tensor', [(i, (i + Z_COUNT) % n) for i in range(n)])  17.9 us
    all_gather x1, blocking collectives, body(): column = lax.all_gather(weight_block, 'dp', axis=0, axis_index_groups=lines)  17.2 us
    ppermute x5, starting transfers between devices, along_y(): return lax.ppermute(x, ('dp', 'tensor'), pairs)  14.7 us
    all_to_all x1, starting transfers between devices, body(): lax.all_to_all(jnp.broadcast_to(stats[None], (n_tensor, 2, SEQ)), 'tensor...  11.3 us
    all_to_all x1, waiting for transfers between devices, body(): lax.all_to_all(jnp.broadcast_to(stats[None], (n_tensor, 2, SEQ)), 'tensor...  11 us
  transfers between devices with their start and end apart: 22, of which 14 were waited for; matrix products, arithmetic and copies ran while one was open for 4% of the time, Pallas kernels for 0%

profile of v10, /device:TPU:1, one launch (start us, length us, event | category | flops | bytes accessed | tf_op | source)
XLA Modules:
  0.0 206.9 jit_solution(8184693457975213644)
XLA Ops:
  7.3 1.1 broadcast_select_fusion.1
  8.3 8.8 %collective-permute-start.1 = (bf16[224,256]{1,0:T(8,128)(2,1)S(1)}, bf16[224,256]{1,0:T(8,128)(2,1)S(1)}, u32[]{:S(2)}, u32[]{:S(2)}) collective-permute-start(bf16[224,256]{1,0:T(8,128)(2,1)S(1)} %get-tuple-element.65), channel_id=1, source_target_pairs={{0,16},{16,0},{32,48},{48,32},{64,80},{80,64},{96,112},{112,96},{1... | collective-permute-start | bytes 344072 | tf_op jit(solution)/shard_map/ppermute | solution.py:24
  17.1 1.0 convert_reduce_fusion.1
  18.1 1.0 fusion.27
  19.1 0.7 pad_maximum_fusion.12
  19.9 0.7 collective-permute-start
  21.1 0.6 broadcast_in_dim.10
  21.7 11.3 %all-to-all-start = ((f32[16,2,128]{2,1,0:T(2,128)}), f32[16,2,128]{2,1,0:T(2,128)S(1)}, u32[]{:S(2)}, u32[]{:S(2)}) async-start(f32[16,2,128]{2,1,0:T(2,128)} %broadcast_in_dim.10), calls=%async_computation | async-start | bytes 32768 | tf_op jit(solution)/shard_map/all_to_all | solution.py:154
  33.3 11.0 %all-to-all-done = f32[16,2,128]{2,1,0:T(2,128)S(1)} async-done(((f32[16,2,128]{2,1,0:T(2,128)}), f32[16,2,128]{2,1,0:T(2,128)S(1)}, u32[]{:S(2)}, u32[]{:S(2)}) %all-to-all-start) | async-done | bytes 16416 | tf_op jit(solution)/shard_map/all_to_all | solution.py:154
  44.3 17.2 %all-gather = bf16[896,512]{1,0:T(8,128)(2,1)S(1)} all-gather(bf16[224,512]{1,0:T(8,128)(2,1)S(1)} %collective-permute-done), channel_id=2, replica_groups={{0,128,256,384},{16,144,272,400},{32,160,288,416},{48,176,304,432},{64,..., dimensions={0}, use_global_device_ids=true | all-gather | bytes 1146880 | tf_op jit(solution)/shard_map/all_gather | solution.py:158
  61.5 4.4 %collective-permute-start.3 = (bf16[4,224,512]{2,1,0:T(8,128)(2,1)S(1)}, bf16[4,224,512]{2,1,0:T(8,128)(2,1)S(1)}, u32[]{:S(2)}, u32[]{:S(2)}) collective-permute-start(bf16[4,224,512]{2,1,0:T(8,128)(2,1)S(1)} %bitcast.162), channel_id=1, source_target_pairs={{0,96},{16,112},{32,0},{48,16},{64,32},{80,48},{96,64},{112,80},{1... | collective-permute-start | bytes 2752520 | tf_op jit(solution)/shard_map/ppermute | solution.py:41
  65.9 1.9 collective-permute-start.2
  67.9 5.5 %collective-permute-start.6 = (f32[2,128]{1,0:T(2,128)S(1)}, f32[2,128]{1,0:T(2,128)S(1)}, u32[]{:S(2)}, u32[]{:S(2)}) collective-permute-start(f32[2,128]{1,0:T(2,128)S(1)} %pad_maximum_fusion.22), channel_id=1, source_target_pairs={{0,16},{16,0},{32,48},{48,32},{64,80},{80,64},{96,112},{112,96},{1... | collective-permute-start | bytes 3080 | tf_op jit(solution)/shard_map/ppermute | solution.py:24
  74.3 7.9 %collective-permute-done.3 = bf16[4,224,512]{2,1,0:T(8,128)(2,1)S(1)} collective-permute-done((bf16[4,224,512]{2,1,0:T(8,128)(2,1)S(1)}, bf16[4,224,512]{2,1,0:T(8,128)(2,1)S(1)}, u32[]{:S(2)}, u32[]{:S(2)}) %collective-permute-start.3) | collective-permute-done | bytes 917536 | tf_op jit(solution)/shard_map/ppermute | solution.py:41
  82.1 5.0 %collective-permute-done.2 = bf16[4,224,512]{2,1,0:T(8,128)(2,1)S(1)} collective-permute-done((bf16[4,224,512]{2,1,0:T(8,128)(2,1)S(1)}, bf16[4,224,512]{2,1,0:T(8,128)(2,1)S(1)}, u32[]{:S(2)}, u32[]{:S(2)}) %collective-permute-start.2) | collective-permute-done | bytes 917536 | tf_op jit(solution)/shard_map/ppermute | solution.py:41
  87.2 2.1 %add_convert_fusion = bf16[1792,256]{1,0:T(8,128)(2,1)S(1)} fusion(f32[1792]{0:T(1024)S(1)} %select_n.255, f32[1792]{0:T(1024)S(1)} %select_n.251, f32[256]{0:T(256)S(1)} %bitcast.214, f32[256]{0:T(256)S(1)} %bitcast.213, bf16[1792,512]{1,0:T(8,128)(2,1)} %all-gather.3.cloned.1.call-done), kind=kLoop, calls=%fused_computation.5 | loop fusion | flops 2752512 | bytes 1851392 | tf_op jit(solution)/shard_map/convert_element_type | solution.py:175
  90.3 0.5 slice-done
  91.4 1.9 collective-permute-start.5
  93.4 3.4 %collective-permute-start.4 = (bf16[2,224,512]{2,1,0:T(8,128)(2,1)S(1)}, bf16[2,224,512]{2,1,0:T(8,128)(2,1)S(1)}, u32[]{:S(2)}, u32[]{:S(2)}) collective-permute-start(bf16[2,224,512]{2,1,0:T(8,128)(2,1)S(1)} %get-tuple-element.34), channel_id=1, source_target_pairs={{0,32},{16,48},{32,64},{48,80},{64,96},{80,112},{96,0},{112,16},{1... | collective-permute-start | bytes 1376264 | tf_op jit(solution)/shard_map/ppermute | solution.py:41
  99.2 1.4 collective-permute-done.5
  101.0 2.8 %collective-permute-done.4 = bf16[2,224,512]{2,1,0:T(8,128)(2,1)S(1)} collective-permute-done((bf16[2,224,512]{2,1,0:T(8,128)(2,1)S(1)}, bf16[2,224,512]{2,1,0:T(8,128)(2,1)S(1)}, u32[]{:S(2)}, u32[]{:S(2)}) %collective-permute-start.4) | collective-permute-done | bytes 458784 | tf_op jit(solution)/shard_map/ppermute | solution.py:41
  105.0 7.6 %collective-permute-start.7 = (f32[2,136,512]{2,1,0:T(8,128)S(1)}, f32[2,136,512]{2,1,0:T(8,128)S(1)}, u32[]{:S(2)}, u32[]{:S(2)}) collective-permute-start(f32[2,136,512]{2,1,0:T(8,128)S(1)} %pad_maximum_fusion.3), channel_id=1, source_target_pairs={{0,16},{16,0},{32,48},{48,32},{64,80},{80,64},{96,112},{112,96},{1... | collective-permute-start | bytes 1671176 | tf_op jit(solution)/shard_map/ppermute | solution.py:24
  113.0 1.2 collective-permute-done.7
  114.4 3.0 %collective-permute-start.8 = (bf16[144,512]{1,0:T(8,128)(2,1)S(1)}, bf16[144,512]{1,0:T(8,128)(2,1)S(1)}, u32[]{:S(2)}, u32[]{:S(2)}) collective-permute-start(bf16[144,512]{1,0:T(8,128)(2,1)S(1)} %pad_maximum_fusion.15), channel_id=1, source_target_pairs={{0,8},{1,9},{2,10},{3,11},{4,12},{5,13},{6,14},{7,15},{8,0},{9,1},... | collective-permute-start | bytes 442376 | tf_op jit(solution)/shard_map/ppermute | solution.py:35
  117.6 9.4 %collective-permute-done.8 = bf16[144,512]{1,0:T(8,128)(2,1)S(1)} collective-permute-done((bf16[144,512]{1,0:T(8,128)(2,1)S(1)}, bf16[144,512]{1,0:T(8,128)(2,1)S(1)}, u32[]{:S(2)}, u32[]{:S(2)}) %collective-permute-start.8) | collective-permute-done | bytes 147488 | tf_op jit(solution)/shard_map/ppermute | solution.py:35
  128.4 1.9 collective-permute-start.9
  130.6 8.5 %collective-permute-done.9 = bf16[144,512]{1,0:T(8,128)(2,1)S(1)} collective-permute-done((bf16[144,512]{1,0:T(8,128)(2,1)S(1)}, bf16[144,512]{1,0:T(8,128)(2,1)S(1)}, u32[]{:S(2)}, u32[]{:S(2)}) %collective-permute-start.9) | collective-permute-done | bytes 147488 | tf_op jit(solution)/shard_map/ppermute | solution.py:35
  139.3 6.4 %collective-permute-start.10 = (bf16[2,144,512]{2,1,0:T(8,128)(2,1)S(1)}, bf16[2,144,512]{2,1,0:T(8,128)(2,1)S(1)}, u32[]{:S(2)}, u32[]{:S(2)}) collective-permute-start(bf16[2,144,512]{2,1,0:T(8,128)(2,1)S(1)} %fusion.18), channel_id=1, source_target_pairs={{0,16},{16,0},{32,48},{48,32},{64,80},{80,64},{96,112},{112,96},{1... | collective-permute-start | bytes 884744 | tf_op jit(solution)/shard_map/ppermute | solution.py:24
  146.3 0.7 collective-permute-done.10
  147.8 0.4 convolution_convert_fusion.1
  148.4 0.7 fusion.38
  149.1 0.7 fusion
  149.8 1.0 pad_maximum_fusion.1
  150.8 3.6 %all-to-all-start.1 = ((bf16[8,240,256]{2,1,0:T(8,128)(2,1)}), bf16[8,240,256]{2,1,0:T(8,128)(2,1)S(1)}, u32[]{:S(2)}, u32[]{:S(2)}) async-start(bf16[8,240,256]{2,1,0:T(8,128)(2,1)} %pad_maximum_fusion.1), calls=%async_computation.1 | async-start | bytes 1966080 | tf_op jit(solution)/shard_map/all_to_all | solution.py:260
  154.4 2.0 collective-permute-start.12
  156.5 4.4 %collective-permute-start.14 = (bf16[4,224,128]{2,1,0:T(8,128)(2,1)S(1)}, bf16[4,224,128]{2,1,0:T(8,128)(2,1)S(1)}, u32[]{:S(2)}, u32[]{:S(2)}) collective-permute-start(bf16[4,224,128]{2,1,0:T(8,128)(2,1)S(1)} %pad_maximum_fusion.14), channel_id=1, source_target_pairs={{0,96},{16,112},{32,0},{48,16},{64,32},{80,48},{96,64},{112,80},{1... | collective-permute-start | bytes 688136 | tf_op jit(solution)/shard_map/ppermute | solution.py:41
  160.9 3.8 %collective-permute-done.12 = bf16[4,224,128]{2,1,0:T(8,128)(2,1)S(1)} collective-permute-done((bf16[4,224,128]{2,1,0:T(8,128)(2,1)S(1)}, bf16[4,224,128]{2,1,0:T(8,128)(2,1)S(1)}, u32[]{:S(2)}, u32[]{:S(2)}) %collective-permute-start.12) | collective-permute-done | bytes 229408 | tf_op jit(solution)/shard_map/ppermute | solution.py:41
  164.8 2.1 collective-permute-start.13
  167.0 7.4 %collective-permute-done.13 = bf16[4,224,128]{2,1,0:T(8,128)(2,1)S(1)} collective-permute-done((bf16[4,224,128]{2,1,0:T(8,128)(2,1)S(1)}, bf16[4,224,128]{2,1,0:T(8,128)(2,1)S(1)}, u32[]{:S(2)}, u32[]{:S(2)}) %collective-permute-start.13) | collective-permute-done | bytes 229408 | tf_op jit(solution)/shard_map/ppermute | solution.py:41
  174.5 0.7 collective-permute-start.15
  175.2 7.4 %collective-permute-start.18 = (bf16[224,128]{1,0:T(8,128)(2,1)S(1)}, bf16[224,128]{1,0:T(8,128)(2,1)S(1)}, u32[]{:S(2)}, u32[]{:S(2)}) collective-permute-start(bf16[224,128]{1,0:T(8,128)(2,1)S(1)} %get-tuple-element.61), channel_id=1, source_target_pairs={{0,136},{1,137},{2,138},{3,139},{4,140},{5,141},{6,142},{7,143},{8... | collective-permute-start | bytes 172040 | tf_op jit(solution)/shard_map/ppermute | solution.py:53
  182.5 2.9 %collective-permute-start.17 = (bf16[224,128]{1,0:T(8,128)(2,1)S(1)}, bf16[224,128]{1,0:T(8,128)(2,1)S(1)}, u32[]{:S(2)}, u32[]{:S(2)}) collective-permute-start(bf16[224,128]{1,0:T(8,128)(2,1)S(1)} %get-tuple-element.62), channel_id=1, source_target_pairs={{0,8},{1,9},{2,10},{3,11},{4,12},{5,13},{6,14},{7,15},{8,264},{9,2... | collective-permute-start | bytes 172040 | tf_op jit(solution)/shard_map/ppermute | solution.py:53
  185.5 3.1 %collective-permute-start.16 = (bf16[224,128]{1,0:T(8,128)(2,1)S(1)}, bf16[224,128]{1,0:T(8,128)(2,1)S(1)}, u32[]{:S(2)}, u32[]{:S(2)}) collective-permute-start(bf16[224,128]{1,0:T(8,128)(2,1)S(1)} %get-tuple-element.63), channel_id=1, source_target_pairs={{0,128},{1,129},{2,130},{3,131},{4,132},{5,133},{6,134},{7,135},{8... | collective-permute-start | bytes 172040 | tf_op jit(solution)/shard_map/ppermute | solution.py:53
  188.7 3.5 %collective-permute-done.16 = bf16[224,128]{1,0:T(8,128)(2,1)S(1)} collective-permute-done((bf16[224,128]{1,0:T(8,128)(2,1)S(1)}, bf16[224,128]{1,0:T(8,128)(2,1)S(1)}, u32[]{:S(2)}, u32[]{:S(2)}) %collective-permute-start.16) | collective-permute-done | bytes 57376 | tf_op jit(solution)/shard_map/ppermute | solution.py:53
  192.2 0.7 add_bitcast_fusion
  193.1 5.3 %collective-permute-start.11 = (f32[224,128]{1,0:T(8,128)S(1)}, f32[224,128]{1,0:T(8,128)S(1)}, u32[]{:S(2)}, u32[]{:S(2)}) collective-permute-start(f32[224,128]{1,0:T(8,128)S(1)} %get-tuple-element.58), channel_id=1, source_target_pairs={{0,16},{16,0},{32,48},{48,32},{64,80},{80,64},{96,112},{112,96},{1... | collective-permute-start | bytes 344072 | tf_op jit(solution)/shard_map/ppermute | solution.py:24
  198.4 0.9 collective-permute-done.11
  199.3 0.8 fusion.55
  (145 shorter events, 11.4 us)
Async XLA Ops:
  7.2 12.7 %copy-start.3 = (bf16[128,224]{0,1:T(8,128)(2,1)S(1)}, bf16[128,224]{0,1:T(8,128)(2,1)}, u32[]{:S(2)}) copy-start(bf16[128,224]{0,1:T(8,128)(2,1)} %param.12) | copy-start | bytes 172036
  7.2 12.7 %copy-start.2 = (bf16[224,384]{1,0:T(8,128)(2,1)S(1)}, bf16[224,384]{1,0:T(8,128)(2,1)}, u32[]{:S(2)}) copy-start(bf16[224,384]{1,0:T(8,128)(2,1)} %param.10) | copy-start | bytes 516100
  7.2 13.4 %copy-start.5 = (f32[7168]{0:T(1024)S(1)}, f32[7168]{0:T(1024)}, u32[]{:S(2)}) copy-start(f32[7168]{0:T(1024)} %param.9) | copy-start | bytes 86020
  7.2 13.5 %copy-start.4 = (f32[7168]{0:T(1024)S(1)}, f32[7168]{0:T(1024)}, u32[]{:S(2)}) copy-start(f32[7168]{0:T(1024)} %param.8) | copy-start | bytes 86020
  7.2 80.0 %all-gather.3.cloned.1.call-start = ((), (), s32[]{:S(2)}) async-start(), calls=%async_computation.2 | async-start | bytes 2064384 | tf_op jit(solution)/shard_map/all_gather | solution.py:164
  8.3 10.8 %collective-permute-start.1 = (bf16[224,256]{1,0:T(8,128)(2,1)S(1)}, bf16[224,256]{1,0:T(8,128)(2,1)S(1)}, u32[]{:S(2)}, u32[]{:S(2)}) collective-permute-start(bf16[224,256]{1,0:T(8,128)(2,1)S(1)} %get-tuple-element.65), channel_id=1, source_target_pairs={{0,16},{16,0},{32,48},{48,32},{64,80},{80,64},{96,112},{112,96},{1... | collective-permute-start | bytes 344072 | tf_op jit(solution)/shard_map/ppermute | solution.py:24
  19.9 24.4 %collective-permute-start = (bf16[224,512]{1,0:T(8,128)(2,1)S(1)}, bf16[224,512]{1,0:T(8,128)(2,1)S(1)}, u32[]{:S(2)}, u32[]{:S(2)}) collective-permute-start(bf16[224,512]{1,0:T(8,128)(2,1)S(1)} %pad_maximum_fusion.11), channel_id=1, source_target_pairs={{0,0},{1,1},{2,2},{3,3},{4,4},{5,5},{6,6},{7,7},{8,256},{9,257},{1... | collective-permute-start | bytes 688136 | tf_op jit(solution)/shard_map/ppermute | solution.py:53
  21.7 22.6 %all-to-all-start = ((f32[16,2,128]{2,1,0:T(2,128)}), f32[16,2,128]{2,1,0:T(2,128)S(1)}, u32[]{:S(2)}, u32[]{:S(2)}) async-start(f32[16,2,128]{2,1,0:T(2,128)} %broadcast_in_dim.10), calls=%async_computation | async-start | bytes 32768 | tf_op jit(solution)/shard_map/all_to_all | solution.py:154
  61.5 20.6 %collective-permute-start.3 = (bf16[4,224,512]{2,1,0:T(8,128)(2,1)S(1)}, bf16[4,224,512]{2,1,0:T(8,128)(2,1)S(1)}, u32[]{:S(2)}, u32[]{:S(2)}) collective-permute-start(bf16[4,224,512]{2,1,0:T(8,128)(2,1)S(1)} %bitcast.162), channel_id=1, source_target_pairs={{0,96},{16,112},{32,0},{48,16},{64,32},{80,48},{96,64},{112,80},{1... | collective-permute-start | bytes 2752520 | tf_op jit(solution)/shard_map/ppermute | solution.py:41
  65.9 21.3 %collective-permute-start.2 = (bf16[4,224,512]{2,1,0:T(8,128)(2,1)S(1)}, bf16[4,224,512]{2,1,0:T(8,128)(2,1)S(1)}, u32[]{:S(2)}, u32[]{:S(2)}) collective-permute-start(bf16[4,224,512]{2,1,0:T(8,128)(2,1)S(1)} %bitcast.163), channel_id=1, source_target_pairs={{0,32},{16,48},{32,64},{48,80},{64,96},{80,112},{96,0},{112,16},{1... | collective-permute-start | bytes 2752520 | tf_op jit(solution)/shard_map/ppermute | solution.py:41
  67.9 6.3 %collective-permute-start.6 = (f32[2,128]{1,0:T(2,128)S(1)}, f32[2,128]{1,0:T(2,128)S(1)}, u32[]{:S(2)}, u32[]{:S(2)}) collective-permute-start(f32[2,128]{1,0:T(2,128)S(1)} %pad_maximum_fusion.22), channel_id=1, source_target_pairs={{0,16},{16,0},{32,48},{48,32},{64,80},{80,64},{96,112},{112,96},{1... | collective-permute-start | bytes 3080 | tf_op jit(solution)/shard_map/ppermute | solution.py:24
  89.6 1.2 slice-start
  91.4 9.2 %collective-permute-start.5 = (bf16[2,224,512]{2,1,0:T(8,128)(2,1)S(1)}, bf16[2,224,512]{2,1,0:T(8,128)(2,1)S(1)}, u32[]{:S(2)}, u32[]{:S(2)}) collective-permute-start(bf16[2,224,512]{2,1,0:T(8,128)(2,1)S(1)} %get-tuple-element.33), channel_id=1, source_target_pairs={{0,96},{16,112},{32,0},{48,16},{64,32},{80,48},{96,64},{112,80},{1... | collective-permute-start | bytes 1376264 | tf_op jit(solution)/shard_map/ppermute | solution.py:41
  93.4 10.4 %collective-permute-start.4 = (bf16[2,224,512]{2,1,0:T(8,128)(2,1)S(1)}, bf16[2,224,512]{2,1,0:T(8,128)(2,1)S(1)}, u32[]{:S(2)}, u32[]{:S(2)}) collective-permute-start(bf16[2,224,512]{2,1,0:T(8,128)(2,1)S(1)} %get-tuple-element.34), channel_id=1, source_target_pairs={{0,32},{16,48},{32,64},{48,80},{64,96},{80,112},{96,0},{112,16},{1... | collective-permute-start | bytes 1376264 | tf_op jit(solution)/shard_map/ppermute | solution.py:41
  105.0 9.2 %collective-permute-start.7 = (f32[2,136,512]{2,1,0:T(8,128)S(1)}, f32[2,136,512]{2,1,0:T(8,128)S(1)}, u32[]{:S(2)}, u32[]{:S(2)}) collective-permute-start(f32[2,136,512]{2,1,0:T(8,128)S(1)} %pad_maximum_fusion.3), channel_id=1, source_target_pairs={{0,16},{16,0},{32,48},{48,32},{64,80},{80,64},{96,112},{112,96},{1... | collective-permute-start | bytes 1671176 | tf_op jit(solution)/shard_map/ppermute | solution.py:24
  114.4 12.7 %copy-start.6 = (f32[384]{0:T(512)S(1)}, f32[384]{0:T(512)}, u32[]{:S(2)}) copy-start(f32[384]{0:T(512)} %param.11) | copy-start | bytes 4612
  114.4 12.5 %collective-permute-start.8 = (bf16[144,512]{1,0:T(8,128)(2,1)S(1)}, bf16[144,512]{1,0:T(8,128)(2,1)S(1)}, u32[]{:S(2)}, u32[]{:S(2)}) collective-permute-start(bf16[144,512]{1,0:T(8,128)(2,1)S(1)} %pad_maximum_fusion.15), channel_id=1, source_target_pairs={{0,8},{1,9},{2,10},{3,11},{4,12},{5,13},{6,14},{7,15},{8,0},{9,1},... | collective-permute-start | bytes 442376 | tf_op jit(solution)/shard_map/ppermute | solution.py:35
  128.4 10.7 %collective-permute-start.9 = (bf16[144,512]{1,0:T(8,128)(2,1)S(1)}, bf16[144,512]{1,0:T(8,128)(2,1)S(1)}, u32[]{:S(2)}, u32[]{:S(2)}) collective-permute-start(bf16[144,512]{1,0:T(8,128)(2,1)S(1)} %fusion.42), channel_id=1, source_target_pairs={{0,8},{1,9},{2,10},{3,11},{4,12},{5,13},{6,14},{7,15},{8,0},{9,1},... | collective-permute-start | bytes 442376 | tf_op jit(solution)/shard_map/ppermute | solution.py:35
  139.3 7.6 %collective-permute-start.10 = (bf16[2,144,512]{2,1,0:T(8,128)(2,1)S(1)}, bf16[2,144,512]{2,1,0:T(8,128)(2,1)S(1)}, u32[]{:S(2)}, u32[]{:S(2)}) collective-permute-start(bf16[2,144,512]{2,1,0:T(8,128)(2,1)S(1)} %fusion.18), channel_id=1, source_target_pairs={{0,16},{16,0},{32,48},{48,32},{64,80},{80,64},{96,112},{112,96},{1... | collective-permute-start | bytes 884744 | tf_op jit(solution)/shard_map/ppermute | solution.py:24
  145.9 1.5 copy-start
  150.8 42.0 %all-to-all-start.1 = ((bf16[8,240,256]{2,1,0:T(8,128)(2,1)}), bf16[8,240,256]{2,1,0:T(8,128)(2,1)S(1)}, u32[]{:S(2)}, u32[]{:S(2)}) async-start(bf16[8,240,256]{2,1,0:T(8,128)(2,1)} %pad_maximum_fusion.1), calls=%async_computation.1 | async-start | bytes 1966080 | tf_op jit(solution)/shard_map/all_to_all | solution.py:260
  154.4 10.3 %collective-permute-start.12 = (bf16[4,224,128]{2,1,0:T(8,128)(2,1)S(1)}, bf16[4,224,128]{2,1,0:T(8,128)(2,1)S(1)}, u32[]{:S(2)}, u32[]{:S(2)}) collective-permute-start(bf16[4,224,128]{2,1,0:T(8,128)(2,1)S(1)} %pad_maximum_fusion.13), channel_id=1, source_target_pairs={{0,32},{16,48},{32,64},{48,80},{64,96},{80,112},{96,0},{112,16},{1... | collective-permute-start | bytes 688136 | tf_op jit(solution)/shard_map/ppermute | solution.py:41
  156.5 10.5 %collective-permute-start.14 = (bf16[4,224,128]{2,1,0:T(8,128)(2,1)S(1)}, bf16[4,224,128]{2,1,0:T(8,128)(2,1)S(1)}, u32[]{:S(2)}, u32[]{:S(2)}) collective-permute-start(bf16[4,224,128]{2,1,0:T(8,128)(2,1)S(1)} %pad_maximum_fusion.14), channel_id=1, source_target_pairs={{0,96},{16,112},{32,0},{48,16},{64,32},{80,48},{96,64},{112,80},{1... | collective-permute-start | bytes 688136 | tf_op jit(solution)/shard_map/ppermute | solution.py:41
  164.8 34.5 %copy-start.1 = (bf16[128,448]{0,1:T(8,128)(2,1)S(1)}, bf16[128,448]{0,1:T(8,128)(2,1)}, u32[]{:S(2)}) copy-start(bf16[128,448]{0,1:T(8,128)(2,1)} %param.7) | copy-start | bytes 344068
  164.8 9.6 %collective-permute-start.13 = (bf16[4,224,128]{2,1,0:T(8,128)(2,1)S(1)}, bf16[4,224,128]{2,1,0:T(8,128)(2,1)S(1)}, u32[]{:S(2)}, u32[]{:S(2)}) collective-permute-start(bf16[4,224,128]{2,1,0:T(8,128)(2,1)S(1)} %add_convert_fusion.2), channel_id=1, source_target_pairs={{0,32},{16,48},{32,64},{48,80},{64,96},{80,112},{96,0},{112,16},{1... | collective-permute-start | bytes 688136 | tf_op jit(solution)/shard_map/ppermute | solution.py:41
  174.5 14.2 %collective-permute-start.15 = (bf16[224,128]{1,0:T(8,128)(2,1)S(1)}, bf16[224,128]{1,0:T(8,128)(2,1)S(1)}, u32[]{:S(2)}, u32[]{:S(2)}) collective-permute-start(bf16[224,128]{1,0:T(8,128)(2,1)S(1)} %get-tuple-element.60), channel_id=1, source_target_pairs={{0,0},{1,1},{2,2},{3,3},{4,4},{5,5},{6,6},{7,7},{8,256},{9,257},{1... | collective-permute-start | bytes 172040 | tf_op jit(solution)/shard_map/ppermute | solution.py:53
  175.2 13.5 %collective-permute-start.18 = (bf16[224,128]{1,0:T(8,128)(2,1)S(1)}, bf16[224,128]{1,0:T(8,128)(2,1)S(1)}, u32[]{:S(2)}, u32[]{:S(2)}) collective-permute-start(bf16[224,128]{1,0:T(8,128)(2,1)S(1)} %get-tuple-element.61), channel_id=1, source_target_pairs={{0,136},{1,137},{2,138},{3,139},{4,140},{5,141},{6,142},{7,143},{8... | collective-permute-start | bytes 172040 | tf_op jit(solution)/shard_map/ppermute | solution.py:53
  182.5 6.1 %collective-permute-start.17 = (bf16[224,128]{1,0:T(8,128)(2,1)S(1)}, bf16[224,128]{1,0:T(8,128)(2,1)S(1)}, u32[]{:S(2)}, u32[]{:S(2)}) collective-permute-start(bf16[224,128]{1,0:T(8,128)(2,1)S(1)} %get-tuple-element.62), channel_id=1, source_target_pairs={{0,8},{1,9},{2,10},{3,11},{4,12},{5,13},{6,14},{7,15},{8,264},{9,2... | collective-permute-start | bytes 172040 | tf_op jit(solution)/shard_map/ppermute | solution.py:53
  185.5 6.7 %collective-permute-start.16 = (bf16[224,128]{1,0:T(8,128)(2,1)S(1)}, bf16[224,128]{1,0:T(8,128)(2,1)S(1)}, u32[]{:S(2)}, u32[]{:S(2)}) collective-permute-start(bf16[224,128]{1,0:T(8,128)(2,1)S(1)} %get-tuple-element.63), channel_id=1, source_target_pairs={{0,128},{1,129},{2,130},{3,131},{4,132},{5,133},{6,134},{7,135},{8... | collective-permute-start | bytes 172040 | tf_op jit(solution)/shard_map/ppermute | solution.py:53
  193.1 6.3 %collective-permute-start.11 = (f32[224,128]{1,0:T(8,128)S(1)}, f32[224,128]{1,0:T(8,128)S(1)}, u32[]{:S(2)}, u32[]{:S(2)}) collective-permute-start(f32[224,128]{1,0:T(8,128)S(1)} %get-tuple-element.58), channel_id=1, source_target_pairs={{0,16},{16,0},{32,48},{48,32},{64,80},{80,64},{96,112},{112,96},{1... | collective-permute-start | bytes 344072 | tf_op jit(solution)/shard_map/ppermute | solution.py:24
Sparse Core Ops, SparseCore 0:
  20.0 38.9 all-gather.2

commit v11 on v10

--- a/solution.py
+++ b/solution.py
@@ -70,10 +70,9 @@
     return lax.dynamic_slice_in_dim(line, X_COUNT - 1 - place, X_COUNT, 1)
 
 
-def ring_scatter_x(part, across):
-    ahead = part(1).astype(f32) + shift_x(across, 1).astype(f32)
-    up, down = shift_x(ahead.astype(bf16), 1), shift_x(part(-1), -1)
-    return part(0).astype(f32) + up.astype(f32) + down.astype(f32)
+def scatter_x(part, across):
+    total = part(0).astype(f32) + shift_x(across, 2).astype(f32)
+    return total + shift_x(part(1), 1).astype(f32) + shift_x(part(-1), -1).astype(f32)
 
 
 def scatter_y(parts, place):
@@ -94,7 +93,7 @@
 
 def split(x):
     high = lax.reduce_precision(x, 8, 7)
-    return high.astype(bf16), (x - high).astype(bf16)
+    return high.astype(bf16), lax.reduce_precision(x - high, 8, 7).astype(bf16)
 
 
 def dot(a, b, dims):
@@ -150,21 +149,30 @@
     slice_f = hidden_t.astype(f32)
     mean_part = jnp.mean(slice_f, axis=0)
     stats = jnp.stack([mean_part, jnp.sum((slice_f - mean_part) ** 2, axis=0)])
-    block, stats = lax.optimization_barrier((block, stats))
-    stats = lax.all_to_all(
-        jnp.broadcast_to(stats[None], (n_tensor, 2, SEQ)), "tensor", 0, 0, tiled=True
+    stats_far = swap_far(stats)
+    gap = stats[0] - stats_far[0]
+    stats = jnp.stack(
+        [
+            0.5 * (stats[0] + stats_far[0]),
+            stats[1] + stats_far[1] + gap * gap * (width / 2),
+        ]
     )
-    weight_block, stats = lax.optimization_barrier((weight_block, stats))
+    stats = jnp.concatenate([stats, swap_cores(stats)], axis=1).reshape(1, 4 * SEQ)
+    high, low = split(stats)
+    lower = (stats - high.astype(f32) - low.astype(f32)).astype(bf16)
+    block = jnp.concatenate([block, high, low, lower, jnp.zeros((13, 4 * SEQ), bf16)])
+
+    weight_block, block = lax.optimization_barrier((weight_block, block))
+    rows = lax.all_gather(block, "tensor", axis=0, axis_index_groups=rings)
     column = lax.all_gather(weight_block, "dp", axis=0, axis_index_groups=lines)
-    mean = jnp.mean(stats[:, 0], axis=0)
-    square = jnp.sum(stats[:, 1], axis=0) + width * jnp.sum((stats[:, 0] - mean) ** 2, axis=0)
-    stats = jnp.stack([mean, lax.rsqrt(square / depth + norm_eps)])
-    mean, inv_std = jnp.concatenate([stats, swap_cores(stats)], axis=1)
-
-    rows = lax.all_gather(block, "tensor", axis=0, tiled=True, axis_index_groups=rings)
     blocks, rows = x_gather(column, x, rows)
-    hidden = rows[:, : 2 * SEQ].astype(f32)
-    grads = rows[:, 2 * SEQ :]
+    hidden = rows[:, :part, : 2 * SEQ].reshape(quarter, 2 * SEQ).astype(f32)
+    grads = rows[:, :part, 2 * SEQ :].reshape(quarter, 2 * SEQ)
+    stats = jnp.sum(rows[:, part : part + 3].astype(f32), axis=1)
+    mean = jnp.mean(stats[:, : 2 * SEQ], axis=0)
+    gap = stats[:, : 2 * SEQ] - mean
+    square = jnp.sum(stats[:, 2 * SEQ :], axis=0) + 2 * width * jnp.sum(gap * gap, axis=0)
+    inv_std = lax.rsqrt(square / depth + norm_eps)
 
     def own_part(vector):
         vector = vector.reshape(2, Z_COUNT, 2, part)
@@ -259,7 +267,7 @@
     payload = jnp.concatenate([group_part.reshape(Z_COUNT, part, 2 * SEQ), extra], axis=1)
     group_parts = lax.all_to_all(payload, "tensor", 0, 0, tiled=True, axis_index_groups=rings)
     total = jnp.sum(group_parts.astype(f32), axis=0)
-    weight_parts = ring_scatter_x(weight_to, across)
+    weight_parts = scatter_x(weight_to, across)
     grad_out_weight = scatter_y(weight_parts, y)
     sums = total[part : part + 2, :SEQ] + total[part + 2 : part + 4, :SEQ]
     total = total[:part]

time: 208 us -> 204 us (0.981)
  waiting for transfers between devices: 63.9 us -> 52.2 us
  blocking collectives: 17.2 us -> 24.9 us
  starting transfers between devices: 88.4 us -> 85.6 us
  local copies, waits for them, and re-layouts: 4.08 us -> 6.88 us
    ppermute x2 -> x3, starting transfers between devices: 4.92 us -> 22.8 us  [swap_far(): return lax.ppermute(x, 'tensor', [(i, (i + Z_COUNT) % n) for i in range(n)])]
    ppermute x5, starting transfers between devices: 33.7 us -> 20.3 us  [swap_cores(): return lax.ppermute(x, 'dp', [(i, i ^ 1) for i in range(n)])]
    all_to_all x1 -> x0, starting transfers between devices: 11.3 us -> none  [body(): lax.all_to_all(jnp.broadcast_to(stats[None], (n_tensor, 2, SEQ)), 'tensor...]
    all_to_all x1 -> x0, waiting for transfers between devices: 11 us -> none  [body(): lax.all_to_all(jnp.broadcast_to(stats[None], (n_tensor, 2, SEQ)), 'tensor...]
    all_gather x1, blocking collectives: 17.2 us -> 24.9 us  [body(): column = lax.all_gather(weight_block, 'dp', axis=0, axis_index_groups=lines)]
    ppermute x2 -> x3, waiting for transfers between devices: 17.9 us -> 13.2 us  [swap_far(): return lax.ppermute(x, 'tensor', [(i, (i + Z_COUNT) % n) for i in range(n)])]
    ppermute x7, waiting for transfers between devices: 28.3 us -> 31.9 us  [shift_x(): lax.ppermute(x, 'dp', [(i, i - i % row + (i + 2 * step) % row) for i in r...]
    ppermute x5, starting transfers between devices: 14.7 us -> 17.7 us  [along_y(): return lax.ppermute(x, ('dp', 'tensor'), pairs)]
  transfers between devices with their start and end apart: 22 -> 22, of which waited for: 14 -> 13; matrix products, arithmetic and copies ran while one was open for 4% -> 5% of each run, Pallas kernels for 0% -> 0%
where the time goes in v11:
time: 204 us; the launch traced here: 203 us
  starting transfers between devices  85.6 us (42%)
  waiting for transfers between devices  52.2 us (26%)
  blocking collectives  24.9 us (12%)
  between operations  15.3 us (8%)
  other arithmetic  9.88 us (5%)
  matrix products  7.83 us (4%)
  local copies, waits for them, and re-layouts  6.88 us (3%)
    ppermute x7, waiting for transfers between devices, shift_x(): lax.ppermute(x, 'dp', [(i, i - i % row + (i + 2 * step) % row) for i in r...  31.9 us
    all_gather x1, blocking collectives, body(): column = lax.all_gather(weight_block, 'dp', axis=0, axis_index_groups=lines)  24.9 us
    ppermute x3, starting transfers between devices, swap_far(): return lax.ppermute(x, 'tensor', [(i, (i + Z_COUNT) % n) for i in range(n)])  22.8 us
    ppermute x5, starting transfers between devices, swap_cores(): return lax.ppermute(x, 'dp', [(i, i ^ 1) for i in range(n)])  20.3 us
    ppermute x7, starting transfers between devices, shift_x(): lax.ppermute(x, 'dp', [(i, i - i % row + (i + 2 * step) % row) for i in r...  19.5 us
    ppermute x5, starting transfers between devices, along_y(): return lax.ppermute(x, ('dp', 'tensor'), pairs)  17.7 us
    ppermute x3, waiting for transfers between devices, swap_far(): return lax.ppermute(x, 'tensor', [(i, (i + Z_COUNT) % n) for i in range(n)])  13.2 us
    dot_general x26, matrix products, dot(): return lax.dot_general(a, b, (dims, ((), ())), preferred_element_type=f32)  7.83 us
  transfers between devices with their start and end apart: 22, of which 13 were waited for; matrix products, arithmetic and copies ran while one was open for 5% of the time, Pallas kernels for 0%

profile of v11, /device:TPU:1, one launch (start us, length us, event | category | flops | bytes accessed | tf_op | source)
XLA Modules:
  0.0 202.7 jit_solution(17378466453978332080)
XLA Ops:
  7.2 1.0 convert_reduce_fusion.1
  8.2 1.0 fusion.31
  9.2 8.3 %collective-permute-start.2 = (f32[2,128]{1,0:T(2,128)S(1)}, f32[2,128]{1,0:T(2,128)S(1)}, u32[]{:S(2)}, u32[]{:S(2)}) collective-permute-start(f32[2,128]{1,0:T(2,128)S(1)} %pad_maximum_fusion.21), channel_id=1, source_target_pairs={{0,8},{1,9},{2,10},{3,11},{4,12},{5,13},{6,14},{7,15},{8,0},{9,1},... | collective-permute-start | bytes 3080 | tf_op jit(solution)/shard_map/ppermute | solution.py:35
  17.5 1.0 broadcast_select_fusion.1
  18.5 2.9 %collective-permute-start.1 = (bf16[224,256]{1,0:T(8,128)(2,1)S(1)}, bf16[224,256]{1,0:T(8,128)(2,1)S(1)}, u32[]{:S(2)}, u32[]{:S(2)}) collective-permute-start(bf16[224,256]{1,0:T(8,128)(2,1)S(1)} %get-tuple-element.67), channel_id=1, source_target_pairs={{0,16},{16,0},{32,48},{48,32},{64,80},{80,64},{96,112},{112,96},{1... | collective-permute-start | bytes 344072 | tf_op jit(solution)/shard_map/ppermute | solution.py:24
  21.4 1.0 pad_maximum_fusion.11
  22.4 0.7 collective-permute-start
  23.1 4.3 %collective-permute-start.3 = (f32[2,128]{1,0:T(2,128)S(1)}, f32[2,128]{1,0:T(2,128)S(1)}, u32[]{:S(2)}, u32[]{:S(2)}) collective-permute-start(f32[2,128]{1,0:T(2,128)S(1)} %pad_maximum_fusion.22), channel_id=1, source_target_pairs={{0,16},{16,0},{32,48},{48,32},{64,80},{80,64},{96,112},{112,96},{1... | collective-permute-start | bytes 3080 | tf_op jit(solution)/shard_map/ppermute | solution.py:24
  27.4 0.8 collective-permute-done.3
  28.3 2.7 %concatenate.96 = bf16[240,512]{1,0:T(8,128)(2,1)} concatenate(bf16[224,512]{1,0:T(8,128)(2,1)S(1)} %pad_maximum_fusion.12, bf16[1,512]{1,0:T(2,128)(2,1)S(1)} %get-tuple-element.82, bf16[1,512]{1,0:T(2,128)(2,1)S(1)} %get-tuple-element.25, bf16[1,512]{1,0:T(2,128)(2,1)S(1)} %get-tuple-element.24, bf16[13,512]{1,0:T(8,128)(2,1)S(1)} %broadcast_in_dim.10), dimensions={0} | concatenate | bytes 491520 | tf_op jit(solution)/shard_map/concatenate | solution.py:163
  31.2 24.9 %all-gather = bf16[896,512]{1,0:T(8,128)(2,1)S(1)} all-gather(bf16[224,512]{1,0:T(8,128)(2,1)S(1)} %collective-permute-done), channel_id=2, replica_groups={{0,128,256,384},{16,144,272,400},{32,160,288,416},{48,176,304,432},{64,..., dimensions={0}, use_global_device_ids=true | all-gather | bytes 1146880 | tf_op jit(solution)/shard_map/all_gather | solution.py:167
  56.1 3.5 %collective-permute-start.5 = (bf16[4,224,512]{2,1,0:T(8,128)(2,1)S(1)}, bf16[4,224,512]{2,1,0:T(8,128)(2,1)S(1)}, u32[]{:S(2)}, u32[]{:S(2)}) collective-permute-start(bf16[4,224,512]{2,1,0:T(8,128)(2,1)S(1)} %bitcast.171), channel_id=1, source_target_pairs={{0,96},{16,112},{32,0},{48,16},{64,32},{80,48},{96,64},{112,80},{1... | collective-permute-start | bytes 2752520 | tf_op jit(solution)/shard_map/ppermute | solution.py:41
  59.7 1.9 collective-permute-start.4
  62.7 15.7 %collective-permute-done.5 = bf16[4,224,512]{2,1,0:T(8,128)(2,1)S(1)} collective-permute-done((bf16[4,224,512]{2,1,0:T(8,128)(2,1)S(1)}, bf16[4,224,512]{2,1,0:T(8,128)(2,1)S(1)}, u32[]{:S(2)}, u32[]{:S(2)}) %collective-permute-start.5) | collective-permute-done | bytes 917536 | tf_op jit(solution)/shard_map/ppermute | solution.py:41
  78.4 4.0 %collective-permute-done.4 = bf16[4,224,512]{2,1,0:T(8,128)(2,1)S(1)} collective-permute-done((bf16[4,224,512]{2,1,0:T(8,128)(2,1)S(1)}, bf16[4,224,512]{2,1,0:T(8,128)(2,1)S(1)}, u32[]{:S(2)}, u32[]{:S(2)}) %collective-permute-start.4) | collective-permute-done | bytes 917536 | tf_op jit(solution)/shard_map/ppermute | solution.py:41
  82.4 0.9 convert_reduce_fusion.2
  83.3 1.6 fusion.94
  85.0 0.5 fusion.4
  87.2 1.9 collective-permute-start.7
  89.2 3.4 %collective-permute-start.6 = (bf16[2,224,512]{2,1,0:T(8,128)(2,1)S(1)}, bf16[2,224,512]{2,1,0:T(8,128)(2,1)S(1)}, u32[]{:S(2)}, u32[]{:S(2)}) collective-permute-start(bf16[2,224,512]{2,1,0:T(8,128)(2,1)S(1)} %get-tuple-element.36), channel_id=1, source_target_pairs={{0,32},{16,48},{32,64},{48,80},{64,96},{80,112},{96,0},{112,16},{1... | collective-permute-start | bytes 1376264 | tf_op jit(solution)/shard_map/ppermute | solution.py:41
  95.0 3.0 %collective-permute-done.7 = bf16[2,224,512]{2,1,0:T(8,128)(2,1)S(1)} collective-permute-done((bf16[2,224,512]{2,1,0:T(8,128)(2,1)S(1)}, bf16[2,224,512]{2,1,0:T(8,128)(2,1)S(1)}, u32[]{:S(2)}, u32[]{:S(2)}) %collective-permute-start.7) | collective-permute-done | bytes 458784 | tf_op jit(solution)/shard_map/ppermute | solution.py:41
  98.3 2.3 %collective-permute-done.6 = bf16[2,224,512]{2,1,0:T(8,128)(2,1)S(1)} collective-permute-done((bf16[2,224,512]{2,1,0:T(8,128)(2,1)S(1)}, bf16[2,224,512]{2,1,0:T(8,128)(2,1)S(1)}, u32[]{:S(2)}, u32[]{:S(2)}) %collective-permute-start.6) | collective-permute-done | bytes 458784 | tf_op jit(solution)/shard_map/ppermute | solution.py:41
  101.8 6.5 %collective-permute-start.8 = (f32[2,136,512]{2,1,0:T(8,128)S(1)}, f32[2,136,512]{2,1,0:T(8,128)S(1)}, u32[]{:S(2)}, u32[]{:S(2)}) collective-permute-start(f32[2,136,512]{2,1,0:T(8,128)S(1)} %pad_maximum_fusion.3), channel_id=1, source_target_pairs={{0,16},{16,0},{32,48},{48,32},{64,80},{80,64},{96,112},{112,96},{1... | collective-permute-start | bytes 1671176 | tf_op jit(solution)/shard_map/ppermute | solution.py:24
  108.7 1.2 collective-permute-done.8
  110.1 6.3 %collective-permute-start.9 = (bf16[144,512]{1,0:T(8,128)(2,1)S(1)}, bf16[144,512]{1,0:T(8,128)(2,1)S(1)}, u32[]{:S(2)}, u32[]{:S(2)}) collective-permute-start(bf16[144,512]{1,0:T(8,128)(2,1)S(1)} %pad_maximum_fusion.16), channel_id=1, source_target_pairs={{0,8},{1,9},{2,10},{3,11},{4,12},{5,13},{6,14},{7,15},{8,0},{9,1},... | collective-permute-start | bytes 442376 | tf_op jit(solution)/shard_map/ppermute | solution.py:35
  116.6 6.4 %collective-permute-done.9 = bf16[144,512]{1,0:T(8,128)(2,1)S(1)} collective-permute-done((bf16[144,512]{1,0:T(8,128)(2,1)S(1)}, bf16[144,512]{1,0:T(8,128)(2,1)S(1)}, u32[]{:S(2)}, u32[]{:S(2)}) %collective-permute-start.9) | collective-permute-done | bytes 147488 | tf_op jit(solution)/shard_map/ppermute | solution.py:35
  124.5 8.2 %collective-permute-start.10 = (bf16[144,512]{1,0:T(8,128)(2,1)S(1)}, bf16[144,512]{1,0:T(8,128)(2,1)S(1)}, u32[]{:S(2)}, u32[]{:S(2)}) collective-permute-start(bf16[144,512]{1,0:T(8,128)(2,1)S(1)} %fusion.46), channel_id=1, source_target_pairs={{0,8},{1,9},{2,10},{3,11},{4,12},{5,13},{6,14},{7,15},{8,0},{9,1},... | collective-permute-start | bytes 442376 | tf_op jit(solution)/shard_map/ppermute | solution.py:35
  133.0 6.7 %collective-permute-done.10 = bf16[144,512]{1,0:T(8,128)(2,1)S(1)} collective-permute-done((bf16[144,512]{1,0:T(8,128)(2,1)S(1)}, bf16[144,512]{1,0:T(8,128)(2,1)S(1)}, u32[]{:S(2)}, u32[]{:S(2)}) %collective-permute-start.10) | collective-permute-done | bytes 147488 | tf_op jit(solution)/shard_map/ppermute | solution.py:35
  139.9 2.5 %collective-permute-start.11 = (bf16[2,144,512]{2,1,0:T(8,128)(2,1)S(1)}, bf16[2,144,512]{2,1,0:T(8,128)(2,1)S(1)}, u32[]{:S(2)}, u32[]{:S(2)}) collective-permute-start(bf16[2,144,512]{2,1,0:T(8,128)(2,1)S(1)} %fusion.22), channel_id=1, source_target_pairs={{0,16},{16,0},{32,48},{48,32},{64,80},{80,64},{96,112},{112,96},{1... | collective-permute-start | bytes 884744 | tf_op jit(solution)/shard_map/ppermute | solution.py:24
  142.9 0.7 collective-permute-done.11
  144.7 0.7 fusion.42
  145.4 0.7 fusion
  146.1 1.0 pad_maximum_fusion.1
  147.1 5.3 %all-to-all-start = ((bf16[8,240,256]{2,1,0:T(8,128)(2,1)}), bf16[8,240,256]{2,1,0:T(8,128)(2,1)S(1)}, u32[]{:S(2)}, u32[]{:S(2)}) async-start(bf16[8,240,256]{2,1,0:T(8,128)(2,1)} %pad_maximum_fusion.1), calls=%async_computation | async-start | bytes 1966080 | tf_op jit(solution)/shard_map/all_to_all | solution.py:268
  152.4 2.2 %collective-permute-start.13 = (bf16[4,224,128]{2,1,0:T(8,128)(2,1)S(1)}, bf16[4,224,128]{2,1,0:T(8,128)(2,1)S(1)}, u32[]{:S(2)}, u32[]{:S(2)}) collective-permute-start(bf16[4,224,128]{2,1,0:T(8,128)(2,1)S(1)} %pad_maximum_fusion.13), channel_id=1, source_target_pairs={{0,64},{16,80},{32,96},{48,112},{64,0},{80,16},{96,32},{112,48},{1... | collective-permute-start | bytes 688136 | tf_op jit(solution)/shard_map/ppermute | solution.py:41
  154.7 1.9 collective-permute-start.14
  156.7 4.6 %collective-permute-start.15 = (bf16[4,224,128]{2,1,0:T(8,128)(2,1)S(1)}, bf16[4,224,128]{2,1,0:T(8,128)(2,1)S(1)}, u32[]{:S(2)}, u32[]{:S(2)}) collective-permute-start(bf16[4,224,128]{2,1,0:T(8,128)(2,1)S(1)} %pad_maximum_fusion.15), channel_id=1, source_target_pairs={{0,96},{16,112},{32,0},{48,16},{64,32},{80,48},{96,64},{112,80},{1... | collective-permute-start | bytes 688136 | tf_op jit(solution)/shard_map/ppermute | solution.py:41
  161.4 1.0 collective-permute-done.13
  162.4 5.9 %collective-permute-done.14 = bf16[4,224,128]{2,1,0:T(8,128)(2,1)S(1)} collective-permute-done((bf16[4,224,128]{2,1,0:T(8,128)(2,1)S(1)}, bf16[4,224,128]{2,1,0:T(8,128)(2,1)S(1)}, u32[]{:S(2)}, u32[]{:S(2)}) %collective-permute-start.14) | collective-permute-done | bytes 229408 | tf_op jit(solution)/shard_map/ppermute | solution.py:41
  168.4 0.7 collective-permute-start.16
  169.1 8.6 %collective-permute-start.19 = (bf16[224,128]{1,0:T(8,128)(2,1)S(1)}, bf16[224,128]{1,0:T(8,128)(2,1)S(1)}, u32[]{:S(2)}, u32[]{:S(2)}) collective-permute-start(bf16[224,128]{1,0:T(8,128)(2,1)S(1)} %get-tuple-element.63), channel_id=1, source_target_pairs={{0,136},{1,137},{2,138},{3,139},{4,140},{5,141},{6,142},{7,143},{8... | collective-permute-start | bytes 172040 | tf_op jit(solution)/shard_map/ppermute | solution.py:53
  177.8 4.6 %collective-permute-start.18 = (bf16[224,128]{1,0:T(8,128)(2,1)S(1)}, bf16[224,128]{1,0:T(8,128)(2,1)S(1)}, u32[]{:S(2)}, u32[]{:S(2)}) collective-permute-start(bf16[224,128]{1,0:T(8,128)(2,1)S(1)} %get-tuple-element.64), channel_id=1, source_target_pairs={{0,8},{1,9},{2,10},{3,11},{4,12},{5,13},{6,14},{7,15},{8,264},{9,2... | collective-permute-start | bytes 172040 | tf_op jit(solution)/shard_map/ppermute | solution.py:53
  182.4 3.1 %collective-permute-start.17 = (bf16[224,128]{1,0:T(8,128)(2,1)S(1)}, bf16[224,128]{1,0:T(8,128)(2,1)S(1)}, u32[]{:S(2)}, u32[]{:S(2)}) collective-permute-start(bf16[224,128]{1,0:T(8,128)(2,1)S(1)} %get-tuple-element.65), channel_id=1, source_target_pairs={{0,128},{1,129},{2,130},{3,131},{4,132},{5,133},{6,134},{7,135},{8... | collective-permute-start | bytes 172040 | tf_op jit(solution)/shard_map/ppermute | solution.py:53
  185.6 3.5 %collective-permute-done.17 = bf16[224,128]{1,0:T(8,128)(2,1)S(1)} collective-permute-done((bf16[224,128]{1,0:T(8,128)(2,1)S(1)}, bf16[224,128]{1,0:T(8,128)(2,1)S(1)}, u32[]{:S(2)}, u32[]{:S(2)}) %collective-permute-start.17) | collective-permute-done | bytes 57376 | tf_op jit(solution)/shard_map/ppermute | solution.py:53
  189.1 0.7 add_bitcast_fusion
  190.0 4.1 %collective-permute-start.12 = (f32[224,128]{1,0:T(8,128)S(1)}, f32[224,128]{1,0:T(8,128)S(1)}, u32[]{:S(2)}, u32[]{:S(2)}) collective-permute-start(f32[224,128]{1,0:T(8,128)S(1)} %get-tuple-element.60), channel_id=1, source_target_pairs={{0,16},{16,0},{32,48},{48,32},{64,80},{80,64},{96,112},{112,96},{1... | collective-permute-start | bytes 344072 | tf_op jit(solution)/shard_map/ppermute | solution.py:24
  194.1 0.9 collective-permute-done.12
  195.0 0.8 fusion.59
  (148 shorter events, 11.2 us)
Async XLA Ops:
  7.2 23.8 %copy-start.2 = (f32[7168]{0:T(1024)S(1)}, f32[7168]{0:T(1024)}, u32[]{:S(2)}) copy-start(f32[7168]{0:T(1024)} %param.9) | copy-start | bytes 86020
  7.2 23.9 %copy-start.1 = (f32[7168]{0:T(1024)S(1)}, f32[7168]{0:T(1024)}, u32[]{:S(2)}) copy-start(f32[7168]{0:T(1024)} %param.8) | copy-start | bytes 86020
  7.2 75.2 %all-gather.4.cloned.1.call-start = ((), (), s32[]{:S(2)}) async-start(), calls=%async_computation.1 | async-start | bytes 2211840 | tf_op jit(solution)/shard_map/all_gather | solution.py:166
  9.2 13.9 %collective-permute-start.2 = (f32[2,128]{1,0:T(2,128)S(1)}, f32[2,128]{1,0:T(2,128)S(1)}, u32[]{:S(2)}, u32[]{:S(2)}) collective-permute-start(f32[2,128]{1,0:T(2,128)S(1)} %pad_maximum_fusion.21), channel_id=1, source_target_pairs={{0,8},{1,9},{2,10},{3,11},{4,12},{5,13},{6,14},{7,15},{8,0},{9,1},... | collective-permute-start | bytes 3080 | tf_op jit(solution)/shard_map/ppermute | solution.py:35
  18.5 9.7 %collective-permute-start.1 = (bf16[224,256]{1,0:T(8,128)(2,1)S(1)}, bf16[224,256]{1,0:T(8,128)(2,1)S(1)}, u32[]{:S(2)}, u32[]{:S(2)}) collective-permute-start(bf16[224,256]{1,0:T(8,128)(2,1)S(1)} %get-tuple-element.67), channel_id=1, source_target_pairs={{0,16},{16,0},{32,48},{48,32},{64,80},{80,64},{96,112},{112,96},{1... | collective-permute-start | bytes 344072 | tf_op jit(solution)/shard_map/ppermute | solution.py:24
  22.4 8.6 %collective-permute-start = (bf16[224,512]{1,0:T(8,128)(2,1)S(1)}, bf16[224,512]{1,0:T(8,128)(2,1)S(1)}, u32[]{:S(2)}, u32[]{:S(2)}) collective-permute-start(bf16[224,512]{1,0:T(8,128)(2,1)S(1)} %pad_maximum_fusion.11), channel_id=1, source_target_pairs={{0,0},{1,1},{2,2},{3,3},{4,4},{5,5},{6,6},{7,7},{8,256},{9,257},{1... | collective-permute-start | bytes 688136 | tf_op jit(solution)/shard_map/ppermute | solution.py:53
  23.1 5.1 %collective-permute-start.3 = (f32[2,128]{1,0:T(2,128)S(1)}, f32[2,128]{1,0:T(2,128)S(1)}, u32[]{:S(2)}, u32[]{:S(2)}) collective-permute-start(f32[2,128]{1,0:T(2,128)S(1)} %pad_maximum_fusion.22), channel_id=1, source_target_pairs={{0,16},{16,0},{32,48},{48,32},{64,80},{80,64},{96,112},{112,96},{1... | collective-permute-start | bytes 3080 | tf_op jit(solution)/shard_map/ppermute | solution.py:24
  56.1 22.3 %collective-permute-start.5 = (bf16[4,224,512]{2,1,0:T(8,128)(2,1)S(1)}, bf16[4,224,512]{2,1,0:T(8,128)(2,1)S(1)}, u32[]{:S(2)}, u32[]{:S(2)}) collective-permute-start(bf16[4,224,512]{2,1,0:T(8,128)(2,1)S(1)} %bitcast.171), channel_id=1, source_target_pairs={{0,96},{16,112},{32,0},{48,16},{64,32},{80,48},{96,64},{112,80},{1... | collective-permute-start | bytes 2752520 | tf_op jit(solution)/shard_map/ppermute | solution.py:41
  59.7 22.7 %collective-permute-start.4 = (bf16[4,224,512]{2,1,0:T(8,128)(2,1)S(1)}, bf16[4,224,512]{2,1,0:T(8,128)(2,1)S(1)}, u32[]{:S(2)}, u32[]{:S(2)}) collective-permute-start(bf16[4,224,512]{2,1,0:T(8,128)(2,1)S(1)} %bitcast.172), channel_id=1, source_target_pairs={{0,32},{16,48},{32,64},{48,80},{64,96},{80,112},{96,0},{112,16},{1... | collective-permute-start | bytes 2752520 | tf_op jit(solution)/shard_map/ppermute | solution.py:41
  84.9 100.6 %copy-start.3 = (f32[256]{0:T(256)}, f32[256]{0:T(256)S(1)}, u32[]{:S(2)}) copy-start(f32[256]{0:T(256)S(1)} %broadcast_multiply_fusion) | copy-start | bytes 3076
  85.0 100.6 %copy-start.4 = (f32[256]{0:T(256)}, f32[256]{0:T(256)S(1)}, u32[]{:S(2)}) copy-start(f32[256]{0:T(256)S(1)} %add_rsqrt_fusion) | copy-start | bytes 3076
  87.2 10.7 %collective-permute-start.7 = (bf16[2,224,512]{2,1,0:T(8,128)(2,1)S(1)}, bf16[2,224,512]{2,1,0:T(8,128)(2,1)S(1)}, u32[]{:S(2)}, u32[]{:S(2)}) collective-permute-start(bf16[2,224,512]{2,1,0:T(8,128)(2,1)S(1)} %get-tuple-element.35), channel_id=1, source_target_pairs={{0,96},{16,112},{32,0},{48,16},{64,32},{80,48},{96,64},{112,80},{1... | collective-permute-start | bytes 1376264 | tf_op jit(solution)/shard_map/ppermute | solution.py:41
  89.2 11.4 %collective-permute-start.6 = (bf16[2,224,512]{2,1,0:T(8,128)(2,1)S(1)}, bf16[2,224,512]{2,1,0:T(8,128)(2,1)S(1)}, u32[]{:S(2)}, u32[]{:S(2)}) collective-permute-start(bf16[2,224,512]{2,1,0:T(8,128)(2,1)S(1)} %get-tuple-element.36), channel_id=1, source_target_pairs={{0,32},{16,48},{32,64},{48,80},{64,96},{80,112},{96,0},{112,16},{1... | collective-permute-start | bytes 1376264 | tf_op jit(solution)/shard_map/ppermute | solution.py:41
  101.8 8.1 %collective-permute-start.8 = (f32[2,136,512]{2,1,0:T(8,128)S(1)}, f32[2,136,512]{2,1,0:T(8,128)S(1)}, u32[]{:S(2)}, u32[]{:S(2)}) collective-permute-start(f32[2,136,512]{2,1,0:T(8,128)S(1)} %pad_maximum_fusion.3), channel_id=1, source_target_pairs={{0,16},{16,0},{32,48},{48,32},{64,80},{80,64},{96,112},{112,96},{1... | collective-permute-start | bytes 1671176 | tf_op jit(solution)/shard_map/ppermute | solution.py:24
  110.0 13.1 %copy-start.5 = (f32[384]{0:T(512)S(1)}, f32[384]{0:T(512)}, u32[]{:S(2)}) copy-start(f32[384]{0:T(512)} %param.11) | copy-start | bytes 4612
  110.1 12.9 %collective-permute-start.9 = (bf16[144,512]{1,0:T(8,128)(2,1)S(1)}, bf16[144,512]{1,0:T(8,128)(2,1)S(1)}, u32[]{:S(2)}, u32[]{:S(2)}) collective-permute-start(bf16[144,512]{1,0:T(8,128)(2,1)S(1)} %pad_maximum_fusion.16), channel_id=1, source_target_pairs={{0,8},{1,9},{2,10},{3,11},{4,12},{5,13},{6,14},{7,15},{8,0},{9,1},... | collective-permute-start | bytes 442376 | tf_op jit(solution)/shard_map/ppermute | solution.py:35
  124.5 15.2 %collective-permute-start.10 = (bf16[144,512]{1,0:T(8,128)(2,1)S(1)}, bf16[144,512]{1,0:T(8,128)(2,1)S(1)}, u32[]{:S(2)}, u32[]{:S(2)}) collective-permute-start(bf16[144,512]{1,0:T(8,128)(2,1)S(1)} %fusion.46), channel_id=1, source_target_pairs={{0,8},{1,9},{2,10},{3,11},{4,12},{5,13},{6,14},{7,15},{8,0},{9,1},... | collective-permute-start | bytes 442376 | tf_op jit(solution)/shard_map/ppermute | solution.py:35
  139.9 3.7 %collective-permute-start.11 = (bf16[2,144,512]{2,1,0:T(8,128)(2,1)S(1)}, bf16[2,144,512]{2,1,0:T(8,128)(2,1)S(1)}, u32[]{:S(2)}, u32[]{:S(2)}) collective-permute-start(bf16[2,144,512]{2,1,0:T(8,128)(2,1)S(1)} %fusion.22), channel_id=1, source_target_pairs={{0,16},{16,0},{32,48},{48,32},{64,80},{80,64},{96,112},{112,96},{1... | collective-permute-start | bytes 884744 | tf_op jit(solution)/shard_map/ppermute | solution.py:24
  147.1 42.7 %all-to-all-start = ((bf16[8,240,256]{2,1,0:T(8,128)(2,1)}), bf16[8,240,256]{2,1,0:T(8,128)(2,1)S(1)}, u32[]{:S(2)}, u32[]{:S(2)}) async-start(bf16[8,240,256]{2,1,0:T(8,128)(2,1)} %pad_maximum_fusion.1), calls=%async_computation | async-start | bytes 1966080 | tf_op jit(solution)/shard_map/all_to_all | solution.py:268
  152.4 9.9 %collective-permute-start.13 = (bf16[4,224,128]{2,1,0:T(8,128)(2,1)S(1)}, bf16[4,224,128]{2,1,0:T(8,128)(2,1)S(1)}, u32[]{:S(2)}, u32[]{:S(2)}) collective-permute-start(bf16[4,224,128]{2,1,0:T(8,128)(2,1)S(1)} %pad_maximum_fusion.13), channel_id=1, source_target_pairs={{0,64},{16,80},{32,96},{48,112},{64,0},{80,16},{96,32},{112,48},{1... | collective-permute-start | bytes 688136 | tf_op jit(solution)/shard_map/ppermute | solution.py:41
  154.7 13.5 %collective-permute-start.14 = (bf16[4,224,128]{2,1,0:T(8,128)(2,1)S(1)}, bf16[4,224,128]{2,1,0:T(8,128)(2,1)S(1)}, u32[]{:S(2)}, u32[]{:S(2)}) collective-permute-start(bf16[4,224,128]{2,1,0:T(8,128)(2,1)S(1)} %pad_maximum_fusion.14), channel_id=1, source_target_pairs={{0,32},{16,48},{32,64},{48,80},{64,96},{80,112},{96,0},{112,16},{1... | collective-permute-start | bytes 688136 | tf_op jit(solution)/shard_map/ppermute | solution.py:41
  156.7 11.6 %collective-permute-start.15 = (bf16[4,224,128]{2,1,0:T(8,128)(2,1)S(1)}, bf16[4,224,128]{2,1,0:T(8,128)(2,1)S(1)}, u32[]{:S(2)}, u32[]{:S(2)}) collective-permute-start(bf16[4,224,128]{2,1,0:T(8,128)(2,1)S(1)} %pad_maximum_fusion.15), channel_id=1, source_target_pairs={{0,96},{16,112},{32,0},{48,16},{64,32},{80,48},{96,64},{112,80},{1... | collective-permute-start | bytes 688136 | tf_op jit(solution)/shard_map/ppermute | solution.py:41
  168.3 26.8 %copy-start = (bf16[128,448]{0,1:T(8,128)(2,1)S(1)}, bf16[128,448]{0,1:T(8,128)(2,1)}, u32[]{:S(2)}) copy-start(bf16[128,448]{0,1:T(8,128)(2,1)} %param.7) | copy-start | bytes 344068
  168.4 17.2 %collective-permute-start.16 = (bf16[224,128]{1,0:T(8,128)(2,1)S(1)}, bf16[224,128]{1,0:T(8,128)(2,1)S(1)}, u32[]{:S(2)}, u32[]{:S(2)}) collective-permute-start(bf16[224,128]{1,0:T(8,128)(2,1)S(1)} %get-tuple-element.62), channel_id=1, source_target_pairs={{0,0},{1,1},{2,2},{3,3},{4,4},{5,5},{6,6},{7,7},{8,256},{9,257},{1... | collective-permute-start | bytes 172040 | tf_op jit(solution)/shard_map/ppermute | solution.py:53
  169.1 16.5 %collective-permute-start.19 = (bf16[224,128]{1,0:T(8,128)(2,1)S(1)}, bf16[224,128]{1,0:T(8,128)(2,1)S(1)}, u32[]{:S(2)}, u32[]{:S(2)}) collective-permute-start(bf16[224,128]{1,0:T(8,128)(2,1)S(1)} %get-tuple-element.63), channel_id=1, source_target_pairs={{0,136},{1,137},{2,138},{3,139},{4,140},{5,141},{6,142},{7,143},{8... | collective-permute-start | bytes 172040 | tf_op jit(solution)/shard_map/ppermute | solution.py:53
  177.8 7.9 %collective-permute-start.18 = (bf16[224,128]{1,0:T(8,128)(2,1)S(1)}, bf16[224,128]{1,0:T(8,128)(2,1)S(1)}, u32[]{:S(2)}, u32[]{:S(2)}) collective-permute-start(bf16[224,128]{1,0:T(8,128)(2,1)S(1)} %get-tuple-element.64), channel_id=1, source_target_pairs={{0,8},{1,9},{2,10},{3,11},{4,12},{5,13},{6,14},{7,15},{8,264},{9,2... | collective-permute-start | bytes 172040 | tf_op jit(solution)/shard_map/ppermute | solution.py:53
  182.4 6.7 %collective-permute-start.17 = (bf16[224,128]{1,0:T(8,128)(2,1)S(1)}, bf16[224,128]{1,0:T(8,128)(2,1)S(1)}, u32[]{:S(2)}, u32[]{:S(2)}) collective-permute-start(bf16[224,128]{1,0:T(8,128)(2,1)S(1)} %get-tuple-element.65), channel_id=1, source_target_pairs={{0,128},{1,129},{2,130},{3,131},{4,132},{5,133},{6,134},{7,135},{8... | collective-permute-start | bytes 172040 | tf_op jit(solution)/shard_map/ppermute | solution.py:53
  185.6 9.5 %slice-start = ((f32[256]{0:T(256)}), f32[128]{0:T(128)S(1)}, s32[]{:S(2)}) async-start(f32[256]{0:T(256)} %copy-done.3), calls=%async_computation.2 | async-start | bytes 1024 | tf_op jit(solution)/shard_map/slice | solution.py:286
  185.6 9.5 %slice-start.1 = ((f32[256]{0:T(256)}), f32[128]{0:T(128)S(1)}, s32[]{:S(2)}) async-start(f32[256]{0:T(256)} %copy-done.4), calls=%async_computation.3 | async-start | bytes 1024 | tf_op jit(solution)/shard_map/slice | solution.py:287
  190.0 5.1 %collective-permute-start.12 = (f32[224,128]{1,0:T(8,128)S(1)}, f32[224,128]{1,0:T(8,128)S(1)}, u32[]{:S(2)}, u32[]{:S(2)}) collective-permute-start(f32[224,128]{1,0:T(8,128)S(1)} %get-tuple-element.60), channel_id=1, source_target_pairs={{0,16},{16,0},{32,48},{48,32},{64,80},{80,64},{96,112},{112,96},{1... | collective-permute-start | bytes 344072 | tf_op jit(solution)/shard_map/ppermute | solution.py:24
Sparse Core Ops, SparseCore 0:
  31.1 47.5 all-gather.3

commit v12 on v11

--- a/solution.py
+++ b/solution.py
@@ -57,12 +57,21 @@
     return along_y(x, lambda half, place: (place // 2, 2 * half + place % 2))
 
 
-def x_gather(own, place, early):
-    middle = own.shape[0] // 2
-    up, down = shift_x(own, 1), shift_x(own, -1)
-    up, down, early = lax.optimization_barrier((up, down, early))
-    across = jnp.concatenate([shift_x(up[:middle], 1), shift_x(down[middle:], -1)])
-    return [own, down, across, up], early
+def gather_both(block, column, place):
+    count = Z_COUNT
+    middle, half = column.shape[0] // 2, block.shape[0] // 32 * 16
+    x_up, x_down = shift_x(column, 1), shift_x(column, -1)
+    found = {0: block}
+    up = down = block
+    for step in range(1, count // 2):
+        up, down = shift_z(up, 1), shift_z(down, -1)
+        found[step], found[count - step] = up, down
+    x_up, x_down, up, down = lax.optimization_barrier((x_up, x_down, up, down))
+    x_across = jnp.concatenate([shift_x(x_up[:middle], 1), shift_x(x_down[middle:], -1)])
+    found[count // 2] = jnp.concatenate([shift_z(up[:half], 1), shift_z(down[half:], -1)])
+    blocks = [found[count - 1 - j] for j in range(count)]
+    rows = lax.dynamic_slice_in_dim(jnp.stack(blocks + blocks[:-1]), count - 1 - place, count, 0)
+    return rows, [column, x_down, x_across, x_up]
 
 
 def in_order(blocks, place):
@@ -144,7 +153,9 @@
     other = swap_cores(jnp.where(core == 0, acts[1], acts[0]))
     block = jnp.concatenate([mine[:, :SEQ], other[:, :SEQ], mine[:, SEQ:], other[:, SEQ:]], axis=1)
 
-    weight_block = move_weights(jnp.concatenate([w_qkv, w_out.T], axis=1))
+    weight_block = jnp.concatenate([w_qkv, w_out.T], axis=1)
+    weight_block, hidden_t = lax.optimization_barrier((weight_block, hidden_t))
+    weight_block = move_weights(weight_block)
 
     slice_f = hidden_t.astype(f32)
     mean_part = jnp.mean(slice_f, axis=0)
@@ -163,9 +174,8 @@
     block = jnp.concatenate([block, high, low, lower, jnp.zeros((13, 4 * SEQ), bf16)])
 
     weight_block, block = lax.optimization_barrier((weight_block, block))
-    rows = lax.all_gather(block, "tensor", axis=0, axis_index_groups=rings)
     column = lax.all_gather(weight_block, "dp", axis=0, axis_index_groups=lines)
-    blocks, rows = x_gather(column, x, rows)
+    rows, blocks = gather_both(block, column, z)
     hidden = rows[:, :part, : 2 * SEQ].reshape(quarter, 2 * SEQ).astype(f32)
     grads = rows[:, :part, 2 * SEQ :].reshape(quarter, 2 * SEQ)
     stats = jnp.sum(rows[:, part : part + 3].astype(f32), axis=1)

time: 204 us -> 206 us (level)
  starting transfers between devices: 85.6 us -> 104 us
  between operations: 15.3 us -> 2.07 us
  waiting for transfers between devices: 52.2 us -> 43.7 us
  local copies, waits for them, and re-layouts: 6.88 us -> 9.58 us
    ppermute x0 -> x8, starting transfers between devices: none -> 27.1 us  [shift_z(): return lax.ppermute(x, 'tensor', pairs)]
    ppermute x7, waiting for transfers between devices: 31.9 us -> 7.27 us  [shift_x(): lax.ppermute(x, 'dp', [(i, i - i % row + (i + 2 * step) % row) for i in r...]
    ppermute x3, starting transfers between devices: 22.8 us -> 8.48 us  [swap_far(): return lax.ppermute(x, 'tensor', [(i, (i + Z_COUNT) % n) for i in range(n)])]
    ppermute x3, waiting for transfers between devices: 13.2 us -> 24.5 us  [swap_far(): return lax.ppermute(x, 'tensor', [(i, (i + Z_COUNT) % n) for i in range(n)])]
    ppermute x5, starting transfers between devices: 20.3 us -> 28.4 us  [swap_cores(): return lax.ppermute(x, 'dp', [(i, i ^ 1) for i in range(n)])]
    ppermute x0 -> x8, waiting for transfers between devices: none -> 8.08 us  [shift_z(): return lax.ppermute(x, 'tensor', pairs)]
    unnamed x17 -> x25, local copies, waits for them, and re-layouts: 0.48 us -> 6.35 us
    ppermute x5, waiting for transfers between devices: 3.5 us -> 0.44 us  [along_y(): return lax.ppermute(x, ('dp', 'tensor'), pairs)]
  transfers between devices with their start and end apart: 22 -> 29, of which waited for: 13 -> 13; matrix products, arithmetic and copies ran while one was open for 5% -> 10% of each run, Pallas kernels for 0% -> 0%
where the time goes in v12:
time: 206 us; the launch traced here: 205 us
  starting transfers between devices  104 us (50%)
  waiting for transfers between devices  43.7 us (21%)
  blocking collectives  26.5 us (13%)
  other arithmetic  10.7 us (5%)
  local copies, waits for them, and re-layouts  9.58 us (5%)
  matrix products  7.83 us (4%)
  between operations  2.07 us (1%)
    ppermute x5, starting transfers between devices, swap_cores(): return lax.ppermute(x, 'dp', [(i, i ^ 1) for i in range(n)])  28.4 us
    ppermute x8, starting transfers between devices, shift_z(): return lax.ppermute(x, 'tensor', pairs)  27.1 us
    all_gather x1, blocking collectives, body(): column = lax.all_gather(weight_block, 'dp', axis=0, axis_index_groups=lines)  26.5 us
    ppermute x3, waiting for transfers between devices, swap_far(): return lax.ppermute(x, 'tensor', [(i, (i + Z_COUNT) % n) for i in range(n)])  24.5 us
    ppermute x7, starting transfers between devices, shift_x(): lax.ppermute(x, 'dp', [(i, i - i % row + (i + 2 * step) % row) for i in r...  21.4 us
    ppermute x5, starting transfers between devices, along_y(): return lax.ppermute(x, ('dp', 'tensor'), pairs)  14.7 us
    ppermute x3, starting transfers between devices, swap_far(): return lax.ppermute(x, 'tensor', [(i, (i + Z_COUNT) % n) for i in range(n)])  8.48 us
    ppermute x8, waiting for transfers between devices, shift_z(): return lax.ppermute(x, 'tensor', pairs)  8.08 us
  transfers between devices with their start and end apart: 29, of which 13 were waited for; matrix products, arithmetic and copies ran while one was open for 10% of the time, Pallas kernels for 0%

profile of v12, /device:TPU:1, one launch (start us, length us, event | category | flops | bytes accessed | tf_op | source)
XLA Modules:
  0.0 204.5 jit_solution(16100823638673974220)
XLA Ops:
  0.6 1.0 broadcast_select_fusion.1
  1.7 8.8 %collective-permute-start.1 = (bf16[224,256]{1,0:T(8,128)(2,1)S(1)}, bf16[224,256]{1,0:T(8,128)(2,1)S(1)}, u32[]{:S(2)}, u32[]{:S(2)}) collective-permute-start(bf16[224,256]{1,0:T(8,128)(2,1)S(1)} %get-tuple-element.73), channel_id=1, source_target_pairs={{0,16},{16,0},{32,48},{48,32},{64,80},{80,64},{96,112},{112,96},{1... | collective-permute-start | bytes 344072 | tf_op jit(solution)/shard_map/ppermute | solution.py:24
  10.5 1.0 pad_maximum_fusion.11
  11.4 1.0 convert_reduce_fusion.1
  12.4 1.0 fusion.31
  13.4 2.1 %collective-permute-start.2 = (f32[2,128]{1,0:T(2,128)S(1)}, f32[2,128]{1,0:T(2,128)S(1)}, u32[]{:S(2)}, u32[]{:S(2)}) collective-permute-start(f32[2,128]{1,0:T(2,128)S(1)} %pad_maximum_fusion.21), channel_id=1, source_target_pairs={{0,8},{1,9},{2,10},{3,11},{4,12},{5,13},{6,14},{7,15},{8,0},{9,1},... | collective-permute-start | bytes 3080 | tf_op jit(solution)/shard_map/ppermute | solution.py:35
  18.1 3.6 %collective-permute-done.2 = f32[2,128]{1,0:T(2,128)S(1)} collective-permute-done((f32[2,128]{1,0:T(2,128)S(1)}, f32[2,128]{1,0:T(2,128)S(1)}, u32[]{:S(2)}, u32[]{:S(2)}) %collective-permute-start.2) | collective-permute-done | bytes 1056 | tf_op jit(solution)/shard_map/ppermute | solution.py:35
  21.8 3.0 %collective-permute-start.3 = (f32[2,128]{1,0:T(2,128)S(1)}, f32[2,128]{1,0:T(2,128)S(1)}, u32[]{:S(2)}, u32[]{:S(2)}) collective-permute-start(f32[2,128]{1,0:T(2,128)S(1)} %pad_maximum_fusion.22), channel_id=1, source_target_pairs={{0,16},{16,0},{32,48},{48,32},{64,80},{80,64},{96,112},{112,96},{1... | collective-permute-start | bytes 3080 | tf_op jit(solution)/shard_map/ppermute | solution.py:24
  26.0 1.9 collective-permute-start.9
  27.9 6.3 %collective-permute-start.4 = (bf16[240,512]{1,0:T(8,128)(2,1)S(1)}, bf16[240,512]{1,0:T(8,128)(2,1)}, u32[]{:S(2)}, u32[]{:S(2)}) collective-permute-start(bf16[240,512]{1,0:T(8,128)(2,1)S(1)} %concatenate.99), channel_id=1, source_target_pairs={{0,7},{1,0},{2,1},{3,2},{4,3},{5,4},{6,5},{7,6},{8,15},{9,8},{10,9... | collective-permute-start | bytes 737288 | tf_op jit(solution)/shard_map/ppermute | solution.py:30
  34.2 26.5 %all-gather = bf16[896,512]{1,0:T(8,128)(2,1)S(1)} all-gather(bf16[224,512]{1,0:T(8,128)(2,1)S(1)} %collective-permute-done), channel_id=2, replica_groups={{0,128,256,384},{16,144,272,400},{32,160,288,416},{48,176,304,432},{64,..., dimensions={0}, use_global_device_ids=true | all-gather | bytes 1146880 | tf_op jit(solution)/shard_map/all_gather | solution.py:177
  60.7 3.1 %collective-permute-start.7 = (bf16[4,224,512]{2,1,0:T(8,128)(2,1)S(1)}, bf16[4,224,512]{2,1,0:T(8,128)(2,1)S(1)}, u32[]{:S(2)}, u32[]{:S(2)}) collective-permute-start(bf16[4,224,512]{2,1,0:T(8,128)(2,1)S(1)} %bitcast.193), channel_id=1, source_target_pairs={{0,32},{16,48},{32,64},{48,80},{64,96},{80,112},{96,0},{112,16},{1... | collective-permute-start | bytes 2752520 | tf_op jit(solution)/shard_map/ppermute | solution.py:41
  63.9 3.4 %collective-permute-start.8 = (bf16[4,224,512]{2,1,0:T(8,128)(2,1)S(1)}, bf16[4,224,512]{2,1,0:T(8,128)(2,1)S(1)}, u32[]{:S(2)}, u32[]{:S(2)}) collective-permute-start(bf16[4,224,512]{2,1,0:T(8,128)(2,1)S(1)} %bitcast.194), channel_id=1, source_target_pairs={{0,96},{16,112},{32,0},{48,16},{64,32},{80,48},{96,64},{112,80},{1... | collective-permute-start | bytes 2752520 | tf_op jit(solution)/shard_map/ppermute | solution.py:41
  67.2 1.9 collective-permute-start.10
  69.2 4.6 %collective-permute-start.5 = (bf16[240,512]{1,0:T(8,128)(2,1)}, bf16[240,512]{1,0:T(8,128)(2,1)}, u32[]{:S(2)}, u32[]{:S(2)}) collective-permute-start(bf16[240,512]{1,0:T(8,128)(2,1)} %collective-permute-done.4), channel_id=1, source_target_pairs={{0,7},{1,0},{2,1},{3,2},{4,3},{5,4},{6,5},{7,6},{8,15},{9,8},{10,9... | collective-permute-start | bytes 737288 | tf_op jit(solution)/shard_map/ppermute | solution.py:30
  74.6 2.6 %collective-permute-done.5 = bf16[240,512]{1,0:T(8,128)(2,1)} collective-permute-done((bf16[240,512]{1,0:T(8,128)(2,1)}, bf16[240,512]{1,0:T(8,128)(2,1)}, u32[]{:S(2)}, u32[]{:S(2)}) %collective-permute-start.5) | collective-permute-done | bytes 245792 | tf_op jit(solution)/shard_map/ppermute | solution.py:30
  77.2 5.2 %collective-permute-start.6 = (bf16[240,512]{1,0:T(8,128)(2,1)}, bf16[240,512]{1,0:T(8,128)(2,1)S(1)}, u32[]{:S(2)}, u32[]{:S(2)}) collective-permute-start(bf16[240,512]{1,0:T(8,128)(2,1)} %collective-permute-done.5), channel_id=1, source_target_pairs={{0,7},{1,0},{2,1},{3,2},{4,3},{5,4},{6,5},{7,6},{8,15},{9,8},{10,9... | collective-permute-start | bytes 737288 | tf_op jit(solution)/shard_map/ppermute | solution.py:30
  82.4 1.0 bitcast_dynamic-update-slice_fusion.15
  83.4 1.9 collective-permute-start.11
  85.3 1.0 bitcast_dynamic-update-slice_fusion.13
  86.3 5.4 %collective-permute-done.11 = bf16[240,512]{1,0:T(8,128)(2,1)S(1)} collective-permute-done((bf16[240,512]{1,0:T(8,128)(2,1)}, bf16[240,512]{1,0:T(8,128)(2,1)S(1)}, u32[]{:S(2)}, u32[]{:S(2)}) %collective-permute-start.11) | collective-permute-done | bytes 245792 | tf_op jit(solution)/shard_map/ppermute | solution.py:30
  91.8 1.9 collective-permute-start.13
  93.7 3.4 %collective-permute-start.12 = (bf16[112,512]{1,0:T(8,128)(2,1)S(1)}, bf16[112,512]{1,0:T(8,128)(2,1)S(1)}, u32[]{:S(2)}, u32[]{:S(2)}) collective-permute-start(bf16[112,512]{1,0:T(8,128)(2,1)S(1)} %slice.387), channel_id=1, source_target_pairs={{0,1},{1,2},{2,3},{3,4},{4,5},{5,6},{6,7},{7,0},{8,9},{9,10},{10,1... | collective-permute-start | bytes 344072 | tf_op jit(solution)/shard_map/ppermute | solution.py:30
  97.2 1.9 collective-permute-start.14
  99.2 4.6 %collective-permute-start.15 = (bf16[2,224,512]{2,1,0:T(8,128)(2,1)S(1)}, bf16[2,224,512]{2,1,0:T(8,128)(2,1)S(1)}, u32[]{:S(2)}, u32[]{:S(2)}) collective-permute-start(bf16[2,224,512]{2,1,0:T(8,128)(2,1)S(1)} %get-tuple-element.41), channel_id=1, source_target_pairs={{0,96},{16,112},{32,0},{48,16},{64,32},{80,48},{96,64},{112,80},{1... | collective-permute-start | bytes 1376264 | tf_op jit(solution)/shard_map/ppermute | solution.py:41
  103.8 1.0 bitcast_dynamic-update-slice_fusion.7
  104.8 1.0 bitcast_dynamic-update-slice_fusion.16
  105.8 1.0 bitcast_dynamic-update-slice_fusion.14
  106.8 1.0 bitcast_dynamic-update-slice_fusion.8
  114.3 8.4 %collective-permute-start.16 = (f32[2,136,512]{2,1,0:T(8,128)S(1)}, f32[2,136,512]{2,1,0:T(8,128)S(1)}, u32[]{:S(2)}, u32[]{:S(2)}) collective-permute-start(f32[2,136,512]{2,1,0:T(8,128)S(1)} %pad_maximum_fusion.3), channel_id=1, source_target_pairs={{0,16},{16,0},{32,48},{48,32},{64,80},{80,64},{96,112},{112,96},{1... | collective-permute-start | bytes 1671176 | tf_op jit(solution)/shard_map/ppermute | solution.py:24
  123.0 1.2 collective-permute-done.16
  124.4 3.6 %collective-permute-start.17 = (bf16[144,512]{1,0:T(8,128)(2,1)S(1)}, bf16[144,512]{1,0:T(8,128)(2,1)S(1)}, u32[]{:S(2)}, u32[]{:S(2)}) collective-permute-start(bf16[144,512]{1,0:T(8,128)(2,1)S(1)} %pad_maximum_fusion.16), channel_id=1, source_target_pairs={{0,8},{1,9},{2,10},{3,11},{4,12},{5,13},{6,14},{7,15},{8,0},{9,1},... | collective-permute-start | bytes 442376 | tf_op jit(solution)/shard_map/ppermute | solution.py:35
  128.1 10.9 %collective-permute-done.17 = bf16[144,512]{1,0:T(8,128)(2,1)S(1)} collective-permute-done((bf16[144,512]{1,0:T(8,128)(2,1)S(1)}, bf16[144,512]{1,0:T(8,128)(2,1)S(1)}, u32[]{:S(2)}, u32[]{:S(2)}) %collective-permute-start.17) | collective-permute-done | bytes 147488 | tf_op jit(solution)/shard_map/ppermute | solution.py:35
  140.5 2.9 %collective-permute-start.18 = (bf16[144,512]{1,0:T(8,128)(2,1)S(1)}, bf16[144,512]{1,0:T(8,128)(2,1)S(1)}, u32[]{:S(2)}, u32[]{:S(2)}) collective-permute-start(bf16[144,512]{1,0:T(8,128)(2,1)S(1)} %fusion.48), channel_id=1, source_target_pairs={{0,8},{1,9},{2,10},{3,11},{4,12},{5,13},{6,14},{7,15},{8,0},{9,1},... | collective-permute-start | bytes 442376 | tf_op jit(solution)/shard_map/ppermute | solution.py:35
  143.6 10.0 %collective-permute-done.18 = bf16[144,512]{1,0:T(8,128)(2,1)S(1)} collective-permute-done((bf16[144,512]{1,0:T(8,128)(2,1)S(1)}, bf16[144,512]{1,0:T(8,128)(2,1)S(1)}, u32[]{:S(2)}, u32[]{:S(2)}) %collective-permute-start.18) | collective-permute-done | bytes 147488 | tf_op jit(solution)/shard_map/ppermute | solution.py:35
  153.8 2.6 %collective-permute-start.19 = (bf16[2,144,512]{2,1,0:T(8,128)(2,1)S(1)}, bf16[2,144,512]{2,1,0:T(8,128)(2,1)S(1)}, u32[]{:S(2)}, u32[]{:S(2)}) collective-permute-start(bf16[2,144,512]{2,1,0:T(8,128)(2,1)S(1)} %fusion.22), channel_id=1, source_target_pairs={{0,16},{16,0},{32,48},{48,32},{64,80},{80,64},{96,112},{112,96},{1... | collective-permute-start | bytes 884744 | tf_op jit(solution)/shard_map/ppermute | solution.py:24
  159.9 1.0 pad_maximum_fusion.1
  160.9 4.0 %all-to-all-start = ((bf16[8,240,256]{2,1,0:T(8,128)(2,1)}), bf16[8,240,256]{2,1,0:T(8,128)(2,1)S(1)}, u32[]{:S(2)}, u32[]{:S(2)}) async-start(bf16[8,240,256]{2,1,0:T(8,128)(2,1)} %pad_maximum_fusion.1), calls=%async_computation | async-start | bytes 1966080 | tf_op jit(solution)/shard_map/all_to_all | solution.py:278
  164.9 1.9 collective-permute-start.22
  166.9 4.6 %collective-permute-start.23 = (bf16[4,224,128]{2,1,0:T(8,128)(2,1)S(1)}, bf16[4,224,128]{2,1,0:T(8,128)(2,1)S(1)}, u32[]{:S(2)}, u32[]{:S(2)}) collective-permute-start(bf16[4,224,128]{2,1,0:T(8,128)(2,1)S(1)} %pad_maximum_fusion.15), channel_id=1, source_target_pairs={{0,96},{16,112},{32,0},{48,16},{64,32},{80,48},{96,64},{112,80},{1... | collective-permute-start | bytes 688136 | tf_op jit(solution)/shard_map/ppermute | solution.py:41
  171.5 1.9 collective-permute-start.21
  173.5 1.0 collective-permute-done.22
  174.5 1.5 collective-permute-done.23
  176.1 4.7 %collective-permute-done.21 = bf16[4,224,128]{2,1,0:T(8,128)(2,1)S(1)} collective-permute-done((bf16[4,224,128]{2,1,0:T(8,128)(2,1)S(1)}, bf16[4,224,128]{2,1,0:T(8,128)(2,1)S(1)}, u32[]{:S(2)}, u32[]{:S(2)}) %collective-permute-start.21) | collective-permute-done | bytes 229408 | tf_op jit(solution)/shard_map/ppermute | solution.py:41
  181.6 1.9 collective-permute-start.25
  183.5 6.5 %collective-permute-start.26 = (bf16[224,128]{1,0:T(8,128)(2,1)S(1)}, bf16[224,128]{1,0:T(8,128)(2,1)S(1)}, u32[]{:S(2)}, u32[]{:S(2)}) collective-permute-start(bf16[224,128]{1,0:T(8,128)(2,1)S(1)} %get-tuple-element.70), channel_id=1, source_target_pairs={{0,8},{1,9},{2,10},{3,11},{4,12},{5,13},{6,14},{7,15},{8,264},{9,2... | collective-permute-start | bytes 172040 | tf_op jit(solution)/shard_map/ppermute | solution.py:53
  190.1 4.9 %collective-permute-start.27 = (bf16[224,128]{1,0:T(8,128)(2,1)S(1)}, bf16[224,128]{1,0:T(8,128)(2,1)S(1)}, u32[]{:S(2)}, u32[]{:S(2)}) collective-permute-start(bf16[224,128]{1,0:T(8,128)(2,1)S(1)} %get-tuple-element.69), channel_id=1, source_target_pairs={{0,136},{1,137},{2,138},{3,139},{4,140},{5,141},{6,142},{7,143},{8... | collective-permute-start | bytes 172040 | tf_op jit(solution)/shard_map/ppermute | solution.py:53
  197.1 5.7 %collective-permute-start.20 = (f32[224,128]{1,0:T(8,128)S(1)}, f32[224,128]{1,0:T(8,128)S(1)}, u32[]{:S(2)}, u32[]{:S(2)}) collective-permute-start(f32[224,128]{1,0:T(8,128)S(1)} %get-tuple-element.66), channel_id=1, source_target_pairs={{0,16},{16,0},{32,48},{48,32},{64,80},{80,64},{96,112},{112,96},{1... | collective-permute-start | bytes 344072 | tf_op jit(solution)/shard_map/ppermute | solution.py:24
  (172 shorter events, 21.3 us)
Async XLA Ops:
  1.7 23.9 %collective-permute-start.1 = (bf16[224,256]{1,0:T(8,128)(2,1)S(1)}, bf16[224,256]{1,0:T(8,128)(2,1)S(1)}, u32[]{:S(2)}, u32[]{:S(2)}) collective-permute-start(bf16[224,256]{1,0:T(8,128)(2,1)S(1)} %get-tuple-element.73), channel_id=1, source_target_pairs={{0,16},{16,0},{32,48},{48,32},{64,80},{80,64},{96,112},{112,96},{1... | collective-permute-start | bytes 344072 | tf_op jit(solution)/shard_map/ppermute | solution.py:24
  13.4 8.3 %collective-permute-start.2 = (f32[2,128]{1,0:T(2,128)S(1)}, f32[2,128]{1,0:T(2,128)S(1)}, u32[]{:S(2)}, u32[]{:S(2)}) collective-permute-start(f32[2,128]{1,0:T(2,128)S(1)} %pad_maximum_fusion.21), channel_id=1, source_target_pairs={{0,8},{1,9},{2,10},{3,11},{4,12},{5,13},{6,14},{7,15},{8,0},{9,1},... | collective-permute-start | bytes 3080 | tf_op jit(solution)/shard_map/ppermute | solution.py:35
  15.5 10.5 %collective-permute-start = (bf16[224,512]{1,0:T(8,128)(2,1)S(1)}, bf16[224,512]{1,0:T(8,128)(2,1)S(1)}, u32[]{:S(2)}, u32[]{:S(2)}) collective-permute-start(bf16[224,512]{1,0:T(8,128)(2,1)S(1)} %pad_maximum_fusion.11), channel_id=1, source_target_pairs={{0,0},{1,1},{2,2},{3,3},{4,4},{5,5},{6,6},{7,7},{8,256},{9,257},{1... | collective-permute-start | bytes 688136 | tf_op jit(solution)/shard_map/ppermute | solution.py:53
  21.8 3.8 %collective-permute-start.3 = (f32[2,128]{1,0:T(2,128)S(1)}, f32[2,128]{1,0:T(2,128)S(1)}, u32[]{:S(2)}, u32[]{:S(2)}) collective-permute-start(f32[2,128]{1,0:T(2,128)S(1)} %pad_maximum_fusion.22), channel_id=1, source_target_pairs={{0,16},{16,0},{32,48},{48,32},{64,80},{80,64},{96,112},{112,96},{1... | collective-permute-start | bytes 3080 | tf_op jit(solution)/shard_map/ppermute | solution.py:24
  25.9 48.2 %copy-start.1 = (bf16[240,512]{1,0:T(8,128)(2,1)}, bf16[240,512]{1,0:T(8,128)(2,1)S(1)}, u32[]{:S(2)}) copy-start(bf16[240,512]{1,0:T(8,128)(2,1)S(1)} %concatenate.99) | copy-start | bytes 737284
  26.0 41.3 %collective-permute-start.9 = (bf16[240,512]{1,0:T(8,128)(2,1)S(1)}, bf16[240,512]{1,0:T(8,128)(2,1)S(1)}, u32[]{:S(2)}, u32[]{:S(2)}) collective-permute-start(bf16[240,512]{1,0:T(8,128)(2,1)S(1)} %concatenate.99), channel_id=1, source_target_pairs={{0,1},{1,2},{2,3},{3,4},{4,5},{5,6},{6,7},{7,0},{8,9},{9,10},{10,1... | collective-permute-start | bytes 737288 | tf_op jit(solution)/shard_map/ppermute | solution.py:30
  27.9 41.3 %collective-permute-start.4 = (bf16[240,512]{1,0:T(8,128)(2,1)S(1)}, bf16[240,512]{1,0:T(8,128)(2,1)}, u32[]{:S(2)}, u32[]{:S(2)}) collective-permute-start(bf16[240,512]{1,0:T(8,128)(2,1)S(1)} %concatenate.99), channel_id=1, source_target_pairs={{0,7},{1,0},{2,1},{3,2},{4,3},{5,4},{6,5},{7,6},{8,15},{9,8},{10,9... | collective-permute-start | bytes 737288 | tf_op jit(solution)/shard_map/ppermute | solution.py:30
  60.7 31.0 %collective-permute-start.7 = (bf16[4,224,512]{2,1,0:T(8,128)(2,1)S(1)}, bf16[4,224,512]{2,1,0:T(8,128)(2,1)S(1)}, u32[]{:S(2)}, u32[]{:S(2)}) collective-permute-start(bf16[4,224,512]{2,1,0:T(8,128)(2,1)S(1)} %bitcast.193), channel_id=1, source_target_pairs={{0,32},{16,48},{32,64},{48,80},{64,96},{80,112},{96,0},{112,16},{1... | collective-permute-start | bytes 2752520 | tf_op jit(solution)/shard_map/ppermute | solution.py:41
  63.9 27.9 %collective-permute-start.8 = (bf16[4,224,512]{2,1,0:T(8,128)(2,1)S(1)}, bf16[4,224,512]{2,1,0:T(8,128)(2,1)S(1)}, u32[]{:S(2)}, u32[]{:S(2)}) collective-permute-start(bf16[4,224,512]{2,1,0:T(8,128)(2,1)S(1)} %bitcast.194), channel_id=1, source_target_pairs={{0,96},{16,112},{32,0},{48,16},{64,32},{80,48},{96,64},{112,80},{1... | collective-permute-start | bytes 2752520 | tf_op jit(solution)/shard_map/ppermute | solution.py:41
  67.2 16.1 %collective-permute-start.10 = (bf16[240,512]{1,0:T(8,128)(2,1)S(1)}, bf16[240,512]{1,0:T(8,128)(2,1)}, u32[]{:S(2)}, u32[]{:S(2)}) collective-permute-start(bf16[240,512]{1,0:T(8,128)(2,1)S(1)} %collective-permute-done.9), channel_id=1, source_target_pairs={{0,1},{1,2},{2,3},{3,4},{4,5},{5,6},{6,7},{7,0},{8,9},{9,10},{10,1... | collective-permute-start | bytes 737288 | tf_op jit(solution)/shard_map/ppermute | solution.py:30
  69.2 8.0 %collective-permute-start.5 = (bf16[240,512]{1,0:T(8,128)(2,1)}, bf16[240,512]{1,0:T(8,128)(2,1)}, u32[]{:S(2)}, u32[]{:S(2)}) collective-permute-start(bf16[240,512]{1,0:T(8,128)(2,1)} %collective-permute-done.4), channel_id=1, source_target_pairs={{0,7},{1,0},{2,1},{3,2},{4,3},{5,4},{6,5},{7,6},{8,15},{9,8},{10,9... | collective-permute-start | bytes 737288 | tf_op jit(solution)/shard_map/ppermute | solution.py:30
  74.6 30.2 %copy-start.2 = (bf16[240,512]{1,0:T(8,128)(2,1)S(1)}, bf16[240,512]{1,0:T(8,128)(2,1)}, u32[]{:S(2)}) copy-start(bf16[240,512]{1,0:T(8,128)(2,1)} %copy-done.1) | copy-start | bytes 737284
  77.2 9.1 %collective-permute-start.6 = (bf16[240,512]{1,0:T(8,128)(2,1)}, bf16[240,512]{1,0:T(8,128)(2,1)S(1)}, u32[]{:S(2)}, u32[]{:S(2)}) collective-permute-start(bf16[240,512]{1,0:T(8,128)(2,1)} %collective-permute-done.5), channel_id=1, source_target_pairs={{0,7},{1,0},{2,1},{3,2},{4,3},{5,4},{6,5},{7,6},{8,15},{9,8},{10,9... | collective-permute-start | bytes 737288 | tf_op jit(solution)/shard_map/ppermute | solution.py:30
  83.4 8.4 %collective-permute-start.11 = (bf16[240,512]{1,0:T(8,128)(2,1)}, bf16[240,512]{1,0:T(8,128)(2,1)S(1)}, u32[]{:S(2)}, u32[]{:S(2)}) collective-permute-start(bf16[240,512]{1,0:T(8,128)(2,1)} %collective-permute-done.10), channel_id=1, source_target_pairs={{0,1},{1,2},{2,3},{3,4},{4,5},{5,6},{6,7},{7,0},{8,9},{9,10},{10,1... | collective-permute-start | bytes 737288 | tf_op jit(solution)/shard_map/ppermute | solution.py:30
  91.8 12.0 %collective-permute-start.13 = (bf16[128,512]{1,0:T(8,128)(2,1)S(1)}, bf16[128,512]{1,0:T(8,128)(2,1)S(1)}, u32[]{:S(2)}, u32[]{:S(2)}) collective-permute-start(bf16[128,512]{1,0:T(8,128)(2,1)S(1)} %slice.388), channel_id=1, source_target_pairs={{0,7},{1,0},{2,1},{3,2},{4,3},{5,4},{6,5},{7,6},{8,15},{9,8},{10,9... | collective-permute-start | bytes 393224 | tf_op jit(solution)/shard_map/ppermute | solution.py:30
  93.7 10.0 %collective-permute-start.12 = (bf16[112,512]{1,0:T(8,128)(2,1)S(1)}, bf16[112,512]{1,0:T(8,128)(2,1)S(1)}, u32[]{:S(2)}, u32[]{:S(2)}) collective-permute-start(bf16[112,512]{1,0:T(8,128)(2,1)S(1)} %slice.387), channel_id=1, source_target_pairs={{0,1},{1,2},{2,3},{3,4},{4,5},{5,6},{6,7},{7,0},{8,9},{9,10},{10,1... | collective-permute-start | bytes 344072 | tf_op jit(solution)/shard_map/ppermute | solution.py:30
  97.2 15.4 %collective-permute-start.14 = (bf16[2,224,512]{2,1,0:T(8,128)(2,1)S(1)}, bf16[2,224,512]{2,1,0:T(8,128)(2,1)S(1)}, u32[]{:S(2)}, u32[]{:S(2)}) collective-permute-start(bf16[2,224,512]{2,1,0:T(8,128)(2,1)S(1)} %get-tuple-element.42), channel_id=1, source_target_pairs={{0,32},{16,48},{32,64},{48,80},{64,96},{80,112},{96,0},{112,16},{1... | collective-permute-start | bytes 1376264 | tf_op jit(solution)/shard_map/ppermute | solution.py:41
  99.2 13.9 %collective-permute-start.15 = (bf16[2,224,512]{2,1,0:T(8,128)(2,1)S(1)}, bf16[2,224,512]{2,1,0:T(8,128)(2,1)S(1)}, u32[]{:S(2)}, u32[]{:S(2)}) collective-permute-start(bf16[2,224,512]{2,1,0:T(8,128)(2,1)S(1)} %get-tuple-element.41), channel_id=1, source_target_pairs={{0,96},{16,112},{32,0},{48,16},{64,32},{80,48},{96,64},{112,80},{1... | collective-permute-start | bytes 1376264 | tf_op jit(solution)/shard_map/ppermute | solution.py:41
  114.3 9.9 %collective-permute-start.16 = (f32[2,136,512]{2,1,0:T(8,128)S(1)}, f32[2,136,512]{2,1,0:T(8,128)S(1)}, u32[]{:S(2)}, u32[]{:S(2)}) collective-permute-start(f32[2,136,512]{2,1,0:T(8,128)S(1)} %pad_maximum_fusion.3), channel_id=1, source_target_pairs={{0,16},{16,0},{32,48},{48,32},{64,80},{80,64},{96,112},{112,96},{1... | collective-permute-start | bytes 1671176 | tf_op jit(solution)/shard_map/ppermute | solution.py:24
  122.8 16.2 %copy-start.3 = (f32[384]{0:T(512)S(1)}, f32[384]{0:T(512)}, u32[]{:S(2)}) copy-start(f32[384]{0:T(512)} %param.11) | copy-start | bytes 4612
  124.4 14.6 %collective-permute-start.17 = (bf16[144,512]{1,0:T(8,128)(2,1)S(1)}, bf16[144,512]{1,0:T(8,128)(2,1)S(1)}, u32[]{:S(2)}, u32[]{:S(2)}) collective-permute-start(bf16[144,512]{1,0:T(8,128)(2,1)S(1)} %pad_maximum_fusion.16), channel_id=1, source_target_pairs={{0,8},{1,9},{2,10},{3,11},{4,12},{5,13},{6,14},{7,15},{8,0},{9,1},... | collective-permute-start | bytes 442376 | tf_op jit(solution)/shard_map/ppermute | solution.py:35
  140.5 13.1 %collective-permute-start.18 = (bf16[144,512]{1,0:T(8,128)(2,1)S(1)}, bf16[144,512]{1,0:T(8,128)(2,1)S(1)}, u32[]{:S(2)}, u32[]{:S(2)}) collective-permute-start(bf16[144,512]{1,0:T(8,128)(2,1)S(1)} %fusion.48), channel_id=1, source_target_pairs={{0,8},{1,9},{2,10},{3,11},{4,12},{5,13},{6,14},{7,15},{8,0},{9,1},... | collective-permute-start | bytes 442376 | tf_op jit(solution)/shard_map/ppermute | solution.py:35
  153.8 3.6 %collective-permute-start.19 = (bf16[2,144,512]{2,1,0:T(8,128)(2,1)S(1)}, bf16[2,144,512]{2,1,0:T(8,128)(2,1)S(1)}, u32[]{:S(2)}, u32[]{:S(2)}) collective-permute-start(bf16[2,144,512]{2,1,0:T(8,128)(2,1)S(1)} %fusion.22), channel_id=1, source_target_pairs={{0,16},{16,0},{32,48},{48,32},{64,80},{80,64},{96,112},{112,96},{1... | collective-permute-start | bytes 884744 | tf_op jit(solution)/shard_map/ppermute | solution.py:24
  160.9 42.8 %copy-start = (bf16[128,448]{0,1:T(8,128)(2,1)S(1)}, bf16[128,448]{0,1:T(8,128)(2,1)}, u32[]{:S(2)}) copy-start(bf16[128,448]{0,1:T(8,128)(2,1)} %param.7) | copy-start | bytes 344068
  160.9 36.0 %all-to-all-start = ((bf16[8,240,256]{2,1,0:T(8,128)(2,1)}), bf16[8,240,256]{2,1,0:T(8,128)(2,1)S(1)}, u32[]{:S(2)}, u32[]{:S(2)}) async-start(bf16[8,240,256]{2,1,0:T(8,128)(2,1)} %pad_maximum_fusion.1), calls=%async_computation | async-start | bytes 1966080 | tf_op jit(solution)/shard_map/all_to_all | solution.py:278
  164.9 9.6 %collective-permute-start.22 = (bf16[4,224,128]{2,1,0:T(8,128)(2,1)S(1)}, bf16[4,224,128]{2,1,0:T(8,128)(2,1)S(1)}, u32[]{:S(2)}, u32[]{:S(2)}) collective-permute-start(bf16[4,224,128]{2,1,0:T(8,128)(2,1)S(1)} %pad_maximum_fusion.14), channel_id=1, source_target_pairs={{0,32},{16,48},{32,64},{48,80},{64,96},{80,112},{96,0},{112,16},{1... | collective-permute-start | bytes 688136 | tf_op jit(solution)/shard_map/ppermute | solution.py:41
  166.9 9.2 %collective-permute-start.23 = (bf16[4,224,128]{2,1,0:T(8,128)(2,1)S(1)}, bf16[4,224,128]{2,1,0:T(8,128)(2,1)S(1)}, u32[]{:S(2)}, u32[]{:S(2)}) collective-permute-start(bf16[4,224,128]{2,1,0:T(8,128)(2,1)S(1)} %pad_maximum_fusion.15), channel_id=1, source_target_pairs={{0,96},{16,112},{32,0},{48,16},{64,32},{80,48},{96,64},{112,80},{1... | collective-permute-start | bytes 688136 | tf_op jit(solution)/shard_map/ppermute | solution.py:41
  171.5 9.3 %collective-permute-start.21 = (bf16[4,224,128]{2,1,0:T(8,128)(2,1)S(1)}, bf16[4,224,128]{2,1,0:T(8,128)(2,1)S(1)}, u32[]{:S(2)}, u32[]{:S(2)}) collective-permute-start(bf16[4,224,128]{2,1,0:T(8,128)(2,1)S(1)} %pad_maximum_fusion.13), channel_id=1, source_target_pairs={{0,64},{16,80},{32,96},{48,112},{64,0},{80,16},{96,32},{112,48},{1... | collective-permute-start | bytes 688136 | tf_op jit(solution)/shard_map/ppermute | solution.py:41
  180.9 14.8 %collective-permute-start.24 = (bf16[224,128]{1,0:T(8,128)(2,1)S(1)}, bf16[224,128]{1,0:T(8,128)(2,1)S(1)}, u32[]{:S(2)}, u32[]{:S(2)}) collective-permute-start(bf16[224,128]{1,0:T(8,128)(2,1)S(1)} %get-tuple-element.68), channel_id=1, source_target_pairs={{0,0},{1,1},{2,2},{3,3},{4,4},{5,5},{6,6},{7,7},{8,256},{9,257},{1... | collective-permute-start | bytes 172040 | tf_op jit(solution)/shard_map/ppermute | solution.py:53
  181.6 14.2 %collective-permute-start.25 = (bf16[224,128]{1,0:T(8,128)(2,1)S(1)}, bf16[224,128]{1,0:T(8,128)(2,1)S(1)}, u32[]{:S(2)}, u32[]{:S(2)}) collective-permute-start(bf16[224,128]{1,0:T(8,128)(2,1)S(1)} %get-tuple-element.71), channel_id=1, source_target_pairs={{0,128},{1,129},{2,130},{3,131},{4,132},{5,133},{6,134},{7,135},{8... | collective-permute-start | bytes 172040 | tf_op jit(solution)/shard_map/ppermute | solution.py:53
  183.5 12.2 %collective-permute-start.26 = (bf16[224,128]{1,0:T(8,128)(2,1)S(1)}, bf16[224,128]{1,0:T(8,128)(2,1)S(1)}, u32[]{:S(2)}, u32[]{:S(2)}) collective-permute-start(bf16[224,128]{1,0:T(8,128)(2,1)S(1)} %get-tuple-element.70), channel_id=1, source_target_pairs={{0,8},{1,9},{2,10},{3,11},{4,12},{5,13},{6,14},{7,15},{8,264},{9,2... | collective-permute-start | bytes 172040 | tf_op jit(solution)/shard_map/ppermute | solution.py:53
  190.1 6.1 %collective-permute-start.27 = (bf16[224,128]{1,0:T(8,128)(2,1)S(1)}, bf16[224,128]{1,0:T(8,128)(2,1)S(1)}, u32[]{:S(2)}, u32[]{:S(2)}) collective-permute-start(bf16[224,128]{1,0:T(8,128)(2,1)S(1)} %get-tuple-element.69), channel_id=1, source_target_pairs={{0,136},{1,137},{2,138},{3,139},{4,140},{5,141},{6,142},{7,143},{8... | collective-permute-start | bytes 172040 | tf_op jit(solution)/shard_map/ppermute | solution.py:53
  197.1 6.7 %collective-permute-start.20 = (f32[224,128]{1,0:T(8,128)S(1)}, f32[224,128]{1,0:T(8,128)S(1)}, u32[]{:S(2)}, u32[]{:S(2)}) collective-permute-start(f32[224,128]{1,0:T(8,128)S(1)} %get-tuple-element.66), channel_id=1, source_target_pairs={{0,16},{16,0},{32,48},{48,32},{64,80},{80,64},{96,112},{112,96},{1... | collective-permute-start | bytes 344072 | tf_op jit(solution)/shard_map/ppermute | solution.py:24

commit v13 on v12

--- a/solution.py
+++ b/solution.py
@@ -147,15 +147,15 @@
     def by_far(own, other):
         return jnp.stack([jnp.where(far == 0, own, other), jnp.where(far == 0, other, own)])
 
-    hidden_t = hidden_in.T
-    acts = jnp.concatenate([hidden_t, out_grad.T], axis=1).reshape(2, part, 2 * SEQ)
+    weight_block = jnp.concatenate([w_qkv, w_out.T], axis=1)
+    weight_block, hidden_t, grad_t = lax.optimization_barrier(
+        (weight_block, hidden_in.T, out_grad.T)
+    )
+    weight_block = move_weights(weight_block)
+    acts = jnp.concatenate([hidden_t, grad_t], axis=1).reshape(2, part, 2 * SEQ)
     mine = jnp.where(core == 0, acts[0], acts[1])
     other = swap_cores(jnp.where(core == 0, acts[1], acts[0]))
     block = jnp.concatenate([mine[:, :SEQ], other[:, :SEQ], mine[:, SEQ:], other[:, SEQ:]], axis=1)
-
-    weight_block = jnp.concatenate([w_qkv, w_out.T], axis=1)
-    weight_block, hidden_t = lax.optimization_barrier((weight_block, hidden_t))
-    weight_block = move_weights(weight_block)
 
     slice_f = hidden_t.astype(f32)
     mean_part = jnp.mean(slice_f, axis=0)
@@ -168,6 +168,7 @@
             stats[1] + stats_far[1] + gap * gap * (width / 2),
         ]
     )
+    weight_block, stats = lax.optimization_barrier((weight_block, stats))
     stats = jnp.concatenate([stats, swap_cores(stats)], axis=1).reshape(1, 4 * SEQ)
     high, low = split(stats)
     lower = (stats - high.astype(f32) - low.astype(f32)).astype(bf16)
@@ -175,6 +176,7 @@
 
     weight_block, block = lax.optimization_barrier((weight_block, block))
     column = lax.all_gather(weight_block, "dp", axis=0, axis_index_groups=lines)
+    column, block = lax.optimization_barrier((column, block))
     rows, blocks = gather_both(block, column, z)
     hidden = rows[:, :part, : 2 * SEQ].reshape(quarter, 2 * SEQ).astype(f32)
     grads = rows[:, :part, 2 * SEQ :].reshape(quarter, 2 * SEQ)

time: 206 us -> 207 us (level)
  local copies, waits for them, and re-layouts: 9.58 us -> 5.82 us
  starting transfers between devices: 104 us -> 107 us
    unnamed x25 -> x22, local copies, waits for them, and re-layouts: 6.35 us -> 1.6 us
    ppermute x8, starting transfers between devices: 27.1 us -> 31.5 us  [shift_z(): return lax.ppermute(x, 'tensor', pairs)]
  transfers between devices with their start and end apart: 29 -> 29, of which waited for: 13 -> 14; matrix products, arithmetic and copies ran while one was open for 10% -> 6% of each run, Pallas kernels for 0% -> 0%
where the time goes in v13:
time: 207 us; the launch traced here: 204 us
  starting transfers between devices  107 us (52%)
  waiting for transfers between devices  45.2 us (22%)
  blocking collectives  26.6 us (13%)
  other arithmetic  9.65 us (5%)
  matrix products  7.87 us (4%)
  local copies, waits for them, and re-layouts  5.82 us (3%)
  between operations  2.12 us (1%)
    ppermute x8, starting transfers between devices, shift_z(): return lax.ppermute(x, 'tensor', pairs)  31.5 us
    ppermute x5, starting transfers between devices, swap_cores(): return lax.ppermute(x, 'dp', [(i, i ^ 1) for i in range(n)])  28.1 us
    all_gather x1, blocking collectives, body(): column = lax.all_gather(weight_block, 'dp', axis=0, axis_index_groups=lines)  26.6 us
    ppermute x3, waiting for transfers between devices, swap_far(): return lax.ppermute(x, 'tensor', [(i, (i + Z_COUNT) % n) for i in range(n)])  24.6 us
    ppermute x7, starting transfers between devices, shift_x(): lax.ppermute(x, 'dp', [(i, i - i % row + (i + 2 * step) % row) for i in r...  23.3 us
    ppermute x5, starting transfers between devices, along_y(): return lax.ppermute(x, ('dp', 'tensor'), pairs)  12.7 us
    ppermute x8, waiting for transfers between devices, shift_z(): return lax.ppermute(x, 'tensor', pairs)  9.24 us
    dot_general x26, matrix products, dot(): return lax.dot_general(a, b, (dims, ((), ())), preferred_element_type=f32)  7.87 us
  transfers between devices with their start and end apart: 29, of which 14 were waited for; matrix products, arithmetic and copies ran while one was open for 6% of the time, Pallas kernels for 0%

profile of v13, /device:TPU:1, one launch (start us, length us, event | category | flops | bytes accessed | tf_op | source)
XLA Modules:
  0.0 204.1 jit_solution(10844136926880499733)
XLA Ops:
  0.6 1.0 pad_maximum_fusion.11
  1.6 0.9 constant_dynamic-update-slice_fusion.1
  2.5 0.9 constant_dynamic-update-slice_fusion
  3.5 8.8 %collective-permute-start.2 = (bf16[224,256]{1,0:T(8,128)(2,1)S(1)}, bf16[224,256]{1,0:T(8,128)(2,1)S(1)}, u32[]{:S(2)}, u32[]{:S(2)}) collective-permute-start(bf16[224,256]{1,0:T(8,128)(2,1)S(1)} %get-tuple-element.85), channel_id=1, source_target_pairs={{0,16},{16,0},{32,48},{48,32},{64,80},{80,64},{96,112},{112,96},{1... | collective-permute-start | bytes 344072 | tf_op jit(solution)/shard_map/ppermute | solution.py:24
  12.3 1.0 convert_reduce_fusion.1
  13.3 1.0 fusion.30
  14.3 2.1 %collective-permute-start.1 = (f32[2,128]{1,0:T(2,128)S(1)}, f32[2,128]{1,0:T(2,128)S(1)}, u32[]{:S(2)}, u32[]{:S(2)}) collective-permute-start(f32[2,128]{1,0:T(2,128)S(1)} %pad_maximum_fusion.20), channel_id=1, source_target_pairs={{0,8},{1,9},{2,10},{3,11},{4,12},{5,13},{6,14},{7,15},{8,0},{9,1},... | collective-permute-start | bytes 3080 | tf_op jit(solution)/shard_map/ppermute | solution.py:35
  17.2 0.8 slice_select_fusion.3
  18.0 0.8 slice_select_fusion.2
  19.4 3.2 %collective-permute-done.1 = f32[2,128]{1,0:T(2,128)S(1)} collective-permute-done((f32[2,128]{1,0:T(2,128)S(1)}, f32[2,128]{1,0:T(2,128)S(1)}, u32[]{:S(2)}, u32[]{:S(2)}) %collective-permute-start.1) | collective-permute-done | bytes 1056 | tf_op jit(solution)/shard_map/ppermute | solution.py:35
  22.6 3.0 %collective-permute-start.3 = (f32[2,128]{1,0:T(2,128)S(1)}, f32[2,128]{1,0:T(2,128)S(1)}, u32[]{:S(2)}, u32[]{:S(2)}) collective-permute-start(f32[2,128]{1,0:T(2,128)S(1)} %pad_maximum_fusion.21), channel_id=1, source_target_pairs={{0,16},{16,0},{32,48},{48,32},{64,80},{80,64},{96,112},{112,96},{1... | collective-permute-start | bytes 3080 | tf_op jit(solution)/shard_map/ppermute | solution.py:24
  26.8 26.6 %all-gather = bf16[896,512]{1,0:T(8,128)(2,1)S(1)} all-gather(bf16[224,512]{1,0:T(8,128)(2,1)S(1)} %collective-permute-done), channel_id=2, replica_groups={{0,128,256,384},{16,144,272,400},{32,160,288,416},{48,176,304,432},{64,..., dimensions={0}, use_global_device_ids=true | all-gather | bytes 1146880 | tf_op jit(solution)/shard_map/all_gather | solution.py:178
  53.4 3.9 %collective-permute-start.9 = (bf16[240,512]{1,0:T(8,128)(2,1)S(1)}, bf16[240,512]{1,0:T(8,128)(2,1)S(1)}, u32[]{:S(2)}, u32[]{:S(2)}) collective-permute-start(bf16[240,512]{1,0:T(8,128)(2,1)S(1)} %concatenate.99), channel_id=1, source_target_pairs={{0,1},{1,2},{2,3},{3,4},{4,5},{5,6},{6,7},{7,0},{8,9},{9,10},{10,1... | collective-permute-start | bytes 737288 | tf_op jit(solution)/shard_map/ppermute | solution.py:30
  57.2 8.6 %collective-permute-start.4 = (bf16[240,512]{1,0:T(8,128)(2,1)S(1)}, bf16[240,512]{1,0:T(8,128)(2,1)S(1)}, u32[]{:S(2)}, u32[]{:S(2)}) collective-permute-start(bf16[240,512]{1,0:T(8,128)(2,1)S(1)} %concatenate.99), channel_id=1, source_target_pairs={{0,7},{1,0},{2,1},{3,2},{4,3},{5,4},{6,5},{7,6},{8,15},{9,8},{10,9... | collective-permute-start | bytes 737288 | tf_op jit(solution)/shard_map/ppermute | solution.py:30
  66.4 3.1 %collective-permute-start.7 = (bf16[4,224,512]{2,1,0:T(8,128)(2,1)S(1)}, bf16[4,224,512]{2,1,0:T(8,128)(2,1)S(1)}, u32[]{:S(2)}, u32[]{:S(2)}) collective-permute-start(bf16[4,224,512]{2,1,0:T(8,128)(2,1)S(1)} %bitcast.193), channel_id=1, source_target_pairs={{0,32},{16,48},{32,64},{48,80},{64,96},{80,112},{96,0},{112,16},{1... | collective-permute-start | bytes 2752520 | tf_op jit(solution)/shard_map/ppermute | solution.py:41
  69.5 3.4 %collective-permute-start.8 = (bf16[4,224,512]{2,1,0:T(8,128)(2,1)S(1)}, bf16[4,224,512]{2,1,0:T(8,128)(2,1)S(1)}, u32[]{:S(2)}, u32[]{:S(2)}) collective-permute-start(bf16[4,224,512]{2,1,0:T(8,128)(2,1)S(1)} %bitcast.194), channel_id=1, source_target_pairs={{0,96},{16,112},{32,0},{48,16},{64,32},{80,48},{96,64},{112,80},{1... | collective-permute-start | bytes 2752520 | tf_op jit(solution)/shard_map/ppermute | solution.py:41
  72.9 1.9 collective-permute-start.10
  74.8 4.6 %collective-permute-start.5 = (bf16[240,512]{1,0:T(8,128)(2,1)S(1)}, bf16[240,512]{1,0:T(8,128)(2,1)S(1)}, u32[]{:S(2)}, u32[]{:S(2)}) collective-permute-start(bf16[240,512]{1,0:T(8,128)(2,1)S(1)} %collective-permute-done.4), channel_id=1, source_target_pairs={{0,7},{1,0},{2,1},{3,2},{4,3},{5,4},{6,5},{7,6},{8,15},{9,8},{10,9... | collective-permute-start | bytes 737288 | tf_op jit(solution)/shard_map/ppermute | solution.py:30
  79.5 3.0 %collective-permute-done.5 = bf16[240,512]{1,0:T(8,128)(2,1)S(1)} collective-permute-done((bf16[240,512]{1,0:T(8,128)(2,1)S(1)}, bf16[240,512]{1,0:T(8,128)(2,1)S(1)}, u32[]{:S(2)}, u32[]{:S(2)}) %collective-permute-start.5) | collective-permute-done | bytes 245792 | tf_op jit(solution)/shard_map/ppermute | solution.py:30
  82.5 5.3 %collective-permute-start.6 = (bf16[240,512]{1,0:T(8,128)(2,1)S(1)}, bf16[240,512]{1,0:T(8,128)(2,1)S(1)}, u32[]{:S(2)}, u32[]{:S(2)}) collective-permute-start(bf16[240,512]{1,0:T(8,128)(2,1)S(1)} %collective-permute-done.5), channel_id=1, source_target_pairs={{0,7},{1,0},{2,1},{3,2},{4,3},{5,4},{6,5},{7,6},{8,15},{9,8},{10,9... | collective-permute-start | bytes 737288 | tf_op jit(solution)/shard_map/ppermute | solution.py:30
  87.9 1.9 collective-permute-start.11
  89.8 1.1 collective-permute-done.6
  91.0 5.0 %collective-permute-done.11 = bf16[240,512]{1,0:T(8,128)(2,1)S(1)} collective-permute-done((bf16[240,512]{1,0:T(8,128)(2,1)S(1)}, bf16[240,512]{1,0:T(8,128)(2,1)S(1)}, u32[]{:S(2)}, u32[]{:S(2)}) %collective-permute-start.11) | collective-permute-done | bytes 245792 | tf_op jit(solution)/shard_map/ppermute | solution.py:30
  96.1 1.9 collective-permute-start.13
  98.0 3.4 %collective-permute-start.12 = (bf16[112,512]{1,0:T(8,128)(2,1)S(1)}, bf16[112,512]{1,0:T(8,128)(2,1)S(1)}, u32[]{:S(2)}, u32[]{:S(2)}) collective-permute-start(bf16[112,512]{1,0:T(8,128)(2,1)S(1)} %slice.387), channel_id=1, source_target_pairs={{0,1},{1,2},{2,3},{3,4},{4,5},{5,6},{6,7},{7,0},{8,9},{9,10},{10,1... | collective-permute-start | bytes 344072 | tf_op jit(solution)/shard_map/ppermute | solution.py:30
  101.5 1.9 collective-permute-start.14
  103.4 4.6 %collective-permute-start.15 = (bf16[2,224,512]{2,1,0:T(8,128)(2,1)S(1)}, bf16[2,224,512]{2,1,0:T(8,128)(2,1)S(1)}, u32[]{:S(2)}, u32[]{:S(2)}) collective-permute-start(bf16[2,224,512]{2,1,0:T(8,128)(2,1)S(1)} %get-tuple-element.51), channel_id=1, source_target_pairs={{0,96},{16,112},{32,0},{48,16},{64,32},{80,48},{96,64},{112,80},{1... | collective-permute-start | bytes 1376264 | tf_op jit(solution)/shard_map/ppermute | solution.py:41
  114.8 8.3 %collective-permute-start.16 = (f32[2,136,512]{2,1,0:T(8,128)S(1)}, f32[2,136,512]{2,1,0:T(8,128)S(1)}, u32[]{:S(2)}, u32[]{:S(2)}) collective-permute-start(f32[2,136,512]{2,1,0:T(8,128)S(1)} %pad_maximum_fusion.3), channel_id=1, source_target_pairs={{0,16},{16,0},{32,48},{48,32},{64,80},{80,64},{96,112},{112,96},{1... | collective-permute-start | bytes 1671176 | tf_op jit(solution)/shard_map/ppermute | solution.py:24
  123.4 1.2 collective-permute-done.16
  124.8 3.0 %collective-permute-start.17 = (bf16[144,512]{1,0:T(8,128)(2,1)S(1)}, bf16[144,512]{1,0:T(8,128)(2,1)S(1)}, u32[]{:S(2)}, u32[]{:S(2)}) collective-permute-start(bf16[144,512]{1,0:T(8,128)(2,1)S(1)} %pad_maximum_fusion.16), channel_id=1, source_target_pairs={{0,8},{1,9},{2,10},{3,11},{4,12},{5,13},{6,14},{7,15},{8,0},{9,1},... | collective-permute-start | bytes 442376 | tf_op jit(solution)/shard_map/ppermute | solution.py:35
  127.9 10.9 %collective-permute-done.17 = bf16[144,512]{1,0:T(8,128)(2,1)S(1)} collective-permute-done((bf16[144,512]{1,0:T(8,128)(2,1)S(1)}, bf16[144,512]{1,0:T(8,128)(2,1)S(1)}, u32[]{:S(2)}, u32[]{:S(2)}) %collective-permute-start.17) | collective-permute-done | bytes 147488 | tf_op jit(solution)/shard_map/ppermute | solution.py:35
  140.4 1.9 collective-permute-start.18
  142.6 10.5 %collective-permute-done.18 = bf16[144,512]{1,0:T(8,128)(2,1)S(1)} collective-permute-done((bf16[144,512]{1,0:T(8,128)(2,1)S(1)}, bf16[144,512]{1,0:T(8,128)(2,1)S(1)}, u32[]{:S(2)}, u32[]{:S(2)}) %collective-permute-start.18) | collective-permute-done | bytes 147488 | tf_op jit(solution)/shard_map/ppermute | solution.py:35
  153.3 3.5 %collective-permute-start.19 = (bf16[2,144,512]{2,1,0:T(8,128)(2,1)S(1)}, bf16[2,144,512]{2,1,0:T(8,128)(2,1)S(1)}, u32[]{:S(2)}, u32[]{:S(2)}) collective-permute-start(bf16[2,144,512]{2,1,0:T(8,128)(2,1)S(1)} %fusion.21), channel_id=1, source_target_pairs={{0,16},{16,0},{32,48},{48,32},{64,80},{80,64},{96,112},{112,96},{1... | collective-permute-start | bytes 884744 | tf_op jit(solution)/shard_map/ppermute | solution.py:24
  160.3 1.0 pad_maximum_fusion.1
  161.3 4.3 %all-to-all-start = ((bf16[8,240,256]{2,1,0:T(8,128)(2,1)}), bf16[8,240,256]{2,1,0:T(8,128)(2,1)S(1)}, u32[]{:S(2)}, u32[]{:S(2)}) async-start(bf16[8,240,256]{2,1,0:T(8,128)(2,1)} %pad_maximum_fusion.1), calls=%async_computation | async-start | bytes 1966080 | tf_op jit(solution)/shard_map/all_to_all | solution.py:280
  165.6 2.6 %collective-permute-start.22 = (bf16[4,224,128]{2,1,0:T(8,128)(2,1)S(1)}, bf16[4,224,128]{2,1,0:T(8,128)(2,1)S(1)}, u32[]{:S(2)}, u32[]{:S(2)}) collective-permute-start(bf16[4,224,128]{2,1,0:T(8,128)(2,1)S(1)} %pad_maximum_fusion.14), channel_id=1, source_target_pairs={{0,32},{16,48},{32,64},{48,80},{64,96},{80,112},{96,0},{112,16},{1... | collective-permute-start | bytes 688136 | tf_op jit(solution)/shard_map/ppermute | solution.py:41
  168.3 4.6 %collective-permute-start.23 = (bf16[4,224,128]{2,1,0:T(8,128)(2,1)S(1)}, bf16[4,224,128]{2,1,0:T(8,128)(2,1)S(1)}, u32[]{:S(2)}, u32[]{:S(2)}) collective-permute-start(bf16[4,224,128]{2,1,0:T(8,128)(2,1)S(1)} %pad_maximum_fusion.15), channel_id=1, source_target_pairs={{0,96},{16,112},{32,0},{48,16},{64,32},{80,48},{96,64},{112,80},{1... | collective-permute-start | bytes 688136 | tf_op jit(solution)/shard_map/ppermute | solution.py:41
  172.9 3.1 %collective-permute-start.21 = (bf16[4,224,128]{2,1,0:T(8,128)(2,1)S(1)}, bf16[4,224,128]{2,1,0:T(8,128)(2,1)S(1)}, u32[]{:S(2)}, u32[]{:S(2)}) collective-permute-start(bf16[4,224,128]{2,1,0:T(8,128)(2,1)S(1)} %pad_maximum_fusion.13), channel_id=1, source_target_pairs={{0,64},{16,80},{32,96},{48,112},{64,0},{80,16},{96,32},{112,48},{1... | collective-permute-start | bytes 688136 | tf_op jit(solution)/shard_map/ppermute | solution.py:41
  176.3 0.9 collective-permute-done.23
  177.2 5.3 %collective-permute-done.21 = bf16[4,224,128]{2,1,0:T(8,128)(2,1)S(1)} collective-permute-done((bf16[4,224,128]{2,1,0:T(8,128)(2,1)S(1)}, bf16[4,224,128]{2,1,0:T(8,128)(2,1)S(1)}, u32[]{:S(2)}, u32[]{:S(2)}) %collective-permute-start.21) | collective-permute-done | bytes 229408 | tf_op jit(solution)/shard_map/ppermute | solution.py:41
  183.3 1.9 collective-permute-start.25
  185.2 5.8 %collective-permute-start.26 = (bf16[224,128]{1,0:T(8,128)(2,1)S(1)}, bf16[224,128]{1,0:T(8,128)(2,1)S(1)}, u32[]{:S(2)}, u32[]{:S(2)}) collective-permute-start(bf16[224,128]{1,0:T(8,128)(2,1)S(1)} %get-tuple-element.82), channel_id=1, source_target_pairs={{0,8},{1,9},{2,10},{3,11},{4,12},{5,13},{6,14},{7,15},{8,264},{9,2... | collective-permute-start | bytes 172040 | tf_op jit(solution)/shard_map/ppermute | solution.py:53
  191.1 3.6 %collective-permute-start.27 = (bf16[224,128]{1,0:T(8,128)(2,1)S(1)}, bf16[224,128]{1,0:T(8,128)(2,1)S(1)}, u32[]{:S(2)}, u32[]{:S(2)}) collective-permute-start(bf16[224,128]{1,0:T(8,128)(2,1)S(1)} %get-tuple-element.81), channel_id=1, source_target_pairs={{0,136},{1,137},{2,138},{3,139},{4,140},{5,141},{6,142},{7,143},{8... | collective-permute-start | bytes 172040 | tf_op jit(solution)/shard_map/ppermute | solution.py:53
  195.5 1.5 collective-permute-done.27
  197.8 4.5 %collective-permute-start.20 = (f32[224,128]{1,0:T(8,128)S(1)}, f32[224,128]{1,0:T(8,128)S(1)}, u32[]{:S(2)}, u32[]{:S(2)}) collective-permute-start(f32[224,128]{1,0:T(8,128)S(1)} %get-tuple-element.78), channel_id=1, source_target_pairs={{0,16},{16,0},{32,48},{48,32},{64,80},{80,64},{96,112},{112,96},{1... | collective-permute-start | bytes 344072 | tf_op jit(solution)/shard_map/ppermute | solution.py:24
  202.3 0.9 collective-permute-done.20
  203.3 0.8 fusion.59
  (171 shorter events, 18.0 us)
Async XLA Ops:
  3.5 19.1 %collective-permute-start.2 = (bf16[224,256]{1,0:T(8,128)(2,1)S(1)}, bf16[224,256]{1,0:T(8,128)(2,1)S(1)}, u32[]{:S(2)}, u32[]{:S(2)}) collective-permute-start(bf16[224,256]{1,0:T(8,128)(2,1)S(1)} %get-tuple-element.85), channel_id=1, source_target_pairs={{0,16},{16,0},{32,48},{48,32},{64,80},{80,64},{96,112},{112,96},{1... | collective-permute-start | bytes 344072 | tf_op jit(solution)/shard_map/ppermute | solution.py:24
  14.3 8.3 %collective-permute-start.1 = (f32[2,128]{1,0:T(2,128)S(1)}, f32[2,128]{1,0:T(2,128)S(1)}, u32[]{:S(2)}, u32[]{:S(2)}) collective-permute-start(f32[2,128]{1,0:T(2,128)S(1)} %pad_maximum_fusion.20), channel_id=1, source_target_pairs={{0,8},{1,9},{2,10},{3,11},{4,12},{5,13},{6,14},{7,15},{8,0},{9,1},... | collective-permute-start | bytes 3080 | tf_op jit(solution)/shard_map/ppermute | solution.py:35
  16.4 6.3 %collective-permute-start = (bf16[224,512]{1,0:T(8,128)(2,1)S(1)}, bf16[224,512]{1,0:T(8,128)(2,1)S(1)}, u32[]{:S(2)}, u32[]{:S(2)}) collective-permute-start(bf16[224,512]{1,0:T(8,128)(2,1)S(1)} %pad_maximum_fusion.11), channel_id=1, source_target_pairs={{0,0},{1,1},{2,2},{3,3},{4,4},{5,5},{6,6},{7,7},{8,256},{9,257},{1... | collective-permute-start | bytes 688136 | tf_op jit(solution)/shard_map/ppermute | solution.py:53
  22.6 3.8 %collective-permute-start.3 = (f32[2,128]{1,0:T(2,128)S(1)}, f32[2,128]{1,0:T(2,128)S(1)}, u32[]{:S(2)}, u32[]{:S(2)}) collective-permute-start(f32[2,128]{1,0:T(2,128)S(1)} %pad_maximum_fusion.21), channel_id=1, source_target_pairs={{0,16},{16,0},{32,48},{48,32},{64,80},{80,64},{96,112},{112,96},{1... | collective-permute-start | bytes 3080 | tf_op jit(solution)/shard_map/ppermute | solution.py:24
  53.4 19.5 %collective-permute-start.9 = (bf16[240,512]{1,0:T(8,128)(2,1)S(1)}, bf16[240,512]{1,0:T(8,128)(2,1)S(1)}, u32[]{:S(2)}, u32[]{:S(2)}) collective-permute-start(bf16[240,512]{1,0:T(8,128)(2,1)S(1)} %concatenate.99), channel_id=1, source_target_pairs={{0,1},{1,2},{2,3},{3,4},{4,5},{5,6},{6,7},{7,0},{8,9},{9,10},{10,1... | collective-permute-start | bytes 737288 | tf_op jit(solution)/shard_map/ppermute | solution.py:30
  57.2 17.6 %collective-permute-start.4 = (bf16[240,512]{1,0:T(8,128)(2,1)S(1)}, bf16[240,512]{1,0:T(8,128)(2,1)S(1)}, u32[]{:S(2)}, u32[]{:S(2)}) collective-permute-start(bf16[240,512]{1,0:T(8,128)(2,1)S(1)} %concatenate.99), channel_id=1, source_target_pairs={{0,7},{1,0},{2,1},{3,2},{4,3},{5,4},{6,5},{7,6},{8,15},{9,8},{10,9... | collective-permute-start | bytes 737288 | tf_op jit(solution)/shard_map/ppermute | solution.py:30
  66.4 29.7 %collective-permute-start.7 = (bf16[4,224,512]{2,1,0:T(8,128)(2,1)S(1)}, bf16[4,224,512]{2,1,0:T(8,128)(2,1)S(1)}, u32[]{:S(2)}, u32[]{:S(2)}) collective-permute-start(bf16[4,224,512]{2,1,0:T(8,128)(2,1)S(1)} %bitcast.193), channel_id=1, source_target_pairs={{0,32},{16,48},{32,64},{48,80},{64,96},{80,112},{96,0},{112,16},{1... | collective-permute-start | bytes 2752520 | tf_op jit(solution)/shard_map/ppermute | solution.py:41
  69.5 26.5 %collective-permute-start.8 = (bf16[4,224,512]{2,1,0:T(8,128)(2,1)S(1)}, bf16[4,224,512]{2,1,0:T(8,128)(2,1)S(1)}, u32[]{:S(2)}, u32[]{:S(2)}) collective-permute-start(bf16[4,224,512]{2,1,0:T(8,128)(2,1)S(1)} %bitcast.194), channel_id=1, source_target_pairs={{0,96},{16,112},{32,0},{48,16},{64,32},{80,48},{96,64},{112,80},{1... | collective-permute-start | bytes 2752520 | tf_op jit(solution)/shard_map/ppermute | solution.py:41
  72.9 15.0 %collective-permute-start.10 = (bf16[240,512]{1,0:T(8,128)(2,1)S(1)}, bf16[240,512]{1,0:T(8,128)(2,1)S(1)}, u32[]{:S(2)}, u32[]{:S(2)}) collective-permute-start(bf16[240,512]{1,0:T(8,128)(2,1)S(1)} %collective-permute-done.9), channel_id=1, source_target_pairs={{0,1},{1,2},{2,3},{3,4},{4,5},{5,6},{6,7},{7,0},{8,9},{9,10},{10,1... | collective-permute-start | bytes 737288 | tf_op jit(solution)/shard_map/ppermute | solution.py:30
  74.8 7.7 %collective-permute-start.5 = (bf16[240,512]{1,0:T(8,128)(2,1)S(1)}, bf16[240,512]{1,0:T(8,128)(2,1)S(1)}, u32[]{:S(2)}, u32[]{:S(2)}) collective-permute-start(bf16[240,512]{1,0:T(8,128)(2,1)S(1)} %collective-permute-done.4), channel_id=1, source_target_pairs={{0,7},{1,0},{2,1},{3,2},{4,3},{5,4},{6,5},{7,6},{8,15},{9,8},{10,9... | collective-permute-start | bytes 737288 | tf_op jit(solution)/shard_map/ppermute | solution.py:30
  82.5 8.4 %collective-permute-start.6 = (bf16[240,512]{1,0:T(8,128)(2,1)S(1)}, bf16[240,512]{1,0:T(8,128)(2,1)S(1)}, u32[]{:S(2)}, u32[]{:S(2)}) collective-permute-start(bf16[240,512]{1,0:T(8,128)(2,1)S(1)} %collective-permute-done.5), channel_id=1, source_target_pairs={{0,7},{1,0},{2,1},{3,2},{4,3},{5,4},{6,5},{7,6},{8,15},{9,8},{10,9... | collective-permute-start | bytes 737288 | tf_op jit(solution)/shard_map/ppermute | solution.py:30
  87.9 8.2 %collective-permute-start.11 = (bf16[240,512]{1,0:T(8,128)(2,1)S(1)}, bf16[240,512]{1,0:T(8,128)(2,1)S(1)}, u32[]{:S(2)}, u32[]{:S(2)}) collective-permute-start(bf16[240,512]{1,0:T(8,128)(2,1)S(1)} %collective-permute-done.10), channel_id=1, source_target_pairs={{0,1},{1,2},{2,3},{3,4},{4,5},{5,6},{6,7},{7,0},{8,9},{9,10},{10,1... | collective-permute-start | bytes 737288 | tf_op jit(solution)/shard_map/ppermute | solution.py:30
  96.1 12.0 %collective-permute-start.13 = (bf16[128,512]{1,0:T(8,128)(2,1)S(1)}, bf16[128,512]{1,0:T(8,128)(2,1)S(1)}, u32[]{:S(2)}, u32[]{:S(2)}) collective-permute-start(bf16[128,512]{1,0:T(8,128)(2,1)S(1)} %slice.388), channel_id=1, source_target_pairs={{0,7},{1,0},{2,1},{3,2},{4,3},{5,4},{6,5},{7,6},{8,15},{9,8},{10,9... | collective-permute-start | bytes 393224 | tf_op jit(solution)/shard_map/ppermute | solution.py:30
  98.0 10.0 %collective-permute-start.12 = (bf16[112,512]{1,0:T(8,128)(2,1)S(1)}, bf16[112,512]{1,0:T(8,128)(2,1)S(1)}, u32[]{:S(2)}, u32[]{:S(2)}) collective-permute-start(bf16[112,512]{1,0:T(8,128)(2,1)S(1)} %slice.387), channel_id=1, source_target_pairs={{0,1},{1,2},{2,3},{3,4},{4,5},{5,6},{6,7},{7,0},{8,9},{9,10},{10,1... | collective-permute-start | bytes 344072 | tf_op jit(solution)/shard_map/ppermute | solution.py:30
  101.5 11.7 %collective-permute-start.14 = (bf16[2,224,512]{2,1,0:T(8,128)(2,1)S(1)}, bf16[2,224,512]{2,1,0:T(8,128)(2,1)S(1)}, u32[]{:S(2)}, u32[]{:S(2)}) collective-permute-start(bf16[2,224,512]{2,1,0:T(8,128)(2,1)S(1)} %get-tuple-element.52), channel_id=1, source_target_pairs={{0,32},{16,48},{32,64},{48,80},{64,96},{80,112},{96,0},{112,16},{1... | collective-permute-start | bytes 1376264 | tf_op jit(solution)/shard_map/ppermute | solution.py:41
  103.4 10.2 %collective-permute-start.15 = (bf16[2,224,512]{2,1,0:T(8,128)(2,1)S(1)}, bf16[2,224,512]{2,1,0:T(8,128)(2,1)S(1)}, u32[]{:S(2)}, u32[]{:S(2)}) collective-permute-start(bf16[2,224,512]{2,1,0:T(8,128)(2,1)S(1)} %get-tuple-element.51), channel_id=1, source_target_pairs={{0,96},{16,112},{32,0},{48,16},{64,32},{80,48},{96,64},{112,80},{1... | collective-permute-start | bytes 1376264 | tf_op jit(solution)/shard_map/ppermute | solution.py:41
  114.8 9.8 %collective-permute-start.16 = (f32[2,136,512]{2,1,0:T(8,128)S(1)}, f32[2,136,512]{2,1,0:T(8,128)S(1)}, u32[]{:S(2)}, u32[]{:S(2)}) collective-permute-start(f32[2,136,512]{2,1,0:T(8,128)S(1)} %pad_maximum_fusion.3), channel_id=1, source_target_pairs={{0,16},{16,0},{32,48},{48,32},{64,80},{80,64},{96,112},{112,96},{1... | collective-permute-start | bytes 1671176 | tf_op jit(solution)/shard_map/ppermute | solution.py:24
  123.3 15.7 %copy-start.1 = (f32[384]{0:T(512)S(1)}, f32[384]{0:T(512)}, u32[]{:S(2)}) copy-start(f32[384]{0:T(512)} %param.11) | copy-start | bytes 4612
  124.8 14.0 %collective-permute-start.17 = (bf16[144,512]{1,0:T(8,128)(2,1)S(1)}, bf16[144,512]{1,0:T(8,128)(2,1)S(1)}, u32[]{:S(2)}, u32[]{:S(2)}) collective-permute-start(bf16[144,512]{1,0:T(8,128)(2,1)S(1)} %pad_maximum_fusion.16), channel_id=1, source_target_pairs={{0,8},{1,9},{2,10},{3,11},{4,12},{5,13},{6,14},{7,15},{8,0},{9,1},... | collective-permute-start | bytes 442376 | tf_op jit(solution)/shard_map/ppermute | solution.py:35
  140.4 12.7 %collective-permute-start.18 = (bf16[144,512]{1,0:T(8,128)(2,1)S(1)}, bf16[144,512]{1,0:T(8,128)(2,1)S(1)}, u32[]{:S(2)}, u32[]{:S(2)}) collective-permute-start(bf16[144,512]{1,0:T(8,128)(2,1)S(1)} %fusion.47), channel_id=1, source_target_pairs={{0,8},{1,9},{2,10},{3,11},{4,12},{5,13},{6,14},{7,15},{8,0},{9,1},... | collective-permute-start | bytes 442376 | tf_op jit(solution)/shard_map/ppermute | solution.py:35
  153.3 4.5 %collective-permute-start.19 = (bf16[2,144,512]{2,1,0:T(8,128)(2,1)S(1)}, bf16[2,144,512]{2,1,0:T(8,128)(2,1)S(1)}, u32[]{:S(2)}, u32[]{:S(2)}) collective-permute-start(bf16[2,144,512]{2,1,0:T(8,128)(2,1)S(1)} %fusion.21), channel_id=1, source_target_pairs={{0,16},{16,0},{32,48},{48,32},{64,80},{80,64},{96,112},{112,96},{1... | collective-permute-start | bytes 884744 | tf_op jit(solution)/shard_map/ppermute | solution.py:24
  161.3 42.0 %copy-start = (bf16[128,448]{0,1:T(8,128)(2,1)S(1)}, bf16[128,448]{0,1:T(8,128)(2,1)}, u32[]{:S(2)}) copy-start(bf16[128,448]{0,1:T(8,128)(2,1)} %param.7) | copy-start | bytes 344068
  161.3 36.3 %all-to-all-start = ((bf16[8,240,256]{2,1,0:T(8,128)(2,1)}), bf16[8,240,256]{2,1,0:T(8,128)(2,1)S(1)}, u32[]{:S(2)}, u32[]{:S(2)}) async-start(bf16[8,240,256]{2,1,0:T(8,128)(2,1)} %pad_maximum_fusion.1), calls=%async_computation | async-start | bytes 1966080 | tf_op jit(solution)/shard_map/all_to_all | solution.py:280
  165.6 10.7 %collective-permute-start.22 = (bf16[4,224,128]{2,1,0:T(8,128)(2,1)S(1)}, bf16[4,224,128]{2,1,0:T(8,128)(2,1)S(1)}, u32[]{:S(2)}, u32[]{:S(2)}) collective-permute-start(bf16[4,224,128]{2,1,0:T(8,128)(2,1)S(1)} %pad_maximum_fusion.14), channel_id=1, source_target_pairs={{0,32},{16,48},{32,64},{48,80},{64,96},{80,112},{96,0},{112,16},{1... | collective-permute-start | bytes 688136 | tf_op jit(solution)/shard_map/ppermute | solution.py:41
  168.3 8.9 %collective-permute-start.23 = (bf16[4,224,128]{2,1,0:T(8,128)(2,1)S(1)}, bf16[4,224,128]{2,1,0:T(8,128)(2,1)S(1)}, u32[]{:S(2)}, u32[]{:S(2)}) collective-permute-start(bf16[4,224,128]{2,1,0:T(8,128)(2,1)S(1)} %pad_maximum_fusion.15), channel_id=1, source_target_pairs={{0,96},{16,112},{32,0},{48,16},{64,32},{80,48},{96,64},{112,80},{1... | collective-permute-start | bytes 688136 | tf_op jit(solution)/shard_map/ppermute | solution.py:41
  172.9 9.6 %collective-permute-start.21 = (bf16[4,224,128]{2,1,0:T(8,128)(2,1)S(1)}, bf16[4,224,128]{2,1,0:T(8,128)(2,1)S(1)}, u32[]{:S(2)}, u32[]{:S(2)}) collective-permute-start(bf16[4,224,128]{2,1,0:T(8,128)(2,1)S(1)} %pad_maximum_fusion.13), channel_id=1, source_target_pairs={{0,64},{16,80},{32,96},{48,112},{64,0},{80,16},{96,32},{112,48},{1... | collective-permute-start | bytes 688136 | tf_op jit(solution)/shard_map/ppermute | solution.py:41
  182.6 12.8 %collective-permute-start.24 = (bf16[224,128]{1,0:T(8,128)(2,1)S(1)}, bf16[224,128]{1,0:T(8,128)(2,1)S(1)}, u32[]{:S(2)}, u32[]{:S(2)}) collective-permute-start(bf16[224,128]{1,0:T(8,128)(2,1)S(1)} %get-tuple-element.80), channel_id=1, source_target_pairs={{0,0},{1,1},{2,2},{3,3},{4,4},{5,5},{6,6},{7,7},{8,256},{9,257},{1... | collective-permute-start | bytes 172040 | tf_op jit(solution)/shard_map/ppermute | solution.py:53
  183.3 12.2 %collective-permute-start.25 = (bf16[224,128]{1,0:T(8,128)(2,1)S(1)}, bf16[224,128]{1,0:T(8,128)(2,1)S(1)}, u32[]{:S(2)}, u32[]{:S(2)}) collective-permute-start(bf16[224,128]{1,0:T(8,128)(2,1)S(1)} %get-tuple-element.83), channel_id=1, source_target_pairs={{0,128},{1,129},{2,130},{3,131},{4,132},{5,133},{6,134},{7,135},{8... | collective-permute-start | bytes 172040 | tf_op jit(solution)/shard_map/ppermute | solution.py:53
  185.2 10.2 %collective-permute-start.26 = (bf16[224,128]{1,0:T(8,128)(2,1)S(1)}, bf16[224,128]{1,0:T(8,128)(2,1)S(1)}, u32[]{:S(2)}, u32[]{:S(2)}) collective-permute-start(bf16[224,128]{1,0:T(8,128)(2,1)S(1)} %get-tuple-element.82), channel_id=1, source_target_pairs={{0,8},{1,9},{2,10},{3,11},{4,12},{5,13},{6,14},{7,15},{8,264},{9,2... | collective-permute-start | bytes 172040 | tf_op jit(solution)/shard_map/ppermute | solution.py:53
  191.1 5.8 %collective-permute-start.27 = (bf16[224,128]{1,0:T(8,128)(2,1)S(1)}, bf16[224,128]{1,0:T(8,128)(2,1)S(1)}, u32[]{:S(2)}, u32[]{:S(2)}) collective-permute-start(bf16[224,128]{1,0:T(8,128)(2,1)S(1)} %get-tuple-element.81), channel_id=1, source_target_pairs={{0,136},{1,137},{2,138},{3,139},{4,140},{5,141},{6,142},{7,143},{8... | collective-permute-start | bytes 172040 | tf_op jit(solution)/shard_map/ppermute | solution.py:53
  197.8 5.5 %collective-permute-start.20 = (f32[224,128]{1,0:T(8,128)S(1)}, f32[224,128]{1,0:T(8,128)S(1)}, u32[]{:S(2)}, u32[]{:S(2)}) collective-permute-start(f32[224,128]{1,0:T(8,128)S(1)} %get-tuple-element.78), channel_id=1, source_target_pairs={{0,16},{16,0},{32,48},{48,32},{64,80},{80,64},{96,112},{112,96},{1... | collective-permute-start | bytes 344072 | tf_op jit(solution)/shard_map/ppermute | solution.py:24

commit v14 on v10

--- a/solution.py
+++ b/solution.py
@@ -28,6 +28,11 @@
     n = lax.axis_size("tensor")
     pairs = [(i, i - i % Z_COUNT + (i + step) % Z_COUNT) for i in range(n)]
     return lax.ppermute(x, "tensor", pairs)
+
+
+def swap_z(x, bit):
+    n = lax.axis_size("tensor")
+    return lax.ppermute(x, "tensor", [(i, i ^ bit) for i in range(n)])
 
 
 def swap_far(x):
@@ -70,10 +75,9 @@
     return lax.dynamic_slice_in_dim(line, X_COUNT - 1 - place, X_COUNT, 1)
 
 
-def ring_scatter_x(part, across):
-    ahead = part(1).astype(f32) + shift_x(across, 1).astype(f32)
-    up, down = shift_x(ahead.astype(bf16), 1), shift_x(part(-1), -1)
-    return part(0).astype(f32) + up.astype(f32) + down.astype(f32)
+def scatter_x(part, across):
+    total = part(0).astype(f32) + shift_x(across, 2).astype(f32)
+    return total + shift_x(part(1), 1).astype(f32) + shift_x(part(-1), -1).astype(f32)
 
 
 def scatter_y(parts, place):
@@ -94,7 +98,7 @@
 
 def split(x):
     high = lax.reduce_precision(x, 8, 7)
-    return high.astype(bf16), (x - high).astype(bf16)
+    return high.astype(bf16), lax.reduce_precision(x - high, 8, 7).astype(bf16)
 
 
 def dot(a, b, dims):
@@ -147,22 +151,31 @@
 
     weight_block = move_weights(jnp.concatenate([w_qkv, w_out.T], axis=1))
 
-    slice_f = hidden_t.astype(f32)
+    rows = lax.all_gather(block, "tensor", axis=0, tiled=True, axis_index_groups=rings)
+    weight_block, _ = lax.optimization_barrier((weight_block, block))
+    column = lax.all_gather(weight_block, "dp", axis=0, axis_index_groups=lines)
+
+    def merge(stats, stats_other, count):
+        gap = stats[0] - stats_other[0]
+        return jnp.stack(
+            [
+                0.5 * (stats[0] + stats_other[0]),
+                stats[1] + stats_other[1] + gap * gap * (count / 2),
+            ]
+        )
+
+    _, slice_f = lax.optimization_barrier((block, hidden_t.astype(f32)))
     mean_part = jnp.mean(slice_f, axis=0)
     stats = jnp.stack([mean_part, jnp.sum((slice_f - mean_part) ** 2, axis=0)])
-    block, stats = lax.optimization_barrier((block, stats))
-    stats = lax.all_to_all(
-        jnp.broadcast_to(stats[None], (n_tensor, 2, SEQ)), "tensor", 0, 0, tiled=True
-    )
-    weight_block, stats = lax.optimization_barrier((weight_block, stats))
-    column = lax.all_gather(weight_block, "dp", axis=0, axis_index_groups=lines)
-    mean = jnp.mean(stats[:, 0], axis=0)
-    square = jnp.sum(stats[:, 1], axis=0) + width * jnp.sum((stats[:, 0] - mean) ** 2, axis=0)
-    stats = jnp.stack([mean, lax.rsqrt(square / depth + norm_eps)])
-    mean, inv_std = jnp.concatenate([stats, swap_cores(stats)], axis=1)
-
-    rows = lax.all_gather(block, "tensor", axis=0, tiled=True, axis_index_groups=rings)
-    blocks, rows = x_gather(column, x, rows)
+    stats = merge(stats, swap_far(stats), width)
+    _, stats = lax.optimization_barrier((column, stats))
+    for bit in (1, 2, 4):
+        stats = merge(stats, swap_z(stats, bit), 2 * width * bit)
+    stats = jnp.stack([stats[0], lax.rsqrt(stats[1] / depth + norm_eps)])
+    stats = jnp.concatenate([stats, swap_cores(stats)], axis=1)
+
+    blocks, (rows, stats) = x_gather(column, x, (rows, stats))
+    mean, inv_std = stats
     hidden = rows[:, : 2 * SEQ].astype(f32)
     grads = rows[:, 2 * SEQ :]
 
@@ -259,7 +272,7 @@
     payload = jnp.concatenate([group_part.reshape(Z_COUNT, part, 2 * SEQ), extra], axis=1)
     group_parts = lax.all_to_all(payload, "tensor", 0, 0, tiled=True, axis_index_groups=rings)
     total = jnp.sum(group_parts.astype(f32), axis=0)
-    weight_parts = ring_scatter_x(weight_to, across)
+    weight_parts = scatter_x(weight_to, across)
     grad_out_weight = scatter_y(weight_parts, y)
     sums = total[part : part + 2, :SEQ] + total[part + 2 : part + 4, :SEQ]
     total = total[:part]

time: 208 us -> 204 us (0.981)
  waiting for transfers between devices: 63.9 us -> 49.2 us
  starting transfers between devices: 88.4 us -> 97.3 us
    ppermute x0 -> x3, starting transfers between devices: none -> 16.8 us  [swap_z(): return lax.ppermute(x, 'tensor', [(i, i ^ bit) for i in range(n)])]
    ppermute x7, waiting for transfers between devices: 28.3 us -> 16.3 us  [shift_x(): lax.ppermute(x, 'dp', [(i, i - i % row + (i + 2 * step) % row) for i in r...]
    all_to_all x1 -> x0, starting transfers between devices: 11.3 us -> none  [body(): lax.all_to_all(jnp.broadcast_to(stats[None], (n_tensor, 2, SEQ)), 'tensor...]
    all_to_all x1 -> x0, waiting for transfers between devices: 11 us -> none  [body(): lax.all_to_all(jnp.broadcast_to(stats[None], (n_tensor, 2, SEQ)), 'tensor...]
    ppermute x2 -> x3, waiting for transfers between devices: 17.9 us -> 25.9 us  [swap_far(): return lax.ppermute(x, 'tensor', [(i, (i + Z_COUNT) % n) for i in range(n)])]
    ppermute x5, starting transfers between devices: 33.7 us -> 27.9 us  [swap_cores(): return lax.ppermute(x, 'dp', [(i, i ^ 1) for i in range(n)])]
    ppermute x2 -> x3, starting transfers between devices: 4.92 us -> 9.3 us  [swap_far(): return lax.ppermute(x, 'tensor', [(i, (i + Z_COUNT) % n) for i in range(n)])]
    all_to_all x1, starting transfers between devices: 3.55 us -> 6.94 us  [body(): lax.all_to_all(payload, 'tensor', 0, 0, tiled=True, axis_index_groups=rings)]
  transfers between devices with their start and end apart: 22 -> 25, of which waited for: 14 -> 14; matrix products, arithmetic and copies ran while one was open for 4% -> 5% of each run, Pallas kernels for 0% -> 0%
where the time goes in v14:
time: 204 us; the launch traced here: 203 us
  starting transfers between devices  97.3 us (48%)
  waiting for transfers between devices  49.2 us (24%)
  blocking collectives  17.4 us (9%)
  between operations  15.3 us (8%)
  other arithmetic  11.9 us (6%)
  matrix products  7.83 us (4%)
  local copies, waits for them, and re-layouts  4.14 us (2%)
    ppermute x5, starting transfers between devices, swap_cores(): return lax.ppermute(x, 'dp', [(i, i ^ 1) for i in range(n)])  27.9 us
    ppermute x3, waiting for transfers between devices, swap_far(): return lax.ppermute(x, 'tensor', [(i, (i + Z_COUNT) % n) for i in range(n)])  25.9 us
    ppermute x7, starting transfers between devices, shift_x(): lax.ppermute(x, 'dp', [(i, i - i % row + (i + 2 * step) % row) for i in r...  21.5 us
    all_gather x1, blocking collectives, body(): column = lax.all_gather(weight_block, 'dp', axis=0, axis_index_groups=lines)  17.4 us
    ppermute x3, starting transfers between devices, swap_z(): return lax.ppermute(x, 'tensor', [(i, i ^ bit) for i in range(n)])  16.8 us
    ppermute x7, waiting for transfers between devices, shift_x(): lax.ppermute(x, 'dp', [(i, i - i % row + (i + 2 * step) % row) for i in r...  16.3 us
    ppermute x5, starting transfers between devices, along_y(): return lax.ppermute(x, ('dp', 'tensor'), pairs)  14.9 us
    ppermute x3, starting transfers between devices, swap_far(): return lax.ppermute(x, 'tensor', [(i, (i + Z_COUNT) % n) for i in range(n)])  9.3 us
  transfers between devices with their start and end apart: 25, of which 14 were waited for; matrix products, arithmetic and copies ran while one was open for 5% of the time, Pallas kernels for 0%

profile of v14, /device:TPU:1, one launch (start us, length us, event | category | flops | bytes accessed | tf_op | source)
XLA Modules:
  0.0 203.1 jit_solution(14676190606654289193)
XLA Ops:
  7.2 1.0 broadcast_select_fusion.1
  8.2 8.8 %collective-permute-start.1 = (bf16[224,256]{1,0:T(8,128)(2,1)S(1)}, bf16[224,256]{1,0:T(8,128)(2,1)S(1)}, u32[]{:S(2)}, u32[]{:S(2)}) collective-permute-start(bf16[224,256]{1,0:T(8,128)(2,1)S(1)} %get-tuple-element.65), channel_id=1, source_target_pairs={{0,16},{16,0},{32,48},{48,32},{64,80},{80,64},{96,112},{112,96},{1... | collective-permute-start | bytes 344072 | tf_op jit(solution)/shard_map/ppermute | solution.py:24
  17.0 1.0 pad_maximum_fusion.11
  18.0 0.7 collective-permute-start
  18.7 0.9 bitcast_convert_fusion
  19.7 0.8 slice_select_fusion.2
  20.5 0.8 slice_select_fusion.3
  21.5 0.7 pad_maximum_fusion.12
  22.7 3.4 %collective-permute-start.4 = (f32[2,128]{1,0:T(2,128)S(1)}, f32[2,128]{1,0:T(2,128)S(1)}, u32[]{:S(2)}, u32[]{:S(2)}) collective-permute-start(f32[2,128]{1,0:T(2,128)S(1)} %pad_maximum_fusion.22), channel_id=1, source_target_pairs={{0,8},{1,9},{2,10},{3,11},{4,12},{5,13},{6,14},{7,15},{8,0},{9,1},... | collective-permute-start | bytes 3080 | tf_op jit(solution)/shard_map/ppermute | solution.py:40
  26.1 4.9 %collective-permute-done.4 = f32[2,128]{1,0:T(2,128)S(1)} collective-permute-done((f32[2,128]{1,0:T(2,128)S(1)}, f32[2,128]{1,0:T(2,128)S(1)}, u32[]{:S(2)}, u32[]{:S(2)}) %collective-permute-start.4) | collective-permute-done | bytes 1056 | tf_op jit(solution)/shard_map/ppermute | solution.py:40
  31.1 17.4 %all-gather = bf16[896,512]{1,0:T(8,128)(2,1)S(1)} all-gather(bf16[224,512]{1,0:T(8,128)(2,1)S(1)} %collective-permute-done), channel_id=2, replica_groups={{0,128,256,384},{16,144,272,400},{32,160,288,416},{48,176,304,432},{64,..., dimensions={0}, use_global_device_ids=true | all-gather | bytes 1146880 | tf_op jit(solution)/shard_map/all_gather | solution.py:156
  48.5 2.9 %collective-permute-start.5 = (f32[2,128]{1,0:T(2,128)S(1)}, f32[2,128]{1,0:T(2,128)S(1)}, u32[]{:S(2)}, u32[]{:S(2)}) collective-permute-start(f32[2,128]{1,0:T(2,128)S(1)} %pad_maximum_fusion.23), channel_id=1, source_target_pairs={{0,1},{1,0},{2,3},{3,2},{4,5},{5,4},{6,7},{7,6},{8,9},{9,8},{10,11... | collective-permute-start | bytes 3080 | tf_op jit(solution)/shard_map/ppermute | solution.py:35
  51.4 4.4 %collective-permute-start.3 = (bf16[4,224,512]{2,1,0:T(8,128)(2,1)S(1)}, bf16[4,224,512]{2,1,0:T(8,128)(2,1)S(1)}, u32[]{:S(2)}, u32[]{:S(2)}) collective-permute-start(bf16[4,224,512]{2,1,0:T(8,128)(2,1)S(1)} %bitcast.162), channel_id=1, source_target_pairs={{0,96},{16,112},{32,0},{48,16},{64,32},{80,48},{96,64},{112,80},{1... | collective-permute-start | bytes 2752520 | tf_op jit(solution)/shard_map/ppermute | solution.py:46
  55.8 1.9 collective-permute-start.2
  57.8 6.0 %collective-permute-start.6 = (f32[2,128]{1,0:T(2,128)S(1)}, f32[2,128]{1,0:T(2,128)S(1)}, u32[]{:S(2)}, u32[]{:S(2)}) collective-permute-start(f32[2,128]{1,0:T(2,128)S(1)} %pad_maximum_fusion.24), channel_id=1, source_target_pairs={{0,2},{1,3},{2,0},{3,1},{4,6},{5,7},{6,4},{7,5},{8,10},{9,11},{10,... | collective-permute-start | bytes 3080 | tf_op jit(solution)/shard_map/ppermute | solution.py:35
  63.8 1.3 collective-permute-done.6
  65.1 7.9 %collective-permute-start.7 = (f32[2,128]{1,0:T(2,128)S(1)}, f32[2,128]{1,0:T(2,128)S(1)}, u32[]{:S(2)}, u32[]{:S(2)}) collective-permute-start(f32[2,128]{1,0:T(2,128)S(1)} %pad_maximum_fusion.25), channel_id=1, source_target_pairs={{0,4},{1,5},{2,6},{3,7},{4,0},{5,1},{6,2},{7,3},{8,12},{9,13},{10,... | collective-permute-start | bytes 3080 | tf_op jit(solution)/shard_map/ppermute | solution.py:35
  73.2 0.8 collective-permute-done.7
  74.0 9.0 %collective-permute-start.8 = (f32[2,128]{1,0:T(2,128)S(1)}, f32[2,128]{1,0:T(2,128)S(1)}, u32[]{:S(2)}, u32[]{:S(2)}) collective-permute-start(f32[2,128]{1,0:T(2,128)S(1)} %pad_maximum_fusion.26), channel_id=1, source_target_pairs={{0,16},{16,0},{32,48},{48,32},{64,80},{80,64},{96,112},{112,96},{1... | collective-permute-start | bytes 3080 | tf_op jit(solution)/shard_map/ppermute | solution.py:24
  83.9 2.1 %add_convert_fusion = bf16[1792,256]{1,0:T(8,128)(2,1)S(1)} fusion(f32[1792]{0:T(1024)S(1)} %select_n.255, f32[1792]{0:T(1024)S(1)} %select_n.251, f32[256]{0:T(256)S(1)} %bitcast.210, f32[256]{0:T(256)S(1)} %bitcast.209, bf16[1792,512]{1,0:T(8,128)(2,1)} %all-gather.3.cloned.1.call-done), kind=kLoop, calls=%fused_computation.5 | loop fusion | flops 2752512 | bytes 1851392 | tf_op jit(solution)/shard_map/convert_element_type | solution.py:188
  88.2 4.9 %collective-permute-start.10 = (bf16[2,224,512]{2,1,0:T(8,128)(2,1)S(1)}, bf16[2,224,512]{2,1,0:T(8,128)(2,1)S(1)}, u32[]{:S(2)}, u32[]{:S(2)}) collective-permute-start(bf16[2,224,512]{2,1,0:T(8,128)(2,1)S(1)} %get-tuple-element.33), channel_id=1, source_target_pairs={{0,96},{16,112},{32,0},{48,16},{64,32},{80,48},{96,64},{112,80},{1... | collective-permute-start | bytes 1376264 | tf_op jit(solution)/shard_map/ppermute | solution.py:46
  93.1 1.9 collective-permute-start.9
  97.5 5.2 %collective-permute-done.10 = bf16[2,224,512]{2,1,0:T(8,128)(2,1)S(1)} collective-permute-done((bf16[2,224,512]{2,1,0:T(8,128)(2,1)S(1)}, bf16[2,224,512]{2,1,0:T(8,128)(2,1)S(1)}, u32[]{:S(2)}, u32[]{:S(2)}) %collective-permute-start.10) | collective-permute-done | bytes 458784 | tf_op jit(solution)/shard_map/ppermute | solution.py:46
  103.0 4.7 %collective-permute-done.9 = bf16[2,224,512]{2,1,0:T(8,128)(2,1)S(1)} collective-permute-done((bf16[2,224,512]{2,1,0:T(8,128)(2,1)S(1)}, bf16[2,224,512]{2,1,0:T(8,128)(2,1)S(1)}, u32[]{:S(2)}, u32[]{:S(2)}) %collective-permute-start.9) | collective-permute-done | bytes 458784 | tf_op jit(solution)/shard_map/ppermute | solution.py:46
  108.9 3.4 %collective-permute-start.11 = (f32[2,136,512]{2,1,0:T(8,128)S(1)}, f32[2,136,512]{2,1,0:T(8,128)S(1)}, u32[]{:S(2)}, u32[]{:S(2)}) collective-permute-start(f32[2,136,512]{2,1,0:T(8,128)S(1)} %pad_maximum_fusion.3), channel_id=1, source_target_pairs={{0,16},{16,0},{32,48},{48,32},{64,80},{80,64},{96,112},{112,96},{1... | collective-permute-start | bytes 1671176 | tf_op jit(solution)/shard_map/ppermute | solution.py:24
  112.6 1.2 collective-permute-done.11
  114.0 3.3 %collective-permute-start.12 = (bf16[144,512]{1,0:T(8,128)(2,1)S(1)}, bf16[144,512]{1,0:T(8,128)(2,1)S(1)}, u32[]{:S(2)}, u32[]{:S(2)}) collective-permute-start(bf16[144,512]{1,0:T(8,128)(2,1)S(1)} %pad_maximum_fusion.16), channel_id=1, source_target_pairs={{0,8},{1,9},{2,10},{3,11},{4,12},{5,13},{6,14},{7,15},{8,0},{9,1},... | collective-permute-start | bytes 442376 | tf_op jit(solution)/shard_map/ppermute | solution.py:40
  117.5 10.9 %collective-permute-done.12 = bf16[144,512]{1,0:T(8,128)(2,1)S(1)} collective-permute-done((bf16[144,512]{1,0:T(8,128)(2,1)S(1)}, bf16[144,512]{1,0:T(8,128)(2,1)S(1)}, u32[]{:S(2)}, u32[]{:S(2)}) %collective-permute-start.12) | collective-permute-done | bytes 147488 | tf_op jit(solution)/shard_map/ppermute | solution.py:40
  129.9 2.6 %collective-permute-start.13 = (bf16[144,512]{1,0:T(8,128)(2,1)S(1)}, bf16[144,512]{1,0:T(8,128)(2,1)S(1)}, u32[]{:S(2)}, u32[]{:S(2)}) collective-permute-start(bf16[144,512]{1,0:T(8,128)(2,1)S(1)} %fusion.38), channel_id=1, source_target_pairs={{0,8},{1,9},{2,10},{3,11},{4,12},{5,13},{6,14},{7,15},{8,0},{9,1},... | collective-permute-start | bytes 442376 | tf_op jit(solution)/shard_map/ppermute | solution.py:40
  132.8 10.0 %collective-permute-done.13 = bf16[144,512]{1,0:T(8,128)(2,1)S(1)} collective-permute-done((bf16[144,512]{1,0:T(8,128)(2,1)S(1)}, bf16[144,512]{1,0:T(8,128)(2,1)S(1)}, u32[]{:S(2)}, u32[]{:S(2)}) %collective-permute-start.13) | collective-permute-done | bytes 147488 | tf_op jit(solution)/shard_map/ppermute | solution.py:40
  143.0 2.6 %collective-permute-start.14 = (bf16[2,144,512]{2,1,0:T(8,128)(2,1)S(1)}, bf16[2,144,512]{2,1,0:T(8,128)(2,1)S(1)}, u32[]{:S(2)}, u32[]{:S(2)}) collective-permute-start(bf16[2,144,512]{2,1,0:T(8,128)(2,1)S(1)} %fusion.18), channel_id=1, source_target_pairs={{0,16},{16,0},{32,48},{48,32},{64,80},{80,64},{96,112},{112,96},{1... | collective-permute-start | bytes 884744 | tf_op jit(solution)/shard_map/ppermute | solution.py:24
  146.2 0.7 collective-permute-done.14
  149.7 1.0 pad_maximum_fusion.1
  150.7 6.9 %all-to-all-start = ((bf16[8,240,256]{2,1,0:T(8,128)(2,1)}), bf16[8,240,256]{2,1,0:T(8,128)(2,1)S(1)}, u32[]{:S(2)}, u32[]{:S(2)}) async-start(bf16[8,240,256]{2,1,0:T(8,128)(2,1)} %pad_maximum_fusion.1), calls=%async_computation | async-start | bytes 1966080 | tf_op jit(solution)/shard_map/all_to_all | solution.py:273
  157.7 1.9 collective-permute-start.16
  159.6 1.9 collective-permute-start.17
  161.6 4.6 %collective-permute-start.18 = (bf16[4,224,128]{2,1,0:T(8,128)(2,1)S(1)}, bf16[4,224,128]{2,1,0:T(8,128)(2,1)S(1)}, u32[]{:S(2)}, u32[]{:S(2)}) collective-permute-start(bf16[4,224,128]{2,1,0:T(8,128)(2,1)S(1)} %pad_maximum_fusion.15), channel_id=1, source_target_pairs={{0,96},{16,112},{32,0},{48,16},{64,32},{80,48},{96,64},{112,80},{1... | collective-permute-start | bytes 688136 | tf_op jit(solution)/shard_map/ppermute | solution.py:46
  166.2 0.8 dynamic_slice.81
  167.0 1.0 collective-permute-done.16
  168.0 5.5 %collective-permute-done.17 = bf16[4,224,128]{2,1,0:T(8,128)(2,1)S(1)} collective-permute-done((bf16[4,224,128]{2,1,0:T(8,128)(2,1)S(1)}, bf16[4,224,128]{2,1,0:T(8,128)(2,1)S(1)}, u32[]{:S(2)}, u32[]{:S(2)}) %collective-permute-start.17) | collective-permute-done | bytes 229408 | tf_op jit(solution)/shard_map/ppermute | solution.py:46
  174.4 5.5 %collective-permute-start.22 = (bf16[224,128]{1,0:T(8,128)(2,1)S(1)}, bf16[224,128]{1,0:T(8,128)(2,1)S(1)}, u32[]{:S(2)}, u32[]{:S(2)}) collective-permute-start(bf16[224,128]{1,0:T(8,128)(2,1)S(1)} %get-tuple-element.61), channel_id=1, source_target_pairs={{0,136},{1,137},{2,138},{3,139},{4,140},{5,141},{6,142},{7,143},{8... | collective-permute-start | bytes 172040 | tf_op jit(solution)/shard_map/ppermute | solution.py:58
  179.9 1.9 collective-permute-start.21
  181.8 6.1 %collective-permute-start.20 = (bf16[224,128]{1,0:T(8,128)(2,1)S(1)}, bf16[224,128]{1,0:T(8,128)(2,1)S(1)}, u32[]{:S(2)}, u32[]{:S(2)}) collective-permute-start(bf16[224,128]{1,0:T(8,128)(2,1)S(1)} %get-tuple-element.63), channel_id=1, source_target_pairs={{0,128},{1,129},{2,130},{3,131},{4,132},{5,133},{6,134},{7,135},{8... | collective-permute-start | bytes 172040 | tf_op jit(solution)/shard_map/ppermute | solution.py:58
  187.9 1.7 collective-permute-done.20
  189.6 0.7 add_bitcast_fusion
  190.5 4.1 %collective-permute-start.15 = (f32[224,128]{1,0:T(8,128)S(1)}, f32[224,128]{1,0:T(8,128)S(1)}, u32[]{:S(2)}, u32[]{:S(2)}) collective-permute-start(f32[224,128]{1,0:T(8,128)S(1)} %get-tuple-element.58), channel_id=1, source_target_pairs={{0,16},{16,0},{32,48},{48,32},{64,80},{80,64},{96,112},{112,96},{1... | collective-permute-start | bytes 344072 | tf_op jit(solution)/shard_map/ppermute | solution.py:24
  194.6 0.9 collective-permute-done.15
  195.5 0.8 fusion.51
  (145 shorter events, 14.3 us)
Async XLA Ops:
  7.2 76.7 %all-gather.3.cloned.1.call-start = ((), (), s32[]{:S(2)}) async-start(), calls=%async_computation.1 | async-start | bytes 2064384 | tf_op jit(solution)/shard_map/all_gather | solution.py:154
  8.2 13.2 %collective-permute-start.1 = (bf16[224,256]{1,0:T(8,128)(2,1)S(1)}, bf16[224,256]{1,0:T(8,128)(2,1)S(1)}, u32[]{:S(2)}, u32[]{:S(2)}) collective-permute-start(bf16[224,256]{1,0:T(8,128)(2,1)S(1)} %get-tuple-element.65), channel_id=1, source_target_pairs={{0,16},{16,0},{32,48},{48,32},{64,80},{80,64},{96,112},{112,96},{1... | collective-permute-start | bytes 344072 | tf_op jit(solution)/shard_map/ppermute | solution.py:24
  18.0 13.0 %collective-permute-start = (bf16[224,512]{1,0:T(8,128)(2,1)S(1)}, bf16[224,512]{1,0:T(8,128)(2,1)S(1)}, u32[]{:S(2)}, u32[]{:S(2)}) collective-permute-start(bf16[224,512]{1,0:T(8,128)(2,1)S(1)} %pad_maximum_fusion.11), channel_id=1, source_target_pairs={{0,0},{1,1},{2,2},{3,3},{4,4},{5,5},{6,6},{7,7},{8,256},{9,257},{1... | collective-permute-start | bytes 688136 | tf_op jit(solution)/shard_map/ppermute | solution.py:58
  22.7 8.3 %collective-permute-start.4 = (f32[2,128]{1,0:T(2,128)S(1)}, f32[2,128]{1,0:T(2,128)S(1)}, u32[]{:S(2)}, u32[]{:S(2)}) collective-permute-start(f32[2,128]{1,0:T(2,128)S(1)} %pad_maximum_fusion.22), channel_id=1, source_target_pairs={{0,8},{1,9},{2,10},{3,11},{4,12},{5,13},{6,14},{7,15},{8,0},{9,1},... | collective-permute-start | bytes 3080 | tf_op jit(solution)/shard_map/ppermute | solution.py:40
  48.5 9.3 %collective-permute-start.5 = (f32[2,128]{1,0:T(2,128)S(1)}, f32[2,128]{1,0:T(2,128)S(1)}, u32[]{:S(2)}, u32[]{:S(2)}) collective-permute-start(f32[2,128]{1,0:T(2,128)S(1)} %pad_maximum_fusion.23), channel_id=1, source_target_pairs={{0,1},{1,0},{2,3},{3,2},{4,5},{5,4},{6,7},{7,6},{8,9},{9,8},{10,11... | collective-permute-start | bytes 3080 | tf_op jit(solution)/shard_map/ppermute | solution.py:35
  51.4 32.5 %collective-permute-start.3 = (bf16[4,224,512]{2,1,0:T(8,128)(2,1)S(1)}, bf16[4,224,512]{2,1,0:T(8,128)(2,1)S(1)}, u32[]{:S(2)}, u32[]{:S(2)}) collective-permute-start(bf16[4,224,512]{2,1,0:T(8,128)(2,1)S(1)} %bitcast.162), channel_id=1, source_target_pairs={{0,96},{16,112},{32,0},{48,16},{64,32},{80,48},{96,64},{112,80},{1... | collective-permute-start | bytes 2752520 | tf_op jit(solution)/shard_map/ppermute | solution.py:46
  55.8 28.1 %collective-permute-start.2 = (bf16[4,224,512]{2,1,0:T(8,128)(2,1)S(1)}, bf16[4,224,512]{2,1,0:T(8,128)(2,1)S(1)}, u32[]{:S(2)}, u32[]{:S(2)}) collective-permute-start(bf16[4,224,512]{2,1,0:T(8,128)(2,1)S(1)} %bitcast.163), channel_id=1, source_target_pairs={{0,32},{16,48},{32,64},{48,80},{64,96},{80,112},{96,0},{112,16},{1... | collective-permute-start | bytes 2752520 | tf_op jit(solution)/shard_map/ppermute | solution.py:46
  57.8 7.3 %collective-permute-start.6 = (f32[2,128]{1,0:T(2,128)S(1)}, f32[2,128]{1,0:T(2,128)S(1)}, u32[]{:S(2)}, u32[]{:S(2)}) collective-permute-start(f32[2,128]{1,0:T(2,128)S(1)} %pad_maximum_fusion.24), channel_id=1, source_target_pairs={{0,2},{1,3},{2,0},{3,1},{4,6},{5,7},{6,4},{7,5},{8,10},{9,11},{10,... | collective-permute-start | bytes 3080 | tf_op jit(solution)/shard_map/ppermute | solution.py:35
  65.1 8.9 %collective-permute-start.7 = (f32[2,128]{1,0:T(2,128)S(1)}, f32[2,128]{1,0:T(2,128)S(1)}, u32[]{:S(2)}, u32[]{:S(2)}) collective-permute-start(f32[2,128]{1,0:T(2,128)S(1)} %pad_maximum_fusion.25), channel_id=1, source_target_pairs={{0,4},{1,5},{2,6},{3,7},{4,0},{5,1},{6,2},{7,3},{8,12},{9,13},{10,... | collective-permute-start | bytes 3080 | tf_op jit(solution)/shard_map/ppermute | solution.py:35
  74.0 9.8 %collective-permute-start.8 = (f32[2,128]{1,0:T(2,128)S(1)}, f32[2,128]{1,0:T(2,128)S(1)}, u32[]{:S(2)}, u32[]{:S(2)}) collective-permute-start(f32[2,128]{1,0:T(2,128)S(1)} %pad_maximum_fusion.26), channel_id=1, source_target_pairs={{0,16},{16,0},{32,48},{48,32},{64,80},{80,64},{96,112},{112,96},{1... | collective-permute-start | bytes 3080 | tf_op jit(solution)/shard_map/ppermute | solution.py:24
  86.4 1.2 slice-start
  88.2 14.4 %collective-permute-start.10 = (bf16[2,224,512]{2,1,0:T(8,128)(2,1)S(1)}, bf16[2,224,512]{2,1,0:T(8,128)(2,1)S(1)}, u32[]{:S(2)}, u32[]{:S(2)}) collective-permute-start(bf16[2,224,512]{2,1,0:T(8,128)(2,1)S(1)} %get-tuple-element.33), channel_id=1, source_target_pairs={{0,96},{16,112},{32,0},{48,16},{64,32},{80,48},{96,64},{112,80},{1... | collective-permute-start | bytes 1376264 | tf_op jit(solution)/shard_map/ppermute | solution.py:46
  93.1 14.6 %collective-permute-start.9 = (bf16[2,224,512]{2,1,0:T(8,128)(2,1)S(1)}, bf16[2,224,512]{2,1,0:T(8,128)(2,1)S(1)}, u32[]{:S(2)}, u32[]{:S(2)}) collective-permute-start(bf16[2,224,512]{2,1,0:T(8,128)(2,1)S(1)} %get-tuple-element.34), channel_id=1, source_target_pairs={{0,32},{16,48},{32,64},{48,80},{64,96},{80,112},{96,0},{112,16},{1... | collective-permute-start | bytes 1376264 | tf_op jit(solution)/shard_map/ppermute | solution.py:46
  108.9 4.9 %collective-permute-start.11 = (f32[2,136,512]{2,1,0:T(8,128)S(1)}, f32[2,136,512]{2,1,0:T(8,128)S(1)}, u32[]{:S(2)}, u32[]{:S(2)}) collective-permute-start(f32[2,136,512]{2,1,0:T(8,128)S(1)} %pad_maximum_fusion.3), channel_id=1, source_target_pairs={{0,16},{16,0},{32,48},{48,32},{64,80},{80,64},{96,112},{112,96},{1... | collective-permute-start | bytes 1671176 | tf_op jit(solution)/shard_map/ppermute | solution.py:24
  113.9 14.6 %copy-start.2 = (f32[384]{0:T(512)S(1)}, f32[384]{0:T(512)}, u32[]{:S(2)}) copy-start(f32[384]{0:T(512)} %param.11) | copy-start | bytes 4612
  114.0 14.4 %collective-permute-start.12 = (bf16[144,512]{1,0:T(8,128)(2,1)S(1)}, bf16[144,512]{1,0:T(8,128)(2,1)S(1)}, u32[]{:S(2)}, u32[]{:S(2)}) collective-permute-start(bf16[144,512]{1,0:T(8,128)(2,1)S(1)} %pad_maximum_fusion.16), channel_id=1, source_target_pairs={{0,8},{1,9},{2,10},{3,11},{4,12},{5,13},{6,14},{7,15},{8,0},{9,1},... | collective-permute-start | bytes 442376 | tf_op jit(solution)/shard_map/ppermute | solution.py:40
  129.9 12.9 %collective-permute-start.13 = (bf16[144,512]{1,0:T(8,128)(2,1)S(1)}, bf16[144,512]{1,0:T(8,128)(2,1)S(1)}, u32[]{:S(2)}, u32[]{:S(2)}) collective-permute-start(bf16[144,512]{1,0:T(8,128)(2,1)S(1)} %fusion.38), channel_id=1, source_target_pairs={{0,8},{1,9},{2,10},{3,11},{4,12},{5,13},{6,14},{7,15},{8,0},{9,1},... | collective-permute-start | bytes 442376 | tf_op jit(solution)/shard_map/ppermute | solution.py:40
  143.0 3.8 %collective-permute-start.14 = (bf16[2,144,512]{2,1,0:T(8,128)(2,1)S(1)}, bf16[2,144,512]{2,1,0:T(8,128)(2,1)S(1)}, u32[]{:S(2)}, u32[]{:S(2)}) collective-permute-start(bf16[2,144,512]{2,1,0:T(8,128)(2,1)S(1)} %fusion.18), channel_id=1, source_target_pairs={{0,16},{16,0},{32,48},{48,32},{64,80},{80,64},{96,112},{112,96},{1... | collective-permute-start | bytes 884744 | tf_op jit(solution)/shard_map/ppermute | solution.py:24
  145.8 1.5 copy-start
  150.7 39.6 %all-to-all-start = ((bf16[8,240,256]{2,1,0:T(8,128)(2,1)}), bf16[8,240,256]{2,1,0:T(8,128)(2,1)S(1)}, u32[]{:S(2)}, u32[]{:S(2)}) async-start(bf16[8,240,256]{2,1,0:T(8,128)(2,1)} %pad_maximum_fusion.1), calls=%async_computation | async-start | bytes 1966080 | tf_op jit(solution)/shard_map/all_to_all | solution.py:273
  157.7 10.3 %collective-permute-start.16 = (bf16[4,224,128]{2,1,0:T(8,128)(2,1)S(1)}, bf16[4,224,128]{2,1,0:T(8,128)(2,1)S(1)}, u32[]{:S(2)}, u32[]{:S(2)}) collective-permute-start(bf16[4,224,128]{2,1,0:T(8,128)(2,1)S(1)} %pad_maximum_fusion.13), channel_id=1, source_target_pairs={{0,64},{16,80},{32,96},{48,112},{64,0},{80,16},{96,32},{112,48},{1... | collective-permute-start | bytes 688136 | tf_op jit(solution)/shard_map/ppermute | solution.py:46
  159.6 13.9 %collective-permute-start.17 = (bf16[4,224,128]{2,1,0:T(8,128)(2,1)S(1)}, bf16[4,224,128]{2,1,0:T(8,128)(2,1)S(1)}, u32[]{:S(2)}, u32[]{:S(2)}) collective-permute-start(bf16[4,224,128]{2,1,0:T(8,128)(2,1)S(1)} %pad_maximum_fusion.14), channel_id=1, source_target_pairs={{0,32},{16,48},{32,64},{48,80},{64,96},{80,112},{96,0},{112,16},{1... | collective-permute-start | bytes 688136 | tf_op jit(solution)/shard_map/ppermute | solution.py:46
  161.6 11.9 %collective-permute-start.18 = (bf16[4,224,128]{2,1,0:T(8,128)(2,1)S(1)}, bf16[4,224,128]{2,1,0:T(8,128)(2,1)S(1)}, u32[]{:S(2)}, u32[]{:S(2)}) collective-permute-start(bf16[4,224,128]{2,1,0:T(8,128)(2,1)S(1)} %pad_maximum_fusion.15), channel_id=1, source_target_pairs={{0,96},{16,112},{32,0},{48,16},{64,32},{80,48},{96,64},{112,80},{1... | collective-permute-start | bytes 688136 | tf_op jit(solution)/shard_map/ppermute | solution.py:46
  167.0 28.5 %copy-start.1 = (bf16[128,448]{0,1:T(8,128)(2,1)S(1)}, bf16[128,448]{0,1:T(8,128)(2,1)}, u32[]{:S(2)}) copy-start(bf16[128,448]{0,1:T(8,128)(2,1)} %param.7) | copy-start | bytes 344068
  173.7 14.2 %collective-permute-start.19 = (bf16[224,128]{1,0:T(8,128)(2,1)S(1)}, bf16[224,128]{1,0:T(8,128)(2,1)S(1)}, u32[]{:S(2)}, u32[]{:S(2)}) collective-permute-start(bf16[224,128]{1,0:T(8,128)(2,1)S(1)} %get-tuple-element.60), channel_id=1, source_target_pairs={{0,0},{1,1},{2,2},{3,3},{4,4},{5,5},{6,6},{7,7},{8,256},{9,257},{1... | collective-permute-start | bytes 172040 | tf_op jit(solution)/shard_map/ppermute | solution.py:58
  174.4 13.6 %collective-permute-start.22 = (bf16[224,128]{1,0:T(8,128)(2,1)S(1)}, bf16[224,128]{1,0:T(8,128)(2,1)S(1)}, u32[]{:S(2)}, u32[]{:S(2)}) collective-permute-start(bf16[224,128]{1,0:T(8,128)(2,1)S(1)} %get-tuple-element.61), channel_id=1, source_target_pairs={{0,136},{1,137},{2,138},{3,139},{4,140},{5,141},{6,142},{7,143},{8... | collective-permute-start | bytes 172040 | tf_op jit(solution)/shard_map/ppermute | solution.py:58
  179.9 8.1 %collective-permute-start.21 = (bf16[224,128]{1,0:T(8,128)(2,1)S(1)}, bf16[224,128]{1,0:T(8,128)(2,1)S(1)}, u32[]{:S(2)}, u32[]{:S(2)}) collective-permute-start(bf16[224,128]{1,0:T(8,128)(2,1)S(1)} %get-tuple-element.62), channel_id=1, source_target_pairs={{0,8},{1,9},{2,10},{3,11},{4,12},{5,13},{6,14},{7,15},{8,264},{9,2... | collective-permute-start | bytes 172040 | tf_op jit(solution)/shard_map/ppermute | solution.py:58
  181.8 7.8 %collective-permute-start.20 = (bf16[224,128]{1,0:T(8,128)(2,1)S(1)}, bf16[224,128]{1,0:T(8,128)(2,1)S(1)}, u32[]{:S(2)}, u32[]{:S(2)}) collective-permute-start(bf16[224,128]{1,0:T(8,128)(2,1)S(1)} %get-tuple-element.63), channel_id=1, source_target_pairs={{0,128},{1,129},{2,130},{3,131},{4,132},{5,133},{6,134},{7,135},{8... | collective-permute-start | bytes 172040 | tf_op jit(solution)/shard_map/ppermute | solution.py:58
  190.5 5.1 %collective-permute-start.15 = (f32[224,128]{1,0:T(8,128)S(1)}, f32[224,128]{1,0:T(8,128)S(1)}, u32[]{:S(2)}, u32[]{:S(2)}) collective-permute-start(f32[224,128]{1,0:T(8,128)S(1)} %get-tuple-element.58), channel_id=1, source_target_pairs={{0,16},{16,0},{32,48},{48,32},{64,80},{80,64},{96,112},{112,96},{1... | collective-permute-start | bytes 344072 | tf_op jit(solution)/shard_map/ppermute | solution.py:24
Sparse Core Ops, SparseCore 0:
  22.4 40.6 all-gather.2

commit v15 on v14

--- a/solution.py
+++ b/solution.py
@@ -28,11 +28,6 @@
     n = lax.axis_size("tensor")
     pairs = [(i, i - i % Z_COUNT + (i + step) % Z_COUNT) for i in range(n)]
     return lax.ppermute(x, "tensor", pairs)
-
-
-def swap_z(x, bit):
-    n = lax.axis_size("tensor")
-    return lax.ppermute(x, "tensor", [(i, i ^ bit) for i in range(n)])
 
 
 def swap_far(x):
@@ -164,18 +159,16 @@
             ]
         )
 
-    _, slice_f = lax.optimization_barrier((block, hidden_t.astype(f32)))
-    mean_part = jnp.mean(slice_f, axis=0)
-    stats = jnp.stack([mean_part, jnp.sum((slice_f - mean_part) ** 2, axis=0)])
-    stats = merge(stats, swap_far(stats), width)
-    _, stats = lax.optimization_barrier((column, stats))
-    for bit in (1, 2, 4):
-        stats = merge(stats, swap_z(stats, bit), 2 * width * bit)
-    stats = jnp.stack([stats[0], lax.rsqrt(stats[1] / depth + norm_eps)])
-    stats = jnp.concatenate([stats, swap_cores(stats)], axis=1)
-
-    blocks, (rows, stats) = x_gather(column, x, (rows, stats))
-    mean, inv_std = stats
+    hidden = rows[:, : 2 * SEQ].astype(f32)
+    mean_part = jnp.sum(hidden, axis=0) / quarter
+    stats = jnp.stack([mean_part, jnp.sum((hidden - mean_part) ** 2, axis=0)])
+    stats = merge(stats, swap_far(stats), quarter)
+    stats_other = swap_cores(stats)
+    stats_other = jnp.concatenate([stats_other[:, SEQ:], stats_other[:, :SEQ]], axis=1)
+    mean, square = merge(stats, stats_other, 2 * quarter)
+    inv_std = lax.rsqrt(square / depth + norm_eps)
+
+    blocks, (rows, mean, inv_std) = x_gather(column, x, (rows, mean, inv_std))
     hidden = rows[:, : 2 * SEQ].astype(f32)
     grads = rows[:, 2 * SEQ :]
 

time: 204 us -> 201 us (0.985)
  waiting for transfers between devices: 49.2 us -> 31.4 us
  blocking collectives: 17.4 us -> 26.6 us
  local copies, waits for them, and re-layouts: 4.14 us -> 9.77 us
    ppermute x3, waiting for transfers between devices: 25.9 us -> 7.22 us  [swap_far(): return lax.ppermute(x, 'tensor', [(i, (i + Z_COUNT) % n) for i in range(n)])]
    ppermute x3 -> x0, starting transfers between devices: 16.8 us -> none  [swap_z(): return lax.ppermute(x, 'tensor', [(i, i ^ bit) for i in range(n)])]
    ppermute x3, starting transfers between devices: 9.3 us -> 21 us  [swap_far(): return lax.ppermute(x, 'tensor', [(i, (i + Z_COUNT) % n) for i in range(n)])]
    all_gather x1, blocking collectives: 17.4 us -> 26.6 us  [body(): column = lax.all_gather(weight_block, 'dp', axis=0, axis_index_groups=lines)]
    ppermute x5, starting transfers between devices: 14.9 us -> 20.3 us  [along_y(): return lax.ppermute(x, ('dp', 'tensor'), pairs)]
    all_gather x1, waiting for transfers between devices: 0.02 us -> 3.94 us  [body(): lax.all_gather(block, 'tensor', axis=0, tiled=True, axis_index_groups=rings)]
    unnamed x10 -> x14, local copies, waits for them, and re-layouts: 0.84 us -> 3.76 us
    reduce_sum x2, other arithmetic: 0.15 us -> 3.04 us  [the longest x1 1.56 us: body(): mean_part = jnp.sum(hidden, axis=0) / quarter]
  transfers between devices with their start and end apart: 25 -> 22, of which waited for: 14 -> 12; matrix products, arithmetic and copies ran while one was open for 5% -> 8% of each run, Pallas kernels for 0% -> 0%
where the time goes in v15:
time: 201 us; the launch traced here: 200 us
  starting transfers between devices  97.9 us (49%)
  waiting for transfers between devices  31.4 us (16%)
  blocking collectives  26.6 us (13%)
  between operations  15.3 us (8%)
  other arithmetic  11.3 us (6%)
  local copies, waits for them, and re-layouts  9.77 us (5%)
  matrix products  7.84 us (4%)
    ppermute x5, starting transfers between devices, swap_cores(): return lax.ppermute(x, 'dp', [(i, i ^ 1) for i in range(n)])  27.6 us
    all_gather x1, blocking collectives, body(): column = lax.all_gather(weight_block, 'dp', axis=0, axis_index_groups=lines)  26.6 us
    ppermute x3, starting transfers between devices, swap_far(): return lax.ppermute(x, 'tensor', [(i, (i + Z_COUNT) % n) for i in range(n)])  21 us
    ppermute x7, starting transfers between devices, shift_x(): lax.ppermute(x, 'dp', [(i, i - i % row + (i + 2 * step) % row) for i in r...  20.9 us
    ppermute x5, starting transfers between devices, along_y(): return lax.ppermute(x, ('dp', 'tensor'), pairs)  20.3 us
    ppermute x7, waiting for transfers between devices, shift_x(): lax.ppermute(x, 'dp', [(i, i - i % row + (i + 2 * step) % row) for i in r...  17.1 us
    all_to_all x1, starting transfers between devices, body(): lax.all_to_all(payload, 'tensor', 0, 0, tiled=True, axis_index_groups=rings)  8.05 us
    dot_general x26, matrix products, dot(): return lax.dot_general(a, b, (dims, ((), ())), preferred_element_type=f32)  7.84 us
  transfers between devices with their start and end apart: 22, of which 12 were waited for; matrix products, arithmetic and copies ran while one was open for 8% of the time, Pallas kernels for 0%

profile of v15, /device:TPU:1, one launch (start us, length us, event | category | flops | bytes accessed | tf_op | source)
XLA Modules:
  0.0 200.1 jit_solution(3028286501479074484)
XLA Ops:
  7.2 1.0 broadcast_select_fusion.1
  8.3 8.8 %collective-permute-start.1 = (bf16[224,256]{1,0:T(8,128)(2,1)S(1)}, bf16[224,256]{1,0:T(8,128)(2,1)S(1)}, u32[]{:S(2)}, u32[]{:S(2)}) collective-permute-start(bf16[224,256]{1,0:T(8,128)(2,1)S(1)} %get-tuple-element.63), channel_id=1, source_target_pairs={{0,16},{16,0},{32,48},{48,32},{64,80},{80,64},{96,112},{112,96},{1... | collective-permute-start | bytes 344072 | tf_op jit(solution)/shard_map/ppermute | solution.py:24
  17.1 0.9 collective-permute-done.1
  18.0 0.7 pad_maximum_fusion.12
  18.7 1.0 pad_maximum_fusion.11
  19.7 0.7 collective-permute-start
  21.0 26.6 %all-gather = bf16[896,512]{1,0:T(8,128)(2,1)S(1)} all-gather(bf16[224,512]{1,0:T(8,128)(2,1)S(1)} %collective-permute-done), channel_id=2, replica_groups={{0,128,256,384},{16,144,272,400},{32,160,288,416},{48,176,304,432},{64,..., dimensions={0}, use_global_device_ids=true | all-gather | bytes 1146880 | tf_op jit(solution)/shard_map/all_gather | solution.py:151
  47.6 4.4 %collective-permute-start.3 = (bf16[4,224,512]{2,1,0:T(8,128)(2,1)S(1)}, bf16[4,224,512]{2,1,0:T(8,128)(2,1)}, u32[]{:S(2)}, u32[]{:S(2)}) collective-permute-start(bf16[4,224,512]{2,1,0:T(8,128)(2,1)S(1)} %bitcast.156), channel_id=1, source_target_pairs={{0,96},{16,112},{32,0},{48,16},{64,32},{80,48},{96,64},{112,80},{1... | collective-permute-start | bytes 2752520 | tf_op jit(solution)/shard_map/ppermute | solution.py:41
  52.0 1.9 collective-permute-start.2
  53.9 3.9 %all-gather.3.cloned.1.call-done = bf16[1792,512]{1,0:T(8,128)(2,1)} async-done(((bf16[224,512]{1,0:T(8,128)(2,1)}), bf16[1792,512]{1,0:T(8,128)(2,1)}) %all-gather.3.cloned.1.call-update) | async-done | bytes 1835024 | tf_op jit(solution)/shard_map/all_gather | solution.py:149
  57.9 1.6 convert_reduce_fusion
  59.5 1.5 fusion.2
  60.9 6.6 %collective-permute-start.4 = (f32[2,256]{1,0:T(2,128)S(1)}, f32[2,256]{1,0:T(2,128)S(1)}, u32[]{:S(2)}, u32[]{:S(2)}) collective-permute-start(f32[2,256]{1,0:T(2,128)S(1)} %pad_maximum_fusion.20), channel_id=1, source_target_pairs={{0,8},{1,9},{2,10},{3,11},{4,12},{5,13},{6,14},{7,15},{8,0},{9,1},... | collective-permute-start | bytes 6152 | tf_op jit(solution)/shard_map/ppermute | solution.py:35
  67.6 1.5 collective-permute-done.4
  69.2 7.6 %collective-permute-start.5 = (f32[2,256]{1,0:T(2,128)S(1)}, f32[2,256]{1,0:T(2,128)S(1)}, u32[]{:S(2)}, u32[]{:S(2)}) collective-permute-start(f32[2,256]{1,0:T(2,128)S(1)} %pad_maximum_fusion.21), channel_id=1, source_target_pairs={{0,16},{16,0},{32,48},{48,32},{64,80},{80,64},{96,112},{112,96},{1... | collective-permute-start | bytes 6152 | tf_op jit(solution)/shard_map/ppermute | solution.py:24
  77.7 1.1 add_convert_fusion
  80.9 1.2 fusion.87
  82.1 4.3 %collective-permute-start.7 = (bf16[2,224,512]{2,1,0:T(8,128)(2,1)S(1)}, bf16[2,224,512]{2,1,0:T(8,128)(2,1)S(1)}, u32[]{:S(2)}, u32[]{:S(2)}) collective-permute-start(bf16[2,224,512]{2,1,0:T(8,128)(2,1)S(1)} %get-tuple-element.31), channel_id=1, source_target_pairs={{0,96},{16,112},{32,0},{48,16},{64,32},{80,48},{96,64},{112,80},{1... | collective-permute-start | bytes 1376264 | tf_op jit(solution)/shard_map/ppermute | solution.py:41
  86.5 1.2 fusion.88
  87.7 1.9 collective-permute-start.6
  92.0 4.0 %collective-permute-done.7 = bf16[2,224,512]{2,1,0:T(8,128)(2,1)S(1)} collective-permute-done((bf16[2,224,512]{2,1,0:T(8,128)(2,1)S(1)}, bf16[2,224,512]{2,1,0:T(8,128)(2,1)S(1)}, u32[]{:S(2)}, u32[]{:S(2)}) %collective-permute-start.7) | collective-permute-done | bytes 458784 | tf_op jit(solution)/shard_map/ppermute | solution.py:41
  96.4 5.8 %collective-permute-done.6 = bf16[2,224,512]{2,1,0:T(8,128)(2,1)S(1)} collective-permute-done((bf16[2,224,512]{2,1,0:T(8,128)(2,1)S(1)}, bf16[2,224,512]{2,1,0:T(8,128)(2,1)S(1)}, u32[]{:S(2)}, u32[]{:S(2)}) %collective-permute-start.6) | collective-permute-done | bytes 458784 | tf_op jit(solution)/shard_map/ppermute | solution.py:41
  103.4 3.4 %collective-permute-start.8 = (f32[2,136,512]{2,1,0:T(8,128)S(1)}, f32[2,136,512]{2,1,0:T(8,128)S(1)}, u32[]{:S(2)}, u32[]{:S(2)}) collective-permute-start(f32[2,136,512]{2,1,0:T(8,128)S(1)} %pad_maximum_fusion.3), channel_id=1, source_target_pairs={{0,16},{16,0},{32,48},{48,32},{64,80},{80,64},{96,112},{112,96},{1... | collective-permute-start | bytes 1671176 | tf_op jit(solution)/shard_map/ppermute | solution.py:24
  106.8 1.2 bitcast_dynamic-update-slice_fusion
  108.1 1.2 bitcast_dynamic-update-slice_fusion.2
  109.6 7.1 %collective-permute-start.9 = (bf16[144,512]{1,0:T(8,128)(2,1)S(1)}, bf16[144,512]{1,0:T(8,128)(2,1)S(1)}, u32[]{:S(2)}, u32[]{:S(2)}) collective-permute-start(bf16[144,512]{1,0:T(8,128)(2,1)S(1)} %pad_maximum_fusion.16), channel_id=1, source_target_pairs={{0,8},{1,9},{2,10},{3,11},{4,12},{5,13},{6,14},{7,15},{8,0},{9,1},... | collective-permute-start | bytes 442376 | tf_op jit(solution)/shard_map/ppermute | solution.py:35
  116.8 4.0 %collective-permute-done.9 = bf16[144,512]{1,0:T(8,128)(2,1)S(1)} collective-permute-done((bf16[144,512]{1,0:T(8,128)(2,1)S(1)}, bf16[144,512]{1,0:T(8,128)(2,1)S(1)}, u32[]{:S(2)}, u32[]{:S(2)}) %collective-permute-start.9) | collective-permute-done | bytes 147488 | tf_op jit(solution)/shard_map/ppermute | solution.py:35
  122.3 7.2 %collective-permute-start.10 = (bf16[144,512]{1,0:T(8,128)(2,1)S(1)}, bf16[144,512]{1,0:T(8,128)(2,1)S(1)}, u32[]{:S(2)}, u32[]{:S(2)}) collective-permute-start(bf16[144,512]{1,0:T(8,128)(2,1)S(1)} %fusion.40), channel_id=1, source_target_pairs={{0,8},{1,9},{2,10},{3,11},{4,12},{5,13},{6,14},{7,15},{8,0},{9,1},... | collective-permute-start | bytes 442376 | tf_op jit(solution)/shard_map/ppermute | solution.py:35
  129.6 1.2 bitcast_dynamic-update-slice_fusion.1
  130.9 1.7 collective-permute-done.10
  132.8 3.7 %collective-permute-start.11 = (bf16[2,144,512]{2,1,0:T(8,128)(2,1)S(1)}, bf16[2,144,512]{2,1,0:T(8,128)(2,1)S(1)}, u32[]{:S(2)}, u32[]{:S(2)}) collective-permute-start(bf16[2,144,512]{2,1,0:T(8,128)(2,1)S(1)} %fusion.20), channel_id=1, source_target_pairs={{0,16},{16,0},{32,48},{48,32},{64,80},{80,64},{96,112},{112,96},{1... | collective-permute-start | bytes 884744 | tf_op jit(solution)/shard_map/ppermute | solution.py:24
  136.5 1.2 bitcast_dynamic-update-slice_fusion.3
  140.6 1.1 pad_maximum_fusion.1
  141.6 8.1 %all-to-all-start = ((bf16[8,240,256]{2,1,0:T(8,128)(2,1)}), bf16[8,240,256]{2,1,0:T(8,128)(2,1)S(1)}, u32[]{:S(2)}, u32[]{:S(2)}) async-start(bf16[8,240,256]{2,1,0:T(8,128)(2,1)} %pad_maximum_fusion.1), calls=%async_computation | async-start | bytes 1966080 | tf_op jit(solution)/shard_map/all_to_all | solution.py:266
  149.7 1.9 collective-permute-start.13
  151.6 1.9 collective-permute-start.14
  153.6 4.6 %collective-permute-start.15 = (bf16[4,224,128]{2,1,0:T(8,128)(2,1)S(1)}, bf16[4,224,128]{2,1,0:T(8,128)(2,1)S(1)}, u32[]{:S(2)}, u32[]{:S(2)}) collective-permute-start(bf16[4,224,128]{2,1,0:T(8,128)(2,1)S(1)} %pad_maximum_fusion.15), channel_id=1, source_target_pairs={{0,96},{16,112},{32,0},{48,16},{64,32},{80,48},{96,64},{112,80},{1... | collective-permute-start | bytes 688136 | tf_op jit(solution)/shard_map/ppermute | solution.py:41
  158.3 1.8 collective-permute-done.13
  160.0 5.5 %collective-permute-done.14 = bf16[4,224,128]{2,1,0:T(8,128)(2,1)S(1)} collective-permute-done((bf16[4,224,128]{2,1,0:T(8,128)(2,1)S(1)}, bf16[4,224,128]{2,1,0:T(8,128)(2,1)S(1)}, u32[]{:S(2)}, u32[]{:S(2)}) %collective-permute-start.14) | collective-permute-done | bytes 229408 | tf_op jit(solution)/shard_map/ppermute | solution.py:41
  165.7 0.7 collective-permute-start.16
  166.4 9.9 %collective-permute-start.19 = (bf16[224,128]{1,0:T(8,128)(2,1)S(1)}, bf16[224,128]{1,0:T(8,128)(2,1)S(1)}, u32[]{:S(2)}, u32[]{:S(2)}) collective-permute-start(bf16[224,128]{1,0:T(8,128)(2,1)S(1)} %get-tuple-element.59), channel_id=1, source_target_pairs={{0,136},{1,137},{2,138},{3,139},{4,140},{5,141},{6,142},{7,143},{8... | collective-permute-start | bytes 172040 | tf_op jit(solution)/shard_map/ppermute | solution.py:53
  176.3 2.7 %collective-permute-start.18 = (bf16[224,128]{1,0:T(8,128)(2,1)S(1)}, bf16[224,128]{1,0:T(8,128)(2,1)S(1)}, u32[]{:S(2)}, u32[]{:S(2)}) collective-permute-start(bf16[224,128]{1,0:T(8,128)(2,1)S(1)} %get-tuple-element.60), channel_id=1, source_target_pairs={{0,8},{1,9},{2,10},{3,11},{4,12},{5,13},{6,14},{7,15},{8,264},{9,2... | collective-permute-start | bytes 172040 | tf_op jit(solution)/shard_map/ppermute | solution.py:53
  178.9 6.4 %collective-permute-start.17 = (bf16[224,128]{1,0:T(8,128)(2,1)S(1)}, bf16[224,128]{1,0:T(8,128)(2,1)S(1)}, u32[]{:S(2)}, u32[]{:S(2)}) collective-permute-start(bf16[224,128]{1,0:T(8,128)(2,1)S(1)} %get-tuple-element.61), channel_id=1, source_target_pairs={{0,128},{1,129},{2,130},{3,131},{4,132},{5,133},{6,134},{7,135},{8... | collective-permute-start | bytes 172040 | tf_op jit(solution)/shard_map/ppermute | solution.py:53
  185.5 1.1 collective-permute-done.17
  186.6 0.7 add_bitcast_fusion
  187.5 4.1 %collective-permute-start.12 = (f32[224,128]{1,0:T(8,128)S(1)}, f32[224,128]{1,0:T(8,128)S(1)}, u32[]{:S(2)}, u32[]{:S(2)}) collective-permute-start(f32[224,128]{1,0:T(8,128)S(1)} %get-tuple-element.56), channel_id=1, source_target_pairs={{0,16},{16,0},{32,48},{48,32},{64,80},{80,64},{96,112},{112,96},{1... | collective-permute-start | bytes 344072 | tf_op jit(solution)/shard_map/ppermute | solution.py:24
  191.6 0.9 collective-permute-done.12
  192.5 0.8 fusion.53
  (138 shorter events, 12.5 us)
Async XLA Ops:
  7.2 13.3 %copy-start.3 = (f32[7168]{0:T(1024)S(1)}, f32[7168]{0:T(1024)}, u32[]{:S(2)}) copy-start(f32[7168]{0:T(1024)} %param.9) | copy-start | bytes 86020
  7.2 13.4 %copy-start.2 = (f32[7168]{0:T(1024)S(1)}, f32[7168]{0:T(1024)}, u32[]{:S(2)}) copy-start(f32[7168]{0:T(1024)} %param.8) | copy-start | bytes 86020
  7.2 50.7 %all-gather.3.cloned.1.call-start = ((), (), s32[]{:S(2)}) async-start(), calls=%async_computation.1 | async-start | bytes 2064384 | tf_op jit(solution)/shard_map/all_gather | solution.py:149
  8.3 9.7 %collective-permute-start.1 = (bf16[224,256]{1,0:T(8,128)(2,1)S(1)}, bf16[224,256]{1,0:T(8,128)(2,1)S(1)}, u32[]{:S(2)}, u32[]{:S(2)}) collective-permute-start(bf16[224,256]{1,0:T(8,128)(2,1)S(1)} %get-tuple-element.63), channel_id=1, source_target_pairs={{0,16},{16,0},{32,48},{48,32},{64,80},{80,64},{96,112},{112,96},{1... | collective-permute-start | bytes 344072 | tf_op jit(solution)/shard_map/ppermute | solution.py:24
  19.7 1.3 collective-permute-start
  47.6 30.1 %collective-permute-start.3 = (bf16[4,224,512]{2,1,0:T(8,128)(2,1)S(1)}, bf16[4,224,512]{2,1,0:T(8,128)(2,1)}, u32[]{:S(2)}, u32[]{:S(2)}) collective-permute-start(bf16[4,224,512]{2,1,0:T(8,128)(2,1)S(1)} %bitcast.156), channel_id=1, source_target_pairs={{0,96},{16,112},{32,0},{48,16},{64,32},{80,48},{96,64},{112,80},{1... | collective-permute-start | bytes 2752520 | tf_op jit(solution)/shard_map/ppermute | solution.py:41
  52.0 25.7 %collective-permute-start.2 = (bf16[4,224,512]{2,1,0:T(8,128)(2,1)S(1)}, bf16[4,224,512]{2,1,0:T(8,128)(2,1)}, u32[]{:S(2)}, u32[]{:S(2)}) collective-permute-start(bf16[4,224,512]{2,1,0:T(8,128)(2,1)S(1)} %bitcast.157), channel_id=1, source_target_pairs={{0,32},{16,48},{32,64},{48,80},{64,96},{80,112},{96,0},{112,16},{1... | collective-permute-start | bytes 2752520 | tf_op jit(solution)/shard_map/ppermute | solution.py:41
  57.9 19.8 %copy-start = (bf16[1792,512]{1,0:T(8,128)(2,1)S(1)}, bf16[1792,512]{1,0:T(8,128)(2,1)}, u32[]{:S(2)}) copy-start(bf16[1792,512]{1,0:T(8,128)(2,1)} %all-gather.3.cloned.1.call-done) | copy-start | bytes 5505028
  60.9 8.2 %collective-permute-start.4 = (f32[2,256]{1,0:T(2,128)S(1)}, f32[2,256]{1,0:T(2,128)S(1)}, u32[]{:S(2)}, u32[]{:S(2)}) collective-permute-start(f32[2,256]{1,0:T(2,128)S(1)} %pad_maximum_fusion.20), channel_id=1, source_target_pairs={{0,8},{1,9},{2,10},{3,11},{4,12},{5,13},{6,14},{7,15},{8,0},{9,1},... | collective-permute-start | bytes 6152 | tf_op jit(solution)/shard_map/ppermute | solution.py:35
  69.2 8.5 %collective-permute-start.5 = (f32[2,256]{1,0:T(2,128)S(1)}, f32[2,256]{1,0:T(2,128)S(1)}, u32[]{:S(2)}, u32[]{:S(2)}) collective-permute-start(f32[2,256]{1,0:T(2,128)S(1)} %pad_maximum_fusion.21), channel_id=1, source_target_pairs={{0,16},{16,0},{32,48},{48,32},{64,80},{80,64},{96,112},{112,96},{1... | collective-permute-start | bytes 6152 | tf_op jit(solution)/shard_map/ppermute | solution.py:24
  79.1 1.2 slice-start
  82.1 13.9 %collective-permute-start.7 = (bf16[2,224,512]{2,1,0:T(8,128)(2,1)S(1)}, bf16[2,224,512]{2,1,0:T(8,128)(2,1)S(1)}, u32[]{:S(2)}, u32[]{:S(2)}) collective-permute-start(bf16[2,224,512]{2,1,0:T(8,128)(2,1)S(1)} %get-tuple-element.31), channel_id=1, source_target_pairs={{0,96},{16,112},{32,0},{48,16},{64,32},{80,48},{96,64},{112,80},{1... | collective-permute-start | bytes 1376264 | tf_op jit(solution)/shard_map/ppermute | solution.py:41
  87.7 14.6 %collective-permute-start.6 = (bf16[2,224,512]{2,1,0:T(8,128)(2,1)S(1)}, bf16[2,224,512]{2,1,0:T(8,128)(2,1)S(1)}, u32[]{:S(2)}, u32[]{:S(2)}) collective-permute-start(bf16[2,224,512]{2,1,0:T(8,128)(2,1)S(1)} %get-tuple-element.32), channel_id=1, source_target_pairs={{0,32},{16,48},{32,64},{48,80},{64,96},{80,112},{96,0},{112,16},{1... | collective-permute-start | bytes 1376264 | tf_op jit(solution)/shard_map/ppermute | solution.py:41
  103.4 5.9 %collective-permute-start.8 = (f32[2,136,512]{2,1,0:T(8,128)S(1)}, f32[2,136,512]{2,1,0:T(8,128)S(1)}, u32[]{:S(2)}, u32[]{:S(2)}) collective-permute-start(f32[2,136,512]{2,1,0:T(8,128)S(1)} %pad_maximum_fusion.3), channel_id=1, source_target_pairs={{0,16},{16,0},{32,48},{48,32},{64,80},{80,64},{96,112},{112,96},{1... | collective-permute-start | bytes 1671176 | tf_op jit(solution)/shard_map/ppermute | solution.py:24
  109.5 11.4 %copy-start.4 = (f32[384]{0:T(512)S(1)}, f32[384]{0:T(512)}, u32[]{:S(2)}) copy-start(f32[384]{0:T(512)} %param.11) | copy-start | bytes 4612
  109.6 11.3 %collective-permute-start.9 = (bf16[144,512]{1,0:T(8,128)(2,1)S(1)}, bf16[144,512]{1,0:T(8,128)(2,1)S(1)}, u32[]{:S(2)}, u32[]{:S(2)}) collective-permute-start(bf16[144,512]{1,0:T(8,128)(2,1)S(1)} %pad_maximum_fusion.16), channel_id=1, source_target_pairs={{0,8},{1,9},{2,10},{3,11},{4,12},{5,13},{6,14},{7,15},{8,0},{9,1},... | collective-permute-start | bytes 442376 | tf_op jit(solution)/shard_map/ppermute | solution.py:35
  122.3 10.3 %collective-permute-start.10 = (bf16[144,512]{1,0:T(8,128)(2,1)S(1)}, bf16[144,512]{1,0:T(8,128)(2,1)S(1)}, u32[]{:S(2)}, u32[]{:S(2)}) collective-permute-start(bf16[144,512]{1,0:T(8,128)(2,1)S(1)} %fusion.40), channel_id=1, source_target_pairs={{0,8},{1,9},{2,10},{3,11},{4,12},{5,13},{6,14},{7,15},{8,0},{9,1},... | collective-permute-start | bytes 442376 | tf_op jit(solution)/shard_map/ppermute | solution.py:35
  132.8 5.3 %collective-permute-start.11 = (bf16[2,144,512]{2,1,0:T(8,128)(2,1)S(1)}, bf16[2,144,512]{2,1,0:T(8,128)(2,1)S(1)}, u32[]{:S(2)}, u32[]{:S(2)}) collective-permute-start(bf16[2,144,512]{2,1,0:T(8,128)(2,1)S(1)} %fusion.20), channel_id=1, source_target_pairs={{0,16},{16,0},{32,48},{48,32},{64,80},{80,64},{96,112},{112,96},{1... | collective-permute-start | bytes 884744 | tf_op jit(solution)/shard_map/ppermute | solution.py:24
  141.6 45.7 %all-to-all-start = ((bf16[8,240,256]{2,1,0:T(8,128)(2,1)}), bf16[8,240,256]{2,1,0:T(8,128)(2,1)S(1)}, u32[]{:S(2)}, u32[]{:S(2)}) async-start(bf16[8,240,256]{2,1,0:T(8,128)(2,1)} %pad_maximum_fusion.1), calls=%async_computation | async-start | bytes 1966080 | tf_op jit(solution)/shard_map/all_to_all | solution.py:266
  149.7 10.3 %collective-permute-start.13 = (bf16[4,224,128]{2,1,0:T(8,128)(2,1)S(1)}, bf16[4,224,128]{2,1,0:T(8,128)(2,1)S(1)}, u32[]{:S(2)}, u32[]{:S(2)}) collective-permute-start(bf16[4,224,128]{2,1,0:T(8,128)(2,1)S(1)} %pad_maximum_fusion.13), channel_id=1, source_target_pairs={{0,64},{16,80},{32,96},{48,112},{64,0},{80,16},{96,32},{112,48},{1... | collective-permute-start | bytes 688136 | tf_op jit(solution)/shard_map/ppermute | solution.py:41
  151.6 13.9 %collective-permute-start.14 = (bf16[4,224,128]{2,1,0:T(8,128)(2,1)S(1)}, bf16[4,224,128]{2,1,0:T(8,128)(2,1)S(1)}, u32[]{:S(2)}, u32[]{:S(2)}) collective-permute-start(bf16[4,224,128]{2,1,0:T(8,128)(2,1)S(1)} %pad_maximum_fusion.14), channel_id=1, source_target_pairs={{0,32},{16,48},{32,64},{48,80},{64,96},{80,112},{96,0},{112,16},{1... | collective-permute-start | bytes 688136 | tf_op jit(solution)/shard_map/ppermute | solution.py:41
  153.6 11.9 %collective-permute-start.15 = (bf16[4,224,128]{2,1,0:T(8,128)(2,1)S(1)}, bf16[4,224,128]{2,1,0:T(8,128)(2,1)S(1)}, u32[]{:S(2)}, u32[]{:S(2)}) collective-permute-start(bf16[4,224,128]{2,1,0:T(8,128)(2,1)S(1)} %pad_maximum_fusion.15), channel_id=1, source_target_pairs={{0,96},{16,112},{32,0},{48,16},{64,32},{80,48},{96,64},{112,80},{1... | collective-permute-start | bytes 688136 | tf_op jit(solution)/shard_map/ppermute | solution.py:41
  165.5 27.0 %copy-start.1 = (bf16[128,448]{0,1:T(8,128)(2,1)S(1)}, bf16[128,448]{0,1:T(8,128)(2,1)}, u32[]{:S(2)}) copy-start(bf16[128,448]{0,1:T(8,128)(2,1)} %param.7) | copy-start | bytes 344068
  165.7 19.8 %collective-permute-start.16 = (bf16[224,128]{1,0:T(8,128)(2,1)S(1)}, bf16[224,128]{1,0:T(8,128)(2,1)S(1)}, u32[]{:S(2)}, u32[]{:S(2)}) collective-permute-start(bf16[224,128]{1,0:T(8,128)(2,1)S(1)} %get-tuple-element.58), channel_id=1, source_target_pairs={{0,0},{1,1},{2,2},{3,3},{4,4},{5,5},{6,6},{7,7},{8,256},{9,257},{1... | collective-permute-start | bytes 172040 | tf_op jit(solution)/shard_map/ppermute | solution.py:53
  166.4 19.1 %collective-permute-start.19 = (bf16[224,128]{1,0:T(8,128)(2,1)S(1)}, bf16[224,128]{1,0:T(8,128)(2,1)S(1)}, u32[]{:S(2)}, u32[]{:S(2)}) collective-permute-start(bf16[224,128]{1,0:T(8,128)(2,1)S(1)} %get-tuple-element.59), channel_id=1, source_target_pairs={{0,136},{1,137},{2,138},{3,139},{4,140},{5,141},{6,142},{7,143},{8... | collective-permute-start | bytes 172040 | tf_op jit(solution)/shard_map/ppermute | solution.py:53
  176.3 9.2 %collective-permute-start.18 = (bf16[224,128]{1,0:T(8,128)(2,1)S(1)}, bf16[224,128]{1,0:T(8,128)(2,1)S(1)}, u32[]{:S(2)}, u32[]{:S(2)}) collective-permute-start(bf16[224,128]{1,0:T(8,128)(2,1)S(1)} %get-tuple-element.60), channel_id=1, source_target_pairs={{0,8},{1,9},{2,10},{3,11},{4,12},{5,13},{6,14},{7,15},{8,264},{9,2... | collective-permute-start | bytes 172040 | tf_op jit(solution)/shard_map/ppermute | solution.py:53
  178.9 7.7 %collective-permute-start.17 = (bf16[224,128]{1,0:T(8,128)(2,1)S(1)}, bf16[224,128]{1,0:T(8,128)(2,1)S(1)}, u32[]{:S(2)}, u32[]{:S(2)}) collective-permute-start(bf16[224,128]{1,0:T(8,128)(2,1)S(1)} %get-tuple-element.61), channel_id=1, source_target_pairs={{0,128},{1,129},{2,130},{3,131},{4,132},{5,133},{6,134},{7,135},{8... | collective-permute-start | bytes 172040 | tf_op jit(solution)/shard_map/ppermute | solution.py:53
  187.5 5.0 %collective-permute-start.12 = (f32[224,128]{1,0:T(8,128)S(1)}, f32[224,128]{1,0:T(8,128)S(1)}, u32[]{:S(2)}, u32[]{:S(2)}) collective-permute-start(f32[224,128]{1,0:T(8,128)S(1)} %get-tuple-element.56), channel_id=1, source_target_pairs={{0,16},{16,0},{32,48},{48,32},{64,80},{80,64},{96,112},{112,96},{1... | collective-permute-start | bytes 344072 | tf_op jit(solution)/shard_map/ppermute | solution.py:24
Sparse Core Ops, SparseCore 0:
  18.9 38.9 all-gather.2
